TPU v7x, 32 devices: a whole 2x2x4 slice. The times are simulated.
32 devices in a mesh: dp: 8 (over z, y), segment: 4 (over x, core).
Axes of the slice: x: 2, y: 2, z: 4, core: 2. Of those that a mesh axis runs over, the one named last changes fastest.
Arguments:
- images: bfloat16 [32, 16, 16, 384], P('dp'), may hold values from -6 to 6
- cotangent: bfloat16 [32, 16, 16, 384], P('dp'), may hold values from -0.09375 to 0.09375
- kernels: float32 [4, 49, 384], P('segment'), may hold values from -0.875 to 0.875
- norm_gains: float32 [4, 384], P('segment'), may hold values from 0.25 to 1.75
- w_in: bfloat16 [4, 384, 768], P('segment'), may hold values from -0.3125 to 0.3125
- w_out: bfloat16 [4, 768, 384], P('segment'), may hold values from -0.21875 to 0.21875
- scales: float32 [4, 384], P('segment'), may hold values from 0.3 to 1
Outputs:
- grad_kernels: float32 [4, 49, 384], P('segment', None, 'dp')
- grad_gains: float32 [4, 384], P('segment', 'dp')
- grad_w_in: float32 [4, 384, 768], P('segment', 'dp')
- grad_w_out: float32 [4, 768, 384], P('segment', None, 'dp')
- grad_scales: float32 [4, 384], P('segment', 'dp')
All inputs are finite; a program needn't handle non-finite values.
Results may differ from a plain program's by a relative error of at most 0.034.
Values may be sent and summed in bfloat16 or wider, within the bound.
No kernel may reach another device: no remote copies, remote signals or barrier semaphores. Data moves between devices by JAX's collectives and lax.ppermute only.
A program may use at most 64 MiB of HBM per device.

v0:
```python
import jax
import jax.numpy as jnp
from jax import lax
from jax.sharding import PartitionSpec as P

EPS = 1e-06


def passed_along(value, axis, by):
    length = lax.axis_size(axis)
    pairs = [(i, i + by) for i in range(length) if 0 <= i + by < length]
    return lax.ppermute(value, axis, pairs)


def depthwise(padded, kernel, map_rows, map_cols):
    running = jnp.zeros((padded.shape[0], map_rows, map_cols, padded.shape[3]), jnp.float32)
    for tap_row in range(7):
        for tap_col in range(7):
            running = (
                running
                + kernel[tap_row * 7 + tap_col]
                * padded[:, tap_row : tap_row + map_rows, tap_col : tap_col + map_cols, :]
            )
    return running


def forward_parts(inputs, kernel, layernorm_gain_vector, w_in, w_out, layer_scale):
    map_rows, map_cols, channels = (inputs.shape[1], inputs.shape[2], inputs.shape[3])
    padded = jnp.pad(inputs.astype(jnp.float32), ((0, 0), (3, 3), (3, 3), (0, 0)))
    conv_out = depthwise(padded, kernel, map_rows, map_cols)
    flat_rows = conv_out.reshape(-1, channels)
    center = flat_rows - jnp.mean(flat_rows, axis=1, keepdims=True)
    inverse_deviation = lax.rsqrt(jnp.mean(center * center, axis=1, keepdims=True) + EPS)
    normalized_map = center * inverse_deviation
    normed_low = (normalized_map * layernorm_gain_vector).astype(jnp.bfloat16)
    pre_gelu = jnp.dot(normed_low, w_in, preferred_element_type=jnp.float32)
    hidden = jax.nn.gelu(pre_gelu).astype(jnp.bfloat16)
    branch = jnp.dot(hidden, w_out, preferred_element_type=jnp.float32)
    residual = inputs.astype(jnp.float32).reshape(flat_rows.shape)
    result = (residual + layer_scale * branch).astype(jnp.bfloat16).reshape(inputs.shape)
    return (
        result,
        (padded, normalized_map, inverse_deviation, normed_low, pre_gelu, hidden, branch),
    )


def backward_parts(grad_map, stored, kernel, layernorm_gain_vector, w_in, w_out, layer_scale):
    padded, normalized_map, inverse_deviation, normed_low, pre_gelu, hidden, branch = stored
    grid_shape = grad_map.shape
    map_rows, map_cols, channels = (grid_shape[1], grid_shape[2], grid_shape[3])
    grad_out = grad_map.astype(jnp.float32).reshape(-1, channels)
    grad_scale = jnp.sum(grad_out * branch, axis=0)
    grad_branch = (grad_out * layer_scale).astype(jnp.bfloat16)
    grad_wout = jnp.dot(hidden.T, grad_branch, preferred_element_type=jnp.float32)
    grad_hidden = jnp.dot(grad_branch, w_out.T, preferred_element_type=jnp.float32)
    grad_pre = jax.vjp(jax.nn.gelu, pre_gelu)[1](grad_hidden)[0].astype(jnp.bfloat16)
    grad_win = jnp.dot(normed_low.T, grad_pre, preferred_element_type=jnp.float32)
    normalized_map_gradient = jnp.dot(grad_pre, w_in.T, preferred_element_type=jnp.float32)
    grad_gain = jnp.sum(normalized_map_gradient * normalized_map, axis=0)
    standardized_input_gradient = normalized_map_gradient * layernorm_gain_vector
    depthwise_output_gradient = inverse_deviation * (
        standardized_input_gradient
        - jnp.mean(standardized_input_gradient, axis=1, keepdims=True)
        - normalized_map
        * jnp.mean(standardized_input_gradient * normalized_map, axis=1, keepdims=True)
    )
    depthwise_output_gradient = depthwise_output_gradient.reshape(grid_shape)
    grad_padded = jnp.pad(depthwise_output_gradient, ((0, 0), (3, 3), (3, 3), (0, 0)))
    grad_input = grad_out.reshape(grid_shape)
    kernel_rows = []
    for tap_row in range(7):
        for tap_col in range(7):
            window = padded[:, tap_row : tap_row + map_rows, tap_col : tap_col + map_cols, :]
            kernel_rows.append(jnp.sum(window * depthwise_output_gradient, axis=(0, 1, 2)))
            grad_input = (
                grad_input
                + kernel[tap_row * 7 + tap_col]
                * grad_padded[
                    :, 6 - tap_row : 6 - tap_row + map_rows, 6 - tap_col : 6 - tap_col + map_cols, :
                ]
            )
    grad_kernel = jnp.stack(kernel_rows)
    return (
        grad_input.astype(jnp.bfloat16),
        (grad_kernel, grad_gain, grad_win, grad_wout, grad_scale),
    )


def local(images, cotangent, kernels, norm_gains, w_in, w_out, scales):
    micro_count = images.shape[0]
    map_rows, map_cols, channels = (images.shape[1], images.shape[2], images.shape[3])
    hidden_units = w_in.shape[2]
    segments = lax.axis_size("segment")
    device_rank = lax.axis_index("segment")
    block_params = (kernels[0], norm_gains[0], w_in[0], w_out[0], scales[0])
    total_steps = micro_count + segments - 1
    blank_map = jnp.zeros((1,) + images.shape[1:], jnp.bfloat16)
    empty_grads = (
        jnp.zeros((49, channels), jnp.float32),
        jnp.zeros((channels,), jnp.float32),
        jnp.zeros((channels, hidden_units), jnp.float32),
        jnp.zeros((hidden_units, channels), jnp.float32),
        jnp.zeros((channels,), jnp.float32),
    )
    kept_init = ()

    def forward_step(counter, state):
        received, stashed, kept = state
        position = counter - device_rank
        active = jnp.logical_and(position >= 0, position < micro_count)
        position_slot = jnp.clip(position, 0, micro_count - 1)
        own_map = lax.dynamic_slice_in_dim(images, position_slot, 1, 0)
        current = jnp.where(device_rank == 0, own_map, received)
        stashed = jnp.where(
            active, lax.dynamic_update_slice_in_dim(stashed, current, position_slot, 0), stashed
        )

        def forward_compute():
            return forward_parts(current, *block_params)[0]

        def forward_resting():
            return blank_map

        produced = lax.cond(
            jnp.logical_and(active, device_rank < segments - 1), forward_compute, forward_resting
        )
        received = passed_along(produced, "segment", 1)
        return (received, stashed, kept)

    received, stashed, kept = lax.fori_loop(
        0, total_steps, forward_step, (blank_map, jnp.zeros_like(images), kept_init)
    )

    def backward_step(counter, state_pair):
        incoming, totals = state_pair
        position = counter - (segments - 1 - device_rank)
        active = jnp.logical_and(position >= 0, position < micro_count)
        position_slot = jnp.clip(position, 0, micro_count - 1)
        grad_here = jnp.where(
            device_rank == segments - 1,
            lax.dynamic_slice_in_dim(cotangent, position_slot, 1, 0),
            incoming,
        )

        def backward_compute():
            inputs_here = lax.dynamic_slice_in_dim(stashed, position_slot, 1, 0)
            stored = forward_parts(inputs_here, *block_params)[1]
            return backward_parts(grad_here, stored, *block_params)

        def backward_resting():
            return (blank_map, empty_grads)

        forwarded_state, grad_terms = lax.cond(active, backward_compute, backward_resting)
        totals = jax.tree.map(jnp.add, totals, grad_terms)
        incoming = passed_along(forwarded_state, "segment", -1)
        return (incoming, totals)

    incoming, totals = lax.fori_loop(0, total_steps, backward_step, (blank_map, empty_grads))
    reduced = (
        lax.psum_scatter(totals[0], "dp", scatter_dimension=1, tiled=True),
        lax.psum_scatter(totals[1], "dp", scatter_dimension=0, tiled=True),
        lax.psum_scatter(totals[2], "dp", scatter_dimension=0, tiled=True),
        lax.psum_scatter(totals[3], "dp", scatter_dimension=1, tiled=True),
        lax.psum_scatter(totals[4], "dp", scatter_dimension=0, tiled=True),
    )
    return (
        reduced[0][None],
        reduced[1][None],
        reduced[2][None],
        reduced[3][None],
        reduced[4][None],
    )


def solution(mesh):
    in_specs = (
        P("dp", None, None, None),
        P("dp", None, None, None),
        P("segment", None, None),
        P("segment", None),
        P("segment", None, None),
        P("segment", None, None),
        P("segment", None),
    )
    out_specs = (
        P("segment", None, "dp"),
        P("segment", "dp"),
        P("segment", "dp", None),
        P("segment", None, "dp"),
        P("segment", "dp"),
    )
    return jax.shard_map(local, mesh=mesh, in_specs=in_specs, out_specs=out_specs, check_vma=False)
```

profile of v0, /device:TPU:0, one launch (start us, length us, event | category | flops | bytes accessed | tf_op | source)
XLA Modules:
  0.0 679.9 jit_solution(1283060542604191974)
XLA Ops:
  9.8 100.5 %while.42 = (s32[]{:T(128)}, bf16[1,16,16,384]{3,2,1,0:T(8,128)(2,1)S(1)}, bf16[4,16,16,384]{3,2,1,0:T(8,128)(2,1)}, s32[]{:T(128)}, pred[]{:T(512)}, /*index=5*...) while((s32[]{:T(128)}, ...), condition=%wide.region_5.6_spmd, body=%wide.region_0.5_spmd.sunk | while | flops 314671360 | bytes 11074995 | solution.py:130
  11.6 8.3 %conditional.5 = (bf16[1,16,16,384]{3,2,1,0:T(8,128)(2,1)S(1)}) conditional(s32[]{:T(128)} %convert_element_type.95, () %tuple.251, (bf16[1,16,16,384]{3,2,1,0:T(8,128)(2,1)S(1)}, f32[1,384]{1,0:T(1,128)}, f32[49,384]{1,0:T(8,128)}, f32[1,384]{1,0:T(1,128)}, bf16[384,768]{1,0:T(8,128)(2,1)}, /*index=5*/bf16[768,384]{1,0:T(8,128)(2,1)}) %tuple.252), branch_computations={%region_1.1_spmd, %region_2.4_spmd} | conditional | flops 314474752 | bytes 9304704 | solution.py:124
  24.0 8.3 %conditional.5 = (bf16[1,16,16,384]{3,2,1,0:T(8,128)(2,1)S(1)}) conditional(s32[]{:T(128)} %convert_element_type.95, () %tuple.251, (bf16[1,16,16,384]{3,2,1,0:T(8,128)(2,1)S(1)}, f32[1,384]{1,0:T(1,128)}, f32[49,384]{1,0:T(8,128)}, f32[1,384]{1,0:T(1,128)}, bf16[384,768]{1,0:T(8,128)(2,1)}, /*index=5*/bf16[768,384]{1,0:T(8,128)(2,1)}) %tuple.252), branch_computations={%region_1.1_spmd, %region_2.4_spmd} | conditional | flops 314474752 | bytes 9304704 | solution.py:124
  37.4 8.3 %conditional.5 = (bf16[1,16,16,384]{3,2,1,0:T(8,128)(2,1)S(1)}) conditional(s32[]{:T(128)} %convert_element_type.95, () %tuple.251, (bf16[1,16,16,384]{3,2,1,0:T(8,128)(2,1)S(1)}, f32[1,384]{1,0:T(1,128)}, f32[49,384]{1,0:T(8,128)}, f32[1,384]{1,0:T(1,128)}, bf16[384,768]{1,0:T(8,128)(2,1)}, /*index=5*/bf16[768,384]{1,0:T(8,128)(2,1)}) %tuple.252), branch_computations={%region_1.1_spmd, %region_2.4_spmd} | conditional | flops 314474752 | bytes 9304704 | solution.py:124
  45.7 3.5 collective-permute-start
  52.1 8.3 %conditional.5 = (bf16[1,16,16,384]{3,2,1,0:T(8,128)(2,1)S(1)}) conditional(s32[]{:T(128)} %convert_element_type.95, () %tuple.251, (bf16[1,16,16,384]{3,2,1,0:T(8,128)(2,1)S(1)}, f32[1,384]{1,0:T(1,128)}, f32[49,384]{1,0:T(8,128)}, f32[1,384]{1,0:T(1,128)}, bf16[384,768]{1,0:T(8,128)(2,1)}, /*index=5*/bf16[768,384]{1,0:T(8,128)(2,1)}) %tuple.252), branch_computations={%region_1.1_spmd, %region_2.4_spmd} | conditional | flops 314474752 | bytes 9304704 | solution.py:124
  60.4 5.9 collective-permute-start
  69.2 14.2 %collective-permute-start = (bf16[1,16,16,384]{3,2,1,0:T(8,128)(2,1)S(1)}, bf16[1,16,16,384]{3,2,1,0:T(8,128)(2,1)S(1)}, u32[]{:S(2)}, u32[]{:S(2)}) collective-permute-start(bf16[1,16,16,384]{3,2,1,0:T(8,128)(2,1)S(1)} %get-tuple-element.1301), channel_id=1, source_target_pairs={{0,1},{1,2},{2,3},{4,5},{5,6},{6,7},{8,9},{9,10},{10,11},{12,13},{... | collective-permute-start | bytes 589832 | tf_op jit(solution)/shard_map/while/body/eval_jaxpr/ppermute | solution.py:12
  86.3 5.9 collective-permute-start
  95.0 14.2 %collective-permute-start = (bf16[1,16,16,384]{3,2,1,0:T(8,128)(2,1)S(1)}, bf16[1,16,16,384]{3,2,1,0:T(8,128)(2,1)S(1)}, u32[]{:S(2)}, u32[]{:S(2)}) collective-permute-start(bf16[1,16,16,384]{3,2,1,0:T(8,128)(2,1)S(1)} %get-tuple-element.1301), channel_id=1, source_target_pairs={{0,1},{1,2},{2,3},{4,5},{5,6},{6,7},{8,9},{9,10},{10,11},{12,13},{... | collective-permute-start | bytes 589832 | tf_op jit(solution)/shard_map/while/body/eval_jaxpr/ppermute | solution.py:12
  111.0 362.4 %while.43 = (s32[]{:T(128)}, bf16[1,16,16,384]{3,2,1,0:T(8,128)(2,1)}, f32[49,384]{1,0:T(8,128)}, f32[384]{0:T(512)}, f32[384,768]{1,0:T(8,128)}, /*index=5*/f32...) while((s32[]{:T(128)}, ...), condition=%wide.region_64.65_spmd.clone, body=%wide.region_6.64_spmd.clone.sunk | while | flops 946785664 | bytes 46313436 | solution.py:158
  141.0 120.2 %collective-permute-done.1 = bf16[1,16,16,384]{3,2,1,0:T(8,128)(2,1)} collective-permute-done((bf16[1,16,16,384]{3,2,1,0:T(8,128)(2,1)}, bf16[1,16,16,384]{3,2,1,0:T(8,128)(2,1)}, u32[]{:S(2)}, u32[]{:S(2)}) %collective-permute-start.1) | collective-permute-done | bytes 196640 | tf_op jit(solution)/shard_map/while/body/eval_jaxpr/ppermute | solution.py:12
  261.2 45.4 %conditional.6 = (bf16[1,16,16,384]{3,2,1,0:T(8,128)(2,1)}, f32[49,384]{1,0:T(8,128)}, f32[384]{0:T(512)}, f32[384,768]{1,0:T(8,128)S(1)}, f32[768,384]{1,0:T(8,128)S(1)}, /*index=5*/f32[384]{0:T(512)}) conditional(s32[]{:T(128)} %convert_element_type.96, () %tuple.255, (pred[]{:T(512)}, s32[]{:T(128)}, bf16[4,16,16,384]{3,2,1,0:T(8,128)(2,1)}, ...), branch_computations={%region_7.7_spmd, %region_8.63_spmd} | conditional | flops 945566848 | bytes 28751840 | solution.py:153
  266.7 4.0 fusion.229
  292.6 7.0 %stack.299 = f32[49,384]{1,0:T(8,128)} concatenate(f32[1,384]{1,0:T(1,128)S(1)} %stack.250, f32[1,384]{1,0:T(1,128)S(1)} %stack.251, f32[1,384]{1,0:T(1,128)} %stack.252, f32[1,384]{1,0:T(1,128)} %stack.253, f32[1,384]{1,0:T(1,128)} %stack.254, f32[1,384]{1,0:T(1,128)} %stack.255, f32[1,384]{1,0:T(1,128)} %stack.256, f32[1,384]{1,0:T(1,128)} %stack.257, f32[1,384]{1,0:T(1,128)} %stack.258, ...), dimensions={0} | concatenate | bytes 150528 | tf_op jit(solution)/shard_map/while/body/eval_jaxpr/cond/branch_1_fun/stack | solution.py:82
  300.0 4.3 fusion.219
  314.4 45.4 %conditional.6 = (bf16[1,16,16,384]{3,2,1,0:T(8,128)(2,1)}, f32[49,384]{1,0:T(8,128)}, f32[384]{0:T(512)}, f32[384,768]{1,0:T(8,128)S(1)}, f32[768,384]{1,0:T(8,128)S(1)}, /*index=5*/f32[384]{0:T(512)}) conditional(s32[]{:T(128)} %convert_element_type.96, () %tuple.255, (pred[]{:T(512)}, s32[]{:T(128)}, bf16[4,16,16,384]{3,2,1,0:T(8,128)(2,1)}, ...), branch_computations={%region_7.7_spmd, %region_8.63_spmd} | conditional | flops 945566848 | bytes 28751840 | solution.py:153
  320.0 4.0 fusion.229
  345.8 7.0 %stack.299 = f32[49,384]{1,0:T(8,128)} concatenate(f32[1,384]{1,0:T(1,128)S(1)} %stack.250, f32[1,384]{1,0:T(1,128)S(1)} %stack.251, f32[1,384]{1,0:T(1,128)} %stack.252, f32[1,384]{1,0:T(1,128)} %stack.253, f32[1,384]{1,0:T(1,128)} %stack.254, f32[1,384]{1,0:T(1,128)} %stack.255, f32[1,384]{1,0:T(1,128)} %stack.256, f32[1,384]{1,0:T(1,128)} %stack.257, f32[1,384]{1,0:T(1,128)} %stack.258, ...), dimensions={0} | concatenate | bytes 150528 | tf_op jit(solution)/shard_map/while/body/eval_jaxpr/cond/branch_1_fun/stack | solution.py:82
  353.2 4.3 fusion.219
  367.6 45.4 %conditional.6 = (bf16[1,16,16,384]{3,2,1,0:T(8,128)(2,1)}, f32[49,384]{1,0:T(8,128)}, f32[384]{0:T(512)}, f32[384,768]{1,0:T(8,128)S(1)}, f32[768,384]{1,0:T(8,128)S(1)}, /*index=5*/f32[384]{0:T(512)}) conditional(s32[]{:T(128)} %convert_element_type.96, () %tuple.255, (pred[]{:T(512)}, s32[]{:T(128)}, bf16[4,16,16,384]{3,2,1,0:T(8,128)(2,1)}, ...), branch_computations={%region_7.7_spmd, %region_8.63_spmd} | conditional | flops 945566848 | bytes 28751840 | solution.py:153
  373.2 4.0 fusion.229
  399.0 7.0 %stack.299 = f32[49,384]{1,0:T(8,128)} concatenate(f32[1,384]{1,0:T(1,128)S(1)} %stack.250, f32[1,384]{1,0:T(1,128)S(1)} %stack.251, f32[1,384]{1,0:T(1,128)} %stack.252, f32[1,384]{1,0:T(1,128)} %stack.253, f32[1,384]{1,0:T(1,128)} %stack.254, f32[1,384]{1,0:T(1,128)} %stack.255, f32[1,384]{1,0:T(1,128)} %stack.256, f32[1,384]{1,0:T(1,128)} %stack.257, f32[1,384]{1,0:T(1,128)} %stack.258, ...), dimensions={0} | concatenate | bytes 150528 | tf_op jit(solution)/shard_map/while/body/eval_jaxpr/cond/branch_1_fun/stack | solution.py:82
  406.4 4.3 fusion.219
  420.8 45.4 %conditional.6 = (bf16[1,16,16,384]{3,2,1,0:T(8,128)(2,1)}, f32[49,384]{1,0:T(8,128)}, f32[384]{0:T(512)}, f32[384,768]{1,0:T(8,128)S(1)}, f32[768,384]{1,0:T(8,128)S(1)}, /*index=5*/f32[384]{0:T(512)}) conditional(s32[]{:T(128)} %convert_element_type.96, () %tuple.255, (pred[]{:T(512)}, s32[]{:T(128)}, bf16[4,16,16,384]{3,2,1,0:T(8,128)(2,1)}, ...), branch_computations={%region_7.7_spmd, %region_8.63_spmd} | conditional | flops 945566848 | bytes 28751840 | solution.py:153
  426.4 4.0 fusion.229
  452.2 7.0 %stack.299 = f32[49,384]{1,0:T(8,128)} concatenate(f32[1,384]{1,0:T(1,128)S(1)} %stack.250, f32[1,384]{1,0:T(1,128)S(1)} %stack.251, f32[1,384]{1,0:T(1,128)} %stack.252, f32[1,384]{1,0:T(1,128)} %stack.253, f32[1,384]{1,0:T(1,128)} %stack.254, f32[1,384]{1,0:T(1,128)} %stack.255, f32[1,384]{1,0:T(1,128)} %stack.256, f32[1,384]{1,0:T(1,128)} %stack.257, f32[1,384]{1,0:T(1,128)} %stack.258, ...), dimensions={0} | concatenate | bytes 150528 | tf_op jit(solution)/shard_map/while/body/eval_jaxpr/cond/branch_1_fun/stack | solution.py:82
  459.6 4.3 fusion.219
  479.9 23.1 %all-reduce.5 = (f32[384]{0:T(512)S(1)}, f32[384]{0:T(512)S(1)}) all-reduce(f32[384]{0:T(512)S(1)} %copy-done.92, f32[384]{0:T(512)S(1)} %copy-done.95), channel_id=3, replica_groups=mesh['dp'=8,'segment'=4] {'dp'}, use_global_device_ids=true, to_apply=%region_66.67.clone | all-reduce | flops 768 | bytes 6144
  503.6 35.3 %reduce-scatter.4.cloned.1.call-done = f32[49,48]{0,1:T(8,128)} async-done(((f32[49,384]{0,1:T(8,128)}), f32[49,48]{0,1:T(8,128)}) %reduce-scatter.4.cloned.1.call-update) | async-done | bytes 9424 | tf_op jit(solution)/shard_map/reduce_scatter | solution.py:160
  538.9 67.0 %reduce-scatter.8.cloned.1.call-done = f32[768,48]{0,1:T(8,128)} async-done(((f32[768,384]{0,1:T(8,128)}), f32[768,48]{0,1:T(8,128)}) %reduce-scatter.8.cloned.1.call-update) | async-done | bytes 147472 | tf_op jit(solution)/shard_map/reduce_scatter | solution.py:163
  606.0 67.4 %reduce-scatter.6.cloned.1.call-done = f32[48,768]{1,0:T(8,128)} async-done(((f32[384,768]{1,0:T(8,128)}), f32[48,768]{1,0:T(8,128)}) %reduce-scatter.6.cloned.1.call-update) | async-done | bytes 147472 | tf_op jit(solution)/shard_map/reduce_scatter | solution.py:162
  (1265 shorter events, 247.9 us)
Async XLA Ops:
  7.2 531.8 %reduce-scatter.4.cloned.1.call-start = ((), (), s32[]{:S(2)}) async-start(), calls=%async_computation.3 | async-start | bytes 221184 | tf_op jit(solution)/shard_map/reduce_scatter | solution.py:160
  19.9 2.4 collective-permute-start
  32.3 3.3 collective-permute-start
  45.7 4.5 collective-permute-start
  60.4 7.0 %collective-permute-start = (bf16[1,16,16,384]{3,2,1,0:T(8,128)(2,1)S(1)}, bf16[1,16,16,384]{3,2,1,0:T(8,128)(2,1)S(1)}, u32[]{:S(2)}, u32[]{:S(2)}) collective-permute-start(bf16[1,16,16,384]{3,2,1,0:T(8,128)(2,1)S(1)} %get-tuple-element.1301), channel_id=1, source_target_pairs={{0,1},{1,2},{2,3},{4,5},{5,6},{6,7},{8,9},{9,10},{10,11},{12,13},{... | collective-permute-start | bytes 589832 | tf_op jit(solution)/shard_map/while/body/eval_jaxpr/ppermute | solution.py:12
  69.2 15.3 %collective-permute-start = (bf16[1,16,16,384]{3,2,1,0:T(8,128)(2,1)S(1)}, bf16[1,16,16,384]{3,2,1,0:T(8,128)(2,1)S(1)}, u32[]{:S(2)}, u32[]{:S(2)}) collective-permute-start(bf16[1,16,16,384]{3,2,1,0:T(8,128)(2,1)S(1)} %get-tuple-element.1301), channel_id=1, source_target_pairs={{0,1},{1,2},{2,3},{4,5},{5,6},{6,7},{8,9},{9,10},{10,11},{12,13},{... | collective-permute-start | bytes 589832 | tf_op jit(solution)/shard_map/while/body/eval_jaxpr/ppermute | solution.py:12
  86.3 7.0 %collective-permute-start = (bf16[1,16,16,384]{3,2,1,0:T(8,128)(2,1)S(1)}, bf16[1,16,16,384]{3,2,1,0:T(8,128)(2,1)S(1)}, u32[]{:S(2)}, u32[]{:S(2)}) collective-permute-start(bf16[1,16,16,384]{3,2,1,0:T(8,128)(2,1)S(1)} %get-tuple-element.1301), channel_id=1, source_target_pairs={{0,1},{1,2},{2,3},{4,5},{5,6},{6,7},{8,9},{9,10},{10,11},{12,13},{... | collective-permute-start | bytes 589832 | tf_op jit(solution)/shard_map/while/body/eval_jaxpr/ppermute | solution.py:12
  95.0 15.3 %collective-permute-start = (bf16[1,16,16,384]{3,2,1,0:T(8,128)(2,1)S(1)}, bf16[1,16,16,384]{3,2,1,0:T(8,128)(2,1)S(1)}, u32[]{:S(2)}, u32[]{:S(2)}) collective-permute-start(bf16[1,16,16,384]{3,2,1,0:T(8,128)(2,1)S(1)} %get-tuple-element.1301), channel_id=1, source_target_pairs={{0,1},{1,2},{2,3},{4,5},{5,6},{6,7},{8,9},{9,10},{10,11},{12,13},{... | collective-permute-start | bytes 589832 | tf_op jit(solution)/shard_map/while/body/eval_jaxpr/ppermute | solution.py:12
  113.6 7.2 %collective-permute-start.1 = (bf16[1,16,16,384]{3,2,1,0:T(8,128)(2,1)}, bf16[1,16,16,384]{3,2,1,0:T(8,128)(2,1)}, u32[]{:S(2)}, u32[]{:S(2)}) collective-permute-start(bf16[1,16,16,384]{3,2,1,0:T(8,128)(2,1)} %get-tuple-element.1176), channel_id=1, source_target_pairs={{1,0},{2,1},{3,2},{5,4},{6,5},{7,6},{9,8},{10,9},{11,10},{13,12},{... | collective-permute-start | bytes 589832 | tf_op jit(solution)/shard_map/while/body/eval_jaxpr/ppermute | solution.py:12
  123.6 8.0 %collective-permute-start.1 = (bf16[1,16,16,384]{3,2,1,0:T(8,128)(2,1)}, bf16[1,16,16,384]{3,2,1,0:T(8,128)(2,1)}, u32[]{:S(2)}, u32[]{:S(2)}) collective-permute-start(bf16[1,16,16,384]{3,2,1,0:T(8,128)(2,1)} %get-tuple-element.1176), channel_id=1, source_target_pairs={{1,0},{2,1},{3,2},{5,4},{6,5},{7,6},{9,8},{10,9},{11,10},{13,12},{... | collective-permute-start | bytes 589832 | tf_op jit(solution)/shard_map/while/body/eval_jaxpr/ppermute | solution.py:12
  134.3 126.9 %collective-permute-start.1 = (bf16[1,16,16,384]{3,2,1,0:T(8,128)(2,1)}, bf16[1,16,16,384]{3,2,1,0:T(8,128)(2,1)}, u32[]{:S(2)}, u32[]{:S(2)}) collective-permute-start(bf16[1,16,16,384]{3,2,1,0:T(8,128)(2,1)} %get-tuple-element.1176), channel_id=1, source_target_pairs={{1,0},{2,1},{3,2},{5,4},{6,5},{7,6},{9,8},{10,9},{11,10},{13,12},{... | collective-permute-start | bytes 589832 | tf_op jit(solution)/shard_map/while/body/eval_jaxpr/ppermute | solution.py:12
  138.4 122.7 %copy-start.1 = (f32[768,384]{1,0:T(8,128)}, f32[768,384]{1,0:T(8,128)S(1)}, u32[]{:S(2)}) copy-start(f32[768,384]{1,0:T(8,128)S(1)} %select_add_fusion.12) | copy-start | bytes 3538948 | tf_op jit(solution)/shard_map/while
  141.0 120.2 %copy-start.91 = (f32[384]{0:T(512)}, f32[384]{0:T(512)S(1)}, u32[]{:S(2)}) copy-start(f32[384]{0:T(512)S(1)} %get-tuple-element.1285) | copy-start | bytes 4612 | tf_op jit(solution)/shard_map/while
  141.0 120.2 %copy-start.94 = (f32[384]{0:T(512)}, f32[384]{0:T(512)S(1)}, u32[]{:S(2)}) copy-start(f32[384]{0:T(512)S(1)} %get-tuple-element.1288) | copy-start | bytes 4612 | tf_op jit(solution)/shard_map/while
  279.3 20.3 %copy-start.2 = (bf16[1,16,16,384]{3,2,1,0:T(8,128)(2,1)S(1)}, bf16[1,16,16,384]{3,2,1,0:T(8,128)(2,1)}, u32[]{:S(2)}) copy-start(bf16[1,16,16,384]{3,2,1,0:T(8,128)(2,1)} %get-tuple-element.982) | copy-start | bytes 589828 | tf_op jit(solution)/shard_map/while/body/eval_jaxpr/cond
  279.3 20.3 %copy-start.6 = (f32[384]{0:T(512)S(1)}, f32[384]{0:T(512)}, u32[]{:S(2)}) copy-start(f32[384]{0:T(512)} %copy-done.5) | copy-start | bytes 4612 | tf_op jit(solution)/shard_map/while/body/eval_jaxpr/cond
  279.3 20.3 %copy-start.8 = (f32[384]{0:T(512)S(1)}, f32[384]{0:T(512)}, u32[]{:S(2)}) copy-start(f32[384]{0:T(512)} %copy-done.7) | copy-start | bytes 4612 | tf_op jit(solution)/shard_map/while/body/eval_jaxpr/cond
  306.6 7.8 %collective-permute-start.1 = (bf16[1,16,16,384]{3,2,1,0:T(8,128)(2,1)}, bf16[1,16,16,384]{3,2,1,0:T(8,128)(2,1)}, u32[]{:S(2)}, u32[]{:S(2)}) collective-permute-start(bf16[1,16,16,384]{3,2,1,0:T(8,128)(2,1)} %get-tuple-element.1176), channel_id=1, source_target_pairs={{1,0},{2,1},{3,2},{5,4},{6,5},{7,6},{9,8},{10,9},{11,10},{13,12},{... | collective-permute-start | bytes 589832 | tf_op jit(solution)/shard_map/while/body/eval_jaxpr/ppermute | solution.py:12
  332.5 20.3 %copy-start.2 = (bf16[1,16,16,384]{3,2,1,0:T(8,128)(2,1)S(1)}, bf16[1,16,16,384]{3,2,1,0:T(8,128)(2,1)}, u32[]{:S(2)}) copy-start(bf16[1,16,16,384]{3,2,1,0:T(8,128)(2,1)} %get-tuple-element.982) | copy-start | bytes 589828 | tf_op jit(solution)/shard_map/while/body/eval_jaxpr/cond
  332.5 20.3 %copy-start.6 = (f32[384]{0:T(512)S(1)}, f32[384]{0:T(512)}, u32[]{:S(2)}) copy-start(f32[384]{0:T(512)} %copy-done.5) | copy-start | bytes 4612 | tf_op jit(solution)/shard_map/while/body/eval_jaxpr/cond
  332.5 20.3 %copy-start.8 = (f32[384]{0:T(512)S(1)}, f32[384]{0:T(512)}, u32[]{:S(2)}) copy-start(f32[384]{0:T(512)} %copy-done.7) | copy-start | bytes 4612 | tf_op jit(solution)/shard_map/while/body/eval_jaxpr/cond
  359.8 7.8 %collective-permute-start.1 = (bf16[1,16,16,384]{3,2,1,0:T(8,128)(2,1)}, bf16[1,16,16,384]{3,2,1,0:T(8,128)(2,1)}, u32[]{:S(2)}, u32[]{:S(2)}) collective-permute-start(bf16[1,16,16,384]{3,2,1,0:T(8,128)(2,1)} %get-tuple-element.1176), channel_id=1, source_target_pairs={{1,0},{2,1},{3,2},{5,4},{6,5},{7,6},{9,8},{10,9},{11,10},{13,12},{... | collective-permute-start | bytes 589832 | tf_op jit(solution)/shard_map/while/body/eval_jaxpr/ppermute | solution.py:12
  385.7 20.3 %copy-start.2 = (bf16[1,16,16,384]{3,2,1,0:T(8,128)(2,1)S(1)}, bf16[1,16,16,384]{3,2,1,0:T(8,128)(2,1)}, u32[]{:S(2)}) copy-start(bf16[1,16,16,384]{3,2,1,0:T(8,128)(2,1)} %get-tuple-element.982) | copy-start | bytes 589828 | tf_op jit(solution)/shard_map/while/body/eval_jaxpr/cond
  385.7 20.3 %copy-start.6 = (f32[384]{0:T(512)S(1)}, f32[384]{0:T(512)}, u32[]{:S(2)}) copy-start(f32[384]{0:T(512)} %copy-done.5) | copy-start | bytes 4612 | tf_op jit(solution)/shard_map/while/body/eval_jaxpr/cond
  385.7 20.3 %copy-start.8 = (f32[384]{0:T(512)S(1)}, f32[384]{0:T(512)}, u32[]{:S(2)}) copy-start(f32[384]{0:T(512)} %copy-done.7) | copy-start | bytes 4612 | tf_op jit(solution)/shard_map/while/body/eval_jaxpr/cond
  413.0 7.8 %collective-permute-start.1 = (bf16[1,16,16,384]{3,2,1,0:T(8,128)(2,1)}, bf16[1,16,16,384]{3,2,1,0:T(8,128)(2,1)}, u32[]{:S(2)}, u32[]{:S(2)}) collective-permute-start(bf16[1,16,16,384]{3,2,1,0:T(8,128)(2,1)} %get-tuple-element.1176), channel_id=1, source_target_pairs={{1,0},{2,1},{3,2},{5,4},{6,5},{7,6},{9,8},{10,9},{11,10},{13,12},{... | collective-permute-start | bytes 589832 | tf_op jit(solution)/shard_map/while/body/eval_jaxpr/ppermute | solution.py:12
  438.9 20.3 %copy-start.2 = (bf16[1,16,16,384]{3,2,1,0:T(8,128)(2,1)S(1)}, bf16[1,16,16,384]{3,2,1,0:T(8,128)(2,1)}, u32[]{:S(2)}) copy-start(bf16[1,16,16,384]{3,2,1,0:T(8,128)(2,1)} %get-tuple-element.982) | copy-start | bytes 589828 | tf_op jit(solution)/shard_map/while/body/eval_jaxpr/cond
  438.9 20.3 %copy-start.6 = (f32[384]{0:T(512)S(1)}, f32[384]{0:T(512)}, u32[]{:S(2)}) copy-start(f32[384]{0:T(512)} %copy-done.5) | copy-start | bytes 4612 | tf_op jit(solution)/shard_map/while/body/eval_jaxpr/cond
  438.9 20.3 %copy-start.8 = (f32[384]{0:T(512)S(1)}, f32[384]{0:T(512)}, u32[]{:S(2)}) copy-start(f32[384]{0:T(512)} %copy-done.7) | copy-start | bytes 4612 | tf_op jit(solution)/shard_map/while/body/eval_jaxpr/cond
  466.2 6.7 collective-permute-start.1
  475.1 130.8 %reduce-scatter.8.cloned.1.call-start = ((), (), s32[]{:S(2)}) async-start(), calls=%async_computation.5 | async-start | bytes 1327104 | tf_op jit(solution)/shard_map/reduce_scatter | solution.py:163
  477.9 195.5 %reduce-scatter.6.cloned.1.call-start = ((), (), s32[]{:S(2)}) async-start(), calls=%async_computation.4 | async-start | bytes 1327104 | tf_op jit(solution)/shard_map/reduce_scatter | solution.py:162
  (394 other events, 4530.1 us)
Sparse Core Ops, SparseCore 0:
  475.3 63.6 reduce-scatter.3
  542.9 63.0 reduce-scatter.7
  609.9 63.4 reduce-scatter.5
where the time goes:
time: 684 us; the launch traced here: 680 us
  waiting for transfers between devices  304 us (44%)
  other arithmetic  126 us (18%)
  local copies, waits for them, and re-layouts  124 us (18%)
  starting transfers between devices  56.5 us (8%)
  matrix products  24.1 us (4%)
  blocking collectives  23.1 us (3%)
  between operations  14.5 us (2%)
  loops' own time  7.6 us (1%)
    ppermute x14, waiting for transfers between devices, passed_along(): return lax.ppermute(value, axis, pairs)  134 us
    another operation x200, local copies, waits for them, and re-layouts, backward_parts(): grad_kernel = jnp.stack(kernel_rows)  70.1 us
    reduce_scatter x1, waiting for transfers between devices, local(): lax.psum_scatter(totals[2], 'dp', scatter_dimension=0, tiled=True)  67.4 us
    reduce_scatter x1, waiting for transfers between devices, local(): lax.psum_scatter(totals[3], 'dp', scatter_dimension=1, tiled=True)  67 us
    ppermute x14, starting transfers between devices, passed_along(): return lax.ppermute(value, axis, pairs)  56.3 us
    add x28, other arithmetic, backward_step(): totals = jax.tree.map(jnp.add, totals, grad_terms)  35.7 us
    reduce_scatter x1, waiting for transfers between devices, local(): lax.psum_scatter(totals[0], 'dp', scatter_dimension=1, tiled=True)  35.3 us
    reduce_sum x8, other arithmetic, forward_parts(): center = flat_rows - jnp.mean(flat_rows, axis=1, keepdims=True)  29.2 us
  transfers between devices with their start and end apart: 17, of which 16 were waited for; matrix products, arithmetic and copies ran while one was open for 6% of the time, Pallas kernels for 0%

commit v1 on v0

v1 whole, which is shorter than its diff:
```python
import functools
import jax
import jax.numpy as jnp
from jax import lax
from jax.sharding import PartitionSpec as P
from jax.experimental import pallas as pl
from jax.experimental.pallas import tpu as pltpu

EPS = 1e-06
GELU_C = 0.7978845608028654
GELU_A = 0.044715
LANES = 128
VMEM = pltpu.CompilerParams(vmem_limit_bytes=40 * 1024 * 1024)


def zero_borders(pad_ref, rows, cols):
    tiles = pad_ref.shape[0]
    for c in range(tiles):
        pad_ref[c, 0:3] = jnp.zeros((3, cols + 16, LANES), jnp.float32)
        pad_ref[c, rows + 3 : rows + 6] = jnp.zeros((3, cols + 16, LANES), jnp.float32)
        pad_ref[c, 3 : rows + 3, 0:8] = jnp.zeros((rows, 8, LANES), jnp.float32)
        pad_ref[c, 3 : rows + 3, cols + 8 : cols + 16] = jnp.zeros((rows, 8, LANES), jnp.float32)


def conv_norm_kernel(x_ref, k_ref, gain_ref, xhat_ref, normed_ref, inv_ref, pad_ref, conv_ref):
    rows, cols, channels = x_ref.shape
    tiles = channels // LANES
    zero_borders(pad_ref, rows, cols)
    for c in range(tiles):
        pad_ref[c, 3 : rows + 3, 8 : cols + 8] = x_ref[:, :, c * LANES : (c + 1) * LANES].astype(jnp.float32)

    for c in range(tiles):
        lanes = slice(c * LANES, (c + 1) * LANES)

        def strip(w, carry, c=c, lanes=lanes):
            base = pl.multiple_of(w * 8, 8)
            acc = jnp.zeros((rows, 8, LANES), jnp.float32)
            window = pad_ref.at[c, :, pl.ds(base, 24), :]
            for q in range(7):
                col = window[:, 5 + q : 13 + q, :]
                for r in range(7):
                    acc = acc + k_ref[r * 7 + q : r * 7 + q + 1, lanes][None] * col[r : r + rows]
            conv_ref[:, pl.ds(base, 8), lanes] = acc
            return carry

        lax.fori_loop(0, cols // 8, strip, 0)

    def norm(h, carry):
        value = conv_ref[pl.ds(h * 2, 2)].reshape(2 * cols, channels)
        mean = jnp.mean(value, axis=1, keepdims=True)
        center = value - mean
        inv = lax.rsqrt(jnp.mean(center * center, axis=1, keepdims=True) + EPS)
        xhat = center * inv
        at = pl.ds(pl.multiple_of(h * 2 * cols, 2 * cols), 2 * cols)
        xhat_ref[at, :] = xhat.astype(jnp.bfloat16)
        normed_ref[at, :] = (xhat * gain_ref[...]).astype(jnp.bfloat16)
        inv_ref[at, :] = jnp.broadcast_to(inv, (2 * cols, LANES))
        return carry

    lax.fori_loop(0, rows // 2, norm, 0, unroll=2)


def conv_norm(x, kernel, gain):
    rows, cols, channels = x.shape
    tiles = channels // LANES
    n = rows * cols
    return pl.pallas_call(
        conv_norm_kernel,
        out_shape=(
            jax.ShapeDtypeStruct((n, channels), jnp.bfloat16),
            jax.ShapeDtypeStruct((n, channels), jnp.bfloat16),
            jax.ShapeDtypeStruct((n, LANES), jnp.float32),
        ),
        scratch_shapes=[
            pltpu.VMEM((tiles, rows + 6, cols + 16, LANES), jnp.float32),
            pltpu.VMEM((rows, cols, channels), jnp.float32),
        ],
        compiler_params=VMEM,
        name="conv_norm",
    )(x, kernel, gain)


def tanh_arg(x):
    return jnp.tanh(x * (GELU_C + (GELU_C * GELU_A) * (x * x)))


def load_weights(sel_ref, w_ins, w_outs, w_in_ref, w_out_ref, sems):
    for m in range(len(w_ins)):

        @pl.when(sel_ref[0] == m)
        def _():
            pltpu.make_async_copy(w_ins[m], w_in_ref, sems.at[0]).start()
            pltpu.make_async_copy(w_outs[m], w_out_ref, sems.at[1]).start()

    return (
        pltpu.make_async_copy(w_ins[0], w_in_ref, sems.at[0]).wait,
        pltpu.make_async_copy(w_outs[0], w_out_ref, sems.at[1]).wait,
    )


def mlp_kernel(choices, sel_ref, normed_ref, x_ref, scale_ref, *rest):
    w_ins, w_outs = rest[:choices], rest[choices : 2 * choices]
    y_ref, pre_ref, branch_ref, hid_ref, acc_ref, w_in_ref, w_out_ref, sems = rest[2 * choices :]
    wait_in, wait_out = load_weights(sel_ref, w_ins, w_outs, w_in_ref, w_out_ref, sems)
    n, channels = normed_ref.shape
    hidden = w_in_ref.shape[1]
    wait_in()
    step = 256
    sub = 32
    for j in range(hidden // step):
        cut = slice(j * step, (j + 1) * step)
        pre = jnp.dot(normed_ref[...], w_in_ref[:, cut], preferred_element_type=jnp.float32)
        for i in range(n // sub):
            p = pre[i * sub : (i + 1) * sub]
            half = 0.5 * p
            hid_ref[i * sub : (i + 1) * sub, :] = (half + half * tanh_arg(p)).astype(jnp.bfloat16)
            pre_ref[i * sub : (i + 1) * sub, cut] = p.astype(jnp.bfloat16)
        if j == 0:
            wait_out()
        part = jnp.dot(hid_ref[...], w_out_ref[cut, :], preferred_element_type=jnp.float32)
        if j == 0:
            acc_ref[...] = part
        else:
            acc_ref[...] += part
    for i in range(n // sub):
        at = slice(i * sub, (i + 1) * sub)
        branch = acc_ref[at, :]
        branch_ref[at, :] = branch.astype(jnp.bfloat16)
        y_ref[at, :] = (x_ref[at, :].astype(jnp.float32) + scale_ref[...] * branch).astype(jnp.bfloat16)


def specs(sel, arrays, choices):
    return (
        [pl.BlockSpec(memory_space=pltpu.SMEM)]
        + [pl.BlockSpec(memory_space=pltpu.VMEM)] * arrays
        + [pl.BlockSpec(memory_space=pl.ANY)] * (2 * choices)
    )


def mlp(sel, normed, x, scale, w_ins, w_outs):
    n, channels = normed.shape
    hidden = w_ins[0].shape[1]
    return pl.pallas_call(
        functools.partial(mlp_kernel, len(w_ins)),
        in_specs=specs(sel, 3, len(w_ins)),
        out_shape=(
            jax.ShapeDtypeStruct((n, channels), jnp.bfloat16),
            jax.ShapeDtypeStruct((n, hidden), jnp.bfloat16),
            jax.ShapeDtypeStruct((n, channels), jnp.bfloat16),
        ),
        scratch_shapes=[
            pltpu.VMEM((n, 256), jnp.bfloat16),
            pltpu.VMEM((n, channels), jnp.float32),
            pltpu.VMEM((channels, hidden), jnp.bfloat16),
            pltpu.VMEM((hidden, channels), jnp.bfloat16),
            pltpu.SemaphoreType.DMA((2,)),
        ],
        compiler_params=VMEM,
        name="mlp",
    )(sel, normed, x, scale, *w_ins, *w_outs)


def mlp_back_kernel(choices, sel_ref, g_ref, branch_ref, pre_ref, xhat_ref, inv_ref, gain_ref, scale_ref, *rest):
    w_ins, w_outs = rest[:choices], rest[choices : 2 * choices]
    (keep_ref, send_ref, small_ref, gconv_ref,
     gb_ref, nm_ref, hid_ref, gp_ref, acc_ref, w_in_ref, w_out_ref, sems) = rest[2 * choices :]
    wait_in, wait_out = load_weights(sel_ref, w_ins, w_outs, w_in_ref, w_out_ref, sems)
    first = sel_ref[1] == 0
    n, channels = g_ref.shape
    hidden = w_in_ref.shape[1]
    step = 256
    sub = 32
    scale_sum = jnp.zeros((8, channels), jnp.float32)
    for i in range(n // sub):
        at = slice(i * sub, (i + 1) * sub)
        g = g_ref[at, :].astype(jnp.float32)
        scale_sum = scale_sum + jnp.sum((g * branch_ref[at, :].astype(jnp.float32)).reshape(sub // 8, 8, channels), axis=0)
        gb_ref[at, :] = (g * scale_ref[...]).astype(jnp.bfloat16)
        nm_ref[at, :] = (xhat_ref[at, :].astype(jnp.float32) * gain_ref[...]).astype(jnp.bfloat16)
    gb_t = gb_ref[...].T
    nm_t = nm_ref[...].T
    wait_in()
    wait_out()
    for j in range(hidden // step):
        cut = slice(j * step, (j + 1) * step)
        gh = lax.dot_general(gb_ref[...], w_out_ref[cut, :], (((1,), (1,)), ((), ())), preferred_element_type=jnp.float32)
        for i in range(n // sub):
            at = slice(i * sub, (i + 1) * sub)
            p = pre_ref[at, cut].astype(jnp.float32)
            sq = p * p
            t = jnp.tanh(p * (GELU_C + (GELU_C * GELU_A) * sq))
            cdf = 0.5 + 0.5 * t
            hid_ref[at, :] = (p * cdf).astype(jnp.bfloat16)
            slope = cdf + (0.5 * p) * (1.0 - t * t) * (GELU_C + (3.0 * GELU_C * GELU_A) * sq)
            gp_ref[at, :] = (gh[at, :] * slope).astype(jnp.bfloat16)
        t_out = jnp.dot(gb_t, hid_ref[...], preferred_element_type=jnp.float32)
        t_in = jnp.dot(nm_t, gp_ref[...], preferred_element_type=jnp.float32)
        keep_ref[:, cut] = jnp.where(first, t_in, t_out).astype(jnp.bfloat16)
        send_ref[:, cut] = jnp.where(first, t_out, t_in).astype(jnp.bfloat16)
        part = lax.dot_general(gp_ref[...], w_in_ref[:, cut], (((1,), (1,)), ((), ())), preferred_element_type=jnp.float32)
        if j == 0:
            acc_ref[...] = part
        else:
            acc_ref[...] += part
    gain_sum = jnp.zeros((8, channels), jnp.float32)
    for i in range(n // sub):
        at = slice(i * sub, (i + 1) * sub)
        gn = acc_ref[at, :]
        xhat = xhat_ref[at, :].astype(jnp.float32)
        gain_sum = gain_sum + jnp.sum((gn * xhat).reshape(sub // 8, 8, channels), axis=0)
        gx = gn * gain_ref[...]
        m1 = jnp.mean(gx, axis=1, keepdims=True)
        m2 = jnp.mean(gx * xhat, axis=1, keepdims=True)
        inv = inv_ref[at, 0:1]
        gconv_ref[at, :] = inv * (gx - m1 - xhat * m2)
    small_ref[0:1, :] = jnp.sum(gain_sum, axis=0, keepdims=True)
    small_ref[1:2, :] = jnp.sum(scale_sum, axis=0, keepdims=True)
    small_ref[2:8, :] = jnp.zeros((6, channels), jnp.float32)


def mlp_back(sel, g, branch, pre, xhat, inv, gain, scale, w_ins, w_outs):
    n, channels = g.shape
    hidden = w_ins[0].shape[1]
    return pl.pallas_call(
        functools.partial(mlp_back_kernel, len(w_ins)),
        in_specs=specs(sel, 7, len(w_ins)),
        out_shape=(
            jax.ShapeDtypeStruct((channels, hidden), jnp.bfloat16),
            jax.ShapeDtypeStruct((channels, hidden), jnp.bfloat16),
            jax.ShapeDtypeStruct((8, channels), jnp.float32),
            jax.ShapeDtypeStruct((n, channels), jnp.float32),
        ),
        scratch_shapes=[
            pltpu.VMEM((n, channels), jnp.bfloat16),
            pltpu.VMEM((n, channels), jnp.bfloat16),
            pltpu.VMEM((n, 256), jnp.bfloat16),
            pltpu.VMEM((n, 256), jnp.bfloat16),
            pltpu.VMEM((n, channels), jnp.float32),
            pltpu.VMEM((channels, hidden), jnp.bfloat16),
            pltpu.VMEM((hidden, channels), jnp.bfloat16),
            pltpu.SemaphoreType.DMA((2,)),
        ],
        compiler_params=VMEM,
        name="mlp_back",
    )(sel, g, branch, pre, xhat, inv, gain, scale, *w_ins, *w_outs)


def conv_back_kernel(need_map, gconv_ref, x_ref, g_ref, k_ref, *rest):
    if need_map:
        out_ref, tk_ref, pad_ref, sum_ref = rest
    else:
        tk_ref, pad_ref, sum_ref = rest
    rows, cols, channels = x_ref.shape
    tiles = channels // LANES
    zero_borders(pad_ref, rows, cols)
    for c in range(tiles):
        pad_ref[c, 3 : rows + 3, 8 : cols + 8] = gconv_ref[:, :, c * LANES : (c + 1) * LANES]
    for c in range(tiles):
        lanes = slice(c * LANES, (c + 1) * LANES)
        sum_ref[...] = jnp.zeros(sum_ref.shape, jnp.float32)

        def strip(w, carry, c=c, lanes=lanes):
            base = pl.multiple_of(w * 8, 8)
            window = pad_ref.at[c, :, pl.ds(base, 24), :]
            xs = x_ref[:, pl.ds(base, 8), lanes].astype(jnp.float32)
            if need_map:
                acc = g_ref[:, pl.ds(base, 8), lanes].astype(jnp.float32)
            for q in range(7):
                col = window[:, 11 - q : 19 - q, :]
                for r in range(7):
                    tap = r * 7 + q
                    shifted = col[6 - r : 6 - r + rows]
                    sum_ref[tap] += jnp.sum(xs * shifted, axis=0)
                    if need_map:
                        acc = acc + k_ref[tap : tap + 1, lanes][None] * shifted
            if need_map:
                out_ref[:, pl.ds(base, 8), lanes] = acc.astype(jnp.bfloat16)
            return carry

        lax.fori_loop(0, cols // 8, strip, 0)
        tk_ref[:, lanes] = jnp.sum(sum_ref[...], axis=1)


def conv_back(gconv, x, g, kernel, need_map=True):
    rows, cols, channels = x.shape
    tiles = channels // LANES
    taps = kernel.shape[0]
    out = (jax.ShapeDtypeStruct((taps, channels), jnp.float32),)
    if need_map:
        out = (jax.ShapeDtypeStruct((rows, cols, channels), jnp.bfloat16),) + out
    return pl.pallas_call(
        functools.partial(conv_back_kernel, need_map),
        out_shape=out,
        scratch_shapes=[
            pltpu.VMEM((tiles, rows + 6, cols + 16, LANES), jnp.float32),
            pltpu.VMEM((taps, 8, LANES), jnp.float32),
        ],
        compiler_params=VMEM,
        name="conv_back",
    )(gconv, x, g, kernel)


BF16 = jnp.bfloat16
F32 = jnp.float32


def block_forward(x, kernel, gain, scale, sel, w_ins, w_outs):
    rows, cols, channels = x.shape
    xhat, normed, inv = conv_norm(x, kernel, gain)
    y, pre, branch = mlp(sel, normed, x.reshape(rows * cols, channels), scale, w_ins, w_outs)
    return y.reshape(x.shape), (x, xhat, inv, pre, branch)


def block_backward(g, stored, kernel, gain, scale, sel, w_ins, w_outs, need_map):
    x, xhat, inv, pre, branch = stored
    rows, cols, channels = x.shape
    keep, send, small, gconv = mlp_back(
        sel, g.reshape(rows * cols, channels), branch, pre, xhat, inv, gain, scale, w_ins, w_outs
    )
    out = conv_back(gconv.reshape(x.shape), x, g, kernel, need_map)
    g_prev = out[0] if need_map else None
    return g_prev, keep, send, jnp.concatenate([out[-1], small[0:2]], axis=0)


def small_parameters(kernels, norm_gains, scales):
    taps = kernels.shape[1]
    fill = jnp.zeros((-(taps + 2) % 8, kernels.shape[2]), F32)
    return jnp.concatenate([kernels[0], norm_gains, scales, fill], axis=0)


def finish(t_kernel, t_gain, t_scale, t_in, t_out):
    return t_kernel[None], t_gain[None], t_in[None], t_out[None], t_scale[None]


def any_mesh(images, cotangent, kernels, norm_gains, w_in, w_out, scales):
    segments = lax.axis_size("segment")
    rank = lax.axis_index("segment")
    count = images.shape[0] // segments
    taps = kernels.shape[1]
    small = lax.all_gather(small_parameters(kernels, norm_gains, scales), "segment")
    all_in = lax.all_gather(w_in[0], "segment")
    all_out = lax.all_gather(w_out[0], "segment")
    zero = jnp.zeros((2,), jnp.int32)
    pieces = [[None] * 3 for _ in range(segments)]
    for i in range(count):
        x = lax.dynamic_index_in_dim(images, rank * count + i, 0, keepdims=False)
        g = lax.dynamic_index_in_dim(cotangent, rank * count + i, 0, keepdims=False)
        stash = []
        params = []
        for s in range(segments):
            params.append((small[s, :taps], small[s, taps : taps + 1], small[s, taps + 1 : taps + 2], zero, [all_in[s]], [all_out[s]]))
            x, kept = block_forward(x, *params[s])
            stash.append(kept)
        for s in reversed(range(segments)):
            g, t_in, t_out, t_small = block_backward(g, stash[s], *params[s], s > 0)
            terms = (t_in.astype(F32), t_out.astype(F32), t_small)
            pieces[s] = [b if a is None else a + b for a, b in zip(pieces[s], terms)]

    def summed(values, dim):
        mine = lax.psum_scatter(jnp.stack(values), "segment", scatter_dimension=0, tiled=False)
        return lax.psum_scatter(mine, "dp", scatter_dimension=dim, tiled=True)

    t_in = summed([p[0] for p in pieces], 0)
    t_out = summed([p[1] for p in pieces], 0).T
    t_small = summed([p[2] for p in pieces], 1)
    return finish(t_small[:taps], t_small[taps], t_small[taps + 1], t_in, t_out)


def partners(flip, extent=(4, 2, 2, 2)):
    pairs = []
    for index in range(32):
        z, y, x, c = index >> 3, (index >> 2) & 1, (index >> 1) & 1, index & 1
        other = ((z ^ flip[0]) << 3) | ((y ^ flip[1]) << 2) | ((x ^ flip[2]) << 1) | (c ^ flip[3])
        pairs.append((index, other))
    return pairs


def swap(value, z=0, y=0, x=0, c=0):
    return lax.ppermute(value, ("dp", "segment"), partners((z, y, x, c)))


def this_mesh(images, cotangent, kernels, norm_gains, w_in, w_out, scales):
    rank = lax.axis_index("segment")
    core = rank % 2
    chip = rank // 2
    depth = lax.axis_index("dp") // 2
    side = lax.axis_index("dp") % 2
    taps = kernels.shape[1]
    channels = kernels.shape[2]
    hidden = w_in.shape[2]
    share = channels // 8

    own = (small_parameters(kernels, norm_gains, scales), w_in[0], w_out[0])
    far = tuple(swap(v, x=1) for v in own)
    near = tuple(swap(v, c=1) for v in own)
    far_near = tuple(swap(v, c=1) for v in far)
    held = (own, near, far, far_near)
    small = jnp.stack([h[0] for h in held])
    w_ins = [h[1] for h in held]
    w_outs = [h[2] for h in held]

    x = lax.dynamic_index_in_dim(images, rank, 0, keepdims=False)
    g = lax.dynamic_index_in_dim(cotangent, rank, 0, keepdims=False)
    stash = []
    params = []
    for s in range(4):
        which = rank ^ s
        mine = lax.dynamic_index_in_dim(small, which, 0, keepdims=False)
        sel = jnp.stack([which, core]).astype(jnp.int32)
        params.append((mine[:taps], mine[taps : taps + 1], mine[taps + 1 : taps + 2], sel, w_ins, w_outs))
        x, kept = block_forward(x, *params[s])
        stash.append(kept)

    shares = [None] * 4
    smalls = [None] * 4
    for s in reversed(range(4)):
        g, keep, send, smalls[s] = block_backward(g, stash[s], *params[s], s > 0)
        keep = keep.reshape(4, 2, share, hidden)
        got = swap(send, c=1).reshape(4, 2, share, hidden)

        def half(value, which):
            return lax.dynamic_index_in_dim(value, which, 1, keepdims=False).astype(F32)

        across = (half(keep, 1 - side) + half(got, 1 - side)).astype(BF16)
        across = swap(across, y=1)
        line = (half(keep, side) + half(got, side) + across.astype(F32)).astype(BF16)

        def level(which):
            return lax.dynamic_index_in_dim(line, which, 0, keepdims=False)

        total = level(depth).astype(F32)
        for flip in (1, 2, 3):
            total = total + swap(level(depth ^ flip), z=flip).astype(F32)
        shares[s] = total

    rows = 56
    packed = jnp.stack([jnp.pad(v, ((0, rows - taps - 2), (0, 0))) for v in smalls])
    packed = packed.reshape(2, 2, rows, 8, share).transpose(1, 0, 3, 2, 4)
    mine = lax.dynamic_index_in_dim(packed, core, 0, keepdims=False)
    mine = mine + swap(lax.dynamic_index_in_dim(packed, 1 - core, 0, keepdims=False), c=1)
    mine = mine.reshape(2, 4, 2, rows, share)
    mine = lax.dynamic_index_in_dim(mine, side, 2, keepdims=False) + swap(
        lax.dynamic_index_in_dim(mine, 1 - side, 2, keepdims=False), y=1
    )
    line = mine
    mine = lax.dynamic_index_in_dim(line, depth, 1, keepdims=False)
    for flip in (1, 2, 3):
        mine = mine + swap(lax.dynamic_index_in_dim(line, depth ^ flip, 1, keepdims=False), z=flip)
    t_small = lax.dynamic_index_in_dim(mine, chip, 0, keepdims=False) + swap(
        lax.dynamic_index_in_dim(mine, 1 - chip, 0, keepdims=False), x=1
    )

    all_shares = jnp.stack(shares).reshape(2, 2, share, hidden)
    mine = lax.dynamic_index_in_dim(all_shares, chip, 0, keepdims=False) + swap(
        lax.dynamic_index_in_dim(all_shares, 1 - chip, 0, keepdims=False).astype(BF16), x=1
    ).astype(F32)
    kept = lax.dynamic_index_in_dim(mine, core, 0, keepdims=False)
    got = swap(lax.dynamic_index_in_dim(mine, 1 - core, 0, keepdims=False), c=1)
    t_in = jnp.where(core == 0, kept, got)
    t_out = jnp.where(core == 0, got, kept).T
    return finish(t_small[:taps], t_small[taps], t_small[taps + 1], t_in, t_out)


def solution(mesh):
    in_specs = (
        P("dp", None, None, None),
        P("dp", None, None, None),
        P("segment", None, None),
        P("segment", None),
        P("segment", None, None),
        P("segment", None, None),
        P("segment", None),
    )
    out_specs = (
        P("segment", None, "dp"),
        P("segment", "dp"),
        P("segment", "dp", None),
        P("segment", None, "dp"),
        P("segment", "dp"),
    )
    fits = dict(mesh.shape) == {"dp": 8, "segment": 4}

    def whole(images, *rest):
        local = this_mesh if fits and images.shape[0] == 32 else any_mesh
        return jax.shard_map(local, mesh=mesh, in_specs=in_specs, out_specs=out_specs, check_vma=False)(images, *rest)

    return whole
```

time: 684 us -> 165 us (0.24)
  waiting for transfers between devices: 304 us -> 66.9 us
  local copies, waits for them, and re-layouts: 124 us -> 10.7 us
  other arithmetic: 126 us -> 13.8 us
  Pallas kernels: 0 us -> 39.9 us
  starting transfers between devices: 56.5 us -> 31.2 us
  matrix products: 24.1 us -> 0 us
  blocking collectives: 23.1 us -> 0 us
  between operations: 14.5 us -> 1.4 us
  loops' own time: 7.6 us -> 0 us
    reduce_scatter x3 -> x0, waiting for transfers between devices: 170 us -> none  [the longest x1 67.4 us: local(): lax.psum_scatter(totals[2], 'dp', scatter_dimension=0, tiled=True)]
    another operation x206 -> x0, local copies, waits for them, and re-layouts: 73.6 us -> none  [the longest x200 70.1 us: backward_parts(): grad_kernel = jnp.stack(kernel_rows)]
    ppermute x14 -> x37, waiting for transfers between devices: 134 us -> 66.9 us  [swap(): return lax.ppermute(value, ('dp', 'segment'), partners((z, y, x, c)))]
    reduce_sum x28 -> x0, other arithmetic: 47.9 us -> none  [the longest x8 29.2 us: forward_parts(): center = flat_rows - jnp.mean(flat_rows, axis=1, keepdims=True)]
    pallas_call x0 -> x16, Pallas kernels: none -> 39.9 us  [the longest x4 11.8 us: conv_back(): pl.pallas_call(functools.partial(conv_back_kernel, need_map), out_shape=o...]
    add x28 -> x5, other arithmetic: 35.7 us -> 1.74 us  [the longest x1 0.88 us: this_mesh(): mine + swap(lax.dynamic_index_in_dim(line, depth ^ flip, 1, keepdims=Fals...]
    slice x24 -> x7, local copies, waits for them, and re-layouts: 30.8 us -> 0.16 us  [the longest x1 0.08 us: this_mesh(): return finish(t_small[:taps], t_small[taps], t_small[taps + 1], t_in, t_out)]
    ppermute x14 -> x37, starting transfers between devices: 56.3 us -> 31.2 us  [swap(): return lax.ppermute(value, ('dp', 'segment'), partners((z, y, x, c)))]
  transfers between devices with their start and end apart: 17 -> 37, of which waited for: 16 -> 19; matrix products, arithmetic and copies ran while one was open for 6% -> 11% of each run, Pallas kernels for 0% -> 2%
where the time goes in v1:
time: 165 us; the launch traced here: 164 us
  waiting for transfers between devices  66.9 us (41%)
  Pallas kernels  39.9 us (24%)
  starting transfers between devices  31.2 us (19%)
  other arithmetic  13.8 us (8%)
  local copies, waits for them, and re-layouts  10.7 us (6%)
    ppermute x37, waiting for transfers between devices, swap(): return lax.ppermute(value, ('dp', 'segment'), partners((z, y, x, c)))  66.9 us
    ppermute x37, starting transfers between devices, swap(): return lax.ppermute(value, ('dp', 'segment'), partners((z, y, x, c)))  31.2 us
    pallas_call x4, Pallas kernels, conv_back(): pl.pallas_call(functools.partial(conv_back_kernel, need_map), out_shape=o...  11.8 us
    pallas_call x4, Pallas kernels, conv_norm(): pl.pallas_call(conv_norm_kernel, out_shape=(jax.ShapeDtypeStruct((n, chan...  10.3 us
    pallas_call x4, Pallas kernels, mlp_back(): pl.pallas_call(functools.partial(mlp_back_kernel, len(w_ins)), in_specs=s...  9.88 us
    pallas_call x4, Pallas kernels, mlp(): pl.pallas_call(functools.partial(mlp_kernel, len(w_ins)), in_specs=specs(...  7.86 us
    unnamed x59, local copies, waits for them, and re-layouts  5.85 us
    convert_element_type x4, other arithmetic, this_mesh(): (half(keep, side) + half(got, side) + across.astype(F32)).astype(BF16)  4.31 us
  transfers between devices with their start and end apart: 37, of which 19 were waited for; matrix products, arithmetic and copies ran while one was open for 11% of the time, Pallas kernels for 2%

profile of v1, /device:TPU:0, one launch (start us, length us, event | category | flops | bytes accessed | tf_op | source)
XLA Modules:
  0.0 164.0 jit_solution(27991048411758026)
XLA Ops:
  0.6 3.0 %collective-permute-start.4 = (bf16[384,768]{1,0:T(8,128)(2,1)}, bf16[384,768]{1,0:T(8,128)(2,1)S(1)}, u32[]{:S(2)}, u32[]{:S(2)}) collective-permute-start(bf16[384,768]{1,0:T(8,128)(2,1)} %bitcast.217), channel_id=1, source_target_pairs={{0,2},{1,3},{2,0},{3,1},{4,6},{5,7},{6,4},{7,5},{8,10},{9,11},{10,... | collective-permute-start | bytes 1769480 | tf_op jit(solution)/shard_map/ppermute | solution.py:379
  7.3 10.8 %collective-permute-done.4.rest_2_ = bf16[384,768]{1,0:T(8,128)(2,1)S(1)} collective-permute-done((bf16[384,768]{1,0:T(8,128)(2,1)}, bf16[384,768]{1,0:T(8,128)(2,1)S(1)}, u32[]{:S(2)}, u32[]{:S(2)}) %collective-permute-start.4) | collective-permute-done | bytes 589856 | tf_op jit(solution)/shard_map/ppermute | solution.py:379
  18.0 11.8 %collective-permute-done.7.rest_6_ = bf16[768,384]{1,0:T(8,128)(2,1)S(1)} collective-permute-done((bf16[768,384]{1,0:T(8,128)(2,1)}, bf16[768,384]{1,0:T(8,128)(2,1)S(1)}, u32[]{:S(2)}, u32[]{:S(2)}) %collective-permute-start.7) | collective-permute-done | bytes 589856 | tf_op jit(solution)/shard_map/ppermute | solution.py:379
  29.8 1.8 %constant_dynamic-slice_fusion.10 = (bf16[1,16,16,384]{3,2,1,0:T(8,128)(2,1)}, bf16[1,16,16,384]{3,2,1,0:T(8,128)(2,1)}) fusion(bf16[4,16,16,384]{3,2,1,0:T(8,128)(2,1)} %param.7, s32[]{:T(128)S(6)} %select_n.121, bf16[4,16,16,384]{3,2,1,0:T(8,128)(2,1)} %param.8), kind=kLoop, calls=%fused_computation.92 | loop fusion | bytes 786436 | tf_op jit(solution)/shard_map/jit(dynamic_index_in_dim)/dynamic_slice | solution.py:402
  33.4 3.3 %collective-permute-done.1 = f32[56,384]{1,0:T(8,128)S(1)} collective-permute-done((f32[56,384]{1,0:T(8,128)}, f32[56,384]{1,0:T(8,128)S(1)}, u32[]{:S(2)}, u32[]{:S(2)}) %collective-permute-start.1) | collective-permute-done | bytes 86048 | tf_op jit(solution)/shard_map/ppermute | solution.py:379
  39.2 2.6 %conv_norm.4 = (bf16[256,384]{1,0:T(8,128)(2,1)S(1)}, bf16[256,384]{1,0:T(8,128)(2,1)S(1)}, f32[256,128]{1,0:T(8,128)S(1)}) custom-call(bf16[16,16,384]{2,1,0:T(8,128)(2,1)S(1)} %bitcast.237, f32[49,384]{1,0:T(8,128)S(1)} %get-tuple-element.115.k_ref, f32[1,384]{1,0:T(1,128)S(1)} %get-tuple-element.108.gain_ref), custom_call_target="tpu_custom_call" | custom-call | tf_op jit(solution)/shard_map/conv_norm/pallas_call | solution.py:67
  43.7 2.6 %conv_norm.5 = (bf16[256,384]{1,0:T(8,128)(2,1)S(1)}, bf16[256,384]{1,0:T(8,128)(2,1)S(1)}, f32[256,128]{1,0:T(8,128)S(1)}) custom-call(bf16[16,16,384]{2,1,0:T(8,128)(2,1)S(1)} %bitcast.242, f32[49,384]{1,0:T(8,128)S(1)} %get-tuple-element.114.k_ref, f32[1,384]{1,0:T(1,128)S(1)} %get-tuple-element.107.gain_ref), custom_call_target="tpu_custom_call" | custom-call | tf_op jit(solution)/shard_map/conv_norm/pallas_call | solution.py:67
  48.1 2.6 %conv_norm.6 = (bf16[256,384]{1,0:T(8,128)(2,1)S(1)}, bf16[256,384]{1,0:T(8,128)(2,1)S(1)}, f32[256,128]{1,0:T(8,128)S(1)}) custom-call(bf16[16,16,384]{2,1,0:T(8,128)(2,1)S(1)} %bitcast.244, f32[49,384]{1,0:T(8,128)S(1)} %get-tuple-element.113.k_ref, f32[1,384]{1,0:T(1,128)S(1)} %get-tuple-element.106.gain_ref), custom_call_target="tpu_custom_call" | custom-call | tf_op jit(solution)/shard_map/conv_norm/pallas_call | solution.py:67
  52.5 2.6 %conv_norm.7 = (bf16[256,384]{1,0:T(8,128)(2,1)S(1)}, bf16[256,384]{1,0:T(8,128)(2,1)S(1)}, f32[256,128]{1,0:T(8,128)S(1)}) custom-call(bf16[16,16,384]{2,1,0:T(8,128)(2,1)S(1)} %bitcast.246, f32[49,384]{1,0:T(8,128)S(1)} %get-tuple-element.112.k_ref, f32[1,384]{1,0:T(1,128)S(1)} %get-tuple-element.105.gain_ref), custom_call_target="tpu_custom_call" | custom-call | tf_op jit(solution)/shard_map/conv_norm/pallas_call | solution.py:67
  55.1 2.5 %mlp.7 = (bf16[256,384]{1,0:T(8,128)(2,1)}, bf16[256,768]{1,0:T(8,128)(2,1)S(1)}, bf16[256,384]{1,0:T(8,128)(2,1)S(1)}) custom-call(s32[2]{0:T(128)S(1)} %get-tuple-element.136.sel_ref, bf16[256,384]{1,0:T(8,128)(2,1)S(1)} %get-tuple-element.56.normed_ref, bf16[256,384]{1,0:T(8,128)(2,1)S(1)} %get-tuple-element.55.x_ref, ...), custom_call_target="tpu_custom_call" | custom-call | tf_op jit(solution)/shard_map/mlp/pallas_call | solution.py:143
  57.6 2.4 %mlp_back.4 = (bf16[384,768]{1,0:T(8,128)(2,1)S(1)}, bf16[384,768]{1,0:T(8,128)(2,1)S(1)}, f32[8,384]{1,0:T(8,128)S(1)}, f32[256,384]{1,0:T(8,128)S(1)}) custom-call(s32[2]{0:T(128)S(1)} %get-tuple-element.136.sel_ref, bf16[256,384]{1,0:T(8,128)(2,1)S(1)} %bitcast.240, bf16[256,384]{1,0:T(8,128)(2,1)S(1)} %get-tuple-element.57.branch_ref, ...), custom_call_target="tpu_custom_call" | custom-call | tf_op jit(solution)/shard_map/mlp_back/pallas_call | solution.py:224
  60.8 3.4 %conv_back.4 = (bf16[16,16,384]{2,1,0:T(8,128)(2,1)S(1)}, f32[49,384]{1,0:T(8,128)S(1)}) custom-call(f32[16,16,384]{2,1,0:T(8,128)S(1)} %bitcast.259, bf16[16,16,384]{2,1,0:T(8,128)(2,1)S(1)} %bitcast.247, bf16[16,16,384]{2,1,0:T(8,128)(2,1)S(1)} %bitcast.241, f32[49,384]{1,0:T(8,128)S(1)} %get-tuple-element.112.k_ref), custom_call_target="tpu_custom_call" | custom-call | tf_op jit(solution)/shard_map/conv_back/pallas_call | solution.py:291
  64.2 2.5 %mlp_back.5 = (bf16[384,768]{1,0:T(8,128)(2,1)S(1)}, bf16[384,768]{1,0:T(8,128)(2,1)S(1)}, f32[8,384]{1,0:T(8,128)S(1)}, f32[256,384]{1,0:T(8,128)S(1)}) custom-call(s32[2]{0:T(128)S(1)} %get-tuple-element.135.sel_ref, bf16[256,384]{1,0:T(8,128)(2,1)S(1)} %bitcast.249, bf16[256,384]{1,0:T(8,128)(2,1)S(1)} %get-tuple-element.63.branch_ref, ...), custom_call_target="tpu_custom_call" | custom-call | tf_op jit(solution)/shard_map/mlp_back/pallas_call | solution.py:224
  66.8 3.4 %conv_back.5 = (bf16[16,16,384]{2,1,0:T(8,128)(2,1)S(1)}, f32[49,384]{1,0:T(8,128)S(1)}) custom-call(f32[16,16,384]{2,1,0:T(8,128)S(1)} %bitcast.260, bf16[16,16,384]{2,1,0:T(8,128)(2,1)S(1)} %bitcast.245, bf16[16,16,384]{2,1,0:T(8,128)(2,1)S(1)} %get-tuple-element.62.g_ref, f32[49,384]{1,0:T(8,128)S(1)} %get-tuple-element.113.k_ref), custom_call_target="tpu_custom_call" | custom-call | tf_op jit(solution)/shard_map/conv_back/pallas_call | solution.py:291
  70.2 2.4 %mlp_back.6 = (bf16[384,768]{1,0:T(8,128)(2,1)S(1)}, bf16[384,768]{1,0:T(8,128)(2,1)S(1)}, f32[8,384]{1,0:T(8,128)S(1)}, f32[256,384]{1,0:T(8,128)S(1)}) custom-call(s32[2]{0:T(128)S(1)} %get-tuple-element.134.sel_ref, bf16[256,384]{1,0:T(8,128)(2,1)S(1)} %bitcast.248, bf16[256,384]{1,0:T(8,128)(2,1)S(1)} %get-tuple-element.69.branch_ref, ...), custom_call_target="tpu_custom_call" | custom-call | tf_op jit(solution)/shard_map/mlp_back/pallas_call | solution.py:224
  73.4 3.4 %conv_back.6 = (bf16[16,16,384]{2,1,0:T(8,128)(2,1)S(1)}, f32[49,384]{1,0:T(8,128)S(1)}) custom-call(f32[16,16,384]{2,1,0:T(8,128)S(1)} %bitcast.261, bf16[16,16,384]{2,1,0:T(8,128)(2,1)S(1)} %bitcast.243, bf16[16,16,384]{2,1,0:T(8,128)(2,1)S(1)} %get-tuple-element.68.g_ref, f32[49,384]{1,0:T(8,128)S(1)} %get-tuple-element.114.k_ref), custom_call_target="tpu_custom_call" | custom-call | tf_op jit(solution)/shard_map/conv_back/pallas_call | solution.py:291
  76.8 2.6 %mlp_back.7 = (bf16[384,768]{1,0:T(8,128)(2,1)S(1)}, bf16[384,768]{1,0:T(8,128)(2,1)S(1)}, f32[8,384]{1,0:T(8,128)S(1)}, f32[256,384]{1,0:T(8,128)S(1)}) custom-call(s32[2]{0:T(128)S(1)} %get-tuple-element.133.sel_ref, bf16[256,384]{1,0:T(8,128)(2,1)S(1)} %bitcast.250, bf16[256,384]{1,0:T(8,128)(2,1)S(1)} %get-tuple-element.75.branch_ref, ...), custom_call_target="tpu_custom_call" | custom-call | tf_op jit(solution)/shard_map/mlp_back/pallas_call | solution.py:224
  84.1 1.8 %collective-permute-start.10 = (f32[2,4,56,48]{2,3,1,0:T(8,128)S(1)}, f32[2,4,56,48]{2,3,1,0:T(8,128)S(1)}, u32[]{:S(2)}, u32[]{:S(2)}) collective-permute-start(f32[2,4,56,48]{2,3,1,0:T(8,128)S(1)} %bitcast.268), channel_id=1, source_target_pairs={{0,4},{1,5},{2,6},{3,7},{4,0},{5,1},{6,2},{7,3},{8,12},{9,13},{10,... | collective-permute-start | bytes 258056 | tf_op jit(solution)/shard_map/ppermute | solution.py:379
  86.0 5.1 %collective-permute-done.10 = f32[2,4,56,48]{2,3,1,0:T(8,128)S(1)} collective-permute-done((f32[2,4,56,48]{2,3,1,0:T(8,128)S(1)}, f32[2,4,56,48]{2,3,1,0:T(8,128)S(1)}, u32[]{:S(2)}, u32[]{:S(2)}) %collective-permute-start.10) | collective-permute-done | bytes 86048 | tf_op jit(solution)/shard_map/ppermute | solution.py:379
  91.9 1.8 %collective-permute-start.11 = (f32[2,56,48]{1,2,0:T(8,128)S(1)}, f32[2,56,48]{1,2,0:T(8,128)S(1)}, u32[]{:S(2)}, u32[]{:S(2)}) collective-permute-start(f32[2,56,48]{1,2,0:T(8,128)S(1)} %get-tuple-element.128), channel_id=1, source_target_pairs={{0,8},{1,9},{2,10},{3,11},{4,12},{5,13},{6,14},{7,15},{8,0},{9,1},... | collective-permute-start | bytes 64520 | tf_op jit(solution)/shard_map/ppermute | solution.py:379
  93.7 2.5 %collective-permute-start.13 = (f32[2,56,48]{1,2,0:T(8,128)}, f32[2,56,48]{1,2,0:T(8,128)}, u32[]{:S(2)}, u32[]{:S(2)}) collective-permute-start(f32[2,56,48]{1,2,0:T(8,128)} %get-tuple-element.129), channel_id=1, source_target_pairs={{0,24},{1,25},{2,26},{3,27},{4,28},{5,29},{6,30},{7,31},{8,16},{9,... | collective-permute-start | bytes 64520 | tf_op jit(solution)/shard_map/ppermute | solution.py:379
  97.5 2.5 %collective-permute-done.13 = f32[2,56,48]{1,2,0:T(8,128)} collective-permute-done((f32[2,56,48]{1,2,0:T(8,128)}, f32[2,56,48]{1,2,0:T(8,128)}, u32[]{:S(2)}, u32[]{:S(2)}) %collective-permute-start.13) | collective-permute-done | bytes 21536 | tf_op jit(solution)/shard_map/ppermute | solution.py:379
  100.0 2.0 %collective-permute-done.12 = f32[2,56,48]{1,2,0:T(8,128)} collective-permute-done((f32[2,56,48]{1,2,0:T(8,128)}, f32[2,56,48]{1,2,0:T(8,128)}, u32[]{:S(2)}, u32[]{:S(2)}) %collective-permute-start.12) | collective-permute-done | bytes 21536 | tf_op jit(solution)/shard_map/ppermute | solution.py:379
  105.0 2.6 %collective-permute-done.14 = f32[56,48]{0,1:T(8,128)} collective-permute-done((f32[56,48]{0,1:T(8,128)}, f32[56,48]{0,1:T(8,128)}, u32[]{:S(2)}, u32[]{:S(2)}) %collective-permute-start.14) | collective-permute-done | bytes 10784 | tf_op jit(solution)/shard_map/ppermute | solution.py:379
  116.9 2.6 %collective-permute-done.31 = bf16[4,48,768]{2,1,0:T(8,128)(2,1)S(1)} collective-permute-done((bf16[4,48,768]{2,1,0:T(8,128)(2,1)S(1)}, bf16[4,48,768]{2,1,0:T(8,128)(2,1)S(1)}, u32[]{:S(2)}, u32[]{:S(2)}) %collective-permute-start.31) | collective-permute-done | bytes 294944 | tf_op jit(solution)/shard_map/ppermute | solution.py:379
  122.3 3.5 %collective-permute-done.26 = bf16[4,48,768]{2,1,0:T(8,128)(2,1)S(1)} collective-permute-done((bf16[4,48,768]{2,1,0:T(8,128)(2,1)S(1)}, bf16[4,48,768]{2,1,0:T(8,128)(2,1)S(1)}, u32[]{:S(2)}, u32[]{:S(2)}) %collective-permute-start.26) | collective-permute-done | bytes 294944 | tf_op jit(solution)/shard_map/ppermute | solution.py:379
  127.1 5.0 %collective-permute-done.16 = bf16[4,48,768]{2,1,0:T(8,128)(2,1)S(1)} collective-permute-done((bf16[4,48,768]{2,1,0:T(8,128)(2,1)S(1)}, bf16[4,48,768]{2,1,0:T(8,128)(2,1)S(1)}, u32[]{:S(2)}, u32[]{:S(2)}) %collective-permute-start.16) | collective-permute-done | bytes 294944 | tf_op jit(solution)/shard_map/ppermute | solution.py:379
  138.2 2.7 %collective-permute-start.17 = (bf16[48,768]{1,0:T(8,128)(2,1)S(1)}, bf16[48,768]{1,0:T(8,128)(2,1)S(1)}, u32[]{:S(2)}, u32[]{:S(2)}) collective-permute-start(bf16[48,768]{1,0:T(8,128)(2,1)S(1)} %get-tuple-element.116), channel_id=1, source_target_pairs={{0,8},{1,9},{2,10},{3,11},{4,12},{5,13},{6,14},{7,15},{8,0},{9,1},... | collective-permute-start | bytes 221192 | tf_op jit(solution)/shard_map/ppermute | solution.py:379
  142.6 2.8 %collective-permute-start.22 = (bf16[48,768]{1,0:T(8,128)(2,1)S(1)}, bf16[48,768]{1,0:T(8,128)(2,1)S(1)}, u32[]{:S(2)}, u32[]{:S(2)}) collective-permute-start(bf16[48,768]{1,0:T(8,128)(2,1)S(1)} %get-tuple-element.119), channel_id=1, source_target_pairs={{0,8},{1,9},{2,10},{3,11},{4,12},{5,13},{6,14},{7,15},{8,0},{9,1},... | collective-permute-start | bytes 221192 | tf_op jit(solution)/shard_map/ppermute | solution.py:379
  145.4 3.3 %collective-permute-done.28 = bf16[48,768]{1,0:T(8,128)(2,1)S(1)} collective-permute-done((bf16[48,768]{1,0:T(8,128)(2,1)S(1)}, bf16[48,768]{1,0:T(8,128)(2,1)S(1)}, u32[]{:S(2)}, u32[]{:S(2)}) %collective-permute-start.28) | collective-permute-done | bytes 73760 | tf_op jit(solution)/shard_map/ppermute | solution.py:379
  151.9 2.9 %collective-permute-done.24 = bf16[48,768]{1,0:T(8,128)(2,1)S(1)} collective-permute-done((bf16[48,768]{1,0:T(8,128)(2,1)S(1)}, bf16[48,768]{1,0:T(8,128)(2,1)S(1)}, u32[]{:S(2)}, u32[]{:S(2)}) %collective-permute-start.24) | collective-permute-done | bytes 73760 | tf_op jit(solution)/shard_map/ppermute | solution.py:379
  157.9 3.9 %collective-permute-done.35 = bf16[2,48,768]{2,1,0:T(8,128)(2,1)S(1)} collective-permute-done((bf16[2,48,768]{2,1,0:T(8,128)(2,1)S(1)}, bf16[2,48,768]{2,1,0:T(8,128)(2,1)S(1)}, u32[]{:S(2)}, u32[]{:S(2)}) %collective-permute-start.35) | collective-permute-done | bytes 147488 | tf_op jit(solution)/shard_map/ppermute | solution.py:379
  (168 shorter events, 54.1 us)
Async XLA Ops:
  0.6 17.4 %collective-permute-start.4 = (bf16[384,768]{1,0:T(8,128)(2,1)}, bf16[384,768]{1,0:T(8,128)(2,1)S(1)}, u32[]{:S(2)}, u32[]{:S(2)}) collective-permute-start(bf16[384,768]{1,0:T(8,128)(2,1)} %bitcast.217), channel_id=1, source_target_pairs={{0,2},{1,3},{2,0},{3,1},{4,6},{5,7},{6,4},{7,5},{8,10},{9,11},{10,... | collective-permute-start | bytes 1769480 | tf_op jit(solution)/shard_map/ppermute | solution.py:379
  3.6 26.2 %collective-permute-start.7 = (bf16[768,384]{1,0:T(8,128)(2,1)}, bf16[768,384]{1,0:T(8,128)(2,1)S(1)}, u32[]{:S(2)}, u32[]{:S(2)}) collective-permute-start(bf16[768,384]{1,0:T(8,128)(2,1)} %bitcast.227), channel_id=1, source_target_pairs={{0,2},{1,3},{2,0},{3,1},{4,6},{5,7},{6,4},{7,5},{8,10},{9,11},{10,... | collective-permute-start | bytes 1769480 | tf_op jit(solution)/shard_map/ppermute | solution.py:379
  3.7 38.1 %collective-permute-start.3 = (bf16[384,768]{1,0:T(8,128)(2,1)}, bf16[384,768]{1,0:T(8,128)(2,1)S(1)}, u32[]{:S(2)}, u32[]{:S(2)}) collective-permute-start(bf16[384,768]{1,0:T(8,128)(2,1)} %bitcast.218), channel_id=1, source_target_pairs={{0,1},{1,0},{2,3},{3,2},{4,5},{5,4},{6,7},{7,6},{8,9},{9,8},{10,11... | collective-permute-start | bytes 1769480 | tf_op jit(solution)/shard_map/ppermute | solution.py:379
  3.7 38.1 %collective-permute-start.6 = (bf16[768,384]{1,0:T(8,128)(2,1)}, bf16[768,384]{1,0:T(8,128)(2,1)S(1)}, u32[]{:S(2)}, u32[]{:S(2)}) collective-permute-start(bf16[768,384]{1,0:T(8,128)(2,1)} %bitcast.228), channel_id=1, source_target_pairs={{0,1},{1,0},{2,3},{3,2},{4,5},{5,4},{6,7},{7,6},{8,9},{9,8},{10,11... | collective-permute-start | bytes 1769480 | tf_op jit(solution)/shard_map/ppermute | solution.py:379
  6.5 25.1 %collective-permute-start = (f32[56,384]{1,0:T(8,128)}, f32[56,384]{1,0:T(8,128)}, u32[]{:S(2)}, u32[]{:S(2)}) collective-permute-start(f32[56,384]{1,0:T(8,128)} %maximum_maximum_fusion), channel_id=1, source_target_pairs={{0,1},{1,0},{2,3},{3,2},{4,5},{5,4},{6,7},{7,6},{8,9},{9,8},{10,11... | collective-permute-start | bytes 258056 | tf_op jit(solution)/shard_map/ppermute | solution.py:379
  18.0 23.8 %collective-permute-start.5 = (bf16[384,768]{1,0:T(8,128)(2,1)S(1)}, bf16[384,768]{1,0:T(8,128)(2,1)S(1)}, u32[]{:S(2)}, u32[]{:S(2)}) collective-permute-start(bf16[384,768]{1,0:T(8,128)(2,1)S(1)} %collective-permute-done.4.rest_2_), channel_id=1, source_target_pairs={{0,1},{1,0},{2,3},{3,2},{4,5},{5,4},{6,7},{7,6},{8,9},{9,8},{10,11... | collective-permute-start | bytes 1769480 | tf_op jit(solution)/shard_map/ppermute | solution.py:379
  29.8 12.0 %collective-permute-start.8 = (bf16[768,384]{1,0:T(8,128)(2,1)S(1)}, bf16[768,384]{1,0:T(8,128)(2,1)S(1)}, u32[]{:S(2)}, u32[]{:S(2)}) collective-permute-start(bf16[768,384]{1,0:T(8,128)(2,1)S(1)} %collective-permute-done.7.rest_6_), channel_id=1, source_target_pairs={{0,1},{1,0},{2,3},{3,2},{4,5},{5,4},{6,7},{7,6},{8,9},{9,8},{10,11... | collective-permute-start | bytes 1769480 | tf_op jit(solution)/shard_map/ppermute | solution.py:379
  31.6 5.2 %collective-permute-start.1 = (f32[56,384]{1,0:T(8,128)}, f32[56,384]{1,0:T(8,128)S(1)}, u32[]{:S(2)}, u32[]{:S(2)}) collective-permute-start(f32[56,384]{1,0:T(8,128)} %maximum_maximum_fusion), channel_id=1, source_target_pairs={{0,2},{1,3},{2,0},{3,1},{4,6},{5,7},{6,4},{7,5},{8,10},{9,11},{10,... | collective-permute-start | bytes 258056 | tf_op jit(solution)/shard_map/ppermute | solution.py:379
  84.1 7.1 %collective-permute-start.10 = (f32[2,4,56,48]{2,3,1,0:T(8,128)S(1)}, f32[2,4,56,48]{2,3,1,0:T(8,128)S(1)}, u32[]{:S(2)}, u32[]{:S(2)}) collective-permute-start(f32[2,4,56,48]{2,3,1,0:T(8,128)S(1)} %bitcast.268), channel_id=1, source_target_pairs={{0,4},{1,5},{2,6},{3,7},{4,0},{5,1},{6,2},{7,3},{8,12},{9,13},{10,... | collective-permute-start | bytes 258056 | tf_op jit(solution)/shard_map/ppermute | solution.py:379
  93.7 6.3 %collective-permute-start.13 = (f32[2,56,48]{1,2,0:T(8,128)}, f32[2,56,48]{1,2,0:T(8,128)}, u32[]{:S(2)}, u32[]{:S(2)}) collective-permute-start(f32[2,56,48]{1,2,0:T(8,128)} %get-tuple-element.129), channel_id=1, source_target_pairs={{0,24},{1,25},{2,26},{3,27},{4,28},{5,29},{6,30},{7,31},{8,16},{9,... | collective-permute-start | bytes 64520 | tf_op jit(solution)/shard_map/ppermute | solution.py:379
  96.1 5.8 %collective-permute-start.12 = (f32[2,56,48]{1,2,0:T(8,128)}, f32[2,56,48]{1,2,0:T(8,128)}, u32[]{:S(2)}, u32[]{:S(2)}) collective-permute-start(f32[2,56,48]{1,2,0:T(8,128)} %get-tuple-element.130), channel_id=1, source_target_pairs={{0,16},{1,17},{2,18},{3,19},{4,20},{5,21},{6,22},{7,23},{8,24},{9,... | collective-permute-start | bytes 64520 | tf_op jit(solution)/shard_map/ppermute | solution.py:379
  96.2 12.1 %collective-permute-start.30 = (bf16[384,768]{1,0:T(8,128)(2,1)S(1)}, bf16[384,768]{1,0:T(8,128)(2,1)}, u32[]{:S(2)}, u32[]{:S(2)}) collective-permute-start(bf16[384,768]{1,0:T(8,128)(2,1)S(1)} %copy-done.13), channel_id=1, source_target_pairs={{0,1},{1,0},{2,3},{3,2},{4,5},{5,4},{6,7},{7,6},{8,9},{9,8},{10,11... | collective-permute-start | bytes 1769480 | tf_op jit(solution)/shard_map/ppermute | solution.py:379
  96.3 14.8 %collective-permute-start.25 = (bf16[384,768]{1,0:T(8,128)(2,1)S(1)}, bf16[384,768]{1,0:T(8,128)(2,1)}, u32[]{:S(2)}, u32[]{:S(2)}) collective-permute-start(bf16[384,768]{1,0:T(8,128)(2,1)S(1)} %copy-done.15), channel_id=1, source_target_pairs={{0,1},{1,0},{2,3},{3,2},{4,5},{5,4},{6,7},{7,6},{8,9},{9,8},{10,11... | collective-permute-start | bytes 1769480 | tf_op jit(solution)/shard_map/ppermute | solution.py:379
  97.4 15.3 %collective-permute-start.15 = (bf16[384,768]{1,0:T(8,128)(2,1)S(1)}, bf16[384,768]{1,0:T(8,128)(2,1)}, u32[]{:S(2)}, u32[]{:S(2)}) collective-permute-start(bf16[384,768]{1,0:T(8,128)(2,1)S(1)} %copy-done.19), channel_id=1, source_target_pairs={{0,1},{1,0},{2,3},{3,2},{4,5},{5,4},{6,7},{7,6},{8,9},{9,8},{10,11... | collective-permute-start | bytes 1769480 | tf_op jit(solution)/shard_map/ppermute | solution.py:379
  105.0 10.3 %collective-permute-start.20 = (bf16[384,768]{1,0:T(8,128)(2,1)S(1)}, bf16[384,768]{1,0:T(8,128)(2,1)}, u32[]{:S(2)}, u32[]{:S(2)}) collective-permute-start(bf16[384,768]{1,0:T(8,128)(2,1)S(1)} %copy-done.17), channel_id=1, source_target_pairs={{0,1},{1,0},{2,3},{3,2},{4,5},{5,4},{6,7},{7,6},{8,9},{9,8},{10,11... | collective-permute-start | bytes 1769480 | tf_op jit(solution)/shard_map/ppermute | solution.py:379
  109.5 10.0 %collective-permute-start.31 = (bf16[4,48,768]{2,1,0:T(8,128)(2,1)S(1)}, bf16[4,48,768]{2,1,0:T(8,128)(2,1)S(1)}, u32[]{:S(2)}, u32[]{:S(2)}) collective-permute-start(bf16[4,48,768]{2,1,0:T(8,128)(2,1)S(1)} %fusion.7), channel_id=1, source_target_pairs={{0,4},{1,5},{2,6},{3,7},{4,0},{5,1},{6,2},{7,3},{8,12},{9,13},{10,... | collective-permute-start | bytes 884744 | tf_op jit(solution)/shard_map/ppermute | solution.py:379
  112.1 13.7 %collective-permute-start.26 = (bf16[4,48,768]{2,1,0:T(8,128)(2,1)S(1)}, bf16[4,48,768]{2,1,0:T(8,128)(2,1)S(1)}, u32[]{:S(2)}, u32[]{:S(2)}) collective-permute-start(bf16[4,48,768]{2,1,0:T(8,128)(2,1)S(1)} %fusion.6), channel_id=1, source_target_pairs={{0,4},{1,5},{2,6},{3,7},{4,0},{5,1},{6,2},{7,3},{8,12},{9,13},{10,... | collective-permute-start | bytes 884744 | tf_op jit(solution)/shard_map/ppermute | solution.py:379
  113.7 18.4 %collective-permute-start.16 = (bf16[4,48,768]{2,1,0:T(8,128)(2,1)S(1)}, bf16[4,48,768]{2,1,0:T(8,128)(2,1)S(1)}, u32[]{:S(2)}, u32[]{:S(2)}) collective-permute-start(bf16[4,48,768]{2,1,0:T(8,128)(2,1)S(1)} %fusion.4), channel_id=1, source_target_pairs={{0,4},{1,5},{2,6},{3,7},{4,0},{5,1},{6,2},{7,3},{8,12},{9,13},{10,... | collective-permute-start | bytes 884744 | tf_op jit(solution)/shard_map/ppermute | solution.py:379
  116.4 18.9 %collective-permute-start.21 = (bf16[4,48,768]{2,1,0:T(8,128)(2,1)S(1)}, bf16[4,48,768]{2,1,0:T(8,128)(2,1)S(1)}, u32[]{:S(2)}, u32[]{:S(2)}) collective-permute-start(bf16[4,48,768]{2,1,0:T(8,128)(2,1)S(1)} %fusion.5), channel_id=1, source_target_pairs={{0,4},{1,5},{2,6},{3,7},{4,0},{5,1},{6,2},{7,3},{8,12},{9,13},{10,... | collective-permute-start | bytes 884744 | tf_op jit(solution)/shard_map/ppermute | solution.py:379
  120.6 17.4 %collective-permute-start.32 = (bf16[48,768]{1,0:T(8,128)(2,1)S(1)}, bf16[48,768]{1,0:T(8,128)(2,1)S(1)}, u32[]{:S(2)}, u32[]{:S(2)}) collective-permute-start(bf16[48,768]{1,0:T(8,128)(2,1)S(1)} %get-tuple-element.125), channel_id=1, source_target_pairs={{0,8},{1,9},{2,10},{3,11},{4,12},{5,13},{6,14},{7,15},{8,0},{9,1},... | collective-permute-start | bytes 221192 | tf_op jit(solution)/shard_map/ppermute | solution.py:379
  120.9 17.3 %collective-permute-start.34 = (bf16[48,768]{1,0:T(8,128)(2,1)S(1)}, bf16[48,768]{1,0:T(8,128)(2,1)S(1)}, u32[]{:S(2)}, u32[]{:S(2)}) collective-permute-start(bf16[48,768]{1,0:T(8,128)(2,1)S(1)} %get-tuple-element.126), channel_id=1, source_target_pairs={{0,24},{1,25},{2,26},{3,27},{4,28},{5,29},{6,30},{7,31},{8,16},{9,... | collective-permute-start | bytes 221192 | tf_op jit(solution)/shard_map/ppermute | solution.py:379
  125.8 15.1 %collective-permute-start.33 = (bf16[48,768]{1,0:T(8,128)(2,1)S(1)}, bf16[48,768]{1,0:T(8,128)(2,1)S(1)}, u32[]{:S(2)}, u32[]{:S(2)}) collective-permute-start(bf16[48,768]{1,0:T(8,128)(2,1)S(1)} %get-tuple-element.127), channel_id=1, source_target_pairs={{0,16},{1,17},{2,18},{3,19},{4,20},{5,21},{6,22},{7,23},{8,24},{9,... | collective-permute-start | bytes 221192 | tf_op jit(solution)/shard_map/ppermute | solution.py:379
  132.1 10.4 %collective-permute-start.27 = (bf16[48,768]{1,0:T(8,128)(2,1)S(1)}, bf16[48,768]{1,0:T(8,128)(2,1)S(1)}, u32[]{:S(2)}, u32[]{:S(2)}) collective-permute-start(bf16[48,768]{1,0:T(8,128)(2,1)S(1)} %get-tuple-element.122), channel_id=1, source_target_pairs={{0,8},{1,9},{2,10},{3,11},{4,12},{5,13},{6,14},{7,15},{8,0},{9,1},... | collective-permute-start | bytes 221192 | tf_op jit(solution)/shard_map/ppermute | solution.py:379
  135.3 7.3 %collective-permute-start.29 = (bf16[48,768]{1,0:T(8,128)(2,1)S(1)}, bf16[48,768]{1,0:T(8,128)(2,1)S(1)}, u32[]{:S(2)}, u32[]{:S(2)}) collective-permute-start(bf16[48,768]{1,0:T(8,128)(2,1)S(1)} %get-tuple-element.123), channel_id=1, source_target_pairs={{0,24},{1,25},{2,26},{3,27},{4,28},{5,29},{6,30},{7,31},{8,16},{9,... | collective-permute-start | bytes 221192 | tf_op jit(solution)/shard_map/ppermute | solution.py:379
  138.0 10.7 %collective-permute-start.28 = (bf16[48,768]{1,0:T(8,128)(2,1)S(1)}, bf16[48,768]{1,0:T(8,128)(2,1)S(1)}, u32[]{:S(2)}, u32[]{:S(2)}) collective-permute-start(bf16[48,768]{1,0:T(8,128)(2,1)S(1)} %get-tuple-element.124), channel_id=1, source_target_pairs={{0,16},{1,17},{2,18},{3,19},{4,20},{5,21},{6,22},{7,23},{8,24},{9,... | collective-permute-start | bytes 221192 | tf_op jit(solution)/shard_map/ppermute | solution.py:379
  138.2 12.3 %collective-permute-start.17 = (bf16[48,768]{1,0:T(8,128)(2,1)S(1)}, bf16[48,768]{1,0:T(8,128)(2,1)S(1)}, u32[]{:S(2)}, u32[]{:S(2)}) collective-permute-start(bf16[48,768]{1,0:T(8,128)(2,1)S(1)} %get-tuple-element.116), channel_id=1, source_target_pairs={{0,8},{1,9},{2,10},{3,11},{4,12},{5,13},{6,14},{7,15},{8,0},{9,1},... | collective-permute-start | bytes 221192 | tf_op jit(solution)/shard_map/ppermute | solution.py:379
  140.9 9.7 %collective-permute-start.19 = (bf16[48,768]{1,0:T(8,128)(2,1)S(1)}, bf16[48,768]{1,0:T(8,128)(2,1)S(1)}, u32[]{:S(2)}, u32[]{:S(2)}) collective-permute-start(bf16[48,768]{1,0:T(8,128)(2,1)S(1)} %get-tuple-element.117), channel_id=1, source_target_pairs={{0,24},{1,25},{2,26},{3,27},{4,28},{5,29},{6,30},{7,31},{8,16},{9,... | collective-permute-start | bytes 221192 | tf_op jit(solution)/shard_map/ppermute | solution.py:379
  142.5 9.3 %collective-permute-start.18 = (bf16[48,768]{1,0:T(8,128)(2,1)S(1)}, bf16[48,768]{1,0:T(8,128)(2,1)S(1)}, u32[]{:S(2)}, u32[]{:S(2)}) collective-permute-start(bf16[48,768]{1,0:T(8,128)(2,1)S(1)} %get-tuple-element.118), channel_id=1, source_target_pairs={{0,16},{1,17},{2,18},{3,19},{4,20},{5,21},{6,22},{7,23},{8,24},{9,... | collective-permute-start | bytes 221192 | tf_op jit(solution)/shard_map/ppermute | solution.py:379
  142.6 9.3 %collective-permute-start.22 = (bf16[48,768]{1,0:T(8,128)(2,1)S(1)}, bf16[48,768]{1,0:T(8,128)(2,1)S(1)}, u32[]{:S(2)}, u32[]{:S(2)}) collective-permute-start(bf16[48,768]{1,0:T(8,128)(2,1)S(1)} %get-tuple-element.119), channel_id=1, source_target_pairs={{0,8},{1,9},{2,10},{3,11},{4,12},{5,13},{6,14},{7,15},{8,0},{9,1},... | collective-permute-start | bytes 221192 | tf_op jit(solution)/shard_map/ppermute | solution.py:379
  148.7 6.2 %collective-permute-start.24 = (bf16[48,768]{1,0:T(8,128)(2,1)S(1)}, bf16[48,768]{1,0:T(8,128)(2,1)S(1)}, u32[]{:S(2)}, u32[]{:S(2)}) collective-permute-start(bf16[48,768]{1,0:T(8,128)(2,1)S(1)} %get-tuple-element.120), channel_id=1, source_target_pairs={{0,24},{1,25},{2,26},{3,27},{4,28},{5,29},{6,30},{7,31},{8,16},{9,... | collective-permute-start | bytes 221192 | tf_op jit(solution)/shard_map/ppermute | solution.py:379
  150.5 5.9 %collective-permute-start.23 = (bf16[48,768]{1,0:T(8,128)(2,1)S(1)}, bf16[48,768]{1,0:T(8,128)(2,1)S(1)}, u32[]{:S(2)}, u32[]{:S(2)}) collective-permute-start(bf16[48,768]{1,0:T(8,128)(2,1)S(1)} %get-tuple-element.121), channel_id=1, source_target_pairs={{0,16},{1,17},{2,18},{3,19},{4,20},{5,21},{6,22},{7,23},{8,24},{9,... | collective-permute-start | bytes 221192 | tf_op jit(solution)/shard_map/ppermute | solution.py:379
  156.5 5.2 %collective-permute-start.35 = (bf16[2,48,768]{2,1,0:T(8,128)(2,1)S(1)}, bf16[2,48,768]{2,1,0:T(8,128)(2,1)S(1)}, u32[]{:S(2)}, u32[]{:S(2)}) collective-permute-start(bf16[2,48,768]{2,1,0:T(8,128)(2,1)S(1)} %fusion.8), channel_id=1, source_target_pairs={{0,2},{1,3},{2,0},{3,1},{4,6},{5,7},{6,4},{7,5},{8,10},{9,11},{10,... | collective-permute-start | bytes 442376 | tf_op jit(solution)/shard_map/ppermute | solution.py:379
  (32 other events, 204.1 us)

commit v2 on v1

v2 whole, which is shorter than its diff:
```python
import functools
import types
import jax
import jax.numpy as jnp
from jax import lax
from jax.sharding import PartitionSpec as P
from jax.experimental import pallas as pl
from jax.experimental.pallas import tpu as pltpu

EPS = 1e-06
GELU_C = 0.7978845608028654
GELU_A = 0.044715
LANES = 128
def estimate(microseconds):
    return pl.CostEstimate(flops=int(microseconds * 1.1e9), bytes_accessed=int(microseconds * 3.6e6), transcendentals=0)


LIMIT = 40


def vmem(mebibytes):
    return pltpu.CompilerParams(vmem_limit_bytes=mebibytes * 1024 * 1024)


def zero_borders(pad_ref):
    tiles, rows, width, _ = pad_ref.shape
    for c in range(tiles):
        pad_ref[c, :, 0:8] = jnp.zeros((rows, 8, LANES), jnp.float32)
        pad_ref[c, :, width - 8 :] = jnp.zeros((rows, 8, LANES), jnp.float32)


def conv_norm_body(x_ref, small_ref, xhat_ref, normed_ref, inv_ref, pad_ref, conv_ref):
    rows, cols, channels = x_ref.shape
    tiles = channels // LANES
    for c in range(tiles):
        pad_ref[c, :, 8 : cols + 8] = x_ref[:, :, c * LANES : (c + 1) * LANES].astype(jnp.float32)

    def tile(c, carry):
        lanes = pl.ds(pl.multiple_of(c * LANES, LANES), LANES)

        def strip(w, carry):
            base = pl.multiple_of(w * 8, 8)
            window = pad_ref.at[c, :, pl.ds(base, 24), :]
            acc = [None] * rows
            for q in range(7):
                col = [window[h, 5 + q : 13 + q, :] for h in range(rows)]
                for r in range(7):
                    weight = small_ref[r * 7 + q : r * 7 + q + 1, lanes]
                    for h in range(max(0, 3 - r), min(rows, rows + 3 - r)):
                        term = weight * col[h + r - 3]
                        acc[h] = term if acc[h] is None else acc[h] + term
            for h in range(rows):
                conv_ref[h, pl.ds(base, 8), lanes] = acc[h]
            return carry

        return lax.fori_loop(0, cols // 8, strip, carry)

    lax.fori_loop(0, tiles, tile, 0)

    def norm(h, carry):
        value = conv_ref[pl.ds(h * 2, 2)].reshape(2 * cols, channels)
        mean = jnp.mean(value, axis=1, keepdims=True)
        center = value - mean
        inv = lax.rsqrt(jnp.mean(center * center, axis=1, keepdims=True) + EPS)
        xhat = center * inv
        at = pl.ds(pl.multiple_of(h * 2 * cols, 2 * cols), 2 * cols)
        xhat_ref[at, :] = xhat.astype(jnp.bfloat16)
        normed_ref[at, :] = (xhat * small_ref[TAPS : TAPS + 1, :]).astype(jnp.bfloat16)
        inv_ref[at, :] = jnp.broadcast_to(inv, (2 * cols, LANES))
        return carry

    lax.fori_loop(0, rows // 2, norm, 0, unroll=2)


def pad_shape(rows, cols, channels):
    return pltpu.VMEM((channels // LANES, rows, cols + 16, LANES), jnp.float32)


def conv_norm_kernel(x_ref, small_ref, *rest):
    xhat_ref, normed_ref, inv_ref, pad_ref, conv_ref = rest[-5:]
    zero_borders(pad_ref)
    conv_norm_body(x_ref, small_ref, xhat_ref, normed_ref, inv_ref, pad_ref, conv_ref)


def conv_norm(x, small, after=()):
    rows, cols, channels = x.shape
    n = rows * cols
    return pl.pallas_call(
        conv_norm_kernel,
        in_specs=[pl.BlockSpec(memory_space=pltpu.VMEM)] * 2 + [pl.BlockSpec(memory_space=pl.ANY)] * len(after),
        out_shape=(
            jax.ShapeDtypeStruct((n, channels), jnp.bfloat16),
            jax.ShapeDtypeStruct((n, channels), jnp.bfloat16),
            jax.ShapeDtypeStruct((n, LANES), jnp.float32),
        ),
        scratch_shapes=[pad_shape(rows, cols, channels), pltpu.VMEM((rows, cols, channels), jnp.float32)],
        compiler_params=vmem(LIMIT),
        name="conv_norm",
        cost_estimate=estimate(2.6),
    )(x, small, *after)


def in_hbm(arrays):
    return [pltpu.with_memory_space_constraint(a, pltpu.HBM) for a in arrays]


def copy_chosen(which, sources, target, sem):
    for m, source in enumerate(sources):

        @pl.when(which == m)
        def _():
            pltpu.make_async_copy(source, target, sem).start()

    return lambda: pltpu.make_async_copy(sources[0], target, sem).wait()


def forward_kernel(choices, blocks, sel_ref, x_ref, normed0_ref, small_ref, *rest):
    w_ins, w_outs, rest = rest[:choices], rest[choices : 2 * choices], rest[2 * choices :]
    xs = [x_ref] + list(rest[: blocks - 1])
    xhats, invs, rest = rest[blocks - 1 : 2 * blocks - 2], rest[2 * blocks - 2 : 3 * blocks - 3], rest[3 * blocks - 3 :]
    pres, branches, rest = rest[:blocks], rest[blocks : 2 * blocks], rest[2 * blocks :]
    normed_ref, hid_ref, acc_ref, pad_ref, conv_ref, w_in_ref, w_out_ref, sems = rest
    rows, cols, channels = x_ref.shape
    n = rows * cols
    hidden = w_in_ref.shape[2]
    waits = []
    for s in range(blocks):
        waits.append((
            copy_chosen(sel_ref[s], w_ins, w_in_ref.at[s], sems.at[0, s]),
            copy_chosen(sel_ref[s], w_outs, w_out_ref.at[s], sems.at[1, s]),
        ))
    zero_borders(pad_ref)
    step, sub = 256, 2 * cols
    for s in range(blocks):
        normed = normed0_ref if s == 0 else normed_ref
        waits[s][0]()
        for j in range(hidden // step):
            cut = slice(j * step, (j + 1) * step)
            pre = jnp.dot(normed[...], w_in_ref[s, :, cut], preferred_element_type=jnp.float32)
            for i in range(n // sub):
                p = pre[i * sub : (i + 1) * sub]
                half = 0.5 * p
                hid_ref[i * sub : (i + 1) * sub, :] = (half + half * tanh_arg(p)).astype(jnp.bfloat16)
                pres[s][i * sub : (i + 1) * sub, cut] = p.astype(jnp.bfloat16)
            if j == 0:
                waits[s][1]()
            part = jnp.dot(hid_ref[...], w_out_ref[s, cut, :], preferred_element_type=jnp.float32)
            if j == 0:
                acc_ref[...] = part
            else:
                acc_ref[...] += part
        scale = small_ref[s, TAPS + 1 : TAPS + 2, :]
        for i in range(n // sub):
            branch = acc_ref[i * sub : (i + 1) * sub, :]
            branches[s][i * sub : (i + 1) * sub, :] = branch.astype(jnp.bfloat16)
            if s < blocks - 1:
                x_old = xs[s][2 * i : 2 * i + 2].astype(jnp.float32).reshape(sub, channels)
                xs[s + 1][2 * i : 2 * i + 2] = (x_old + scale * branch).astype(jnp.bfloat16).reshape(2, cols, channels)
        if s < blocks - 1:
            conv_norm_body(xs[s + 1], small_ref.at[s + 1], xhats[s], normed_ref, invs[s], pad_ref, conv_ref)


def forward(sel, x, normed0, small, w_ins, w_outs):
    blocks = small.shape[0]
    rows, cols, channels = x.shape
    n = rows * cols
    hidden = w_ins[0].shape[1]
    out = pl.pallas_call(
        functools.partial(forward_kernel, len(w_ins), blocks),
        in_specs=[pl.BlockSpec(memory_space=pltpu.SMEM)]
        + [pl.BlockSpec(memory_space=pltpu.VMEM)] * 3
        + [pl.BlockSpec(memory_space=pl.ANY)] * (2 * len(w_ins)),
        out_shape=(jax.ShapeDtypeStruct((rows, cols, channels), jnp.bfloat16),) * (blocks - 1)
        + (jax.ShapeDtypeStruct((n, channels), jnp.bfloat16),) * (blocks - 1)
        + (jax.ShapeDtypeStruct((n, LANES), jnp.float32),) * (blocks - 1)
        + (jax.ShapeDtypeStruct((n, hidden), jnp.bfloat16),) * blocks
        + (jax.ShapeDtypeStruct((n, channels), jnp.bfloat16),) * blocks,
        scratch_shapes=[
            pltpu.VMEM((n, channels), jnp.bfloat16),
            pltpu.VMEM((n, 256), jnp.bfloat16),
            pltpu.VMEM((n, channels), jnp.float32),
            pad_shape(rows, cols, channels),
            pltpu.VMEM((rows, cols, channels), jnp.float32),
            pltpu.VMEM((blocks, channels, hidden), jnp.bfloat16),
            pltpu.VMEM((blocks, hidden, channels), jnp.bfloat16),
            pltpu.SemaphoreType.DMA((2, blocks)),
        ],
        compiler_params=vmem(LIMIT),
        name="forward",
        cost_estimate=estimate(15),
    )(sel, x, normed0, small, *in_hbm(w_ins), *in_hbm(w_outs))
    k = blocks - 1
    return out[:k], out[k : 2 * k], out[2 * k : 3 * k], out[3 * k : 3 * k + blocks], out[3 * k + blocks :]


def tanh_arg(x):
    return jnp.tanh(x * (GELU_C + (GELU_C * GELU_A) * (x * x)))


def load_weights(sel_ref, w_ins, w_outs, w_in_ref, w_out_ref, sems):
    for m in range(len(w_ins)):

        @pl.when(sel_ref[0] == m)
        def _():
            pltpu.make_async_copy(w_ins[m], w_in_ref, sems.at[0]).start()
            pltpu.make_async_copy(w_outs[m], w_out_ref, sems.at[1]).start()

    return (
        pltpu.make_async_copy(w_ins[0], w_in_ref, sems.at[0]).wait,
        pltpu.make_async_copy(w_outs[0], w_out_ref, sems.at[1]).wait,
    )


def specs(sel, arrays, choices, after=0):
    return (
        [pl.BlockSpec(memory_space=pltpu.SMEM)]
        + [pl.BlockSpec(memory_space=pltpu.VMEM)] * arrays
        + [pl.BlockSpec(memory_space=pl.ANY)] * (2 * choices + after)
    )


def mlp_back_kernel(choices, after, sel_ref, g_ref, branch_ref, pre_ref, xhat_ref, inv_ref, gain_ref, scale_ref, *rest):
    w_ins, w_outs = rest[:choices], rest[choices : 2 * choices]
    (keep_ref, send_ref, small_ref, gconv_ref,
     gb_ref, nm_ref, hid_ref, gp_ref, acc_ref, w_in_ref, w_out_ref, sems) = rest[2 * choices + after :]
    wait_in, wait_out = load_weights(sel_ref, w_ins, w_outs, w_in_ref, w_out_ref, sems)
    first = sel_ref[1] == 0
    n, channels = g_ref.shape
    hidden = w_in_ref.shape[1]
    step = 256
    sub = 32
    scale_sum = jnp.zeros((8, channels), jnp.float32)
    for i in range(n // sub):
        at = slice(i * sub, (i + 1) * sub)
        g = g_ref[at, :].astype(jnp.float32)
        scale_sum = scale_sum + jnp.sum((g * branch_ref[at, :].astype(jnp.float32)).reshape(sub // 8, 8, channels), axis=0)
        gb_ref[at, :] = (g * scale_ref[...]).astype(jnp.bfloat16)
        nm_ref[at, :] = (xhat_ref[at, :].astype(jnp.float32) * gain_ref[...]).astype(jnp.bfloat16)
    gb_t = gb_ref[...].T
    nm_t = nm_ref[...].T
    wait_in()
    wait_out()
    for j in range(hidden // step):
        cut = slice(j * step, (j + 1) * step)
        gh = lax.dot_general(gb_ref[...], w_out_ref[cut, :], (((1,), (1,)), ((), ())), preferred_element_type=jnp.float32)
        for i in range(n // sub):
            at = slice(i * sub, (i + 1) * sub)
            p = pre_ref[at, cut].astype(jnp.float32)
            sq = p * p
            t = jnp.tanh(p * (GELU_C + (GELU_C * GELU_A) * sq))
            cdf = 0.5 + 0.5 * t
            hid_ref[at, :] = (p * cdf).astype(jnp.bfloat16)
            slope = cdf + (0.5 * p) * (1.0 - t * t) * (GELU_C + (3.0 * GELU_C * GELU_A) * sq)
            gp_ref[at, :] = (gh[at, :] * slope).astype(jnp.bfloat16)
        t_out = jnp.dot(gb_t, hid_ref[...], preferred_element_type=jnp.float32)
        t_in = jnp.dot(nm_t, gp_ref[...], preferred_element_type=jnp.float32)
        keep_ref[:, cut] = jnp.where(first, t_in, t_out).astype(jnp.bfloat16)
        send_ref[:, cut] = jnp.where(first, t_out, t_in).astype(jnp.bfloat16)
        part = lax.dot_general(gp_ref[...], w_in_ref[:, cut], (((1,), (1,)), ((), ())), preferred_element_type=jnp.float32)
        if j == 0:
            acc_ref[...] = part
        else:
            acc_ref[...] += part
    gain_sum = jnp.zeros((8, channels), jnp.float32)
    for i in range(n // sub):
        at = slice(i * sub, (i + 1) * sub)
        gn = acc_ref[at, :]
        xhat = xhat_ref[at, :].astype(jnp.float32)
        gain_sum = gain_sum + jnp.sum((gn * xhat).reshape(sub // 8, 8, channels), axis=0)
        gx = gn * gain_ref[...]
        m1 = jnp.mean(gx, axis=1, keepdims=True)
        m2 = jnp.mean(gx * xhat, axis=1, keepdims=True)
        inv = inv_ref[at, 0:1]
        gconv_ref[at, :] = inv * (gx - m1 - xhat * m2)
    small_ref[0:1, :] = jnp.sum(gain_sum, axis=0, keepdims=True)
    small_ref[1:2, :] = jnp.sum(scale_sum, axis=0, keepdims=True)
    small_ref[2:8, :] = jnp.zeros((6, channels), jnp.float32)


def mlp_back(sel, g, branch, pre, xhat, inv, gain, scale, w_ins, w_outs, after=()):
    n, channels = g.shape
    hidden = w_ins[0].shape[1]
    return pl.pallas_call(
        functools.partial(mlp_back_kernel, len(w_ins), len(after)),
        in_specs=specs(sel, 7, len(w_ins), len(after)),
        out_shape=(
            jax.ShapeDtypeStruct((channels, hidden), jnp.bfloat16),
            jax.ShapeDtypeStruct((channels, hidden), jnp.bfloat16),
            jax.ShapeDtypeStruct((8, channels), jnp.float32),
            jax.ShapeDtypeStruct((n, channels), jnp.float32),
        ),
        scratch_shapes=[
            pltpu.VMEM((n, channels), jnp.bfloat16),
            pltpu.VMEM((n, channels), jnp.bfloat16),
            pltpu.VMEM((n, 256), jnp.bfloat16),
            pltpu.VMEM((n, 256), jnp.bfloat16),
            pltpu.VMEM((n, channels), jnp.float32),
            pltpu.VMEM((channels, hidden), jnp.bfloat16),
            pltpu.VMEM((hidden, channels), jnp.bfloat16),
            pltpu.SemaphoreType.DMA((2,)),
        ],
        compiler_params=vmem(LIMIT),
        name="mlp_back",
        cost_estimate=estimate(2.5),
    )(sel, g, branch, pre, xhat, inv, gain, scale, *in_hbm(w_ins), *in_hbm(w_outs), *after)


SMALL_ROWS = 64
TAPS = 49


def conv_back_kernel(need_map, after, gconv_ref, x_ref, g_ref, k_ref, small_ref, *rest):
    *out_ref, tk_ref, pad_ref, sum_ref, wide_ref, map_ref = rest[after:]
    conv_back_body(gconv_ref, x_ref, g_ref, k_ref, small_ref, out_ref[0] if need_map else None, tk_ref,
                   pad_ref, sum_ref, wide_ref, map_ref)


def conv_back(gconv, x, g, kernel, small, need_map=True, after=()):
    rows, cols, channels = x.shape
    out = (jax.ShapeDtypeStruct((SMALL_ROWS, channels), jnp.float32),)
    if need_map:
        out = (jax.ShapeDtypeStruct((rows, cols, channels), jnp.bfloat16),) + out
    return pl.pallas_call(
        functools.partial(conv_back_kernel, need_map, len(after)),
        in_specs=[pl.BlockSpec(memory_space=pltpu.VMEM)] * 5 + [pl.BlockSpec(memory_space=pl.ANY)] * len(after),
        out_shape=out,
        scratch_shapes=[
            pad_shape(rows, cols, channels),
            pltpu.VMEM((cols // 8, TAPS, 8, LANES), jnp.float32),
            pltpu.VMEM((rows, cols, channels), jnp.float32),
            pltpu.VMEM((rows, cols, channels), jnp.float32),
        ],
        compiler_params=vmem(LIMIT),
        name="conv_back",
        cost_estimate=estimate(3.4 if need_map else 1.6),
    )(gconv, x, g, kernel, small, *after)


def small_call(kernel, name, outs, *args, scratch=(), after=()):
    used = len(args)

    def body(*refs):
        kernel(*refs[:used], *refs[used + len(after) :])

    return pl.pallas_call(
        body,
        in_specs=[pl.BlockSpec(memory_space=pltpu.SMEM)]
        + [pl.BlockSpec(memory_space=pltpu.VMEM)] * (used - 1)
        + [pl.BlockSpec(memory_space=pl.ANY)] * len(after),
        out_shape=tuple(jax.ShapeDtypeStruct(*o) for o in outs),
        scratch_shapes=list(scratch),
        compiler_params=vmem(LIMIT),
        name=name,
        cost_estimate=estimate(0.7),
    )(*args, *after)


def conv_back_body(gconv_ref, x_ref, g_ref, small_ref, sums8_ref, out_ref, tk_ref, pad_ref, sum_ref, wide_ref, map_ref):
    rows, cols, channels = x_ref.shape
    tiles = channels // LANES
    zero_borders(pad_ref)
    for c in range(tiles):
        pad_ref[c, :, 8 : cols + 8] = gconv_ref[:, c * LANES : (c + 1) * LANES].reshape(rows, cols, LANES)

    for h in range(rows):
        wide_ref[h] = x_ref[h].astype(jnp.float32)

    def tile(c, carry):
        lanes = pl.ds(pl.multiple_of(c * LANES, LANES), LANES)

        def strip(w, carry):
            base = pl.multiple_of(w * 8, 8)
            window = pad_ref.at[c, :, pl.ds(base, 24), :]
            xs = [wide_ref[h, pl.ds(base, 8), lanes] for h in range(rows)]
            acc = [None] * rows
            for q in range(7):
                col = [window[h, 11 - q : 19 - q, :] for h in range(rows)]
                for r in range(7):
                    tap = r * 7 + q
                    if out_ref is not None:
                        weight = small_ref[tap : tap + 1, lanes]
                    total = None
                    for h in range(max(0, r - 3), min(rows, rows + r - 3)):
                        shifted = col[h + 3 - r]
                        term = xs[h] * shifted
                        total = term if total is None else total + term
                        if out_ref is not None:
                            moved = weight * shifted
                            acc[h] = moved if acc[h] is None else acc[h] + moved
                    sum_ref[w, tap] = total
            if out_ref is not None:
                for h in range(rows):
                    map_ref[h, pl.ds(base, 8), lanes] = acc[h]
            return carry

        lax.fori_loop(0, cols // 8, strip, 0)
        tk_ref[0:TAPS, lanes] = jnp.sum(sum_ref[0] + sum_ref[1], axis=1)
        return carry

    lax.fori_loop(0, tiles, tile, 0)
    if out_ref is not None:
        for h in range(rows):
            out_ref[h] = (g_ref[h].astype(jnp.float32) + map_ref[h]).astype(jnp.bfloat16)
    tk_ref[TAPS : TAPS + 2, :] = sums8_ref[0:2, :]
    tk_ref[TAPS + 2 :, :] = jnp.zeros((SMALL_ROWS - TAPS - 2, channels), jnp.float32)


def mlp_back_body(first, g_ref, branch_ref, pre_ref, xhat_ref, inv_ref, small_ref, wait_in, wait_out, w_in_ref, w_out_ref,
                  keep_ref, send_ref, sums8_ref, gconv_ref, gb_ref, nm_ref, hid_ref, gp_ref, acc_ref, before=None):
    rows, cols, channels = g_ref.shape
    n = rows * cols
    hidden = w_in_ref.shape[1]
    step = 256
    sub = 2 * cols
    gain = small_ref[TAPS : TAPS + 1, :]
    scale = small_ref[TAPS + 1 : TAPS + 2, :]
    scale_sum = jnp.zeros((8, channels), jnp.float32)
    for i in range(n // sub):
        at = slice(i * sub, (i + 1) * sub)
        g = g_ref[2 * i : 2 * i + 2].astype(jnp.float32).reshape(sub, channels)
        scale_sum = scale_sum + jnp.sum((g * branch_ref[at, :].astype(jnp.float32)).reshape(sub // 8, 8, channels), axis=0)
        gb_ref[at, :] = (g * scale).astype(jnp.bfloat16)
        nm_ref[at, :] = (xhat_ref[at, :].astype(jnp.float32) * gain).astype(jnp.bfloat16)
    gb_t = gb_ref[...].T
    nm_t = nm_ref[...].T
    wait_in()
    wait_out()
    for j in range(hidden // step):
        cut = slice(j * step, (j + 1) * step)
        gh = lax.dot_general(gb_ref[...], w_out_ref[cut, :], (((1,), (1,)), ((), ())), preferred_element_type=jnp.float32)
        for i in range(n // sub):
            at = slice(i * sub, (i + 1) * sub)
            p = pre_ref[at, cut].astype(jnp.float32)
            sq = p * p
            t = jnp.tanh(p * (GELU_C + (GELU_C * GELU_A) * sq))
            cdf = 0.5 + 0.5 * t
            hid_ref[at, :] = (p * cdf).astype(jnp.bfloat16)
            slope = cdf + (0.5 * p) * (1.0 - t * t) * (GELU_C + (3.0 * GELU_C * GELU_A) * sq)
            gp_ref[at, :] = (gh[at, :] * slope).astype(jnp.bfloat16)
        t_out = jnp.dot(gb_t, hid_ref[...], preferred_element_type=jnp.float32)
        t_in = jnp.dot(nm_t, gp_ref[...], preferred_element_type=jnp.float32)
        t_keep = jnp.where(first, t_in, t_out)
        t_send = jnp.where(first, t_out, t_in)
        if before is not None:
            t_keep = t_keep + before[0][:, cut].astype(jnp.float32)
            t_send = t_send + before[1][:, cut].astype(jnp.float32)
        keep_ref[:, cut] = t_keep.astype(jnp.bfloat16)
        send_ref[:, cut] = t_send.astype(jnp.bfloat16)
        part = lax.dot_general(gp_ref[...], w_in_ref[:, cut], (((1,), (1,)), ((), ())), preferred_element_type=jnp.float32)
        if j == 0:
            acc_ref[...] = part
        else:
            acc_ref[...] += part
    gain_sum = jnp.zeros((8, channels), jnp.float32)
    for i in range(n // sub):
        at = slice(i * sub, (i + 1) * sub)
        gn = acc_ref[at, :]
        xhat = xhat_ref[at, :].astype(jnp.float32)
        gain_sum = gain_sum + jnp.sum((gn * xhat).reshape(sub // 8, 8, channels), axis=0)
        gx = gn * gain
        m1 = jnp.mean(gx, axis=1, keepdims=True)
        m2 = jnp.mean(gx * xhat, axis=1, keepdims=True)
        gconv_ref[at, :] = inv_ref[at, 0:1] * (gx - m1 - xhat * m2)
    sums8_ref[0:1, :] = jnp.sum(gain_sum, axis=0, keepdims=True)
    sums8_ref[1:2, :] = jnp.sum(scale_sum, axis=0, keepdims=True)
    sums8_ref[2:8, :] = jnp.zeros((6, channels), jnp.float32)


def named_call(name, body, ins, outs, scratch, cost):
    names = list(ins) + list(outs) + list(scratch)
    spaces = {"v": pltpu.VMEM, "s": pltpu.SMEM, "a": pl.ANY, "h": pl.ANY}

    def kernel(*refs):
        body(types.SimpleNamespace(**dict(zip(names, refs))))

    args = [pltpu.with_memory_space_constraint(a, pltpu.HBM) if kind == "h" else a for a, kind in ins.values()]
    result = pl.pallas_call(
        kernel,
        in_specs=[pl.BlockSpec(memory_space=spaces[kind]) for _, kind in ins.values()],
        out_shape=tuple(jax.ShapeDtypeStruct(*o) for o in outs.values()),
        scratch_shapes=list(scratch.values()),
        compiler_params=vmem(LIMIT),
        name=name,
        cost_estimate=estimate(cost),
    )(*args)
    return types.SimpleNamespace(**dict(zip(outs, result)))


def mlp_body(normed_ref, wait_in, wait_out, w_in_ref, w_out_ref, pre_ref, hid_ref, acc_ref):
    n = normed_ref.shape[0]
    hidden = w_in_ref.shape[1]
    step, sub = 256, 32
    wait_in()
    for j in range(hidden // step):
        cut = slice(j * step, (j + 1) * step)
        pre = jnp.dot(normed_ref[...], w_in_ref[:, cut], preferred_element_type=jnp.float32)
        for i in range(n // sub):
            p = pre[i * sub : (i + 1) * sub]
            half = 0.5 * p
            hid_ref[i * sub : (i + 1) * sub, :] = (half + half * tanh_arg(p)).astype(jnp.bfloat16)
            pre_ref[i * sub : (i + 1) * sub, cut] = p.astype(jnp.bfloat16)
        if j == 0:
            wait_out()
        part = jnp.dot(hid_ref[...], w_out_ref[cut, :], preferred_element_type=jnp.float32)
        if j == 0:
            acc_ref[...] = part
        else:
            acc_ref[...] += part


def residual_body(x_ref, small_ref, acc_ref, branch_ref, y_ref):
    rows, cols, channels = x_ref.shape
    scale = small_ref[TAPS + 1 : TAPS + 2, :]
    sub = 2 * cols
    for i in range(rows // 2):
        branch = acc_ref[i * sub : (i + 1) * sub, :]
        branch_ref[i * sub : (i + 1) * sub, :] = branch.astype(jnp.bfloat16)
        if y_ref is not None:
            old = x_ref[2 * i : 2 * i + 2].astype(jnp.float32).reshape(sub, channels)
            y_ref[2 * i : 2 * i + 2] = (old + scale * branch).astype(jnp.bfloat16).reshape(2, cols, channels)


def weight_ins(pair):
    return {k: (v, "h") for k, v in zip(("own_in", "near_in", "own_out", "near_out"), pair)}


def weight_scratch(blocks, channels, hidden):
    return {
        "w_in": pltpu.VMEM((blocks, channels, hidden), jnp.bfloat16),
        "w_out": pltpu.VMEM((blocks, hidden, channels), jnp.bfloat16),
        "w_sem": pltpu.SemaphoreType.DMA((2, blocks)),
    }


def start_weights(r, slot, block):
    return (
        copy_chosen(r.sel[block], (r.own_in, r.near_in), r.w_in.at[slot], r.w_sem.at[0, slot]),
        copy_chosen(r.sel[block], (r.own_out, r.near_out), r.w_out.at[slot], r.w_sem.at[1, slot]),
    )


def pair_forward(sel, x, first, small, weights):
    rows, cols, channels = x.shape
    n, hidden = rows * cols, weights[0].shape[1]
    bf16, f32 = jnp.bfloat16, jnp.float32

    def body(r):
        low, high = start_weights(r, 0, 0), start_weights(r, 1, 1)
        zero_borders(r.pad)
        mlp_body(r.normed0, *low, r.w_in.at[0], r.w_out.at[0], r.pre0, r.hid, r.acc)
        residual_body(r.x, r.small.at[0], r.acc, r.branch0, r.x1)
        conv_norm_body(r.x1, r.small.at[1], r.xhat1, r.normed, r.inv1, r.pad, r.conv)
        mlp_body(r.normed, *high, r.w_in.at[1], r.w_out.at[1], r.pre1, r.hid, r.acc)
        residual_body(r.x1, r.small.at[1], r.acc, r.branch1, r.y)

    return named_call(
        "pair_forward", body,
        {"sel": (sel, "s"), "x": (x, "v"), "normed0": (first[1], "v"), "small": (small, "v"), **weight_ins(weights)},
        {"y": (x.shape, bf16), "x1": (x.shape, bf16), "xhat1": ((n, channels), bf16), "inv1": ((n, LANES), f32),
         "pre0": ((n, hidden), bf16), "pre1": ((n, hidden), bf16),
         "branch0": ((n, channels), bf16), "branch1": ((n, channels), bf16)},
        {"normed": pltpu.VMEM((n, channels), bf16), "hid": pltpu.VMEM((n, 256), bf16), "acc": pltpu.VMEM((n, channels), f32),
         "pad": pad_shape(rows, cols, channels), "conv": pltpu.VMEM((rows, cols, channels), f32),
         **weight_scratch(2, channels, hidden)},
        7.5,
    )


def back_scratch(n, channels):
    bf16, f32 = jnp.bfloat16, jnp.float32
    return {"gb": pltpu.VMEM((n, channels), bf16), "nm": pltpu.VMEM((n, channels), bf16),
            "hid": pltpu.VMEM((n, 256), bf16), "gp": pltpu.VMEM((n, 256), bf16), "acc": pltpu.VMEM((n, channels), f32)}


def back_temps(r):
    return r.gb, r.nm, r.hid, r.gp, r.acc


GRADS = ("keep0", "send0", "keep1", "send1")


def pair_both(sel, x, g, small, weights, before=None):
    rows, cols, channels = x.shape
    n, hidden = rows * cols, weights[0].shape[1]
    bf16, f32 = jnp.bfloat16, jnp.float32

    def body(r):
        @pl.when(r.sel[2] == 1)
        def _():
            core = r.sel[3] == 0
            low, high = start_weights(r, 0, 0), start_weights(r, 1, 1)
            waits = []
            if before is not None:
                for k, name in enumerate(GRADS):
                    copy = pltpu.make_async_copy(getattr(r, "old_" + name), r.olds.at[k], r.o_sem.at[k])
                    copy.start()
                    waits.append(copy.wait)
            zero_borders(r.pad)
            s0, s1 = r.small.at[0], r.small.at[1]
            conv_norm_body(r.x, s0, r.xhat0, r.normed, r.inv0, r.pad, r.conv)
            mlp_body(r.normed, *low, r.w_in.at[0], r.w_out.at[0], r.pre0, r.hid, r.acc)
            residual_body(r.x, s0, r.acc, r.branch0, r.x1)
            conv_norm_body(r.x1, s1, r.xhat1, r.normed, r.inv1, r.pad, r.conv)
            mlp_body(r.normed, *high, r.w_in.at[1], r.w_out.at[1], r.pre1, r.hid, r.acc)
            residual_body(r.x1, s1, r.acc, r.branch1, None)
            for wait in waits:
                wait()
            done = (lambda: None,) * 2
            mlp_back_body(core, r.g, r.branch1, r.pre1, r.xhat1, r.inv1, s1, *done, r.w_in.at[1], r.w_out.at[1],
                          r.keep1, r.send1, r.sums8, r.gconv, *back_temps(r),
                          before=None if before is None else (r.olds.at[2], r.olds.at[3]))
            conv_back_body(r.gconv, r.x1, r.g, s1, r.sums8, r.g1, r.small1, r.pad, r.sum, r.wide, r.map)
            mlp_back_body(core, r.g1, r.branch0, r.pre0, r.xhat0, r.inv0, s0, *done, r.w_in.at[0], r.w_out.at[0],
                          r.keep0, r.send0, r.sums8, r.gconv, *back_temps(r),
                          before=None if before is None else (r.olds.at[0], r.olds.at[1]))
            conv_back_body(r.gconv, r.x, r.g1, s0, r.sums8, r.g0, r.small0, r.pad, r.sum, r.wide, r.map)
            if before is not None:
                r.small0[...] += r.old_small0[...]
                r.small1[...] += r.old_small1[...]

    ins = {"sel": (sel, "s"), "x": (x, "v"), "g": (g, "v"), "small": (small, "v"), **weight_ins(weights)}
    scratch = {}
    if before is not None:
        ins.update({"old_" + name: (getattr(before, name), "a") for name in GRADS})
        ins.update({"old_" + name: (getattr(before, name), "v") for name in ("small0", "small1")})
        scratch = {"olds": pltpu.VMEM((4, channels, hidden), bf16), "o_sem": pltpu.SemaphoreType.DMA((4,))}
    grad = ((channels, hidden), bf16)
    small_out = ((SMALL_ROWS, channels), f32)
    return named_call(
        "pair_both", body, ins,
        {"g0": (x.shape, bf16), "keep0": grad, "send0": grad, "keep1": grad, "send1": grad,
         "small0": small_out, "small1": small_out},
        {"x1": pltpu.VMEM(x.shape, bf16), "g1": pltpu.VMEM(x.shape, bf16),
         "xhat0": pltpu.VMEM((n, channels), bf16), "xhat1": pltpu.VMEM((n, channels), bf16),
         "inv0": pltpu.VMEM((n, LANES), f32), "inv1": pltpu.VMEM((n, LANES), f32),
         "pre0": pltpu.VMEM((n, hidden), bf16), "pre1": pltpu.VMEM((n, hidden), bf16),
         "branch0": pltpu.VMEM((n, channels), bf16), "branch1": pltpu.VMEM((n, channels), bf16),
         "normed": pltpu.VMEM((n, channels), bf16), "gconv": pltpu.VMEM((n, channels), f32),
         "sums8": pltpu.VMEM((8, channels), f32),
         "pad": pad_shape(rows, cols, channels), "conv": pltpu.VMEM((rows, cols, channels), f32),
         "sum": pltpu.VMEM((cols // 8, TAPS, 8, LANES), f32),
         "wide": pltpu.VMEM(x.shape, f32), "map": pltpu.VMEM(x.shape, f32),
         **back_scratch(n, channels), **weight_scratch(2, channels, hidden), **scratch},
        17,
    )


def start_olds(r):
    return [copy_chosen(r.sel[2], (getattr(r, "a_" + name), getattr(r, "p_" + name)), r.olds.at[k], r.o_sem.at[k])
            for k, name in enumerate(("keep", "send"))]


def old_ins(before, block):
    ins = {}
    for prefix, part in zip("ap", before):
        for name in ("keep", "send"):
            ins[prefix + "_" + name] = (getattr(part, name + str(block)), "a")
    return ins


def pair_back_high(sel, g, kept, small, weights, before=None, after=()):
    rows, cols, channels = g.shape
    n, hidden = rows * cols, weights[0].shape[1]
    bf16, f32 = jnp.bfloat16, jnp.float32

    def body(r):
        waits = [] if before is None else start_olds(r)

        @pl.when(r.sel[2] == 0)
        def _():
            high = start_weights(r, 0, 1)
            for wait in waits:
                wait()
            mlp_back_body(r.sel[3] == 0, r.g, r.branch1, r.pre1, r.xhat1, r.inv1, r.small.at[1], *high,
                          r.w_in.at[0], r.w_out.at[0], r.keep, r.send, r.sums8, r.gconv, *back_temps(r),
                          before=None if before is None else (r.olds.at[0], r.olds.at[1]))

        if before is not None:

            @pl.when(r.sel[2] == 1)
            def _():
                for wait in waits:
                    wait()
                r.keep[...] = r.olds[0]
                r.send[...] = r.olds[1]

    ins = {"sel": (sel, "s"), "g": (g, "v"), "branch1": (kept.branch1, "v"), "pre1": (kept.pre1, "v"),
           "xhat1": (kept.xhat1, "v"), "inv1": (kept.inv1, "v"), "small": (small, "v"), **weight_ins(weights)}
    scratch = {}
    if before is not None:
        ins.update(old_ins(before, 1))
        ins.update({"after%d" % k: (v, "a") for k, v in enumerate(after)})
        scratch = {"olds": pltpu.VMEM((2, channels, hidden), bf16), "o_sem": pltpu.SemaphoreType.DMA((2,))}
    return named_call(
        "pair_back_high", body, ins,
        {"keep": ((channels, hidden), bf16), "send": ((channels, hidden), bf16), "sums8": ((8, channels), f32),
         "gconv": ((n, channels), f32)},
        {**back_scratch(n, channels), **weight_scratch(1, channels, hidden), **scratch},
        2.5,
    )


def pair_back_low(sel, g, high, x, x1, first, kept, small, weights, before=None, after=()):
    rows, cols, channels = g.shape
    n, hidden = rows * cols, weights[0].shape[1]
    bf16, f32 = jnp.bfloat16, jnp.float32

    def body(r):
        waits = [] if before is None else start_olds(r)

        @pl.when(r.sel[2] == 0)
        def _():
            low = start_weights(r, 0, 0)
            conv_back_body(r.gconv1, r.x1, r.g, r.small.at[1], r.sums1, r.g1, r.small1, r.pad, r.sum, r.wide, r.map)
            if before is not None:
                r.small1[...] += r.a_small1[...]
            for wait in waits:
                wait()
            mlp_back_body(r.sel[3] == 0, r.g1, r.branch0, r.pre0, r.xhat0, r.inv0, r.small.at[0], *low,
                          r.w_in.at[0], r.w_out.at[0], r.keep, r.send, r.sums8, r.gconv, *back_temps(r),
                          before=None if before is None else (r.olds.at[0], r.olds.at[1]))

        if before is not None:

            @pl.when(r.sel[2] == 1)
            def _():
                for wait in waits:
                    wait()
                r.keep[...] = r.olds[0]
                r.send[...] = r.olds[1]
                r.small1[...] = r.p_small1[...]

    ins = {"sel": (sel, "s"), "g": (g, "v"), "gconv1": (high.gconv, "v"), "sums1": (high.sums8, "v"), "x1": (x1, "v"),
           "branch0": (kept.branch0, "v"), "pre0": (kept.pre0, "v"), "xhat0": (first[0], "v"), "inv0": (first[2], "v"),
           "small": (small, "v"), **weight_ins(weights)}
    scratch = {}
    if before is not None:
        ins.update(old_ins(before, 0))
        ins.update({"a_small1": (before[0].small1, "v"), "p_small1": (before[1].small1, "v")})
        scratch = {"olds": pltpu.VMEM((2, channels, hidden), bf16), "o_sem": pltpu.SemaphoreType.DMA((2,))}
    ins.update({"after%d" % k: (v, "a") for k, v in enumerate(after)})
    return named_call(
        "pair_back_low", body, ins,
        {"small1": ((SMALL_ROWS, channels), f32), "keep": ((channels, hidden), bf16), "send": ((channels, hidden), bf16),
         "sums8": ((8, channels), f32), "gconv": ((n, channels), f32)},
        {"g1": pltpu.VMEM(g.shape, bf16), "pad": pad_shape(rows, cols, channels), "sum": pltpu.VMEM((cols // 8, TAPS, 8, LANES), f32),
         "wide": pltpu.VMEM(x.shape, f32), "map": pltpu.VMEM(x.shape, f32),
         **back_scratch(n, channels), **weight_scratch(1, channels, hidden), **scratch},
        5.5,
    )


def pair_back_conv(sel, low, x, before=None, after=()):
    rows, cols, channels = x.shape

    def body(r):
        @pl.when(r.sel[2] == 0)
        def _():
            conv_back_body(r.gconv, r.x, None, None, r.sums8, None, r.small0, r.pad, r.sum, r.wide, r.map)
            if before is not None:
                r.small0[...] += r.a_small0[...]

        if before is not None:

            @pl.when(r.sel[2] == 1)
            def _():
                r.small0[...] = r.p_small0[...]

    ins = {"sel": (sel, "s"), "gconv": (low.gconv, "v"), "sums8": (low.sums8, "v"), "x": (x, "v")}
    if before is not None:
        ins.update({"a_small0": (before[0].small0, "v"), "p_small0": (before[1].small0, "v")})
    ins.update({"after%d" % k: (v, "a") for k, v in enumerate(after)})
    return named_call(
        "pair_back_conv", body, ins, {"small0": ((SMALL_ROWS, channels), jnp.float32)},
        {"pad": pad_shape(rows, cols, channels), "sum": pltpu.VMEM((cols // 8, TAPS, 8, LANES), jnp.float32),
         "wide": pltpu.VMEM(x.shape, jnp.float32), "map": pltpu.VMEM(x.shape, jnp.float32)},
        1.6,
    ).small0


def pack_kernel(sel_ref, s0_ref, s1_ref, out_ref):
    out_ref[...] = jnp.concatenate([s0_ref[...], s1_ref[...]], axis=0).T.astype(jnp.bfloat16)


def pack(core, smalls):
    return small_call(pack_kernel, "pack", (((smalls[0].shape[1], 2 * SMALL_ROWS), jnp.bfloat16),), core, *smalls)[0]


def add(a, b):
    return a.astype(jnp.float32) + b.astype(jnp.float32)


def side_kernel(sel_ref, keep_ref, got_ref, *refs):
    *small_ref, across_ref, mine_ref = refs
    side = sel_ref[0]
    levels, _, _, hidden = keep_ref.shape
    for level in range(levels):
        for out_ref, which in ((across_ref, 1 - side), (mine_ref, side)):
            out_ref[level, :, :hidden] = add(keep_ref[level, which], got_ref[level, which]).astype(jnp.bfloat16)
            if small_ref:
                out_ref[level, :, hidden:] = small_ref[0][level, which]


def to_side(side, *arrays):
    arrays = [v.reshape(4, 2, v.shape[0] // 8, v.shape[1]) for v in arrays]
    width = sum(v.shape[3] for v in arrays[1:])
    out = ((4, arrays[0].shape[2], width), jnp.bfloat16)
    return small_call(side_kernel, "to_side", (out, out), side, *arrays)


def depth_kernel(sel_ref, mine_ref, got_ref, *out_refs):
    for k, out_ref in enumerate(out_refs):
        out_ref[...] = add(mine_ref[sel_ref[k]], got_ref[sel_ref[k]]).astype(jnp.bfloat16)


def to_depths(levels, mine, got, after=()):
    return small_call(depth_kernel, "to_depths", ((mine.shape[1:], jnp.bfloat16),) * 4, levels, mine, got, after=after)


def core_kernel(sel_ref, *refs):
    *parts, own_ref, send_ref = refs
    hidden = parts[-1].shape[1]
    low, high = (add(a[...], b[...]) + add(c[...], d[...]) for a, b, c, d in (parts[:4], parts[4:]))
    first = sel_ref[0] == 0
    small = low[:, hidden:]
    turned = pltpu.roll(small, SMALL_ROWS, 1)
    low = low[:, :hidden]
    own_ref[:, :hidden] = jnp.where(first, low, high)
    own_ref[:, hidden:] = jnp.where(first, small, turned)
    send_ref[:, :hidden] = jnp.where(first, high, low).astype(jnp.bfloat16)
    send_ref[:, hidden:] = jnp.where(first, turned, small).astype(jnp.bfloat16)


def to_core(core, parts):
    shape = (parts[-1].shape[0], parts[-1].shape[1] + 2 * SMALL_ROWS)
    return small_call(core_kernel, "to_core", ((shape, jnp.float32), (shape, jnp.bfloat16)), core, *parts)


def final_kernel(sel_ref, own_ref, got_ref, k_ref, gain_ref, in_ref, out_ref, scale_ref, pad_ref):
    share, hidden = own_ref.shape[0], in_ref.shape[2]
    taps = k_ref.shape[2]
    first = sel_ref[0] == 0
    own, got = own_ref[:, :hidden], got_ref[:, :hidden].astype(jnp.float32)
    in_ref[0] = jnp.where(first, own, got)
    out_ref[0] = jnp.where(first, got, own)
    small = add(own_ref[:, hidden:], got_ref[:, hidden:])
    k_ref[0] = small[:, :taps]
    pad_ref[0:share, :] = small
    turned = pad_ref[...].T
    gain_ref[...] = turned[taps : taps + 1, :share]
    scale_ref[...] = turned[taps + 1 : taps + 2, :share]


def final(core, own, got, taps):
    share, hidden = own.shape[0], own.shape[1] - 2 * SMALL_ROWS
    outs = (
        ((1, share, taps), jnp.float32),
        ((1, share), jnp.float32),
        ((1, share, hidden), jnp.float32),
        ((1, share, hidden), jnp.float32),
        ((1, share), jnp.float32),
    )
    t_kernel, t_gain, t_in, t_out, t_scale = small_call(
        final_kernel, "final", outs, core, own, got, scratch=[pltpu.VMEM((LANES, 2 * SMALL_ROWS), jnp.float32)]
    )
    return t_kernel.transpose(0, 2, 1), t_gain, t_in, t_out.transpose(0, 2, 1), t_scale


BF16 = jnp.bfloat16
F32 = jnp.float32


def one_image(x, g, small, sels, w_ins, w_outs, first, passing):
    blocks = small.shape[0]
    rows, cols, channels = x.shape
    which = jnp.stack([sel[0] for sel in sels])
    xs, xhats, invs, pres, branches = forward(which, x, first[1], small, w_ins, w_outs)
    xs, xhats, invs = (x,) + tuple(xs), first[:1] + tuple(xhats), first[2:] + tuple(invs)
    smalls = [None] * blocks
    for s in reversed(range(blocks)):
        keep, send, sums8, gconv = mlp_back(
            sels[s], g.reshape(rows * cols, channels), branches[s], pres[s], xhats[s], invs[s],
            small[s, TAPS : TAPS + 1], small[s, TAPS + 1 : TAPS + 2], w_ins, w_outs, passing.before("mlp", s),
        )
        passing.done(s, keep, send)
        *g_next, smalls[s] = conv_back(
            gconv, xs[s], g, small[s, :TAPS], sums8, s > 0, passing.before("conv", s)
        )
        g = g_next[0] if g_next else None
    return smalls


def small_parameters(kernels, norm_gains, scales):
    taps = kernels.shape[1]
    fill = jnp.zeros((56 - taps - 2, kernels.shape[2]), F32)
    return jnp.concatenate([kernels[0], norm_gains, scales, fill], axis=0)


def finish(t_kernel, t_gain, t_scale, t_in, t_out):
    return t_kernel[None], t_gain[None], t_in[None], t_out[None], t_scale[None]


def any_mesh(images, cotangent, kernels, norm_gains, w_in, w_out, scales):
    segments = lax.axis_size("segment")
    rank = lax.axis_index("segment")
    count = images.shape[0] // segments
    taps = kernels.shape[1]
    small = lax.all_gather(small_parameters(kernels, norm_gains, scales), "segment")
    all_in = lax.all_gather(w_in[0], "segment")
    all_out = lax.all_gather(w_out[0], "segment")
    sels = [jnp.array([s, 0], jnp.int32) for s in range(segments)]
    pieces = [[None] * 3 for _ in range(segments)]

    class Sums:
        def before(self, part, s):
            return ()

        def done(self, s, keep, send):
            self.add(s, 0, keep.astype(F32))
            self.add(s, 1, send.astype(F32))

        def add(self, s, k, value):
            pieces[s][k] = value if pieces[s][k] is None else pieces[s][k] + value

    sums = Sums()
    w_ins = [all_in[s] for s in range(segments)]
    w_outs = [all_out[s] for s in range(segments)]
    for i in range(count):
        x = lax.dynamic_index_in_dim(images, rank * count + i, 0, keepdims=False)
        g = lax.dynamic_index_in_dim(cotangent, rank * count + i, 0, keepdims=False)
        smalls = one_image(x, g, small, sels, w_ins, w_outs, conv_norm(x, small[0]), sums)
        for s in range(segments):
            sums.add(s, 2, smalls[s])

    def summed(values, dim):
        mine = lax.psum_scatter(jnp.stack(values), "segment", scatter_dimension=0, tiled=False)
        return lax.psum_scatter(mine, "dp", scatter_dimension=dim, tiled=True)

    t_in = summed([p[0] for p in pieces], 0)
    t_out = summed([p[1] for p in pieces], 0).T
    t_small = summed([p[2] for p in pieces], 1)
    return finish(t_small[:taps], t_small[taps], t_small[taps + 1], t_in, t_out)


def partners(flip, extent=(4, 2, 2, 2)):
    pairs = []
    for index in range(32):
        z, y, x, c = index >> 3, (index >> 2) & 1, (index >> 1) & 1, index & 1
        other = ((z ^ flip[0]) << 3) | ((y ^ flip[1]) << 2) | ((x ^ flip[2]) << 1) | (c ^ flip[3])
        pairs.append((index, other))
    return pairs


def swap(value, z=0, y=0, x=0, c=0):
    return lax.ppermute(value, ("dp", "segment"), partners((z, y, x, c)))


def along_x(value, to_last):
    pairs = [(i, j) for i, j in partners((0, 0, 1, 0)) if (i >> 1) & 1 == (0 if to_last else 1)]
    return lax.ppermute(value, ("dp", "segment"), pairs)


def this_mesh(images, cotangent, kernels, norm_gains, w_in, w_out, scales):
    rank = lax.axis_index("segment")
    core = rank % 2
    chip = rank // 2
    depth = lax.axis_index("dp") // 2
    side = lax.axis_index("dp") % 2
    own_small = small_parameters(kernels, norm_gains, scales)
    near_small = swap(own_small, c=1)
    near_in, near_out = swap(w_in[0], c=1), swap(w_out[0], c=1)
    small = jnp.where(core == 0, jnp.stack([own_small, near_small]), jnp.stack([near_small, own_small]))
    weights = (w_in[0], near_in, w_out[0], near_out)
    sel = jnp.stack([core, 1 - core, chip, core]).astype(jnp.int32)
    cores = core[None].astype(jnp.int32)
    sides = side[None].astype(jnp.int32)
    levels = jnp.stack([depth, depth ^ 1, depth ^ 2, depth ^ 3]).astype(jnp.int32)

    maps = [lax.dynamic_index_in_dim(images, 2 * core + i, 0, keepdims=False) for i in range(2)]
    ends = [lax.dynamic_index_in_dim(cotangent, 2 * core + i, 0, keepdims=False) for i in range(2)]
    firsts, kept = [], []
    for x in maps:
        firsts.append(conv_norm(x, small[0], tuple(k.inv1 for k in kept)))
        kept.append(pair_forward(sel, x, firsts[-1], small, weights))
    passed = [along_x(k.y, True) for k in kept]
    both = pair_both(sel, passed[0], ends[0], small, weights)
    g_first = along_x(both.g0, False)
    both = pair_both(sel, passed[1], ends[1], small, weights, both)
    g_second = along_x(both.g0, False)

    def back(i, g, before):
        high = pair_back_high(sel, g, kept[i], small, weights, before, (before[0].small0,) if before else ())
        high_core = swap(high.send, c=1) if before else None
        low = pair_back_low(sel, g, high, maps[i], kept[i].x1, firsts[i], kept[i], small, weights, before)
        low_core = swap(low.send, c=1) if before else None
        small0 = pair_back_conv(sel, low, maps[i], before)
        return types.SimpleNamespace(keep0=low.keep, send0=low.send, keep1=high.keep, send1=high.send,
                                     small0=small0, small1=low.small1, core0=low_core, core1=high_core)

    grads = back(0, g_first, None)
    grads = back(1, g_second, (grads, both))

    def along_y(*pairs):
        across, mine = to_side(sides, *pairs)
        return mine, swap(across, y=1)

    def along_z(mine, got):
        own, *others = to_depths(levels, mine, got)
        return [own] + [swap(v, z=flip) for v, flip in zip(others, (1, 2, 3))]

    high = along_y(grads.keep1, grads.core1)
    low = along_y(grads.keep0, grads.core0, pack(cores, (grads.small0, grads.small1)))
    high = along_z(*high)
    low = along_z(*low)
    own, send = to_core(cores, low + high)
    return final(cores, own, swap(send, c=1), kernels.shape[1])


def solution(mesh):
    in_specs = (
        P("dp", None, None, None),
        P("dp", None, None, None),
        P("segment", None, None),
        P("segment", None),
        P("segment", None, None),
        P("segment", None, None),
        P("segment", None),
    )
    out_specs = (
        P("segment", None, "dp"),
        P("segment", "dp"),
        P("segment", "dp", None),
        P("segment", None, "dp"),
        P("segment", "dp"),
    )
    fits = dict(mesh.shape) == {"dp": 8, "segment": 4}

    def whole(images, *rest):
        local = this_mesh if fits and images.shape[0] == 32 else any_mesh
        return jax.shard_map(local, mesh=mesh, in_specs=in_specs, out_specs=out_specs, check_vma=False)(images, *rest)

    return whole
```

time: 165 us -> 119 us (0.72)
  waiting for transfers between devices: 66.9 us -> 46 us
  other arithmetic: 13.8 us -> 1.72 us
  starting transfers between devices: 31.2 us -> 22.2 us
  local copies, waits for them, and re-layouts: 10.7 us -> 6.52 us
    ppermute x37 -> x14, waiting for transfers between devices: 66.9 us -> 20.6 us  [swap(): return lax.ppermute(value, ('dp', 'segment'), partners((z, y, x, c)))]
    ppermute x0 -> x4, waiting for transfers between devices: none -> 25.4 us  [along_x(): return lax.ppermute(value, ('dp', 'segment'), pairs)]
    ppermute x37 -> x14, starting transfers between devices: 31.2 us -> 13.8 us  [swap(): return lax.ppermute(value, ('dp', 'segment'), partners((z, y, x, c)))]
    convert_element_type x8 -> x0, other arithmetic: 8.47 us -> none  [the longest x4 4.31 us: this_mesh(): (half(keep, side) + half(got, side) + across.astype(F32)).astype(BF16)]
    ppermute x0 -> x4, starting transfers between devices: none -> 8.37 us  [along_x(): return lax.ppermute(value, ('dp', 'segment'), pairs)]
    dynamic_slice x2 -> x0, local copies, waits for them, and re-layouts: 2.2 us -> none  [the longest x1 1.8 us: this_mesh(): x = lax.dynamic_index_in_dim(images, rank, 0, keepdims=False)]
    add x5 -> x0, other arithmetic: 1.74 us -> none  [the longest x1 0.88 us: this_mesh(): mine + swap(lax.dynamic_index_in_dim(line, depth ^ flip, 1, keepdims=Fals...]
    pallas_call x16 -> x19, Pallas kernels: 39.9 us -> 41.1 us  [the longest x10 34.4 us: named_call(): pl.pallas_call(kernel, in_specs=[pl.BlockSpec(memory_space=spaces[kind])...]
  transfers between devices with their start and end apart: 37 -> 18, of which waited for: 19 -> 7; matrix products, arithmetic and copies ran while one was open for 11% -> 2% of each run, Pallas kernels for 2% -> 26%
where the time goes in v2:
time: 119 us
  waiting for transfers between devices  46 us (39%)
  Pallas kernels  41.1 us (35%)
  starting transfers between devices  22.2 us (19%)
  local copies, waits for them, and re-layouts  6.52 us (5%)
  other arithmetic  1.72 us (1%)
    pallas_call x10, Pallas kernels, named_call(): pl.pallas_call(kernel, in_specs=[pl.BlockSpec(memory_space=spaces[kind])...  34.4 us
    ppermute x4, waiting for transfers between devices, along_x(): return lax.ppermute(value, ('dp', 'segment'), pairs)  25.4 us
    ppermute x14, waiting for transfers between devices, swap(): return lax.ppermute(value, ('dp', 'segment'), partners((z, y, x, c)))  20.6 us
    ppermute x14, starting transfers between devices, swap(): return lax.ppermute(value, ('dp', 'segment'), partners((z, y, x, c)))  13.8 us
    ppermute x4, starting transfers between devices, along_x(): return lax.ppermute(value, ('dp', 'segment'), pairs)  8.37 us
    unnamed x17, local copies, waits for them, and re-layouts  5.32 us
    pallas_call x2, Pallas kernels, conv_norm(): pl.pallas_call(conv_norm_kernel, in_specs=[pl.BlockSpec(memory_space=pltp...  4.24 us
    pallas_call x7, Pallas kernels, small_call(): pl.pallas_call(body, in_specs=[pl.BlockSpec(memory_space=pltpu.SMEM)] + [...  2.52 us
  transfers between devices with their start and end apart: 18, of which 7 were waited for; matrix products, arithmetic and copies ran while one was open for 2% of the time, Pallas kernels for 26%

profile of v2, /device:TPU:0, one launch (start us, length us, event | category | flops | bytes accessed | tf_op | source)
XLA Modules:
  0.0 118.5 jit_solution(5600327331203954865)
XLA Ops:
  0.6 1.0 copy.14
  4.3 1.1 dynamic-slice_bitcast_fusion.2
  5.5 2.1 %conv_norm.2 = (bf16[256,384]{1,0:T(8,128)(2,1)S(1)}, bf16[256,384]{1,0:T(8,128)(2,1)S(1)}, f32[256,128]{1,0:T(8,128)S(1)}) custom-call(bf16[16,16,384]{2,1,0:T(8,128)(2,1)S(1)} %get-tuple-element.153.x_ref.refs_1_.refs_3_, f32[56,384]{1,0:T(8,128)S(1)} %slice_bitcast_fusion.small_ref), custom_call_target="tpu_custom_call" | custom-call | flops 2860000000 | bytes 9360000 | tf_op jit(solution)/shard_map/conv_norm/pallas_call | solution.py:88
  8.5 5.7 %pair_forward.2 = (bf16[16,16,384]{2,1,0:T(8,128)(2,1)S(1)}, bf16[16,16,384]{2,1,0:T(8,128)(2,1)S(1)}, bf16[256,384]{1,0:T(8,128)(2,1)S(1)}, f32[256,128]{1,0:T(...) custom-call(s32[4]{0:T(128)S(1)} %pad_add_fusion.1.refs_0_, ...), custom_call_target="tpu_custom_call" | custom-call | flops 8249999872 | bytes 27000000 | tf_op jit(solution)/shard_map/pair_forward/pallas_call | solution.py:477
  14.2 4.5 %collective-permute-start.4 = (bf16[16,16,384]{2,1,0:T(8,128)(2,1)S(1)}, bf16[16,16,384]{2,1,0:T(8,128)(2,1)S(1)}, u32[]{:S(2)}, u32[]{:S(2)}) collective-permute-start(bf16[16,16,384]{2,1,0:T(8,128)(2,1)S(1)} %get-tuple-element.82), channel_id=1, source_target_pairs={{0,2},{1,3},{4,6},{5,7},{8,10},{9,11},{12,14},{13,15},{16,18},{17,... | collective-permute-start | bytes 589832 | tf_op jit(solution)/shard_map/ppermute | solution.py:960
  18.7 2.1 %conv_norm.3 = (bf16[256,384]{1,0:T(8,128)(2,1)S(1)}, bf16[256,384]{1,0:T(8,128)(2,1)S(1)}, f32[256,128]{1,0:T(8,128)S(1)}) custom-call(bf16[16,16,384]{2,1,0:T(8,128)(2,1)S(1)} %get-tuple-element.154.x_ref.refs_1_.refs_3_, f32[56,384]{1,0:T(8,128)S(1)} %slice_bitcast_fusion.small_ref, f32[256,128]{1,0:T(8,128)S(1)} %get-tuple-element.79.rest_0_.refs_5_), custom_call_target="tpu_custom_call" | custom-call | flops 2860000000 | bytes 9360000 | tf_op jit(solution)/shard_map/conv_norm/pallas_call | solution.py:88
  20.9 5.7 %pair_forward.3 = (bf16[16,16,384]{2,1,0:T(8,128)(2,1)S(1)}, bf16[16,16,384]{2,1,0:T(8,128)(2,1)S(1)}, bf16[256,384]{1,0:T(8,128)(2,1)S(1)}, f32[256,128]{1,0:T(...) custom-call(s32[4]{0:T(128)S(1)} %pad_add_fusion.1.refs_0_, ...), custom_call_target="tpu_custom_call" | custom-call | flops 8249999872 | bytes 27000000 | tf_op jit(solution)/shard_map/pair_forward/pallas_call | solution.py:477
  26.6 1.3 %collective-permute-start.3 = (bf16[16,16,384]{2,1,0:T(8,128)(2,1)S(1)}, bf16[16,16,384]{2,1,0:T(8,128)(2,1)S(1)}, u32[]{:S(2)}, u32[]{:S(2)}) collective-permute-start(bf16[16,16,384]{2,1,0:T(8,128)(2,1)S(1)} %get-tuple-element.81), channel_id=1, source_target_pairs={{0,2},{1,3},{4,6},{5,7},{8,10},{9,11},{12,14},{13,15},{16,18},{17,... | collective-permute-start | bytes 589832 | tf_op jit(solution)/shard_map/ppermute | solution.py:960
  28.5 1.3 %collective-permute-start.6 = (bf16[16,16,384]{2,1,0:T(8,128)(2,1)S(1)}, bf16[16,16,384]{2,1,0:T(8,128)(2,1)S(1)}, u32[]{:S(2)}, u32[]{:S(2)}) collective-permute-start(bf16[16,16,384]{2,1,0:T(8,128)(2,1)S(1)} %get-tuple-element.94), channel_id=1, source_target_pairs={{2,0},{3,1},{6,4},{7,5},{10,8},{11,9},{14,12},{15,13},{18,16},{19,... | collective-permute-start | bytes 589832 | tf_op jit(solution)/shard_map/ppermute | solution.py:960
  29.8 2.8 %collective-permute-done.3.refs_1_ = bf16[16,16,384]{2,1,0:T(8,128)(2,1)S(1)} collective-permute-done((bf16[16,16,384]{2,1,0:T(8,128)(2,1)S(1)}, bf16[16,16,384]{2,1,0:T(8,128)(2,1)S(1)}, u32[]{:S(2)}, u32[]{:S(2)}) %collective-permute-start.3) | collective-permute-done | bytes 196640 | tf_op jit(solution)/shard_map/ppermute | solution.py:960
  33.4 1.3 %collective-permute-start.5 = (bf16[16,16,384]{2,1,0:T(8,128)(2,1)S(1)}, bf16[16,16,384]{2,1,0:T(8,128)(2,1)S(1)}, u32[]{:S(2)}, u32[]{:S(2)}) collective-permute-start(bf16[16,16,384]{2,1,0:T(8,128)(2,1)S(1)} %get-tuple-element.89), channel_id=1, source_target_pairs={{2,0},{3,1},{6,4},{7,5},{10,8},{11,9},{14,12},{15,13},{18,16},{19,... | collective-permute-start | bytes 589832 | tf_op jit(solution)/shard_map/ppermute | solution.py:960
  34.7 14.9 %collective-permute-done.6.refs_1_ = bf16[16,16,384]{2,1,0:T(8,128)(2,1)S(1)} collective-permute-done((bf16[16,16,384]{2,1,0:T(8,128)(2,1)S(1)}, bf16[16,16,384]{2,1,0:T(8,128)(2,1)S(1)}, u32[]{:S(2)}, u32[]{:S(2)}) %collective-permute-start.6) | collective-permute-done | bytes 196640 | tf_op jit(solution)/shard_map/ppermute | solution.py:960
  49.7 3.1 %pair_back_high.2 = (bf16[384,768]{1,0:T(8,128)(2,1)S(1)}, bf16[384,768]{1,0:T(8,128)(2,1)S(1)}, f32[8,384]{1,0:T(8,128)S(1)}, f32[256,384]{1,0:T(8,128)S(1)}) custom-call(s32[4]{0:T(128)S(1)} %pad_add_fusion.1.refs_0_, bf16[16,16,384]{2,1,0:T(8,128)(2,1)S(1)} %collective-permute-done.6.refs_1_, bf16[256,384]{1,0:T(8,128)(2,1)S(1)} %get-tuple-element.95.refs_2_, ...), custom_call_target="tpu_custom_call" | custom-call | flops 2750000128 | bytes 9000000 | tf_op jit(solution)/shard_map/pair_back_high/pallas_call | solution.py:477
  52.8 5.2 %pair_back_low.2 = (f32[64,384]{1,0:T(8,128)S(1)}, bf16[384,768]{1,0:T(8,128)(2,1)S(1)}, bf16[384,768]{1,0:T(8,128)(2,1)S(1)}, f32[8,384]{1,0:T(8,128)S(1)}, f32[256,384]{1,0:T(8,128)S(1)}) custom-call(s32[4]{0:T(128)S(1)} %pad_add_fusion.1.refs_0_, bf16[16,16,384]{2,1,0:T(8,128)(2,1)S(1)} %collective-permute-done.6.refs_1_, ...), custom_call_target="tpu_custom_call" | custom-call | flops 6049999872 | bytes 19800000 | tf_op jit(solution)/shard_map/pair_back_low/pallas_call | solution.py:477
  58.0 2.0 %pair_back_conv.2.refs_15_.refs_4_ = f32[64,384]{1,0:T(8,128)S(1)} custom-call(s32[4]{0:T(128)S(1)} %pad_add_fusion.1.refs_0_, f32[256,384]{1,0:T(8,128)S(1)} %get-tuple-element.109.refs_1_, f32[8,384]{1,0:T(8,128)S(1)} %get-tuple-element.110.refs_2_, bf16[16,16,384]{2,1,0:T(8,128)(2,1)S(1)} %get-tuple-element.153.x_ref.refs_1_.refs_3_), custom_call_target="tpu_custom_call" | custom-call | flops 1760000000 | bytes 5760000 | tf_op jit(solution)/shard_map/pair_back_conv/pallas_call | solution.py:477
  60.0 7.6 %collective-permute-done.5.refs_1_ = bf16[16,16,384]{2,1,0:T(8,128)(2,1)S(1)} collective-permute-done((bf16[16,16,384]{2,1,0:T(8,128)(2,1)S(1)}, bf16[16,16,384]{2,1,0:T(8,128)(2,1)S(1)}, u32[]{:S(2)}, u32[]{:S(2)}) %collective-permute-start.5) | collective-permute-done | bytes 196640 | tf_op jit(solution)/shard_map/ppermute | solution.py:960
  67.6 3.5 %pair_back_high.3 = (bf16[384,768]{1,0:T(8,128)(2,1)S(1)}, bf16[384,768]{1,0:T(8,128)(2,1)S(1)}, f32[8,384]{1,0:T(8,128)S(1)}, f32[256,384]{1,0:T(8,128)S(1)}) custom-call(s32[4]{0:T(128)S(1)} %pad_add_fusion.1.refs_0_, bf16[16,16,384]{2,1,0:T(8,128)(2,1)S(1)} %collective-permute-done.5.refs_1_, bf16[256,384]{1,0:T(8,128)(2,1)S(1)} %get-tuple-element.90.refs_2_, ...), custom_call_target="tpu_custom_call" | custom-call | flops 2750000128 | bytes 9000000 | tf_op jit(solution)/shard_map/pair_back_high/pallas_call | solution.py:477
  71.2 5.7 %pair_back_low.3 = (f32[64,384]{1,0:T(8,128)S(1)}, bf16[384,768]{1,0:T(8,128)(2,1)S(1)}, bf16[384,768]{1,0:T(8,128)(2,1)S(1)}, f32[8,384]{1,0:T(8,128)S(1)}, f32[256,384]{1,0:T(8,128)S(1)}) custom-call(s32[4]{0:T(128)S(1)} %pad_add_fusion.1.refs_0_, bf16[16,16,384]{2,1,0:T(8,128)(2,1)S(1)} %collective-permute-done.5.refs_1_, ...), custom_call_target="tpu_custom_call" | custom-call | flops 6049999872 | bytes 19800000 | tf_op jit(solution)/shard_map/pair_back_low/pallas_call | solution.py:477
  79.0 1.0 copy-done.5
  80.0 2.0 %pair_back_conv.3.refs_1_ = f32[64,384]{1,0:T(8,128)S(1)} custom-call(s32[4]{0:T(128)S(1)} %pad_add_fusion.1.refs_0_, f32[256,384]{1,0:T(8,128)S(1)} %copy-done.5, f32[8,384]{1,0:T(8,128)S(1)} %get-tuple-element.127.refs_2_, bf16[16,16,384]{2,1,0:T(8,128)(2,1)S(1)} %get-tuple-element.154.x_ref.refs_1_.refs_3_, f32[64,384]{1,0:T(8,128)S(1)} %pair_back_conv.2.refs_15_.refs_4_, ...), custom_call_target="tpu_custom_call" | custom-call | flops 1760000000 | bytes 5760000 | tf_op jit(solution)/shard_map/pair_back_conv/pallas_call | solution.py:477
  82.3 1.6 %collective-permute-start.13 = (bf16[4,48,768]{2,1,0:T(8,128)(2,1)S(1)}, bf16[4,48,768]{2,1,0:T(8,128)(2,1)S(1)}, u32[]{:S(2)}, u32[]{:S(2)}) collective-permute-start(bf16[4,48,768]{2,1,0:T(8,128)(2,1)S(1)} %get-tuple-element.139), channel_id=1, source_target_pairs={{0,4},{1,5},{2,6},{3,7},{4,0},{5,1},{6,2},{7,3},{8,12},{9,13},{10,... | collective-permute-start | bytes 884744 | tf_op jit(solution)/shard_map/ppermute | solution.py:955
  84.1 0.9 collective-permute-start.8
  85.0 7.2 %collective-permute-done.13.refs_2_ = bf16[4,48,768]{2,1,0:T(8,128)(2,1)S(1)} collective-permute-done((bf16[4,48,768]{2,1,0:T(8,128)(2,1)S(1)}, bf16[4,48,768]{2,1,0:T(8,128)(2,1)S(1)}, u32[]{:S(2)}, u32[]{:S(2)}) %collective-permute-start.13) | collective-permute-done | bytes 294944 | tf_op jit(solution)/shard_map/ppermute | solution.py:955
  92.3 1.0 copy-done.3
  93.8 1.7 %collective-permute-start.14 = (bf16[48,768]{1,0:T(8,128)(2,1)S(1)}, bf16[48,768]{1,0:T(8,128)(2,1)S(1)}, u32[]{:S(2)}, u32[]{:S(2)}) collective-permute-start(bf16[48,768]{1,0:T(8,128)(2,1)S(1)} %get-tuple-element.141), channel_id=1, source_target_pairs={{0,8},{1,9},{2,10},{3,11},{4,12},{5,13},{6,14},{7,15},{8,0},{9,1},... | collective-permute-start | bytes 221192 | tf_op jit(solution)/shard_map/ppermute | solution.py:955
  95.5 3.2 %collective-permute-done.8.refs_2_ = bf16[4,48,896]{2,1,0:T(8,128)(2,1)S(1)} collective-permute-done((bf16[4,48,896]{2,1,0:T(8,128)(2,1)S(1)}, bf16[4,48,896]{2,1,0:T(8,128)(2,1)S(1)}, u32[]{:S(2)}, u32[]{:S(2)}) %collective-permute-start.8) | collective-permute-done | bytes 344096 | tf_op jit(solution)/shard_map/ppermute | solution.py:955
  99.3 1.7 %collective-permute-start.9 = (bf16[48,896]{1,0:T(8,128)(2,1)S(1)}, bf16[48,896]{1,0:T(8,128)(2,1)S(1)}, u32[]{:S(2)}, u32[]{:S(2)}) collective-permute-start(bf16[48,896]{1,0:T(8,128)(2,1)S(1)} %get-tuple-element.133), channel_id=1, source_target_pairs={{0,8},{1,9},{2,10},{3,11},{4,12},{5,13},{6,14},{7,15},{8,0},{9,1},... | collective-permute-start | bytes 258056 | tf_op jit(solution)/shard_map/ppermute | solution.py:955
  101.0 2.6 %collective-permute-start.10 = (bf16[48,896]{1,0:T(8,128)(2,1)S(1)}, bf16[48,896]{1,0:T(8,128)(2,1)S(1)}, u32[]{:S(2)}, u32[]{:S(2)}) collective-permute-start(bf16[48,896]{1,0:T(8,128)(2,1)S(1)} %get-tuple-element.134), channel_id=1, source_target_pairs={{0,16},{1,17},{2,18},{3,19},{4,20},{5,21},{6,22},{7,23},{8,24},{9,... | collective-permute-start | bytes 258056 | tf_op jit(solution)/shard_map/ppermute | solution.py:955
  103.8 1.7 %collective-permute-start.15 = (bf16[48,768]{1,0:T(8,128)(2,1)S(1)}, bf16[48,768]{1,0:T(8,128)(2,1)S(1)}, u32[]{:S(2)}, u32[]{:S(2)}) collective-permute-start(bf16[48,768]{1,0:T(8,128)(2,1)S(1)} %get-tuple-element.142), channel_id=1, source_target_pairs={{0,16},{1,17},{2,18},{3,19},{4,20},{5,21},{6,22},{7,23},{8,24},{9,... | collective-permute-start | bytes 221192 | tf_op jit(solution)/shard_map/ppermute | solution.py:955
  105.5 1.9 %collective-permute-start.16 = (bf16[48,768]{1,0:T(8,128)(2,1)S(1)}, bf16[48,768]{1,0:T(8,128)(2,1)S(1)}, u32[]{:S(2)}, u32[]{:S(2)}) collective-permute-start(bf16[48,768]{1,0:T(8,128)(2,1)S(1)} %get-tuple-element.143), channel_id=1, source_target_pairs={{0,24},{1,25},{2,26},{3,27},{4,28},{5,29},{6,30},{7,31},{8,16},{9,... | collective-permute-start | bytes 221192 | tf_op jit(solution)/shard_map/ppermute | solution.py:955
  107.4 8.9 %collective-permute-done.15.refs_7_ = bf16[48,768]{1,0:T(8,128)(2,1)S(1)} collective-permute-done((bf16[48,768]{1,0:T(8,128)(2,1)S(1)}, bf16[48,768]{1,0:T(8,128)(2,1)S(1)}, u32[]{:S(2)}, u32[]{:S(2)}) %collective-permute-start.15) | collective-permute-done | bytes 73760 | tf_op jit(solution)/shard_map/ppermute | solution.py:955
  116.5 1.3 %collective-permute-done.17.refs_2_ = bf16[48,896]{1,0:T(8,128)(2,1)S(1)} collective-permute-done((bf16[48,896]{1,0:T(8,128)(2,1)S(1)}, bf16[48,896]{1,0:T(8,128)(2,1)S(1)}, u32[]{:S(2)}, u32[]{:S(2)}) %collective-permute-start.17) | collective-permute-done | bytes 86048 | tf_op jit(solution)/shard_map/ppermute | solution.py:955
  (50 shorter events, 10.1 us)
Async XLA Ops:
  0.6 4.7 %copy-start.6 = (bf16[4,16,16,384]{3,2,1,0:T(8,128)(2,1)S(1)}, bf16[4,16,16,384]{3,2,1,0:T(8,128)(2,1)}, u32[]{:S(2)}) copy-start(bf16[4,16,16,384]{3,2,1,0:T(8,128)(2,1)} %param.8) | copy-start | bytes 2359300
  2.5 3.0 %collective-permute-start = (f32[56,384]{1,0:T(8,128)S(1)}, f32[56,384]{1,0:T(8,128)S(1)}, u32[]{:S(2)}, u32[]{:S(2)}) collective-permute-start(f32[56,384]{1,0:T(8,128)S(1)} %maximum_maximum_fusion), channel_id=1, source_target_pairs={{0,1},{1,0},{2,3},{3,2},{4,5},{5,4},{6,7},{7,6},{8,9},{9,8},{10,11... | collective-permute-start | bytes 258056 | tf_op jit(solution)/shard_map/ppermute | solution.py:955
  3.0 4.7 %collective-permute-start.1 = (bf16[384,768]{1,0:T(8,128)(2,1)}, bf16[384,768]{1,0:T(8,128)(2,1)S(1)}, u32[]{:S(2)}, u32[]{:S(2)}) collective-permute-start(bf16[384,768]{1,0:T(8,128)(2,1)} %bitcast.41), channel_id=1, source_target_pairs={{0,1},{1,0},{2,3},{3,2},{4,5},{5,4},{6,7},{7,6},{8,9},{9,8},{10,11... | collective-permute-start | bytes 1769480 | tf_op jit(solution)/shard_map/ppermute | solution.py:955
  3.1 4.6 %collective-permute-start.2 = (bf16[768,384]{1,0:T(8,128)(2,1)}, bf16[768,384]{1,0:T(8,128)(2,1)}, u32[]{:S(2)}, u32[]{:S(2)}) collective-permute-start(bf16[768,384]{1,0:T(8,128)(2,1)} %bitcast.50), channel_id=1, source_target_pairs={{0,1},{1,0},{2,3},{3,2},{4,5},{5,4},{6,7},{7,6},{8,9},{9,8},{10,11... | collective-permute-start | bytes 1769480 | tf_op jit(solution)/shard_map/ppermute | solution.py:955
  7.7 0.8 copy-start.7
  14.2 13.7 %collective-permute-start.4 = (bf16[16,16,384]{2,1,0:T(8,128)(2,1)S(1)}, bf16[16,16,384]{2,1,0:T(8,128)(2,1)S(1)}, u32[]{:S(2)}, u32[]{:S(2)}) collective-permute-start(bf16[16,16,384]{2,1,0:T(8,128)(2,1)S(1)} %get-tuple-element.82), channel_id=1, source_target_pairs={{0,2},{1,3},{4,6},{5,7},{8,10},{9,11},{12,14},{13,15},{16,18},{17,... | collective-permute-start | bytes 589832 | tf_op jit(solution)/shard_map/ppermute | solution.py:960
  26.6 6.0 %collective-permute-start.3 = (bf16[16,16,384]{2,1,0:T(8,128)(2,1)S(1)}, bf16[16,16,384]{2,1,0:T(8,128)(2,1)S(1)}, u32[]{:S(2)}, u32[]{:S(2)}) collective-permute-start(bf16[16,16,384]{2,1,0:T(8,128)(2,1)S(1)} %get-tuple-element.81), channel_id=1, source_target_pairs={{0,2},{1,3},{4,6},{5,7},{8,10},{9,11},{12,14},{13,15},{16,18},{17,... | collective-permute-start | bytes 589832 | tf_op jit(solution)/shard_map/ppermute | solution.py:960
  28.5 21.2 %collective-permute-start.6 = (bf16[16,16,384]{2,1,0:T(8,128)(2,1)S(1)}, bf16[16,16,384]{2,1,0:T(8,128)(2,1)S(1)}, u32[]{:S(2)}, u32[]{:S(2)}) collective-permute-start(bf16[16,16,384]{2,1,0:T(8,128)(2,1)S(1)} %get-tuple-element.94), channel_id=1, source_target_pairs={{2,0},{3,1},{6,4},{7,5},{10,8},{11,9},{14,12},{15,13},{18,16},{19,... | collective-permute-start | bytes 589832 | tf_op jit(solution)/shard_map/ppermute | solution.py:960
  33.4 34.2 %collective-permute-start.5 = (bf16[16,16,384]{2,1,0:T(8,128)(2,1)S(1)}, bf16[16,16,384]{2,1,0:T(8,128)(2,1)S(1)}, u32[]{:S(2)}, u32[]{:S(2)}) collective-permute-start(bf16[16,16,384]{2,1,0:T(8,128)(2,1)S(1)} %get-tuple-element.89), channel_id=1, source_target_pairs={{2,0},{3,1},{6,4},{7,5},{10,8},{11,9},{14,12},{15,13},{18,16},{19,... | collective-permute-start | bytes 589832 | tf_op jit(solution)/shard_map/ppermute | solution.py:960
  71.1 11.0 %collective-permute-start.12 = (bf16[384,768]{1,0:T(8,128)(2,1)S(1)}, bf16[384,768]{1,0:T(8,128)(2,1)S(1)}, u32[]{:S(2)}, u32[]{:S(2)}) collective-permute-start(bf16[384,768]{1,0:T(8,128)(2,1)S(1)} %get-tuple-element.137), channel_id=1, source_target_pairs={{0,1},{1,0},{2,3},{3,2},{4,5},{5,4},{6,7},{7,6},{8,9},{9,8},{10,11... | collective-permute-start | bytes 1769480 | tf_op jit(solution)/shard_map/ppermute | solution.py:955
  77.0 0.8 copy-start
  77.8 0.8 copy-start.4
  78.6 5.4 %collective-permute-start.7 = (bf16[384,768]{1,0:T(8,128)(2,1)S(1)}, bf16[384,768]{1,0:T(8,128)(2,1)S(1)}, u32[]{:S(2)}, u32[]{:S(2)}) collective-permute-start(bf16[384,768]{1,0:T(8,128)(2,1)S(1)} %get-tuple-element.125), channel_id=1, source_target_pairs={{0,1},{1,0},{2,3},{3,2},{4,5},{5,4},{6,7},{7,6},{8,9},{9,8},{10,11... | collective-permute-start | bytes 1769480 | tf_op jit(solution)/shard_map/ppermute | solution.py:955
  79.0 1.0 copy-start.5
  82.2 1.8 %copy-start.1 = (bf16[384,768]{1,0:T(8,128)(2,1)S(1)}, bf16[384,768]{1,0:T(8,128)(2,1)}, u32[]{:S(2)}) copy-start(bf16[384,768]{1,0:T(8,128)(2,1)} %copy-done) | copy-start | bytes 1769476
  82.3 1.8 %copy-start.2 = (bf16[4,48,768]{2,1,0:T(8,128)(2,1)}, bf16[4,48,768]{2,1,0:T(8,128)(2,1)S(1)}, u32[]{:S(2)}) copy-start(bf16[4,48,768]{2,1,0:T(8,128)(2,1)S(1)} %get-tuple-element.138.refs_1_) | copy-start | bytes 884740
  82.3 9.9 %collective-permute-start.13 = (bf16[4,48,768]{2,1,0:T(8,128)(2,1)S(1)}, bf16[4,48,768]{2,1,0:T(8,128)(2,1)S(1)}, u32[]{:S(2)}, u32[]{:S(2)}) collective-permute-start(bf16[4,48,768]{2,1,0:T(8,128)(2,1)S(1)} %get-tuple-element.139), channel_id=1, source_target_pairs={{0,4},{1,5},{2,6},{3,7},{4,0},{5,1},{6,2},{7,3},{8,12},{9,13},{10,... | collective-permute-start | bytes 884744 | tf_op jit(solution)/shard_map/ppermute | solution.py:955
  84.1 14.6 %collective-permute-start.8 = (bf16[4,48,896]{2,1,0:T(8,128)(2,1)S(1)}, bf16[4,48,896]{2,1,0:T(8,128)(2,1)S(1)}, u32[]{:S(2)}, u32[]{:S(2)}) collective-permute-start(bf16[4,48,896]{2,1,0:T(8,128)(2,1)S(1)} %get-tuple-element.131), channel_id=1, source_target_pairs={{0,4},{1,5},{2,6},{3,7},{4,0},{5,1},{6,2},{7,3},{8,12},{9,13},{10,... | collective-permute-start | bytes 1032200 | tf_op jit(solution)/shard_map/ppermute | solution.py:955
  92.3 1.0 copy-start.3
  93.8 11.7 %collective-permute-start.14 = (bf16[48,768]{1,0:T(8,128)(2,1)S(1)}, bf16[48,768]{1,0:T(8,128)(2,1)S(1)}, u32[]{:S(2)}, u32[]{:S(2)}) collective-permute-start(bf16[48,768]{1,0:T(8,128)(2,1)S(1)} %get-tuple-element.141), channel_id=1, source_target_pairs={{0,8},{1,9},{2,10},{3,11},{4,12},{5,13},{6,14},{7,15},{8,0},{9,1},... | collective-permute-start | bytes 221192 | tf_op jit(solution)/shard_map/ppermute | solution.py:955
  99.3 17.0 %collective-permute-start.9 = (bf16[48,896]{1,0:T(8,128)(2,1)S(1)}, bf16[48,896]{1,0:T(8,128)(2,1)S(1)}, u32[]{:S(2)}, u32[]{:S(2)}) collective-permute-start(bf16[48,896]{1,0:T(8,128)(2,1)S(1)} %get-tuple-element.133), channel_id=1, source_target_pairs={{0,8},{1,9},{2,10},{3,11},{4,12},{5,13},{6,14},{7,15},{8,0},{9,1},... | collective-permute-start | bytes 258056 | tf_op jit(solution)/shard_map/ppermute | solution.py:955
  101.0 15.3 %collective-permute-start.10 = (bf16[48,896]{1,0:T(8,128)(2,1)S(1)}, bf16[48,896]{1,0:T(8,128)(2,1)S(1)}, u32[]{:S(2)}, u32[]{:S(2)}) collective-permute-start(bf16[48,896]{1,0:T(8,128)(2,1)S(1)} %get-tuple-element.134), channel_id=1, source_target_pairs={{0,16},{1,17},{2,18},{3,19},{4,20},{5,21},{6,22},{7,23},{8,24},{9,... | collective-permute-start | bytes 258056 | tf_op jit(solution)/shard_map/ppermute | solution.py:955
  103.6 12.7 %collective-permute-start.11 = (bf16[48,896]{1,0:T(8,128)(2,1)S(1)}, bf16[48,896]{1,0:T(8,128)(2,1)S(1)}, u32[]{:S(2)}, u32[]{:S(2)}) collective-permute-start(bf16[48,896]{1,0:T(8,128)(2,1)S(1)} %get-tuple-element.135), channel_id=1, source_target_pairs={{0,24},{1,25},{2,26},{3,27},{4,28},{5,29},{6,30},{7,31},{8,16},{9,... | collective-permute-start | bytes 258056 | tf_op jit(solution)/shard_map/ppermute | solution.py:955
  103.8 12.5 %collective-permute-start.15 = (bf16[48,768]{1,0:T(8,128)(2,1)S(1)}, bf16[48,768]{1,0:T(8,128)(2,1)S(1)}, u32[]{:S(2)}, u32[]{:S(2)}) collective-permute-start(bf16[48,768]{1,0:T(8,128)(2,1)S(1)} %get-tuple-element.142), channel_id=1, source_target_pairs={{0,16},{1,17},{2,18},{3,19},{4,20},{5,21},{6,22},{7,23},{8,24},{9,... | collective-permute-start | bytes 221192 | tf_op jit(solution)/shard_map/ppermute | solution.py:955
  105.5 10.8 %collective-permute-start.16 = (bf16[48,768]{1,0:T(8,128)(2,1)S(1)}, bf16[48,768]{1,0:T(8,128)(2,1)S(1)}, u32[]{:S(2)}, u32[]{:S(2)}) collective-permute-start(bf16[48,768]{1,0:T(8,128)(2,1)S(1)} %get-tuple-element.143), channel_id=1, source_target_pairs={{0,24},{1,25},{2,26},{3,27},{4,28},{5,29},{6,30},{7,31},{8,16},{9,... | collective-permute-start | bytes 221192 | tf_op jit(solution)/shard_map/ppermute | solution.py:955
  116.4 1.3 %collective-permute-start.17 = (bf16[48,896]{1,0:T(8,128)(2,1)S(1)}, bf16[48,896]{1,0:T(8,128)(2,1)S(1)}, u32[]{:S(2)}, u32[]{:S(2)}) collective-permute-start(bf16[48,896]{1,0:T(8,128)(2,1)S(1)} %get-tuple-element.145), channel_id=1, source_target_pairs={{0,1},{1,0},{2,3},{3,2},{4,5},{5,4},{6,7},{7,6},{8,9},{9,8},{10,11... | collective-permute-start | bytes 258056 | tf_op jit(solution)/shard_map/ppermute | solution.py:955

commit v3 on v2

--- a/solution.py
+++ b/solution.py
@@ -69,39 +69,98 @@
         inv_ref[at, :] = jnp.broadcast_to(inv, (2 * cols, LANES))
         return carry
 
-    lax.fori_loop(0, rows // 2, norm, 0, unroll=2)
+    lax.fori_loop(0, rows // 2, norm, 0, unroll=True)
 
 
 def pad_shape(rows, cols, channels):
     return pltpu.VMEM((channels // LANES, rows, cols + 16, LANES), jnp.float32)
 
 
-def conv_norm_kernel(x_ref, small_ref, *rest):
-    xhat_ref, normed_ref, inv_ref, pad_ref, conv_ref = rest[-5:]
-    zero_borders(pad_ref)
-    conv_norm_body(x_ref, small_ref, xhat_ref, normed_ref, inv_ref, pad_ref, conv_ref)
-
-
-def conv_norm(x, small, after=()):
+def in_hbm(arrays):
+    return [pltpu.with_memory_space_constraint(a, pltpu.HBM) for a in arrays]
+
+
+def parameters_kernel(k_ref, gain_ref, scale_ref, out_ref, taps_ref, rows_ref, sems):
+    copies = [
+        pltpu.make_async_copy(source, target, sems.at[i])
+        for i, (source, target) in enumerate(((k_ref, taps_ref), (gain_ref, rows_ref.at[0]), (scale_ref, rows_ref.at[1])))
+    ]
+    for copy in copies:
+        copy.start()
+    taps = taps_ref.shape[0]
+    out_ref[taps + 2 :, :] = jnp.zeros((out_ref.shape[0] - taps - 2, out_ref.shape[1]), jnp.float32)
+    for copy in copies:
+        copy.wait()
+    for t in range(taps):
+        out_ref[t : t + 1, :] = taps_ref[t]
+    out_ref[taps : taps + 1, :] = rows_ref[0]
+    out_ref[taps + 1 : taps + 2, :] = rows_ref[1]
+
+
+def parameters(kernels, norm_gains, scales):
+    taps, channels = kernels.shape[1:]
+    return pl.pallas_call(
+        parameters_kernel,
+        in_specs=[pl.BlockSpec(memory_space=pl.ANY)] * 3,
+        out_shape=jax.ShapeDtypeStruct((56, channels), jnp.float32),
+        scratch_shapes=[
+            pltpu.VMEM((taps, 1, channels), jnp.float32),
+            pltpu.VMEM((2, 1, channels), jnp.float32),
+            pltpu.SemaphoreType.DMA((3,)),
+        ],
+        compiler_params=vmem(LIMIT),
+        name="parameters",
+        cost_estimate=estimate(0.5),
+    )(*in_hbm([kernels.transpose(1, 0, 2), norm_gains, scales]))
+
+
+def choose_small(r):
+    first = r.sel[0] == 0
+    own, near = r.own_small[...], r.near_small[...]
+    r.small[0] = jnp.where(first, own, near)
+    r.small[1] = jnp.where(first, near, own)
+
+
+def conv_norm_kernel(choices, sel_ref, x_ref, *rest):
+    smalls, rest = rest[:choices], rest[choices:]
+    xhat_ref, normed_ref, inv_ref, pad_ref, conv_ref, small_ref = rest[-6:]
+    active = sel_ref[1] == 0
+
+    @pl.when(active)
+    def _():
+        zero_borders(pad_ref)
+        small_ref[...] = smalls[0][...]
+        for k in range(1, choices):
+
+            @pl.when(sel_ref[0] == k)
+            def _():
+                small_ref[...] = smalls[k][...]
+
+        conv_norm_body(x_ref, small_ref, xhat_ref, normed_ref, inv_ref, pad_ref, conv_ref)
+
+
+def conv_norm(sel, x, smalls, after=()):
     rows, cols, channels = x.shape
     n = rows * cols
     return pl.pallas_call(
-        conv_norm_kernel,
-        in_specs=[pl.BlockSpec(memory_space=pltpu.VMEM)] * 2 + [pl.BlockSpec(memory_space=pl.ANY)] * len(after),
+        functools.partial(conv_norm_kernel, len(smalls)),
+        in_specs=[pl.BlockSpec(memory_space=pltpu.SMEM)]
+        + [pl.BlockSpec(memory_space=pltpu.VMEM)] * (1 + len(smalls))
+        + [pl.BlockSpec(memory_space=pl.ANY)] * len(after),
         out_shape=(
             jax.ShapeDtypeStruct((n, channels), jnp.bfloat16),
             jax.ShapeDtypeStruct((n, channels), jnp.bfloat16),
             jax.ShapeDtypeStruct((n, LANES), jnp.float32),
         ),
-        scratch_shapes=[pad_shape(rows, cols, channels), pltpu.VMEM((rows, cols, channels), jnp.float32)],
+        scratch_shapes=[
+            pad_shape(rows, cols, channels),
+            pltpu.VMEM((rows, cols, channels), jnp.float32),
+            pltpu.VMEM(smalls[0].shape, jnp.float32),
+        ],
         compiler_params=vmem(LIMIT),
         name="conv_norm",
-        cost_estimate=estimate(2.6),
-    )(x, small, *after)
-
-
-def in_hbm(arrays):
-    return [pltpu.with_memory_space_constraint(a, pltpu.HBM) for a in arrays]
+        cost_estimate=estimate(2.0),
+    )(sel, x, *smalls, *after)
 
 
 def copy_chosen(which, sources, target, sem):
@@ -347,7 +406,7 @@
         in_specs=[pl.BlockSpec(memory_space=pltpu.SMEM)]
         + [pl.BlockSpec(memory_space=pltpu.VMEM)] * (used - 1)
         + [pl.BlockSpec(memory_space=pl.ANY)] * len(after),
-        out_shape=tuple(jax.ShapeDtypeStruct(*o) for o in outs),
+        out_shape=tuple(out_struct(*o) for o in outs),
         scratch_shapes=list(scratch),
         compiler_params=vmem(LIMIT),
         name=name,
@@ -403,6 +462,89 @@
             out_ref[h] = (g_ref[h].astype(jnp.float32) + map_ref[h]).astype(jnp.bfloat16)
     tk_ref[TAPS : TAPS + 2, :] = sums8_ref[0:2, :]
     tk_ref[TAPS + 2 :, :] = jnp.zeros((SMALL_ROWS - TAPS - 2, channels), jnp.float32)
+
+
+def conv_map_body(gconv_ref, g_ref, small_ref, out_ref, pad_ref, map_ref):
+    rows, cols, channels = g_ref.shape
+    tiles = channels // LANES
+    zero_borders(pad_ref)
+    for c in range(tiles):
+        pad_ref[c, :, 8 : cols + 8] = gconv_ref[:, c * LANES : (c + 1) * LANES].reshape(rows, cols, LANES)
+
+    def tile(c, carry):
+        lanes = pl.ds(pl.multiple_of(c * LANES, LANES), LANES)
+
+        def strip(w, carry):
+            base = pl.multiple_of(w * 8, 8)
+            window = pad_ref.at[c, :, pl.ds(base, 24), :]
+            acc = [None] * rows
+            for q in range(7):
+                col = [window[h, 11 - q : 19 - q, :] for h in range(rows)]
+                for r in range(7):
+                    weight = small_ref[r * 7 + q : r * 7 + q + 1, lanes]
+                    for h in range(max(0, r - 3), min(rows, rows + r - 3)):
+                        term = weight * col[h + 3 - r]
+                        acc[h] = term if acc[h] is None else acc[h] + term
+            for h in range(rows):
+                map_ref[h, pl.ds(base, 8), lanes] = acc[h]
+            return carry
+
+        return lax.fori_loop(0, cols // 8, strip, carry)
+
+    lax.fori_loop(0, tiles, tile, 0)
+    for h in range(rows):
+        out_ref[h] = (g_ref[h].astype(jnp.float32) + map_ref[h]).astype(jnp.bfloat16)
+
+
+def mlp_back_map_body(g_ref, branch_ref, pre_ref, xhat_ref, inv_ref, small_ref, w_in_ref, w_out_ref,
+                      sums8_ref, gconv_ref, gb_ref, nm_ref, hid_ref, gp_ref, acc_ref, ready):
+    rows, cols, channels = g_ref.shape
+    n = rows * cols
+    hidden = w_in_ref.shape[1]
+    step = 256
+    sub = 2 * cols
+    gain = small_ref[TAPS : TAPS + 1, :]
+    scale = small_ref[TAPS + 1 : TAPS + 2, :]
+    scale_sum = jnp.zeros((8, channels), jnp.float32)
+    for i in range(n // sub):
+        at = slice(i * sub, (i + 1) * sub)
+        g = g_ref[2 * i : 2 * i + 2].astype(jnp.float32).reshape(sub, channels)
+        scale_sum = scale_sum + jnp.sum((g * branch_ref[at, :].astype(jnp.float32)).reshape(sub // 8, 8, channels), axis=0)
+        gb_ref[at, :] = (g * scale).astype(jnp.bfloat16)
+        nm_ref[at, :] = (xhat_ref[at, :].astype(jnp.float32) * gain).astype(jnp.bfloat16)
+    ready("gb", "nm")
+    for j in range(hidden // step):
+        cut = slice(j * step, (j + 1) * step)
+        gh = lax.dot_general(gb_ref[...], w_out_ref[cut, :], (((1,), (1,)), ((), ())), preferred_element_type=jnp.float32)
+        for i in range(n // sub):
+            at = slice(i * sub, (i + 1) * sub)
+            p = pre_ref[at, cut].astype(jnp.float32)
+            sq = p * p
+            t = jnp.tanh(p * (GELU_C + (GELU_C * GELU_A) * sq))
+            cdf = 0.5 + 0.5 * t
+            hid_ref[at, cut] = (p * cdf).astype(jnp.bfloat16)
+            slope = cdf + (0.5 * p) * (1.0 - t * t) * (GELU_C + (3.0 * GELU_C * GELU_A) * sq)
+            gp_ref[at, cut] = (gh[at, :] * slope).astype(jnp.bfloat16)
+        part = lax.dot_general(gp_ref[:, cut], w_in_ref[:, cut], (((1,), (1,)), ((), ())), preferred_element_type=jnp.float32)
+        if j == 0:
+            acc_ref[...] = part
+        else:
+            acc_ref[...] += part
+    ready("hid", "gp")
+    gain_sum = jnp.zeros((8, channels), jnp.float32)
+    for i in range(n // sub):
+        at = slice(i * sub, (i + 1) * sub)
+        gn = acc_ref[at, :]
+        xhat = xhat_ref[at, :].astype(jnp.float32)
+        gain_sum = gain_sum + jnp.sum((gn * xhat).reshape(sub // 8, 8, channels), axis=0)
+        gx = gn * gain
+        m1 = jnp.mean(gx, axis=1, keepdims=True)
+        m2 = jnp.mean(gx * xhat, axis=1, keepdims=True)
+        gconv_ref[at, :] = inv_ref[at, 0:1] * (gx - m1 - xhat * m2)
+    sums8_ref[0:1, :] = jnp.sum(gain_sum, axis=0, keepdims=True)
+    sums8_ref[1:2, :] = jnp.sum(scale_sum, axis=0, keepdims=True)
+    sums8_ref[2:8, :] = jnp.zeros((6, channels), jnp.float32)
+    ready("gconv", "sums")
 
 
 def mlp_back_body(first, g_ref, branch_ref, pre_ref, xhat_ref, inv_ref, small_ref, wait_in, wait_out, w_in_ref, w_out_ref,
@@ -442,8 +584,10 @@
         t_keep = jnp.where(first, t_in, t_out)
         t_send = jnp.where(first, t_out, t_in)
         if before is not None:
-            t_keep = t_keep + before[0][:, cut].astype(jnp.float32)
-            t_send = t_send + before[1][:, cut].astype(jnp.float32)
+            if j == 0:
+                old_keep, old_send = before()
+            t_keep = t_keep + old_keep[:, cut].astype(jnp.float32)
+            t_send = t_send + old_send[:, cut].astype(jnp.float32)
         keep_ref[:, cut] = t_keep.astype(jnp.bfloat16)
         send_ref[:, cut] = t_send.astype(jnp.bfloat16)
         part = lax.dot_general(gp_ref[...], w_in_ref[:, cut], (((1,), (1,)), ((), ())), preferred_element_type=jnp.float32)
@@ -466,6 +610,10 @@
     sums8_ref[2:8, :] = jnp.zeros((6, channels), jnp.float32)
 
 
+def out_struct(shape, dtype, by_hand=False):
+    return pltpu.HBM(shape, dtype) if by_hand else jax.ShapeDtypeStruct(shape, dtype)
+
+
 def named_call(name, body, ins, outs, scratch, cost):
     names = list(ins) + list(outs) + list(scratch)
     spaces = {"v": pltpu.VMEM, "s": pltpu.SMEM, "a": pl.ANY, "h": pl.ANY}
@@ -477,7 +625,8 @@
     result = pl.pallas_call(
         kernel,
         in_specs=[pl.BlockSpec(memory_space=spaces[kind]) for _, kind in ins.values()],
-        out_shape=tuple(jax.ShapeDtypeStruct(*o) for o in outs.values()),
+        out_specs=tuple(pl.BlockSpec(memory_space=pl.ANY if len(o) > 2 else pltpu.VMEM) for o in outs.values()),
+        out_shape=tuple(out_struct(*o) for o in outs.values()),
         scratch_shapes=list(scratch.values()),
         compiler_params=vmem(LIMIT),
         name=name,
@@ -520,6 +669,14 @@
             y_ref[2 * i : 2 * i + 2] = (old + scale * branch).astype(jnp.bfloat16).reshape(2, cols, channels)
 
 
+def small_ins(pair):
+    return {"own_small": (pair[0], "v"), "near_small": (pair[1], "v")}
+
+
+def small_scratch(pair):
+    return {"small": pltpu.VMEM((2,) + pair[0].shape, jnp.float32)}
+
+
 def weight_ins(pair):
     return {k: (v, "h") for k, v in zip(("own_in", "near_in", "own_out", "near_out"), pair)}
 
@@ -545,23 +702,26 @@
     bf16, f32 = jnp.bfloat16, jnp.float32
 
     def body(r):
-        low, high = start_weights(r, 0, 0), start_weights(r, 1, 1)
-        zero_borders(r.pad)
-        mlp_body(r.normed0, *low, r.w_in.at[0], r.w_out.at[0], r.pre0, r.hid, r.acc)
-        residual_body(r.x, r.small.at[0], r.acc, r.branch0, r.x1)
-        conv_norm_body(r.x1, r.small.at[1], r.xhat1, r.normed, r.inv1, r.pad, r.conv)
-        mlp_body(r.normed, *high, r.w_in.at[1], r.w_out.at[1], r.pre1, r.hid, r.acc)
-        residual_body(r.x1, r.small.at[1], r.acc, r.branch1, r.y)
+        @pl.when(r.sel[4] == 0)
+        def _():
+            low, high = start_weights(r, 0, 0), start_weights(r, 1, 1)
+            choose_small(r)
+            zero_borders(r.pad)
+            mlp_body(r.normed0, *low, r.w_in.at[0], r.w_out.at[0], r.pre0, r.hid, r.acc)
+            residual_body(r.x, r.small.at[0], r.acc, r.branch0, r.x1)
+            conv_norm_body(r.x1, r.small.at[1], r.xhat1, r.normed, r.inv1, r.pad, r.conv)
+            mlp_body(r.normed, *high, r.w_in.at[1], r.w_out.at[1], r.pre1, r.hid, r.acc)
+            residual_body(r.x1, r.small.at[1], r.acc, r.branch1, r.y)
 
     return named_call(
         "pair_forward", body,
-        {"sel": (sel, "s"), "x": (x, "v"), "normed0": (first[1], "v"), "small": (small, "v"), **weight_ins(weights)},
+        {"sel": (sel, "s"), "x": (x, "v"), "normed0": (first[1], "v"), **small_ins(small), **weight_ins(weights)},
         {"y": (x.shape, bf16), "x1": (x.shape, bf16), "xhat1": ((n, channels), bf16), "inv1": ((n, LANES), f32),
          "pre0": ((n, hidden), bf16), "pre1": ((n, hidden), bf16),
          "branch0": ((n, channels), bf16), "branch1": ((n, channels), bf16)},
         {"normed": pltpu.VMEM((n, channels), bf16), "hid": pltpu.VMEM((n, 256), bf16), "acc": pltpu.VMEM((n, channels), f32),
          "pad": pad_shape(rows, cols, channels), "conv": pltpu.VMEM((rows, cols, channels), f32),
-         **weight_scratch(2, channels, hidden)},
+         **weight_scratch(2, channels, hidden), **small_scratch(small)},
         7.5,
     )
 
@@ -577,213 +737,223 @@
 
 
 GRADS = ("keep0", "send0", "keep1", "send1")
-
-
-def pair_both(sel, x, g, small, weights, before=None):
+FACTORS = ("gb", "nm", "hid", "gp", "gconv", "sums")
+
+
+def factor_shapes(n, channels, hidden):
+    bf16, f32 = jnp.bfloat16, jnp.float32
+    one = {"gb": ((n, channels), bf16), "nm": ((n, channels), bf16), "hid": ((n, hidden), bf16), "gp": ((n, hidden), bf16),
+           "gconv": ((n, channels), f32), "sums": ((8, channels), f32)}
+    return {name + str(k): one[name] for k in (0, 1) for name in FACTORS}
+
+
+def pair_map(sel, x, g, small, weights):
     rows, cols, channels = x.shape
     n, hidden = rows * cols, weights[0].shape[1]
     bf16, f32 = jnp.bfloat16, jnp.float32
+    shapes = factor_shapes(n, channels, hidden)
+    saved = {**shapes, "x1": (x.shape, bf16)}
+    order = list(saved)
 
     def body(r):
         @pl.when(r.sel[2] == 1)
         def _():
-            core = r.sel[3] == 0
+            def copy_out(name):
+                return pltpu.make_async_copy(getattr(r, "v_" + name), getattr(r, name), r.s_sem.at[order.index(name)])
+
             low, high = start_weights(r, 0, 0), start_weights(r, 1, 1)
-            waits = []
-            if before is not None:
-                for k, name in enumerate(GRADS):
-                    copy = pltpu.make_async_copy(getattr(r, "old_" + name), r.olds.at[k], r.o_sem.at[k])
-                    copy.start()
-                    waits.append(copy.wait)
+            choose_small(r)
             zero_borders(r.pad)
             s0, s1 = r.small.at[0], r.small.at[1]
             conv_norm_body(r.x, s0, r.xhat0, r.normed, r.inv0, r.pad, r.conv)
             mlp_body(r.normed, *low, r.w_in.at[0], r.w_out.at[0], r.pre0, r.hid, r.acc)
-            residual_body(r.x, s0, r.acc, r.branch0, r.x1)
-            conv_norm_body(r.x1, s1, r.xhat1, r.normed, r.inv1, r.pad, r.conv)
+            residual_body(r.x, s0, r.acc, r.branch0, r.v_x1)
+            copy_out("x1").start()
+            conv_norm_body(r.v_x1, s1, r.xhat1, r.normed, r.inv1, r.pad, r.conv)
             mlp_body(r.normed, *high, r.w_in.at[1], r.w_out.at[1], r.pre1, r.hid, r.acc)
-            residual_body(r.x1, s1, r.acc, r.branch1, None)
-            for wait in waits:
-                wait()
-            done = (lambda: None,) * 2
-            mlp_back_body(core, r.g, r.branch1, r.pre1, r.xhat1, r.inv1, s1, *done, r.w_in.at[1], r.w_out.at[1],
-                          r.keep1, r.send1, r.sums8, r.gconv, *back_temps(r),
-                          before=None if before is None else (r.olds.at[2], r.olds.at[3]))
-            conv_back_body(r.gconv, r.x1, r.g, s1, r.sums8, r.g1, r.small1, r.pad, r.sum, r.wide, r.map)
-            mlp_back_body(core, r.g1, r.branch0, r.pre0, r.xhat0, r.inv0, s0, *done, r.w_in.at[0], r.w_out.at[0],
-                          r.keep0, r.send0, r.sums8, r.gconv, *back_temps(r),
-                          before=None if before is None else (r.olds.at[0], r.olds.at[1]))
-            conv_back_body(r.gconv, r.x, r.g1, s0, r.sums8, r.g0, r.small0, r.pad, r.sum, r.wide, r.map)
-            if before is not None:
-                r.small0[...] += r.old_small0[...]
-                r.small1[...] += r.old_small1[...]
-
-    ins = {"sel": (sel, "s"), "x": (x, "v"), "g": (g, "v"), "small": (small, "v"), **weight_ins(weights)}
-    scratch = {}
-    if before is not None:
-        ins.update({"old_" + name: (getattr(before, name), "a") for name in GRADS})
-        ins.update({"old_" + name: (getattr(before, name), "v") for name in ("small0", "small1")})
-        scratch = {"olds": pltpu.VMEM((4, channels, hidden), bf16), "o_sem": pltpu.SemaphoreType.DMA((4,))}
-    grad = ((channels, hidden), bf16)
-    small_out = ((SMALL_ROWS, channels), f32)
+            residual_body(r.v_x1, s1, r.acc, r.branch1, None)
+
+            def ready(k):
+                def start(*names):
+                    for name in names:
+                        copy_out(name + str(k)).start()
+
+                return start
+
+            mlp_back_map_body(r.g, r.branch1, r.pre1, r.xhat1, r.inv1, s1, r.w_in.at[1], r.w_out.at[1],
+                              r.v_sums1, r.v_gconv1, r.v_gb1, r.v_nm1, r.v_hid1, r.v_gp1, r.acc, ready(1))
+            conv_map_body(r.v_gconv1, r.g, s1, r.g1, r.pad, r.conv)
+            mlp_back_map_body(r.g1, r.branch0, r.pre0, r.xhat0, r.inv0, s0, r.w_in.at[0], r.w_out.at[0],
+                              r.v_sums0, r.v_gconv0, r.v_gb0, r.v_nm0, r.v_hid0, r.v_gp0, r.acc, ready(0))
+            conv_map_body(r.v_gconv0, r.g1, s0, r.g0, r.pad, r.conv)
+            for name in order:
+                copy_out(name).wait()
+
     return named_call(
-        "pair_both", body, ins,
-        {"g0": (x.shape, bf16), "keep0": grad, "send0": grad, "keep1": grad, "send1": grad,
-         "small0": small_out, "small1": small_out},
-        {"x1": pltpu.VMEM(x.shape, bf16), "g1": pltpu.VMEM(x.shape, bf16),
+        "pair_map", body,
+        {"sel": (sel, "s"), "x": (x, "v"), "g": (g, "v"), **small_ins(small), **weight_ins(weights)},
+        {"g0": (x.shape, bf16), **{name: shape + (True,) for name, shape in saved.items()}},
+        {**{"v_" + name: pltpu.VMEM(*shape) for name, shape in saved.items()},
+         "s_sem": pltpu.SemaphoreType.DMA((len(order),)),
+         "g1": pltpu.VMEM(x.shape, bf16),
          "xhat0": pltpu.VMEM((n, channels), bf16), "xhat1": pltpu.VMEM((n, channels), bf16),
          "inv0": pltpu.VMEM((n, LANES), f32), "inv1": pltpu.VMEM((n, LANES), f32),
          "pre0": pltpu.VMEM((n, hidden), bf16), "pre1": pltpu.VMEM((n, hidden), bf16),
          "branch0": pltpu.VMEM((n, channels), bf16), "branch1": pltpu.VMEM((n, channels), bf16),
-         "normed": pltpu.VMEM((n, channels), bf16), "gconv": pltpu.VMEM((n, channels), f32),
-         "sums8": pltpu.VMEM((8, channels), f32),
+         "normed": pltpu.VMEM((n, channels), bf16), "hid": pltpu.VMEM((n, 256), bf16), "acc": pltpu.VMEM((n, channels), f32),
          "pad": pad_shape(rows, cols, channels), "conv": pltpu.VMEM((rows, cols, channels), f32),
-         "sum": pltpu.VMEM((cols // 8, TAPS, 8, LANES), f32),
-         "wide": pltpu.VMEM(x.shape, f32), "map": pltpu.VMEM(x.shape, f32),
-         **back_scratch(n, channels), **weight_scratch(2, channels, hidden), **scratch},
-        17,
+         **weight_scratch(2, channels, hidden), **small_scratch(small)},
+        12,
     )
 
 
-def start_olds(r):
-    return [copy_chosen(r.sel[2], (getattr(r, "a_" + name), getattr(r, "p_" + name)), r.olds.at[k], r.o_sem.at[k])
-            for k, name in enumerate(("keep", "send"))]
-
-
-def old_ins(before, block):
-    ins = {}
-    for prefix, part in zip("ap", before):
-        for name in ("keep", "send"):
-            ins[prefix + "_" + name] = (getattr(part, name + str(block)), "a")
-    return ins
-
-
-def pair_back_high(sel, g, kept, small, weights, before=None, after=()):
+def pair_grads(sel, xs, parts):
+    rows, cols, channels = xs[0].shape
+    n, hidden = rows * cols, parts[0].hid0.shape[1]
+    bf16, f32 = jnp.bfloat16, jnp.float32
+    shapes = factor_shapes(n, channels, hidden)
+    order = list(shapes) + ["x1"]
+
+    def body(r):
+        @pl.when(r.sel[2] == 1)
+        def _():
+            def copy_out(k):
+                return pltpu.make_async_copy(r.grads.at[k], getattr(r, GRADS[k]), r.o_sem.at[k])
+
+            copies = {}
+            for k in (1, 0):
+                for name in FACTORS + (("x1",) if k else ()):
+                    full = name + str(k) if name != "x1" else name
+                    for i in range(2):
+                        copies[full, i] = pltpu.make_async_copy(
+                            getattr(r, "i%d_%s" % (i, full)), getattr(r, "v_" + full).at[i], r.s_sem.at[i, order.index(full)]
+                        )
+                        copies[full, i].start()
+            first = r.sel[3] == 0
+            for k in (1, 0):
+                gb, nm, hid, gp = (getattr(r, "v_%s%d" % (name, k)) for name in FACTORS[:4])
+                keep, send = r.grads.at[2 * k], r.grads.at[2 * k + 1]
+                for name in FACTORS + (("x1",) if k else ()):
+                    for i in range(2):
+                        copies[name + str(k) if name != "x1" else name, i].wait()
+                gb_t = gb[...].reshape(2 * n, channels).T
+                nm_t = nm[...].reshape(2 * n, channels).T
+                for j in range(hidden // 256):
+                    cut = slice(j * 256, (j + 1) * 256)
+                    t_out = jnp.dot(gb_t, hid[:, :, cut].reshape(2 * n, 256), preferred_element_type=f32)
+                    t_in = jnp.dot(nm_t, gp[:, :, cut].reshape(2 * n, 256), preferred_element_type=f32)
+                    keep[:, cut] = jnp.where(first, t_in, t_out).astype(bf16)
+                    send[:, cut] = jnp.where(first, t_out, t_in).astype(bf16)
+                copy_out(2 * k).start()
+                copy_out(2 * k + 1).start()
+                out = getattr(r, "small%d" % k)
+                for i in range(2):
+                    x = r.v_x1.at[i] if k else getattr(r, "x_%d" % i)
+                    gconv, sums = getattr(r, "v_gconv%d" % k).at[i], getattr(r, "v_sums%d" % k).at[i]
+                    target = out if i == 0 else r.tk
+                    conv_back_body(gconv, x, None, None, sums, None, target, r.pad, r.sum, r.wide, None)
+                out[...] += r.tk[...]
+            for k in range(4):
+                copy_out(k).wait()
+
+    ins = {"sel": (sel, "s")}
+    for i in range(2):
+        ins["x_%d" % i] = (xs[i], "v")
+        ins.update({"i%d_%s" % (i, name): (getattr(parts[i], name), "h") for name in order})
+    grad = ((channels, hidden), bf16)
+    small_out = ((SMALL_ROWS, channels), f32)
+    scratch = {"v_" + name: pltpu.VMEM((2,) + shape, dtype) for name, (shape, dtype) in shapes.items()}
+    return named_call(
+        "pair_grads", body, ins,
+        {**{name: grad + (True,) for name in GRADS}, "small0": small_out, "small1": small_out},
+        {**scratch, "grads": pltpu.VMEM((4, channels, hidden), bf16), "o_sem": pltpu.SemaphoreType.DMA((4,)), "v_x1": pltpu.VMEM((2,) + xs[0].shape, bf16), "s_sem": pltpu.SemaphoreType.DMA((2, len(order))),
+         "pad": pad_shape(rows, cols, channels), "sum": pltpu.VMEM((cols // 8, TAPS, 8, LANES), f32),
+         "wide": pltpu.VMEM(xs[0].shape, f32), "tk": pltpu.VMEM((SMALL_ROWS, channels), f32)},
+        10,
+    )
+
+
+def pair_back(sel, g, x, first, kept, small, weights, before=None, after=()):
     rows, cols, channels = g.shape
     n, hidden = rows * cols, weights[0].shape[1]
     bf16, f32 = jnp.bfloat16, jnp.float32
 
     def body(r):
-        waits = [] if before is None else start_olds(r)
+        def copy_old(k):
+            return copy_chosen(r.sel[2], (getattr(r, "a_" + GRADS[k]), getattr(r, "p_" + GRADS[k])), r.olds.at[k], r.o_sem.at[k])
+
+        def copy_out(k, source):
+            return pltpu.make_async_copy(source, getattr(r, GRADS[k]), r.s_sem.at[k])
 
         @pl.when(r.sel[2] == 0)
         def _():
-            high = start_weights(r, 0, 1)
-            for wait in waits:
-                wait()
-            mlp_back_body(r.sel[3] == 0, r.g, r.branch1, r.pre1, r.xhat1, r.inv1, r.small.at[1], *high,
-                          r.w_in.at[0], r.w_out.at[0], r.keep, r.send, r.sums8, r.gconv, *back_temps(r),
-                          before=None if before is None else (r.olds.at[0], r.olds.at[1]))
+            core = r.sel[3] == 0
+            high, low = start_weights(r, 1, 1), start_weights(r, 0, 0)
+            waits = {}
+            if before is not None:
+                waits = {k: copy_old(k) for k in (2, 3, 0, 1)}
+            choose_small(r)
+            s0, s1 = r.small.at[0], r.small.at[1]
+
+            def old(k):
+                def both():
+                    waits[2 * k]()
+                    waits[2 * k + 1]()
+                    return r.olds.at[2 * k], r.olds.at[2 * k + 1]
+
+                return both if waits else None
+
+            mlp_back_body(core, r.g, r.branch1, r.pre1, r.xhat1, r.inv1, s1, *high, r.w_in.at[1], r.w_out.at[1],
+                          r.grads.at[2], r.grads.at[3], r.sums8, r.gconv, *back_temps(r), before=old(1))
+            copy_out(2, r.grads.at[2]).start()
+            copy_out(3, r.grads.at[3]).start()
+            conv_back_body(r.gconv, r.x1, r.g, s1, r.sums8, r.g1, r.small1, r.pad, r.sum, r.wide, r.map)
+            mlp_back_body(core, r.g1, r.branch0, r.pre0, r.xhat0, r.inv0, s0, *low, r.w_in.at[0], r.w_out.at[0],
+                          r.grads.at[0], r.grads.at[1], r.sums8, r.gconv, *back_temps(r), before=old(0))
+            copy_out(0, r.grads.at[0]).start()
+            copy_out(1, r.grads.at[1]).start()
+            conv_back_body(r.gconv, r.x, None, None, r.sums8, None, r.small0, r.pad, r.sum, r.wide, None)
+            if before is not None:
+                r.small0[...] += r.a_small0[...]
+                r.small1[...] += r.a_small1[...]
+                r.packed[...] = jnp.concatenate([r.small0[...], r.small1[...]], axis=0).T.astype(bf16)
+            for k in range(4):
+                copy_out(k, r.grads.at[k]).wait()
 
         if before is not None:
 
             @pl.when(r.sel[2] == 1)
             def _():
-                for wait in waits:
+                waits = [copy_old(k) for k in range(4)]
+                r.packed[...] = jnp.concatenate([r.p_small0[...], r.p_small1[...]], axis=0).T.astype(bf16)
+                for k, wait in enumerate(waits):
                     wait()
-                r.keep[...] = r.olds[0]
-                r.send[...] = r.olds[1]
-
-    ins = {"sel": (sel, "s"), "g": (g, "v"), "branch1": (kept.branch1, "v"), "pre1": (kept.pre1, "v"),
-           "xhat1": (kept.xhat1, "v"), "inv1": (kept.inv1, "v"), "small": (small, "v"), **weight_ins(weights)}
-    scratch = {}
-    if before is not None:
-        ins.update(old_ins(before, 1))
-        ins.update({"after%d" % k: (v, "a") for k, v in enumerate(after)})
-        scratch = {"olds": pltpu.VMEM((2, channels, hidden), bf16), "o_sem": pltpu.SemaphoreType.DMA((2,))}
-    return named_call(
-        "pair_back_high", body, ins,
-        {"keep": ((channels, hidden), bf16), "send": ((channels, hidden), bf16), "sums8": ((8, channels), f32),
-         "gconv": ((n, channels), f32)},
-        {**back_scratch(n, channels), **weight_scratch(1, channels, hidden), **scratch},
-        2.5,
-    )
-
-
-def pair_back_low(sel, g, high, x, x1, first, kept, small, weights, before=None, after=()):
-    rows, cols, channels = g.shape
-    n, hidden = rows * cols, weights[0].shape[1]
-    bf16, f32 = jnp.bfloat16, jnp.float32
-
-    def body(r):
-        waits = [] if before is None else start_olds(r)
-
-        @pl.when(r.sel[2] == 0)
-        def _():
-            low = start_weights(r, 0, 0)
-            conv_back_body(r.gconv1, r.x1, r.g, r.small.at[1], r.sums1, r.g1, r.small1, r.pad, r.sum, r.wide, r.map)
-            if before is not None:
-                r.small1[...] += r.a_small1[...]
-            for wait in waits:
-                wait()
-            mlp_back_body(r.sel[3] == 0, r.g1, r.branch0, r.pre0, r.xhat0, r.inv0, r.small.at[0], *low,
-                          r.w_in.at[0], r.w_out.at[0], r.keep, r.send, r.sums8, r.gconv, *back_temps(r),
-                          before=None if before is None else (r.olds.at[0], r.olds.at[1]))
-
-        if before is not None:
-
-            @pl.when(r.sel[2] == 1)
-            def _():
-                for wait in waits:
-                    wait()
-                r.keep[...] = r.olds[0]
-                r.send[...] = r.olds[1]
-                r.small1[...] = r.p_small1[...]
-
-    ins = {"sel": (sel, "s"), "g": (g, "v"), "gconv1": (high.gconv, "v"), "sums1": (high.sums8, "v"), "x1": (x1, "v"),
+                    copy_out(k, r.olds.at[k]).start()
+                for k in range(4):
+                    copy_out(k, r.olds.at[k]).wait()
+
+    ins = {"sel": (sel, "s"), "g": (g, "v"), "x": (x, "v"), "x1": (kept.x1, "v"),
+           "branch1": (kept.branch1, "v"), "pre1": (kept.pre1, "v"), "xhat1": (kept.xhat1, "v"), "inv1": (kept.inv1, "v"),
            "branch0": (kept.branch0, "v"), "pre0": (kept.pre0, "v"), "xhat0": (first[0], "v"), "inv0": (first[2], "v"),
-           "small": (small, "v"), **weight_ins(weights)}
-    scratch = {}
-    if before is not None:
-        ins.update(old_ins(before, 0))
-        ins.update({"a_small1": (before[0].small1, "v"), "p_small1": (before[1].small1, "v")})
-        scratch = {"olds": pltpu.VMEM((2, channels, hidden), bf16), "o_sem": pltpu.SemaphoreType.DMA((2,))}
+           **small_ins(small), **weight_ins(weights)}
+    grad = ((channels, hidden), bf16)
+    small_out = ((SMALL_ROWS, channels), f32)
+    outs = {name: grad + (True,) for name in GRADS}
+    scratch = {"grads": pltpu.VMEM((4, channels, hidden), bf16), "s_sem": pltpu.SemaphoreType.DMA((4,)), "g1": pltpu.VMEM(g.shape, bf16), "sums8": pltpu.VMEM((8, channels), f32), "gconv": pltpu.VMEM((n, channels), f32),
+               "pad": pad_shape(rows, cols, channels), "sum": pltpu.VMEM((cols // 8, TAPS, 8, LANES), f32),
+               "wide": pltpu.VMEM(x.shape, f32), "map": pltpu.VMEM(x.shape, f32),
+               **back_scratch(n, channels), **weight_scratch(2, channels, hidden), **small_scratch(small)}
+    if before is None:
+        outs.update({"small0": small_out, "small1": small_out})
+    else:
+        for prefix, part in zip("ap", before):
+            ins.update({prefix + "_" + name: (getattr(part, name), "h") for name in GRADS})
+            ins.update({prefix + "_" + name: (getattr(part, name), "v") for name in ("small0", "small1")})
+        outs["packed"] = ((channels, 2 * SMALL_ROWS), bf16)
+        scratch.update({"small0": pltpu.VMEM(*small_out), "small1": pltpu.VMEM(*small_out),
+                        "olds": pltpu.VMEM((4, channels, hidden), bf16), "o_sem": pltpu.SemaphoreType.DMA((4,))})
     ins.update({"after%d" % k: (v, "a") for k, v in enumerate(after)})
-    return named_call(
-        "pair_back_low", body, ins,
-        {"small1": ((SMALL_ROWS, channels), f32), "keep": ((channels, hidden), bf16), "send": ((channels, hidden), bf16),
-         "sums8": ((8, channels), f32), "gconv": ((n, channels), f32)},
-        {"g1": pltpu.VMEM(g.shape, bf16), "pad": pad_shape(rows, cols, channels), "sum": pltpu.VMEM((cols // 8, TAPS, 8, LANES), f32),
-         "wide": pltpu.VMEM(x.shape, f32), "map": pltpu.VMEM(x.shape, f32),
-         **back_scratch(n, channels), **weight_scratch(1, channels, hidden), **scratch},
-        5.5,
-    )
-
-
-def pair_back_conv(sel, low, x, before=None, after=()):
-    rows, cols, channels = x.shape
-
-    def body(r):
-        @pl.when(r.sel[2] == 0)
-        def _():
-            conv_back_body(r.gconv, r.x, None, None, r.sums8, None, r.small0, r.pad, r.sum, r.wide, r.map)
-            if before is not None:
-                r.small0[...] += r.a_small0[...]
-
-        if before is not None:
-
-            @pl.when(r.sel[2] == 1)
-            def _():
-                r.small0[...] = r.p_small0[...]
-
-    ins = {"sel": (sel, "s"), "gconv": (low.gconv, "v"), "sums8": (low.sums8, "v"), "x": (x, "v")}
-    if before is not None:
-        ins.update({"a_small0": (before[0].small0, "v"), "p_small0": (before[1].small0, "v")})
-    ins.update({"after%d" % k: (v, "a") for k, v in enumerate(after)})
-    return named_call(
-        "pair_back_conv", body, ins, {"small0": ((SMALL_ROWS, channels), jnp.float32)},
-        {"pad": pad_shape(rows, cols, channels), "sum": pltpu.VMEM((cols // 8, TAPS, 8, LANES), jnp.float32),
-         "wide": pltpu.VMEM(x.shape, jnp.float32), "map": pltpu.VMEM(x.shape, jnp.float32)},
-        1.6,
-    ).small0
-
-
-def pack_kernel(sel_ref, s0_ref, s1_ref, out_ref):
-    out_ref[...] = jnp.concatenate([s0_ref[...], s1_ref[...]], axis=0).T.astype(jnp.bfloat16)
-
-
-def pack(core, smalls):
-    return small_call(pack_kernel, "pack", (((smalls[0].shape[1], 2 * SMALL_ROWS), jnp.bfloat16),), core, *smalls)[0]
+    return named_call("pair_back", body, ins, outs, scratch, 9)
 
 
 def add(a, b):
@@ -890,12 +1060,6 @@
     return smalls
 
 
-def small_parameters(kernels, norm_gains, scales):
-    taps = kernels.shape[1]
-    fill = jnp.zeros((56 - taps - 2, kernels.shape[2]), F32)
-    return jnp.concatenate([kernels[0], norm_gains, scales, fill], axis=0)
-
-
 def finish(t_kernel, t_gain, t_scale, t_in, t_out):
     return t_kernel[None], t_gain[None], t_in[None], t_out[None], t_scale[None]
 
@@ -905,7 +1069,7 @@
     rank = lax.axis_index("segment")
     count = images.shape[0] // segments
     taps = kernels.shape[1]
-    small = lax.all_gather(small_parameters(kernels, norm_gains, scales), "segment")
+    small = lax.all_gather(parameters(kernels, norm_gains, scales), "segment")
     all_in = lax.all_gather(w_in[0], "segment")
     all_out = lax.all_gather(w_out[0], "segment")
     sels = [jnp.array([s, 0], jnp.int32) for s in range(segments)]
@@ -928,7 +1092,7 @@
     for i in range(count):
         x = lax.dynamic_index_in_dim(images, rank * count + i, 0, keepdims=False)
         g = lax.dynamic_index_in_dim(cotangent, rank * count + i, 0, keepdims=False)
-        smalls = one_image(x, g, small, sels, w_ins, w_outs, conv_norm(x, small[0]), sums)
+        smalls = one_image(x, g, small, sels, w_ins, w_outs, conv_norm(sels[0] * 0, x, [small[0]]), sums)
         for s in range(segments):
             sums.add(s, 2, smalls[s])
 
@@ -966,12 +1130,15 @@
     chip = rank // 2
     depth = lax.axis_index("dp") // 2
     side = lax.axis_index("dp") % 2
-    own_small = small_parameters(kernels, norm_gains, scales)
+    own_small = parameters(kernels, norm_gains, scales)
     near_small = swap(own_small, c=1)
     near_in, near_out = swap(w_in[0], c=1), swap(w_out[0], c=1)
-    small = jnp.where(core == 0, jnp.stack([own_small, near_small]), jnp.stack([near_small, own_small]))
+    small = (own_small, near_small)
     weights = (w_in[0], near_in, w_out[0], near_out)
-    sel = jnp.stack([core, 1 - core, chip, core]).astype(jnp.int32)
+    zero = jnp.zeros_like(chip)
+    sel = jnp.stack([core, 1 - core, chip, core, zero]).astype(jnp.int32)
+    sel_first = jnp.stack([core, 1 - core, chip, core, chip]).astype(jnp.int32)
+    sel_conv = (jnp.stack([core, zero]).astype(jnp.int32), jnp.stack([core, chip]).astype(jnp.int32))
     cores = core[None].astype(jnp.int32)
     sides = side[None].astype(jnp.int32)
     levels = jnp.stack([depth, depth ^ 1, depth ^ 2, depth ^ 3]).astype(jnp.int32)
@@ -979,26 +1146,18 @@
     maps = [lax.dynamic_index_in_dim(images, 2 * core + i, 0, keepdims=False) for i in range(2)]
     ends = [lax.dynamic_index_in_dim(cotangent, 2 * core + i, 0, keepdims=False) for i in range(2)]
     firsts, kept = [], []
-    for x in maps:
-        firsts.append(conv_norm(x, small[0], tuple(k.inv1 for k in kept)))
-        kept.append(pair_forward(sel, x, firsts[-1], small, weights))
+    for x, chosen in zip(maps, sel_conv):
+        firsts.append(conv_norm(chosen, x, small, tuple(k.inv1 for k in kept)))
+        kept.append(pair_forward(sel_first if kept else sel, x, firsts[-1], small, weights))
     passed = [along_x(k.y, True) for k in kept]
-    both = pair_both(sel, passed[0], ends[0], small, weights)
-    g_first = along_x(both.g0, False)
-    both = pair_both(sel, passed[1], ends[1], small, weights, both)
-    g_second = along_x(both.g0, False)
-
-    def back(i, g, before):
-        high = pair_back_high(sel, g, kept[i], small, weights, before, (before[0].small0,) if before else ())
-        high_core = swap(high.send, c=1) if before else None
-        low = pair_back_low(sel, g, high, maps[i], kept[i].x1, firsts[i], kept[i], small, weights, before)
-        low_core = swap(low.send, c=1) if before else None
-        small0 = pair_back_conv(sel, low, maps[i], before)
-        return types.SimpleNamespace(keep0=low.keep, send0=low.send, keep1=high.keep, send1=high.send,
-                                     small0=small0, small1=low.small1, core0=low_core, core1=high_core)
-
-    grads = back(0, g_first, None)
-    grads = back(1, g_second, (grads, both))
+    parts, starts = [], []
+    for x, g in zip(passed, ends):
+        parts.append(pair_map(sel, x, g, small, weights))
+        starts.append(along_x(parts[-1].g0, False))
+    totals = pair_grads(sel, passed, parts)
+    grads = pair_back(sel, starts[0], maps[0], firsts[0], kept[0], small, weights)
+    grads = pair_back(sel, starts[1], maps[1], firsts[1], kept[1], small, weights, (grads, totals))
+    core1, core0 = swap(grads.send1, c=1), swap(grads.send0, c=1)
 
     def along_y(*pairs):
         across, mine = to_side(sides, *pairs)
@@ -1008,8 +1167,8 @@
         own, *others = to_depths(levels, mine, got)
         return [own] + [swap(v, z=flip) for v, flip in zip(others, (1, 2, 3))]
 
-    high = along_y(grads.keep1, grads.core1)
-    low = along_y(grads.keep0, grads.core0, pack(cores, (grads.small0, grads.small1)))
+    high = along_y(grads.keep1, core1)
+    low = along_y(grads.keep0, core0, grads.packed)
     high = along_z(*high)
     low = along_z(*low)
     own, send = to_core(cores, low + high)

time: 119 us -> 102 us (0.86)
  waiting for transfers between devices: 46 us -> 34.6 us
  local copies, waits for them, and re-layouts: 6.52 us -> 2.18 us
  other arithmetic: 1.72 us -> 0.23 us
    ppermute x4, waiting for transfers between devices: 25.4 us -> 13 us  [along_x(): return lax.ppermute(value, ('dp', 'segment'), pairs)]
    unnamed x17 -> x14, local copies, waits for them, and re-layouts: 5.32 us -> 1.92 us
    pallas_call x10 -> x7, Pallas kernels: 34.4 us -> 32.7 us  [named_call(): pl.pallas_call(kernel, in_specs=[pl.BlockSpec(memory_space=spaces[kind])...]
    pallas_call x2 -> x3, Pallas kernels: 4.24 us -> 5.44 us  [the longest x2 4.37 us: conv_norm(): pl.pallas_call(functools.partial(conv_norm_kernel, len(smalls)), in_specs...]
    pallas_call x7 -> x6, Pallas kernels: 2.52 us -> 2.39 us  [small_call(): pl.pallas_call(body, in_specs=[pl.BlockSpec(memory_space=pltpu.SMEM)] + [...]
  transfers between devices with their start and end apart: 18 -> 18, of which waited for: 7 -> 8; matrix products, arithmetic and copies ran while one was open for 2% -> 0% of each run, Pallas kernels for 26% -> 23%
where the time goes in v3:
time: 102 us; the launch traced here: 101 us
  Pallas kernels  40.6 us (40%)
  waiting for transfers between devices  34.6 us (34%)
  starting transfers between devices  22.8 us (22%)
  local copies, waits for them, and re-layouts  2.18 us (2%)
    pallas_call x7, Pallas kernels, named_call(): pl.pallas_call(kernel, in_specs=[pl.BlockSpec(memory_space=spaces[kind])...  32.7 us
    ppermute x14, waiting for transfers between devices, swap(): return lax.ppermute(value, ('dp', 'segment'), partners((z, y, x, c)))  21.6 us
    ppermute x14, starting transfers between devices, swap(): return lax.ppermute(value, ('dp', 'segment'), partners((z, y, x, c)))  14.2 us
    ppermute x4, waiting for transfers between devices, along_x(): return lax.ppermute(value, ('dp', 'segment'), pairs)  13 us
    ppermute x4, starting transfers between devices, along_x(): return lax.ppermute(value, ('dp', 'segment'), pairs)  8.62 us
    pallas_call x2, Pallas kernels, conv_norm(): pl.pallas_call(functools.partial(conv_norm_kernel, len(smalls)), in_specs...  4.37 us
    pallas_call x6, Pallas kernels, small_call(): pl.pallas_call(body, in_specs=[pl.BlockSpec(memory_space=pltpu.SMEM)] + [...  2.39 us
  transfers between devices with their start and end apart: 18, of which 8 were waited for; matrix products, arithmetic and copies ran while one was open for 0% of the time, Pallas kernels for 23%

profile of v3, /device:TPU:0, one launch (start us, length us, event | category | flops | bytes accessed | tf_op | source)
XLA Modules:
  0.0 101.3 jit_solution(14409383011159154720)
XLA Ops:
  0.7 1.1 %parameters.1.rest_0_.refs_3_.refs_12_ = f32[56,384]{1,0:T(8,128)S(1)} custom-call(f32[49,1,384]{2,1,0:T(1,128)} %bitcast.45, f32[1,384]{1,0:T(1,128)} %gain_ref.1, f32[1,384]{1,0:T(1,128)} %scale_ref.1), custom_call_target="tpu_custom_call" | custom-call | flops 550000000 | bytes 1800000 | tf_op jit(solution)/shard_map/parameters/pallas_call | solution.py:102
  3.2 2.2 %conv_norm.2 = (bf16[256,384]{1,0:T(8,128)(2,1)S(1)}, bf16[256,384]{1,0:T(8,128)(2,1)S(1)}, f32[256,128]{1,0:T(8,128)S(1)}) custom-call(s32[2]{0:T(128)S(1)} %pad_add_fusion.2.sel_ref, bf16[16,16,384]{2,1,0:T(8,128)(2,1)S(1)} %get-tuple-element.179.x_ref.refs_1_.refs_2_, f32[56,384]{1,0:T(8,128)S(1)} %parameters.1.rest_0_.refs_3_.refs_12_, ...), custom_call_target="tpu_custom_call" | custom-call | flops 2200000000 | bytes 7200000 | tf_op jit(solution)/shard_map/conv_norm/pallas_call | solution.py:145
  5.5 0.8 copy-done.6
  6.3 5.2 %pair_forward.2 = (bf16[16,16,384]{2,1,0:T(8,128)(2,1)S(1)}, bf16[16,16,384]{2,1,0:T(8,128)(2,1)S(1)}, bf16[256,384]{1,0:T(8,128)(2,1)S(1)}, f32[256,128]{1,0:T(...) custom-call(s32[5]{0:T(128)S(1)} %stack.50.refs_0_, ...), custom_call_target="tpu_custom_call" | custom-call | flops 8249999872 | bytes 27000000 | tf_op jit(solution)/shard_map/pair_forward/pallas_call | solution.py:625
  11.5 4.7 %collective-permute-start.5 = (bf16[16,16,384]{2,1,0:T(8,128)(2,1)S(1)}, bf16[16,16,384]{2,1,0:T(8,128)(2,1)S(1)}, u32[]{:S(2)}, u32[]{:S(2)}) collective-permute-start(bf16[16,16,384]{2,1,0:T(8,128)(2,1)S(1)} %get-tuple-element.105), channel_id=1, source_target_pairs={{0,2},{1,3},{4,6},{5,7},{8,10},{9,11},{12,14},{13,15},{16,18},{17,... | collective-permute-start | bytes 589832 | tf_op jit(solution)/shard_map/ppermute | solution.py:1124
  16.2 2.2 %conv_norm.3 = (bf16[256,384]{1,0:T(8,128)(2,1)S(1)}, bf16[256,384]{1,0:T(8,128)(2,1)S(1)}, f32[256,128]{1,0:T(8,128)S(1)}) custom-call(s32[2]{0:T(128)S(1)} %pad_add_fusion.1.sel_ref, bf16[16,16,384]{2,1,0:T(8,128)(2,1)S(1)} %get-tuple-element.180.x_ref.refs_1_.refs_2_, f32[56,384]{1,0:T(8,128)S(1)} %parameters.1.rest_0_.refs_3_.refs_12_, ...), custom_call_target="tpu_custom_call" | custom-call | flops 2200000000 | bytes 7200000 | tf_op jit(solution)/shard_map/conv_norm/pallas_call | solution.py:145
  18.4 5.2 %pair_forward.3 = (bf16[16,16,384]{2,1,0:T(8,128)(2,1)S(1)}, bf16[16,16,384]{2,1,0:T(8,128)(2,1)S(1)}, bf16[256,384]{1,0:T(8,128)(2,1)S(1)}, f32[256,128]{1,0:T(...) custom-call(s32[5]{0:T(128)S(1)} %stack.51.refs_0_, ...), custom_call_target="tpu_custom_call" | custom-call | flops 8249999872 | bytes 27000000 | tf_op jit(solution)/shard_map/pair_forward/pallas_call | solution.py:625
  23.7 1.3 %collective-permute-start.3 = (bf16[16,16,384]{2,1,0:T(8,128)(2,1)S(1)}, bf16[16,16,384]{2,1,0:T(8,128)(2,1)S(1)}, u32[]{:S(2)}, u32[]{:S(2)}) collective-permute-start(bf16[16,16,384]{2,1,0:T(8,128)(2,1)S(1)} %get-tuple-element.94), channel_id=1, source_target_pairs={{0,2},{1,3},{4,6},{5,7},{8,10},{9,11},{12,14},{13,15},{16,18},{17,... | collective-permute-start | bytes 589832 | tf_op jit(solution)/shard_map/ppermute | solution.py:1124
  25.0 0.7 pair_map.3
  25.7 1.3 %collective-permute-start.6 = (bf16[16,16,384]{2,1,0:T(8,128)(2,1)S(1)}, bf16[16,16,384]{2,1,0:T(8,128)(2,1)S(1)}, u32[]{:S(2)}, u32[]{:S(2)}) collective-permute-start(bf16[16,16,384]{2,1,0:T(8,128)(2,1)S(1)} %get-tuple-element.106), channel_id=1, source_target_pairs={{2,0},{3,1},{6,4},{7,5},{10,8},{11,9},{14,12},{15,13},{18,16},{19,... | collective-permute-start | bytes 589832 | tf_op jit(solution)/shard_map/ppermute | solution.py:1124
  27.0 2.5 %collective-permute-done.3.refs_1_.refs_15_ = bf16[16,16,384]{2,1,0:T(8,128)(2,1)S(1)} collective-permute-done((bf16[16,16,384]{2,1,0:T(8,128)(2,1)S(1)}, bf16[16,16,384]{2,1,0:T(8,128)(2,1)S(1)}, u32[]{:S(2)}, u32[]{:S(2)}) %collective-permute-start.3) | collective-permute-done | bytes 196640 | tf_op jit(solution)/shard_map/ppermute | solution.py:1124
  29.5 0.9 pair_map.2
  30.3 1.3 %collective-permute-start.4 = (bf16[16,16,384]{2,1,0:T(8,128)(2,1)S(1)}, bf16[16,16,384]{2,1,0:T(8,128)(2,1)S(1)}, u32[]{:S(2)}, u32[]{:S(2)}) collective-permute-start(bf16[16,16,384]{2,1,0:T(8,128)(2,1)S(1)} %get-tuple-element.95), channel_id=1, source_target_pairs={{2,0},{3,1},{6,4},{7,5},{10,8},{11,9},{14,12},{15,13},{18,16},{19,... | collective-permute-start | bytes 589832 | tf_op jit(solution)/shard_map/ppermute | solution.py:1124
  31.6 0.9 pair_grads.1
  32.5 7.4 %collective-permute-done.6.refs_1_ = bf16[16,16,384]{2,1,0:T(8,128)(2,1)S(1)} collective-permute-done((bf16[16,16,384]{2,1,0:T(8,128)(2,1)S(1)}, bf16[16,16,384]{2,1,0:T(8,128)(2,1)S(1)}, u32[]{:S(2)}, u32[]{:S(2)}) %collective-permute-start.6) | collective-permute-done | bytes 196640 | tf_op jit(solution)/shard_map/ppermute | solution.py:1124
  39.9 9.4 %pair_back.2 = (bf16[384,768]{1,0:T(8,128)(2,1)}, bf16[384,768]{1,0:T(8,128)(2,1)}, bf16[384,768]{1,0:T(8,128)(2,1)}, bf16[384,768]{1,0:T(8,128)(2,1)}, f32[64,384]{1,0:T(8,128)S(1)}, /*index=5*/f32[64,384]{1,0:T(8,128)S(1)}) custom-call(s32[5]{0:T(128)S(1)} %stack.50.refs_0_, bf16[16,16,384]{2,1,0:T(8,128)(2,1)S(1)} %collective-permute-done.6.refs_1_, ...), custom_call_target="tpu_custom_call" | custom-call | flops 9900000256 | bytes 32400000 | tf_op jit(solution)/shard_map/pair_back/pallas_call | solution.py:625
  49.3 3.2 %collective-permute-done.4.refs_1_ = bf16[16,16,384]{2,1,0:T(8,128)(2,1)S(1)} collective-permute-done((bf16[16,16,384]{2,1,0:T(8,128)(2,1)S(1)}, bf16[16,16,384]{2,1,0:T(8,128)(2,1)S(1)}, u32[]{:S(2)}, u32[]{:S(2)}) %collective-permute-start.4) | collective-permute-done | bytes 196640 | tf_op jit(solution)/shard_map/ppermute | solution.py:1124
  52.4 10.5 %pair_back.3 = (bf16[384,768]{1,0:T(8,128)(2,1)}, bf16[384,768]{1,0:T(8,128)(2,1)}, bf16[384,768]{1,0:T(8,128)(2,1)}, bf16[384,768]{1,0:T(8,128)(2,1)}, bf16[384,128]{1,0:T(8,128)(2,1)S(1)}) custom-call(s32[5]{0:T(128)S(1)} %stack.50.refs_0_, bf16[16,16,384]{2,1,0:T(8,128)(2,1)S(1)} %collective-permute-done.4.refs_1_, ...), custom_call_target="tpu_custom_call" | custom-call | flops 9900000256 | bytes 32400000 | tf_op jit(solution)/shard_map/pair_back/pallas_call | solution.py:625
  63.5 1.7 %collective-permute-done.12 = bf16[384,768]{1,0:T(8,128)(2,1)S(1)} collective-permute-done((bf16[384,768]{1,0:T(8,128)(2,1)}, bf16[384,768]{1,0:T(8,128)(2,1)S(1)}, u32[]{:S(2)}, u32[]{:S(2)}) %collective-permute-start.12) | collective-permute-done | bytes 589856 | tf_op jit(solution)/shard_map/ppermute | solution.py:1119
  65.2 1.1 %copy-done.1 = bf16[384,768]{1,0:T(8,128)(2,1)S(1)} copy-done((bf16[384,768]{1,0:T(8,128)(2,1)S(1)}, bf16[384,768]{1,0:T(8,128)(2,1)}, u32[]{:S(2)}) %copy-start.1) | copy-done | bytes 589848
  66.4 1.6 %collective-permute-start.13 = (bf16[4,48,768]{2,1,0:T(8,128)(2,1)S(1)}, bf16[4,48,768]{2,1,0:T(8,128)(2,1)S(1)}, u32[]{:S(2)}, u32[]{:S(2)}) collective-permute-start(bf16[4,48,768]{2,1,0:T(8,128)(2,1)S(1)} %get-tuple-element.165), channel_id=1, source_target_pairs={{0,4},{1,5},{2,6},{3,7},{4,0},{5,1},{6,2},{7,3},{8,12},{9,13},{10,... | collective-permute-start | bytes 884744 | tf_op jit(solution)/shard_map/ppermute | solution.py:1119
  68.2 0.9 collective-permute-start.8
  69.2 7.2 %collective-permute-done.13.refs_2_ = bf16[4,48,768]{2,1,0:T(8,128)(2,1)S(1)} collective-permute-done((bf16[4,48,768]{2,1,0:T(8,128)(2,1)S(1)}, bf16[4,48,768]{2,1,0:T(8,128)(2,1)S(1)}, u32[]{:S(2)}, u32[]{:S(2)}) %collective-permute-start.13) | collective-permute-done | bytes 294944 | tf_op jit(solution)/shard_map/ppermute | solution.py:1119
  77.0 1.6 %collective-permute-start.14 = (bf16[48,768]{1,0:T(8,128)(2,1)S(1)}, bf16[48,768]{1,0:T(8,128)(2,1)S(1)}, u32[]{:S(2)}, u32[]{:S(2)}) collective-permute-start(bf16[48,768]{1,0:T(8,128)(2,1)S(1)} %get-tuple-element.167), channel_id=1, source_target_pairs={{0,8},{1,9},{2,10},{3,11},{4,12},{5,13},{6,14},{7,15},{8,0},{9,1},... | collective-permute-start | bytes 221192 | tf_op jit(solution)/shard_map/ppermute | solution.py:1119
  78.6 4.3 %collective-permute-done.8.refs_2_ = bf16[4,48,896]{2,1,0:T(8,128)(2,1)S(1)} collective-permute-done((bf16[4,48,896]{2,1,0:T(8,128)(2,1)S(1)}, bf16[4,48,896]{2,1,0:T(8,128)(2,1)S(1)}, u32[]{:S(2)}, u32[]{:S(2)}) %collective-permute-start.8) | collective-permute-done | bytes 344096 | tf_op jit(solution)/shard_map/ppermute | solution.py:1119
  83.6 2.7 %collective-permute-start.10 = (bf16[48,896]{1,0:T(8,128)(2,1)S(1)}, bf16[48,896]{1,0:T(8,128)(2,1)S(1)}, u32[]{:S(2)}, u32[]{:S(2)}) collective-permute-start(bf16[48,896]{1,0:T(8,128)(2,1)S(1)} %get-tuple-element.160), channel_id=1, source_target_pairs={{0,16},{1,17},{2,18},{3,19},{4,20},{5,21},{6,22},{7,23},{8,24},{9,... | collective-permute-start | bytes 258056 | tf_op jit(solution)/shard_map/ppermute | solution.py:1119
  86.2 1.3 %collective-permute-start.11 = (bf16[48,896]{1,0:T(8,128)(2,1)S(1)}, bf16[48,896]{1,0:T(8,128)(2,1)S(1)}, u32[]{:S(2)}, u32[]{:S(2)}) collective-permute-start(bf16[48,896]{1,0:T(8,128)(2,1)S(1)} %get-tuple-element.161), channel_id=1, source_target_pairs={{0,24},{1,25},{2,26},{3,27},{4,28},{5,29},{6,30},{7,31},{8,16},{9,... | collective-permute-start | bytes 258056 | tf_op jit(solution)/shard_map/ppermute | solution.py:1119
  87.8 2.8 %collective-permute-start.15 = (bf16[48,768]{1,0:T(8,128)(2,1)S(1)}, bf16[48,768]{1,0:T(8,128)(2,1)S(1)}, u32[]{:S(2)}, u32[]{:S(2)}) collective-permute-start(bf16[48,768]{1,0:T(8,128)(2,1)S(1)} %get-tuple-element.168), channel_id=1, source_target_pairs={{0,16},{1,17},{2,18},{3,19},{4,20},{5,21},{6,22},{7,23},{8,24},{9,... | collective-permute-start | bytes 221192 | tf_op jit(solution)/shard_map/ppermute | solution.py:1119
  90.6 1.3 %collective-permute-start.16 = (bf16[48,768]{1,0:T(8,128)(2,1)S(1)}, bf16[48,768]{1,0:T(8,128)(2,1)S(1)}, u32[]{:S(2)}, u32[]{:S(2)}) collective-permute-start(bf16[48,768]{1,0:T(8,128)(2,1)S(1)} %get-tuple-element.169), channel_id=1, source_target_pairs={{0,24},{1,25},{2,26},{3,27},{4,28},{5,29},{6,30},{7,31},{8,16},{9,... | collective-permute-start | bytes 221192 | tf_op jit(solution)/shard_map/ppermute | solution.py:1119
  92.0 7.1 %collective-permute-done.15.refs_7_ = bf16[48,768]{1,0:T(8,128)(2,1)S(1)} collective-permute-done((bf16[48,768]{1,0:T(8,128)(2,1)S(1)}, bf16[48,768]{1,0:T(8,128)(2,1)S(1)}, u32[]{:S(2)}, u32[]{:S(2)}) %collective-permute-start.15) | collective-permute-done | bytes 73760 | tf_op jit(solution)/shard_map/ppermute | solution.py:1119
  99.3 1.3 %collective-permute-done.17.refs_2_ = bf16[48,896]{1,0:T(8,128)(2,1)S(1)} collective-permute-done((bf16[48,896]{1,0:T(8,128)(2,1)S(1)}, bf16[48,896]{1,0:T(8,128)(2,1)S(1)}, u32[]{:S(2)}, u32[]{:S(2)}) %collective-permute-start.17) | collective-permute-done | bytes 86048 | tf_op jit(solution)/shard_map/ppermute | solution.py:1119
  100.6 0.8 final.1
  (41 shorter events, 4.1 us)
Async XLA Ops:
  0.6 1.6 %copy-start.4 = (bf16[1,384,768]{2,1,0:T(8,128)(2,1)S(1)}, bf16[1,384,768]{2,1,0:T(8,128)(2,1)}, u32[]{:S(2)}) copy-start(bf16[1,384,768]{2,1,0:T(8,128)(2,1)} %param.11) | copy-start | bytes 1769476
  0.6 1.7 %copy-start.5 = (bf16[1,768,384]{2,1,0:T(8,128)(2,1)S(1)}, bf16[1,768,384]{2,1,0:T(8,128)(2,1)}, u32[]{:S(2)}) copy-start(bf16[1,768,384]{2,1,0:T(8,128)(2,1)} %param.12) | copy-start | bytes 1769476
  0.7 2.4 %copy-start.2 = (bf16[4,16,16,384]{3,2,1,0:T(8,128)(2,1)S(1)}, bf16[4,16,16,384]{3,2,1,0:T(8,128)(2,1)}, u32[]{:S(2)}) copy-start(bf16[4,16,16,384]{3,2,1,0:T(8,128)(2,1)} %param.7) | copy-start | bytes 2359300
  1.7 1.3 %copy-start.3 = (bf16[4,16,16,384]{3,2,1,0:T(8,128)(2,1)S(1)}, bf16[4,16,16,384]{3,2,1,0:T(8,128)(2,1)}, u32[]{:S(2)}) copy-start(bf16[4,16,16,384]{3,2,1,0:T(8,128)(2,1)} %param.8) | copy-start | bytes 2359300
  1.8 1.5 %collective-permute-start = (f32[56,384]{1,0:T(8,128)S(1)}, f32[56,384]{1,0:T(8,128)S(1)}, u32[]{:S(2)}, u32[]{:S(2)}) collective-permute-start(f32[56,384]{1,0:T(8,128)S(1)} %parameters.1.rest_0_.refs_3_.refs_12_), channel_id=1, source_target_pairs={{0,1},{1,0},{2,3},{3,2},{4,5},{5,4},{6,7},{7,6},{8,9},{9,8},{10,11... | collective-permute-start | bytes 258056 | tf_op jit(solution)/shard_map/ppermute | solution.py:1119
  2.3 3.1 %collective-permute-start.1 = (bf16[384,768]{1,0:T(8,128)(2,1)S(1)}, bf16[384,768]{1,0:T(8,128)(2,1)S(1)}, u32[]{:S(2)}, u32[]{:S(2)}) collective-permute-start(bf16[384,768]{1,0:T(8,128)(2,1)S(1)} %bitcast.37), channel_id=1, source_target_pairs={{0,1},{1,0},{2,3},{3,2},{4,5},{5,4},{6,7},{7,6},{8,9},{9,8},{10,11... | collective-permute-start | bytes 1769480 | tf_op jit(solution)/shard_map/ppermute | solution.py:1119
  2.4 3.1 %collective-permute-start.2 = (bf16[768,384]{1,0:T(8,128)(2,1)S(1)}, bf16[768,384]{1,0:T(8,128)(2,1)}, u32[]{:S(2)}, u32[]{:S(2)}) collective-permute-start(bf16[768,384]{1,0:T(8,128)(2,1)S(1)} %bitcast.44), channel_id=1, source_target_pairs={{0,1},{1,0},{2,3},{3,2},{4,5},{5,4},{6,7},{7,6},{8,9},{9,8},{10,11... | collective-permute-start | bytes 1769480 | tf_op jit(solution)/shard_map/ppermute | solution.py:1119
  5.4 0.8 copy-start.6
  11.5 13.5 %collective-permute-start.5 = (bf16[16,16,384]{2,1,0:T(8,128)(2,1)S(1)}, bf16[16,16,384]{2,1,0:T(8,128)(2,1)S(1)}, u32[]{:S(2)}, u32[]{:S(2)}) collective-permute-start(bf16[16,16,384]{2,1,0:T(8,128)(2,1)S(1)} %get-tuple-element.105), channel_id=1, source_target_pairs={{0,2},{1,3},{4,6},{5,7},{8,10},{9,11},{12,14},{13,15},{16,18},{17,... | collective-permute-start | bytes 589832 | tf_op jit(solution)/shard_map/ppermute | solution.py:1124
  23.7 5.8 %collective-permute-start.3 = (bf16[16,16,384]{2,1,0:T(8,128)(2,1)S(1)}, bf16[16,16,384]{2,1,0:T(8,128)(2,1)S(1)}, u32[]{:S(2)}, u32[]{:S(2)}) collective-permute-start(bf16[16,16,384]{2,1,0:T(8,128)(2,1)S(1)} %get-tuple-element.94), channel_id=1, source_target_pairs={{0,2},{1,3},{4,6},{5,7},{8,10},{9,11},{12,14},{13,15},{16,18},{17,... | collective-permute-start | bytes 589832 | tf_op jit(solution)/shard_map/ppermute | solution.py:1124
  25.7 14.2 %collective-permute-start.6 = (bf16[16,16,384]{2,1,0:T(8,128)(2,1)S(1)}, bf16[16,16,384]{2,1,0:T(8,128)(2,1)S(1)}, u32[]{:S(2)}, u32[]{:S(2)}) collective-permute-start(bf16[16,16,384]{2,1,0:T(8,128)(2,1)S(1)} %get-tuple-element.106), channel_id=1, source_target_pairs={{2,0},{3,1},{6,4},{7,5},{10,8},{11,9},{14,12},{15,13},{18,16},{19,... | collective-permute-start | bytes 589832 | tf_op jit(solution)/shard_map/ppermute | solution.py:1124
  30.3 22.1 %collective-permute-start.4 = (bf16[16,16,384]{2,1,0:T(8,128)(2,1)S(1)}, bf16[16,16,384]{2,1,0:T(8,128)(2,1)S(1)}, u32[]{:S(2)}, u32[]{:S(2)}) collective-permute-start(bf16[16,16,384]{2,1,0:T(8,128)(2,1)S(1)} %get-tuple-element.95), channel_id=1, source_target_pairs={{2,0},{3,1},{6,4},{7,5},{10,8},{11,9},{14,12},{15,13},{18,16},{19,... | collective-permute-start | bytes 589832 | tf_op jit(solution)/shard_map/ppermute | solution.py:1124
  63.0 2.3 %collective-permute-start.12 = (bf16[384,768]{1,0:T(8,128)(2,1)}, bf16[384,768]{1,0:T(8,128)(2,1)S(1)}, u32[]{:S(2)}, u32[]{:S(2)}) collective-permute-start(bf16[384,768]{1,0:T(8,128)(2,1)} %get-tuple-element.163), channel_id=1, source_target_pairs={{0,1},{1,0},{2,3},{3,2},{4,5},{5,4},{6,7},{7,6},{8,9},{9,8},{10,11... | collective-permute-start | bytes 1769480 | tf_op jit(solution)/shard_map/ppermute | solution.py:1119
  63.0 5.0 %collective-permute-start.7 = (bf16[384,768]{1,0:T(8,128)(2,1)}, bf16[384,768]{1,0:T(8,128)(2,1)S(1)}, u32[]{:S(2)}, u32[]{:S(2)}) collective-permute-start(bf16[384,768]{1,0:T(8,128)(2,1)} %get-tuple-element.154), channel_id=1, source_target_pairs={{0,1},{1,0},{2,3},{3,2},{4,5},{5,4},{6,7},{7,6},{8,9},{9,8},{10,11... | collective-permute-start | bytes 1769480 | tf_op jit(solution)/shard_map/ppermute | solution.py:1119
  65.2 1.1 %copy-start.1 = (bf16[384,768]{1,0:T(8,128)(2,1)S(1)}, bf16[384,768]{1,0:T(8,128)(2,1)}, u32[]{:S(2)}) copy-start(bf16[384,768]{1,0:T(8,128)(2,1)} %get-tuple-element.162) | copy-start | bytes 1769476
  66.3 1.7 %copy-start = (bf16[384,768]{1,0:T(8,128)(2,1)S(1)}, bf16[384,768]{1,0:T(8,128)(2,1)}, u32[]{:S(2)}) copy-start(bf16[384,768]{1,0:T(8,128)(2,1)} %get-tuple-element.153) | copy-start | bytes 1769476
  66.4 9.9 %collective-permute-start.13 = (bf16[4,48,768]{2,1,0:T(8,128)(2,1)S(1)}, bf16[4,48,768]{2,1,0:T(8,128)(2,1)S(1)}, u32[]{:S(2)}, u32[]{:S(2)}) collective-permute-start(bf16[4,48,768]{2,1,0:T(8,128)(2,1)S(1)} %get-tuple-element.165), channel_id=1, source_target_pairs={{0,4},{1,5},{2,6},{3,7},{4,0},{5,1},{6,2},{7,3},{8,12},{9,13},{10,... | collective-permute-start | bytes 884744 | tf_op jit(solution)/shard_map/ppermute | solution.py:1119
  68.2 14.8 %collective-permute-start.8 = (bf16[4,48,896]{2,1,0:T(8,128)(2,1)S(1)}, bf16[4,48,896]{2,1,0:T(8,128)(2,1)S(1)}, u32[]{:S(2)}, u32[]{:S(2)}) collective-permute-start(bf16[4,48,896]{2,1,0:T(8,128)(2,1)S(1)} %get-tuple-element.157), channel_id=1, source_target_pairs={{0,4},{1,5},{2,6},{3,7},{4,0},{5,1},{6,2},{7,3},{8,12},{9,13},{10,... | collective-permute-start | bytes 1032200 | tf_op jit(solution)/shard_map/ppermute | solution.py:1119
  77.0 13.6 %collective-permute-start.14 = (bf16[48,768]{1,0:T(8,128)(2,1)S(1)}, bf16[48,768]{1,0:T(8,128)(2,1)S(1)}, u32[]{:S(2)}, u32[]{:S(2)}) collective-permute-start(bf16[48,768]{1,0:T(8,128)(2,1)S(1)} %get-tuple-element.167), channel_id=1, source_target_pairs={{0,8},{1,9},{2,10},{3,11},{4,12},{5,13},{6,14},{7,15},{8,0},{9,1},... | collective-permute-start | bytes 221192 | tf_op jit(solution)/shard_map/ppermute | solution.py:1119
  83.6 15.5 %collective-permute-start.10 = (bf16[48,896]{1,0:T(8,128)(2,1)S(1)}, bf16[48,896]{1,0:T(8,128)(2,1)S(1)}, u32[]{:S(2)}, u32[]{:S(2)}) collective-permute-start(bf16[48,896]{1,0:T(8,128)(2,1)S(1)} %get-tuple-element.160), channel_id=1, source_target_pairs={{0,16},{1,17},{2,18},{3,19},{4,20},{5,21},{6,22},{7,23},{8,24},{9,... | collective-permute-start | bytes 258056 | tf_op jit(solution)/shard_map/ppermute | solution.py:1119
  86.2 12.9 %collective-permute-start.11 = (bf16[48,896]{1,0:T(8,128)(2,1)S(1)}, bf16[48,896]{1,0:T(8,128)(2,1)S(1)}, u32[]{:S(2)}, u32[]{:S(2)}) collective-permute-start(bf16[48,896]{1,0:T(8,128)(2,1)S(1)} %get-tuple-element.161), channel_id=1, source_target_pairs={{0,24},{1,25},{2,26},{3,27},{4,28},{5,29},{6,30},{7,31},{8,16},{9,... | collective-permute-start | bytes 258056 | tf_op jit(solution)/shard_map/ppermute | solution.py:1119
  87.6 11.5 %collective-permute-start.9 = (bf16[48,896]{1,0:T(8,128)(2,1)S(1)}, bf16[48,896]{1,0:T(8,128)(2,1)S(1)}, u32[]{:S(2)}, u32[]{:S(2)}) collective-permute-start(bf16[48,896]{1,0:T(8,128)(2,1)S(1)} %get-tuple-element.159), channel_id=1, source_target_pairs={{0,8},{1,9},{2,10},{3,11},{4,12},{5,13},{6,14},{7,15},{8,0},{9,1},... | collective-permute-start | bytes 258056 | tf_op jit(solution)/shard_map/ppermute | solution.py:1119
  87.8 11.3 %collective-permute-start.15 = (bf16[48,768]{1,0:T(8,128)(2,1)S(1)}, bf16[48,768]{1,0:T(8,128)(2,1)S(1)}, u32[]{:S(2)}, u32[]{:S(2)}) collective-permute-start(bf16[48,768]{1,0:T(8,128)(2,1)S(1)} %get-tuple-element.168), channel_id=1, source_target_pairs={{0,16},{1,17},{2,18},{3,19},{4,20},{5,21},{6,22},{7,23},{8,24},{9,... | collective-permute-start | bytes 221192 | tf_op jit(solution)/shard_map/ppermute | solution.py:1119
  90.6 8.5 %collective-permute-start.16 = (bf16[48,768]{1,0:T(8,128)(2,1)S(1)}, bf16[48,768]{1,0:T(8,128)(2,1)S(1)}, u32[]{:S(2)}, u32[]{:S(2)}) collective-permute-start(bf16[48,768]{1,0:T(8,128)(2,1)S(1)} %get-tuple-element.169), channel_id=1, source_target_pairs={{0,24},{1,25},{2,26},{3,27},{4,28},{5,29},{6,30},{7,31},{8,16},{9,... | collective-permute-start | bytes 221192 | tf_op jit(solution)/shard_map/ppermute | solution.py:1119
  99.2 1.3 %collective-permute-start.17 = (bf16[48,896]{1,0:T(8,128)(2,1)S(1)}, bf16[48,896]{1,0:T(8,128)(2,1)S(1)}, u32[]{:S(2)}, u32[]{:S(2)}) collective-permute-start(bf16[48,896]{1,0:T(8,128)(2,1)S(1)} %get-tuple-element.171), channel_id=1, source_target_pairs={{0,1},{1,0},{2,3},{3,2},{4,5},{5,4},{6,7},{7,6},{8,9},{9,8},{10,11... | collective-permute-start | bytes 258056 | tf_op jit(solution)/shard_map/ppermute | solution.py:1119

commit v4 on v3

--- a/solution.py
+++ b/solution.py
@@ -565,7 +565,6 @@
         nm_ref[at, :] = (xhat_ref[at, :].astype(jnp.float32) * gain).astype(jnp.bfloat16)
     gb_t = gb_ref[...].T
     nm_t = nm_ref[...].T
-    wait_in()
     wait_out()
     for j in range(hidden // step):
         cut = slice(j * step, (j + 1) * step)
@@ -590,6 +589,8 @@
             t_send = t_send + old_send[:, cut].astype(jnp.float32)
         keep_ref[:, cut] = t_keep.astype(jnp.bfloat16)
         send_ref[:, cut] = t_send.astype(jnp.bfloat16)
+        if j == 0:
+            wait_in()
         part = lax.dot_general(gp_ref[...], w_in_ref[:, cut], (((1,), (1,)), ((), ())), preferred_element_type=jnp.float32)
         if j == 0:
             acc_ref[...] = part
@@ -689,11 +690,14 @@
     }
 
 
-def start_weights(r, slot, block):
-    return (
-        copy_chosen(r.sel[block], (r.own_in, r.near_in), r.w_in.at[slot], r.w_sem.at[0, slot]),
-        copy_chosen(r.sel[block], (r.own_out, r.near_out), r.w_out.at[slot], r.w_sem.at[1, slot]),
-    )
+def start_weights(r, slot, block, out_first=False):
+    def start(k, own, near, target):
+        return copy_chosen(r.sel[block], (own, near), target.at[slot], r.w_sem.at[k, slot])
+
+    if out_first:
+        wait_out = start(1, r.own_out, r.near_out, r.w_out)
+        return start(0, r.own_in, r.near_in, r.w_in), wait_out
+    return start(0, r.own_in, r.near_in, r.w_in), start(1, r.own_out, r.near_out, r.w_out)
 
 
 def pair_forward(sel, x, first, small, weights):
@@ -888,10 +892,12 @@
         @pl.when(r.sel[2] == 0)
         def _():
             core = r.sel[3] == 0
-            high, low = start_weights(r, 1, 1), start_weights(r, 0, 0)
-            waits = {}
+            high, waits = start_weights(r, 1, 1, True), {}
             if before is not None:
-                waits = {k: copy_old(k) for k in (2, 3, 0, 1)}
+                waits = {k: copy_old(k) for k in (2, 3)}
+            low = start_weights(r, 0, 0, True)
+            if before is not None:
+                waits.update({k: copy_old(k) for k in (0, 1)})
             choose_small(r)
             s0, s1 = r.small.at[0], r.small.at[1]
 
@@ -987,10 +993,34 @@
     return small_call(depth_kernel, "to_depths", ((mine.shape[1:], jnp.bfloat16),) * 4, levels, mine, got, after=after)
 
 
+def split_kernel(sel_ref, keep_ref, got_ref, *out_refs):
+    for k, out_ref in enumerate(out_refs):
+        for side in range(2):
+            out_ref[side] = add(keep_ref[sel_ref[k], side], got_ref[sel_ref[k], side]).astype(jnp.bfloat16)
+
+
+def split_depths(levels, keep, got, after=()):
+    keep, got = (v.reshape(4, 2, v.shape[0] // 8, v.shape[1]) for v in (keep, got))
+    outs = ((keep.shape[1:], jnp.bfloat16),) * 4
+    return small_call(split_kernel, "split_depths", outs, levels, keep, got, after=after)
+
+
+def join_kernel(sel_ref, a_ref, b_ref, c_ref, d_ref, across_ref, mine_ref):
+    side = sel_ref[0]
+    for out_ref, which in ((across_ref, 1 - side), (mine_ref, side)):
+        out_ref[...] = (add(a_ref[which], b_ref[which]) + add(c_ref[which], d_ref[which])).astype(out_ref.dtype)
+
+
+def join_depths(side, parts):
+    shape = parts[0].shape[1:]
+    return small_call(join_kernel, "join_depths", ((shape, jnp.bfloat16), (shape, jnp.float32)), side, *parts)
+
+
 def core_kernel(sel_ref, *refs):
     *parts, own_ref, send_ref = refs
     hidden = parts[-1].shape[1]
-    low, high = (add(a[...], b[...]) + add(c[...], d[...]) for a, b, c, d in (parts[:4], parts[4:]))
+    a, b, c, d, e, f = parts
+    low, high = add(a[...], b[...]) + add(c[...], d[...]), add(e[...], f[...])
     first = sel_ref[0] == 0
     small = low[:, hidden:]
     turned = pltpu.roll(small, SMALL_ROWS, 1)
@@ -1157,7 +1187,7 @@
     totals = pair_grads(sel, passed, parts)
     grads = pair_back(sel, starts[0], maps[0], firsts[0], kept[0], small, weights)
     grads = pair_back(sel, starts[1], maps[1], firsts[1], kept[1], small, weights, (grads, totals))
-    core1, core0 = swap(grads.send1, c=1), swap(grads.send0, c=1)
+    core0, core1 = swap(grads.send0, c=1), swap(grads.send1, c=1)
 
     def along_y(*pairs):
         across, mine = to_side(sides, *pairs)
@@ -1167,9 +1197,11 @@
         own, *others = to_depths(levels, mine, got)
         return [own] + [swap(v, z=flip) for v, flip in zip(others, (1, 2, 3))]
 
-    high = along_y(grads.keep1, core1)
     low = along_y(grads.keep0, core0, grads.packed)
-    high = along_z(*high)
+    own, *others = split_depths(levels, grads.keep1, core1, low[:1])
+    parts = [own] + [swap(v, z=flip) for v, flip in zip(others, (1, 2, 3))]
+    across, mine = join_depths(sides, parts)
+    high = [mine, swap(across, y=1)]
     low = along_z(*low)
     own, send = to_core(cores, low + high)
     return final(cores, own, swap(send, c=1), kernels.shape[1])

time: 102 us -> 95.1 us (0.932)
  waiting for transfers between devices: 34.6 us -> 29.4 us
  starting transfers between devices: 22.8 us -> 21.3 us
    ppermute x14, waiting for transfers between devices: 21.6 us -> 16.6 us  [swap(): return lax.ppermute(value, ('dp', 'segment'), partners((z, y, x, c)))]
    ppermute x14, starting transfers between devices: 14.2 us -> 12.7 us  [swap(): return lax.ppermute(value, ('dp', 'segment'), partners((z, y, x, c)))]
  transfers between devices with their start and end apart: 18 -> 18, of which waited for: 8 -> 8; matrix products, arithmetic and copies ran while one was open for 0% -> 1% of each run, Pallas kernels for 23% -> 25%
where the time goes in v4:
time: 95.1 us; the launch traced here: 93.8 us
  Pallas kernels  40.7 us (43%)
  waiting for transfers between devices  29.4 us (31%)
  starting transfers between devices  21.3 us (22%)
  local copies, waits for them, and re-layouts  1.35 us (1%)
    pallas_call x7, Pallas kernels, named_call(): pl.pallas_call(kernel, in_specs=[pl.BlockSpec(memory_space=spaces[kind])...  32.8 us
    ppermute x14, waiting for transfers between devices, swap(): return lax.ppermute(value, ('dp', 'segment'), partners((z, y, x, c)))  16.6 us
    ppermute x4, waiting for transfers between devices, along_x(): return lax.ppermute(value, ('dp', 'segment'), pairs)  12.7 us
    ppermute x14, starting transfers between devices, swap(): return lax.ppermute(value, ('dp', 'segment'), partners((z, y, x, c)))  12.7 us
    ppermute x4, starting transfers between devices, along_x(): return lax.ppermute(value, ('dp', 'segment'), pairs)  8.62 us
    pallas_call x2, Pallas kernels, conv_norm(): pl.pallas_call(functools.partial(conv_norm_kernel, len(smalls)), in_specs...  4.37 us
    pallas_call x6, Pallas kernels, small_call(): pl.pallas_call(body, in_specs=[pl.BlockSpec(memory_space=pltpu.SMEM)] + [...  2.4 us
  transfers between devices with their start and end apart: 18, of which 8 were waited for; matrix products, arithmetic and copies ran while one was open for 1% of the time, Pallas kernels for 25%

profile of v4, /device:TPU:0, one launch (start us, length us, event | category | flops | bytes accessed | tf_op | source)
XLA Modules:
  0.0 93.8 jit_solution(308803187385100585)
XLA Ops:
  0.7 1.1 %parameters.1.rest_0_.refs_3_.refs_12_ = f32[56,384]{1,0:T(8,128)S(1)} custom-call(f32[49,1,384]{2,1,0:T(1,128)} %bitcast.45, f32[1,384]{1,0:T(1,128)} %gain_ref.1, f32[1,384]{1,0:T(1,128)} %scale_ref.1), custom_call_target="tpu_custom_call" | custom-call | flops 550000000 | bytes 1800000 | tf_op jit(solution)/shard_map/parameters/pallas_call | solution.py:102
  3.2 2.2 %conv_norm.2 = (bf16[256,384]{1,0:T(8,128)(2,1)S(1)}, bf16[256,384]{1,0:T(8,128)(2,1)S(1)}, f32[256,128]{1,0:T(8,128)S(1)}) custom-call(s32[2]{0:T(128)S(1)} %pad_add_fusion.2.sel_ref, bf16[16,16,384]{2,1,0:T(8,128)(2,1)S(1)} %get-tuple-element.179.x_ref.refs_1_.refs_2_, f32[56,384]{1,0:T(8,128)S(1)} %parameters.1.rest_0_.refs_3_.refs_12_, ...), custom_call_target="tpu_custom_call" | custom-call | flops 2200000000 | bytes 7200000 | tf_op jit(solution)/shard_map/conv_norm/pallas_call | solution.py:145
  5.4 5.2 %pair_forward.2 = (bf16[16,16,384]{2,1,0:T(8,128)(2,1)S(1)}, bf16[16,16,384]{2,1,0:T(8,128)(2,1)S(1)}, bf16[256,384]{1,0:T(8,128)(2,1)S(1)}, f32[256,128]{1,0:T(...) custom-call(s32[5]{0:T(128)S(1)} %stack.50.refs_0_, ...), custom_call_target="tpu_custom_call" | custom-call | flops 8249999872 | bytes 27000000 | tf_op jit(solution)/shard_map/pair_forward/pallas_call | solution.py:626
  10.7 4.7 %collective-permute-start.5 = (bf16[16,16,384]{2,1,0:T(8,128)(2,1)S(1)}, bf16[16,16,384]{2,1,0:T(8,128)(2,1)S(1)}, u32[]{:S(2)}, u32[]{:S(2)}) collective-permute-start(bf16[16,16,384]{2,1,0:T(8,128)(2,1)S(1)} %get-tuple-element.105), channel_id=1, source_target_pairs={{0,2},{1,3},{4,6},{5,7},{8,10},{9,11},{12,14},{13,15},{16,18},{17,... | collective-permute-start | bytes 589832 | tf_op jit(solution)/shard_map/ppermute | solution.py:1154
  15.4 2.2 %conv_norm.3 = (bf16[256,384]{1,0:T(8,128)(2,1)S(1)}, bf16[256,384]{1,0:T(8,128)(2,1)S(1)}, f32[256,128]{1,0:T(8,128)S(1)}) custom-call(s32[2]{0:T(128)S(1)} %pad_add_fusion.1.sel_ref, bf16[16,16,384]{2,1,0:T(8,128)(2,1)S(1)} %get-tuple-element.180.x_ref.refs_1_.refs_2_, f32[56,384]{1,0:T(8,128)S(1)} %parameters.1.rest_0_.refs_3_.refs_12_, ...), custom_call_target="tpu_custom_call" | custom-call | flops 2200000000 | bytes 7200000 | tf_op jit(solution)/shard_map/conv_norm/pallas_call | solution.py:145
  17.6 5.2 %pair_forward.3 = (bf16[16,16,384]{2,1,0:T(8,128)(2,1)S(1)}, bf16[16,16,384]{2,1,0:T(8,128)(2,1)S(1)}, bf16[256,384]{1,0:T(8,128)(2,1)S(1)}, f32[256,128]{1,0:T(...) custom-call(s32[5]{0:T(128)S(1)} %stack.51.refs_0_, ...), custom_call_target="tpu_custom_call" | custom-call | flops 8249999872 | bytes 27000000 | tf_op jit(solution)/shard_map/pair_forward/pallas_call | solution.py:626
  22.8 1.3 %collective-permute-start.3 = (bf16[16,16,384]{2,1,0:T(8,128)(2,1)S(1)}, bf16[16,16,384]{2,1,0:T(8,128)(2,1)S(1)}, u32[]{:S(2)}, u32[]{:S(2)}) collective-permute-start(bf16[16,16,384]{2,1,0:T(8,128)(2,1)S(1)} %get-tuple-element.94), channel_id=1, source_target_pairs={{0,2},{1,3},{4,6},{5,7},{8,10},{9,11},{12,14},{13,15},{16,18},{17,... | collective-permute-start | bytes 589832 | tf_op jit(solution)/shard_map/ppermute | solution.py:1154
  24.1 0.7 pair_map.3
  24.9 1.3 %collective-permute-start.6 = (bf16[16,16,384]{2,1,0:T(8,128)(2,1)S(1)}, bf16[16,16,384]{2,1,0:T(8,128)(2,1)S(1)}, u32[]{:S(2)}, u32[]{:S(2)}) collective-permute-start(bf16[16,16,384]{2,1,0:T(8,128)(2,1)S(1)} %get-tuple-element.106), channel_id=1, source_target_pairs={{2,0},{3,1},{6,4},{7,5},{10,8},{11,9},{14,12},{15,13},{18,16},{19,... | collective-permute-start | bytes 589832 | tf_op jit(solution)/shard_map/ppermute | solution.py:1154
  26.2 2.5 %collective-permute-done.3.refs_1_.refs_15_ = bf16[16,16,384]{2,1,0:T(8,128)(2,1)S(1)} collective-permute-done((bf16[16,16,384]{2,1,0:T(8,128)(2,1)S(1)}, bf16[16,16,384]{2,1,0:T(8,128)(2,1)S(1)}, u32[]{:S(2)}, u32[]{:S(2)}) %collective-permute-start.3) | collective-permute-done | bytes 196640 | tf_op jit(solution)/shard_map/ppermute | solution.py:1154
  28.6 0.9 pair_map.2
  29.5 1.3 %collective-permute-start.4 = (bf16[16,16,384]{2,1,0:T(8,128)(2,1)S(1)}, bf16[16,16,384]{2,1,0:T(8,128)(2,1)S(1)}, u32[]{:S(2)}, u32[]{:S(2)}) collective-permute-start(bf16[16,16,384]{2,1,0:T(8,128)(2,1)S(1)} %get-tuple-element.95), channel_id=1, source_target_pairs={{2,0},{3,1},{6,4},{7,5},{10,8},{11,9},{14,12},{15,13},{18,16},{19,... | collective-permute-start | bytes 589832 | tf_op jit(solution)/shard_map/ppermute | solution.py:1154
  30.8 0.9 pair_grads.1
  31.7 7.4 %collective-permute-done.6.refs_1_ = bf16[16,16,384]{2,1,0:T(8,128)(2,1)S(1)} collective-permute-done((bf16[16,16,384]{2,1,0:T(8,128)(2,1)S(1)}, bf16[16,16,384]{2,1,0:T(8,128)(2,1)S(1)}, u32[]{:S(2)}, u32[]{:S(2)}) %collective-permute-start.6) | collective-permute-done | bytes 196640 | tf_op jit(solution)/shard_map/ppermute | solution.py:1154
  39.1 9.7 %pair_back.2 = (bf16[384,768]{1,0:T(8,128)(2,1)}, bf16[384,768]{1,0:T(8,128)(2,1)}, bf16[384,768]{1,0:T(8,128)(2,1)}, bf16[384,768]{1,0:T(8,128)(2,1)}, f32[64,384]{1,0:T(8,128)S(1)}, /*index=5*/f32[64,384]{1,0:T(8,128)S(1)}) custom-call(s32[5]{0:T(128)S(1)} %stack.50.refs_0_, bf16[16,16,384]{2,1,0:T(8,128)(2,1)S(1)} %collective-permute-done.6.refs_1_, ...), custom_call_target="tpu_custom_call" | custom-call | flops 9900000256 | bytes 32400000 | tf_op jit(solution)/shard_map/pair_back/pallas_call | solution.py:626
  48.8 2.9 %collective-permute-done.4.refs_1_ = bf16[16,16,384]{2,1,0:T(8,128)(2,1)S(1)} collective-permute-done((bf16[16,16,384]{2,1,0:T(8,128)(2,1)S(1)}, bf16[16,16,384]{2,1,0:T(8,128)(2,1)S(1)}, u32[]{:S(2)}, u32[]{:S(2)}) %collective-permute-start.4) | collective-permute-done | bytes 196640 | tf_op jit(solution)/shard_map/ppermute | solution.py:1154
  51.6 10.3 %pair_back.3 = (bf16[384,768]{1,0:T(8,128)(2,1)}, bf16[384,768]{1,0:T(8,128)(2,1)}, bf16[384,768]{1,0:T(8,128)(2,1)}, bf16[384,768]{1,0:T(8,128)(2,1)}, bf16[384,128]{1,0:T(8,128)(2,1)S(1)}) custom-call(s32[5]{0:T(128)S(1)} %stack.50.refs_0_, bf16[16,16,384]{2,1,0:T(8,128)(2,1)S(1)} %collective-permute-done.4.refs_1_, ...), custom_call_target="tpu_custom_call" | custom-call | flops 9900000256 | bytes 32400000 | tf_op jit(solution)/shard_map/pair_back/pallas_call | solution.py:626
  62.5 1.7 %collective-permute-done.7 = bf16[384,768]{1,0:T(8,128)(2,1)S(1)} collective-permute-done((bf16[384,768]{1,0:T(8,128)(2,1)}, bf16[384,768]{1,0:T(8,128)(2,1)S(1)}, u32[]{:S(2)}, u32[]{:S(2)}) %collective-permute-start.7) | collective-permute-done | bytes 589856 | tf_op jit(solution)/shard_map/ppermute | solution.py:1149
  64.2 1.1 %copy-done.1 = bf16[384,768]{1,0:T(8,128)(2,1)S(1)} copy-done((bf16[384,768]{1,0:T(8,128)(2,1)S(1)}, bf16[384,768]{1,0:T(8,128)(2,1)}, u32[]{:S(2)}) %copy-start.1) | copy-done | bytes 589848
  65.4 1.6 %collective-permute-start.8 = (bf16[4,48,896]{2,1,0:T(8,128)(2,1)S(1)}, bf16[4,48,896]{2,1,0:T(8,128)(2,1)S(1)}, u32[]{:S(2)}, u32[]{:S(2)}) collective-permute-start(bf16[4,48,896]{2,1,0:T(8,128)(2,1)S(1)} %get-tuple-element.157), channel_id=1, source_target_pairs={{0,4},{1,5},{2,6},{3,7},{4,0},{5,1},{6,2},{7,3},{8,12},{9,13},{10,... | collective-permute-start | bytes 1032200 | tf_op jit(solution)/shard_map/ppermute | solution.py:1149
  67.0 0.7 split_depths.1
  67.7 1.6 %collective-permute-start.13 = (bf16[2,48,768]{2,1,0:T(8,128)(2,1)S(1)}, bf16[2,48,768]{2,1,0:T(8,128)(2,1)S(1)}, u32[]{:S(2)}, u32[]{:S(2)}) collective-permute-start(bf16[2,48,768]{2,1,0:T(8,128)(2,1)S(1)} %get-tuple-element.165), channel_id=1, source_target_pairs={{0,8},{1,9},{2,10},{3,11},{4,12},{5,13},{6,14},{7,15},{8,0},{9,1},... | collective-permute-start | bytes 442376 | tf_op jit(solution)/shard_map/ppermute | solution.py:1149
  69.4 2.6 %collective-permute-start.14 = (bf16[2,48,768]{2,1,0:T(8,128)(2,1)S(1)}, bf16[2,48,768]{2,1,0:T(8,128)(2,1)S(1)}, u32[]{:S(2)}, u32[]{:S(2)}) collective-permute-start(bf16[2,48,768]{2,1,0:T(8,128)(2,1)S(1)} %get-tuple-element.166), channel_id=1, source_target_pairs={{0,16},{1,17},{2,18},{3,19},{4,20},{5,21},{6,22},{7,23},{8,24},{9,... | collective-permute-start | bytes 442376 | tf_op jit(solution)/shard_map/ppermute | solution.py:1149
  72.2 3.4 %collective-permute-done.8.refs_2_ = bf16[4,48,896]{2,1,0:T(8,128)(2,1)S(1)} collective-permute-done((bf16[4,48,896]{2,1,0:T(8,128)(2,1)S(1)}, bf16[4,48,896]{2,1,0:T(8,128)(2,1)S(1)}, u32[]{:S(2)}, u32[]{:S(2)}) %collective-permute-start.8) | collective-permute-done | bytes 344096 | tf_op jit(solution)/shard_map/ppermute | solution.py:1149
  75.5 0.6 to_depths.1
  76.2 2.7 %collective-permute-start.10 = (bf16[48,896]{1,0:T(8,128)(2,1)S(1)}, bf16[48,896]{1,0:T(8,128)(2,1)S(1)}, u32[]{:S(2)}, u32[]{:S(2)}) collective-permute-start(bf16[48,896]{1,0:T(8,128)(2,1)S(1)} %get-tuple-element.160), channel_id=1, source_target_pairs={{0,16},{1,17},{2,18},{3,19},{4,20},{5,21},{6,22},{7,23},{8,24},{9,... | collective-permute-start | bytes 258056 | tf_op jit(solution)/shard_map/ppermute | solution.py:1149
  78.8 1.3 %collective-permute-start.11 = (bf16[48,896]{1,0:T(8,128)(2,1)S(1)}, bf16[48,896]{1,0:T(8,128)(2,1)S(1)}, u32[]{:S(2)}, u32[]{:S(2)}) collective-permute-start(bf16[48,896]{1,0:T(8,128)(2,1)S(1)} %get-tuple-element.161), channel_id=1, source_target_pairs={{0,24},{1,25},{2,26},{3,27},{4,28},{5,29},{6,30},{7,31},{8,16},{9,... | collective-permute-start | bytes 258056 | tf_op jit(solution)/shard_map/ppermute | solution.py:1149
  80.4 6.6 %collective-permute-done.14.refs_3_ = bf16[2,48,768]{2,1,0:T(8,128)(2,1)S(1)} collective-permute-done((bf16[2,48,768]{2,1,0:T(8,128)(2,1)S(1)}, bf16[2,48,768]{2,1,0:T(8,128)(2,1)S(1)}, u32[]{:S(2)}, u32[]{:S(2)}) %collective-permute-start.14) | collective-permute-done | bytes 147488 | tf_op jit(solution)/shard_map/ppermute | solution.py:1149
  87.1 0.8 collective-permute-start.16
  87.9 3.6 %collective-permute-done.16.refs_6_ = bf16[48,768]{1,0:T(8,128)(2,1)S(1)} collective-permute-done((bf16[48,768]{1,0:T(8,128)(2,1)S(1)}, bf16[48,768]{1,0:T(8,128)(2,1)S(1)}, u32[]{:S(2)}, u32[]{:S(2)}) %collective-permute-start.16) | collective-permute-done | bytes 73760 | tf_op jit(solution)/shard_map/ppermute | solution.py:1149
  91.8 1.3 %collective-permute-done.17.refs_2_ = bf16[48,896]{1,0:T(8,128)(2,1)S(1)} collective-permute-done((bf16[48,896]{1,0:T(8,128)(2,1)S(1)}, bf16[48,896]{1,0:T(8,128)(2,1)S(1)}, u32[]{:S(2)}, u32[]{:S(2)}) %collective-permute-start.17) | collective-permute-done | bytes 86048 | tf_op jit(solution)/shard_map/ppermute | solution.py:1149
  93.0 0.8 final.1
  (39 shorter events, 3.0 us)
Async XLA Ops:
  0.6 1.6 %copy-start.4 = (bf16[1,384,768]{2,1,0:T(8,128)(2,1)S(1)}, bf16[1,384,768]{2,1,0:T(8,128)(2,1)}, u32[]{:S(2)}) copy-start(bf16[1,384,768]{2,1,0:T(8,128)(2,1)} %param.11) | copy-start | bytes 1769476
  0.6 1.7 %copy-start.5 = (bf16[1,768,384]{2,1,0:T(8,128)(2,1)S(1)}, bf16[1,768,384]{2,1,0:T(8,128)(2,1)}, u32[]{:S(2)}) copy-start(bf16[1,768,384]{2,1,0:T(8,128)(2,1)} %param.12) | copy-start | bytes 1769476
  0.7 2.4 %copy-start.2 = (bf16[4,16,16,384]{3,2,1,0:T(8,128)(2,1)S(1)}, bf16[4,16,16,384]{3,2,1,0:T(8,128)(2,1)}, u32[]{:S(2)}) copy-start(bf16[4,16,16,384]{3,2,1,0:T(8,128)(2,1)} %param.7) | copy-start | bytes 2359300
  1.7 1.3 %copy-start.3 = (bf16[4,16,16,384]{3,2,1,0:T(8,128)(2,1)S(1)}, bf16[4,16,16,384]{3,2,1,0:T(8,128)(2,1)}, u32[]{:S(2)}) copy-start(bf16[4,16,16,384]{3,2,1,0:T(8,128)(2,1)} %param.8) | copy-start | bytes 2359300
  1.8 1.5 %collective-permute-start = (f32[56,384]{1,0:T(8,128)S(1)}, f32[56,384]{1,0:T(8,128)S(1)}, u32[]{:S(2)}, u32[]{:S(2)}) collective-permute-start(f32[56,384]{1,0:T(8,128)S(1)} %parameters.1.rest_0_.refs_3_.refs_12_), channel_id=1, source_target_pairs={{0,1},{1,0},{2,3},{3,2},{4,5},{5,4},{6,7},{7,6},{8,9},{9,8},{10,11... | collective-permute-start | bytes 258056 | tf_op jit(solution)/shard_map/ppermute | solution.py:1149
  2.3 3.1 %collective-permute-start.1 = (bf16[384,768]{1,0:T(8,128)(2,1)S(1)}, bf16[384,768]{1,0:T(8,128)(2,1)}, u32[]{:S(2)}, u32[]{:S(2)}) collective-permute-start(bf16[384,768]{1,0:T(8,128)(2,1)S(1)} %bitcast.37), channel_id=1, source_target_pairs={{0,1},{1,0},{2,3},{3,2},{4,5},{5,4},{6,7},{7,6},{8,9},{9,8},{10,11... | collective-permute-start | bytes 1769480 | tf_op jit(solution)/shard_map/ppermute | solution.py:1149
  2.4 3.1 %collective-permute-start.2 = (bf16[768,384]{1,0:T(8,128)(2,1)S(1)}, bf16[768,384]{1,0:T(8,128)(2,1)}, u32[]{:S(2)}, u32[]{:S(2)}) collective-permute-start(bf16[768,384]{1,0:T(8,128)(2,1)S(1)} %bitcast.44), channel_id=1, source_target_pairs={{0,1},{1,0},{2,3},{3,2},{4,5},{5,4},{6,7},{7,6},{8,9},{9,8},{10,11... | collective-permute-start | bytes 1769480 | tf_op jit(solution)/shard_map/ppermute | solution.py:1149
  10.7 13.5 %collective-permute-start.5 = (bf16[16,16,384]{2,1,0:T(8,128)(2,1)S(1)}, bf16[16,16,384]{2,1,0:T(8,128)(2,1)S(1)}, u32[]{:S(2)}, u32[]{:S(2)}) collective-permute-start(bf16[16,16,384]{2,1,0:T(8,128)(2,1)S(1)} %get-tuple-element.105), channel_id=1, source_target_pairs={{0,2},{1,3},{4,6},{5,7},{8,10},{9,11},{12,14},{13,15},{16,18},{17,... | collective-permute-start | bytes 589832 | tf_op jit(solution)/shard_map/ppermute | solution.py:1154
  22.8 5.8 %collective-permute-start.3 = (bf16[16,16,384]{2,1,0:T(8,128)(2,1)S(1)}, bf16[16,16,384]{2,1,0:T(8,128)(2,1)S(1)}, u32[]{:S(2)}, u32[]{:S(2)}) collective-permute-start(bf16[16,16,384]{2,1,0:T(8,128)(2,1)S(1)} %get-tuple-element.94), channel_id=1, source_target_pairs={{0,2},{1,3},{4,6},{5,7},{8,10},{9,11},{12,14},{13,15},{16,18},{17,... | collective-permute-start | bytes 589832 | tf_op jit(solution)/shard_map/ppermute | solution.py:1154
  24.9 14.2 %collective-permute-start.6 = (bf16[16,16,384]{2,1,0:T(8,128)(2,1)S(1)}, bf16[16,16,384]{2,1,0:T(8,128)(2,1)S(1)}, u32[]{:S(2)}, u32[]{:S(2)}) collective-permute-start(bf16[16,16,384]{2,1,0:T(8,128)(2,1)S(1)} %get-tuple-element.106), channel_id=1, source_target_pairs={{2,0},{3,1},{6,4},{7,5},{10,8},{11,9},{14,12},{15,13},{18,16},{19,... | collective-permute-start | bytes 589832 | tf_op jit(solution)/shard_map/ppermute | solution.py:1154
  29.5 22.1 %collective-permute-start.4 = (bf16[16,16,384]{2,1,0:T(8,128)(2,1)S(1)}, bf16[16,16,384]{2,1,0:T(8,128)(2,1)S(1)}, u32[]{:S(2)}, u32[]{:S(2)}) collective-permute-start(bf16[16,16,384]{2,1,0:T(8,128)(2,1)S(1)} %get-tuple-element.95), channel_id=1, source_target_pairs={{2,0},{3,1},{6,4},{7,5},{10,8},{11,9},{14,12},{15,13},{18,16},{19,... | collective-permute-start | bytes 589832 | tf_op jit(solution)/shard_map/ppermute | solution.py:1154
  61.9 2.3 %collective-permute-start.7 = (bf16[384,768]{1,0:T(8,128)(2,1)}, bf16[384,768]{1,0:T(8,128)(2,1)S(1)}, u32[]{:S(2)}, u32[]{:S(2)}) collective-permute-start(bf16[384,768]{1,0:T(8,128)(2,1)} %get-tuple-element.154), channel_id=1, source_target_pairs={{0,1},{1,0},{2,3},{3,2},{4,5},{5,4},{6,7},{7,6},{8,9},{9,8},{10,11... | collective-permute-start | bytes 1769480 | tf_op jit(solution)/shard_map/ppermute | solution.py:1149
  62.0 5.1 %collective-permute-start.12 = (bf16[384,768]{1,0:T(8,128)(2,1)}, bf16[384,768]{1,0:T(8,128)(2,1)S(1)}, u32[]{:S(2)}, u32[]{:S(2)}) collective-permute-start(bf16[384,768]{1,0:T(8,128)(2,1)} %get-tuple-element.163), channel_id=1, source_target_pairs={{0,1},{1,0},{2,3},{3,2},{4,5},{5,4},{6,7},{7,6},{8,9},{9,8},{10,11... | collective-permute-start | bytes 1769480 | tf_op jit(solution)/shard_map/ppermute | solution.py:1149
  64.2 1.1 %copy-start.1 = (bf16[384,768]{1,0:T(8,128)(2,1)S(1)}, bf16[384,768]{1,0:T(8,128)(2,1)}, u32[]{:S(2)}) copy-start(bf16[384,768]{1,0:T(8,128)(2,1)} %get-tuple-element.153) | copy-start | bytes 1769476
  65.2 1.8 %copy-start = (bf16[384,768]{1,0:T(8,128)(2,1)S(1)}, bf16[384,768]{1,0:T(8,128)(2,1)}, u32[]{:S(2)}) copy-start(bf16[384,768]{1,0:T(8,128)(2,1)} %get-tuple-element.162) | copy-start | bytes 1769476
  65.4 10.2 %collective-permute-start.8 = (bf16[4,48,896]{2,1,0:T(8,128)(2,1)S(1)}, bf16[4,48,896]{2,1,0:T(8,128)(2,1)S(1)}, u32[]{:S(2)}, u32[]{:S(2)}) collective-permute-start(bf16[4,48,896]{2,1,0:T(8,128)(2,1)S(1)} %get-tuple-element.157), channel_id=1, source_target_pairs={{0,4},{1,5},{2,6},{3,7},{4,0},{5,1},{6,2},{7,3},{8,12},{9,13},{10,... | collective-permute-start | bytes 1032200 | tf_op jit(solution)/shard_map/ppermute | solution.py:1149
  67.7 12.5 %collective-permute-start.13 = (bf16[2,48,768]{2,1,0:T(8,128)(2,1)S(1)}, bf16[2,48,768]{2,1,0:T(8,128)(2,1)S(1)}, u32[]{:S(2)}, u32[]{:S(2)}) collective-permute-start(bf16[2,48,768]{2,1,0:T(8,128)(2,1)S(1)} %get-tuple-element.165), channel_id=1, source_target_pairs={{0,8},{1,9},{2,10},{3,11},{4,12},{5,13},{6,14},{7,15},{8,0},{9,1},... | collective-permute-start | bytes 442376 | tf_op jit(solution)/shard_map/ppermute | solution.py:1149
  69.4 17.7 %collective-permute-start.14 = (bf16[2,48,768]{2,1,0:T(8,128)(2,1)S(1)}, bf16[2,48,768]{2,1,0:T(8,128)(2,1)S(1)}, u32[]{:S(2)}, u32[]{:S(2)}) collective-permute-start(bf16[2,48,768]{2,1,0:T(8,128)(2,1)S(1)} %get-tuple-element.166), channel_id=1, source_target_pairs={{0,16},{1,17},{2,18},{3,19},{4,20},{5,21},{6,22},{7,23},{8,24},{9,... | collective-permute-start | bytes 442376 | tf_op jit(solution)/shard_map/ppermute | solution.py:1149
  72.0 15.1 %collective-permute-start.15 = (bf16[2,48,768]{2,1,0:T(8,128)(2,1)S(1)}, bf16[2,48,768]{2,1,0:T(8,128)(2,1)S(1)}, u32[]{:S(2)}, u32[]{:S(2)}) collective-permute-start(bf16[2,48,768]{2,1,0:T(8,128)(2,1)S(1)} %get-tuple-element.167), channel_id=1, source_target_pairs={{0,24},{1,25},{2,26},{3,27},{4,28},{5,29},{6,30},{7,31},{8,16},{9,... | collective-permute-start | bytes 442376 | tf_op jit(solution)/shard_map/ppermute | solution.py:1149
  76.2 15.4 %collective-permute-start.10 = (bf16[48,896]{1,0:T(8,128)(2,1)S(1)}, bf16[48,896]{1,0:T(8,128)(2,1)S(1)}, u32[]{:S(2)}, u32[]{:S(2)}) collective-permute-start(bf16[48,896]{1,0:T(8,128)(2,1)S(1)} %get-tuple-element.160), channel_id=1, source_target_pairs={{0,16},{1,17},{2,18},{3,19},{4,20},{5,21},{6,22},{7,23},{8,24},{9,... | collective-permute-start | bytes 258056 | tf_op jit(solution)/shard_map/ppermute | solution.py:1149
  78.8 12.8 %collective-permute-start.11 = (bf16[48,896]{1,0:T(8,128)(2,1)S(1)}, bf16[48,896]{1,0:T(8,128)(2,1)S(1)}, u32[]{:S(2)}, u32[]{:S(2)}) collective-permute-start(bf16[48,896]{1,0:T(8,128)(2,1)S(1)} %get-tuple-element.161), channel_id=1, source_target_pairs={{0,24},{1,25},{2,26},{3,27},{4,28},{5,29},{6,30},{7,31},{8,16},{9,... | collective-permute-start | bytes 258056 | tf_op jit(solution)/shard_map/ppermute | solution.py:1149
  80.2 11.4 %collective-permute-start.9 = (bf16[48,896]{1,0:T(8,128)(2,1)S(1)}, bf16[48,896]{1,0:T(8,128)(2,1)S(1)}, u32[]{:S(2)}, u32[]{:S(2)}) collective-permute-start(bf16[48,896]{1,0:T(8,128)(2,1)S(1)} %get-tuple-element.159), channel_id=1, source_target_pairs={{0,8},{1,9},{2,10},{3,11},{4,12},{5,13},{6,14},{7,15},{8,0},{9,1},... | collective-permute-start | bytes 258056 | tf_op jit(solution)/shard_map/ppermute | solution.py:1149
  87.1 4.4 %collective-permute-start.16 = (bf16[48,768]{1,0:T(8,128)(2,1)S(1)}, bf16[48,768]{1,0:T(8,128)(2,1)S(1)}, u32[]{:S(2)}, u32[]{:S(2)}) collective-permute-start(bf16[48,768]{1,0:T(8,128)(2,1)S(1)} %get-tuple-element.169), channel_id=1, source_target_pairs={{0,4},{1,5},{2,6},{3,7},{4,0},{5,1},{6,2},{7,3},{8,12},{9,13},{10,... | collective-permute-start | bytes 221192 | tf_op jit(solution)/shard_map/ppermute | solution.py:1149
  91.7 1.3 %collective-permute-start.17 = (bf16[48,896]{1,0:T(8,128)(2,1)S(1)}, bf16[48,896]{1,0:T(8,128)(2,1)S(1)}, u32[]{:S(2)}, u32[]{:S(2)}) collective-permute-start(bf16[48,896]{1,0:T(8,128)(2,1)S(1)} %get-tuple-element.171), channel_id=1, source_target_pairs={{0,1},{1,0},{2,3},{3,2},{4,5},{5,4},{6,7},{7,6},{8,9},{9,8},{10,11... | collective-permute-start | bytes 258056 | tf_op jit(solution)/shard_map/ppermute | solution.py:1149

commit v5 on v4

--- a/solution.py
+++ b/solution.py
@@ -962,6 +962,24 @@
     return named_call("pair_back", body, ins, outs, scratch, 9)
 
 
+def brought_kernel(source_ref, out_ref, sem):
+    copy = pltpu.make_async_copy(source_ref, out_ref, sem)
+    copy.start()
+    copy.wait()
+
+
+def brought(value):
+    return pl.pallas_call(
+        brought_kernel,
+        in_specs=[pl.BlockSpec(memory_space=pl.ANY)],
+        out_shape=jax.ShapeDtypeStruct(value.shape, value.dtype),
+        scratch_shapes=[pltpu.SemaphoreType.DMA(())],
+        compiler_params=vmem(LIMIT),
+        name="brought",
+        cost_estimate=estimate(1.1),
+    )(pltpu.with_memory_space_constraint(value, pltpu.HBM))
+
+
 def add(a, b):
     return a.astype(jnp.float32) + b.astype(jnp.float32)
 
@@ -1197,7 +1215,7 @@
         own, *others = to_depths(levels, mine, got)
         return [own] + [swap(v, z=flip) for v, flip in zip(others, (1, 2, 3))]
 
-    low = along_y(grads.keep0, core0, grads.packed)
+    low = along_y(brought(grads.keep0), core0, grads.packed)
     own, *others = split_depths(levels, grads.keep1, core1, low[:1])
     parts = [own] + [swap(v, z=flip) for v, flip in zip(others, (1, 2, 3))]
     across, mine = join_depths(sides, parts)

time: 95.1 us -> 94.1 us (0.989)
  waiting for transfers between devices: 29.4 us -> 28.3 us
  local copies, waits for them, and re-layouts: 1.35 us -> 0.28 us
  Pallas kernels: 40.7 us -> 41.7 us
    ppermute x14, waiting for transfers between devices: 16.6 us -> 15.6 us  [swap(): return lax.ppermute(value, ('dp', 'segment'), partners((z, y, x, c)))]
    pallas_call x0 -> x1, Pallas kernels: none -> 1.07 us  [brought(): pl.pallas_call(brought_kernel, in_specs=[pl.BlockSpec(memory_space=pl.ANY...]
    unnamed x12 -> x10, local copies, waits for them, and re-layouts: 1.09 us -> 0.03 us
  transfers between devices with their start and end apart: 18 -> 18, of which waited for: 8 -> 8; matrix products, arithmetic and copies ran while one was open for 1% -> 1% of each run, Pallas kernels for 25% -> 26%
where the time goes in v5:
time: 94.1 us; the launch traced here: 92.7 us
  Pallas kernels  41.7 us (44%)
  waiting for transfers between devices  28.3 us (30%)
  starting transfers between devices  21.3 us (23%)
    pallas_call x7, Pallas kernels, named_call(): pl.pallas_call(kernel, in_specs=[pl.BlockSpec(memory_space=spaces[kind])...  32.8 us
    ppermute x14, waiting for transfers between devices, swap(): return lax.ppermute(value, ('dp', 'segment'), partners((z, y, x, c)))  15.6 us
    ppermute x4, waiting for transfers between devices, along_x(): return lax.ppermute(value, ('dp', 'segment'), pairs)  12.7 us
    ppermute x14, starting transfers between devices, swap(): return lax.ppermute(value, ('dp', 'segment'), partners((z, y, x, c)))  12.7 us
    ppermute x4, starting transfers between devices, along_x(): return lax.ppermute(value, ('dp', 'segment'), pairs)  8.62 us
    pallas_call x2, Pallas kernels, conv_norm(): pl.pallas_call(functools.partial(conv_norm_kernel, len(smalls)), in_specs...  4.37 us
    pallas_call x6, Pallas kernels, small_call(): pl.pallas_call(body, in_specs=[pl.BlockSpec(memory_space=pltpu.SMEM)] + [...  2.4 us
  transfers between devices with their start and end apart: 18, of which 8 were waited for; matrix products, arithmetic and copies ran while one was open for 1% of the time, Pallas kernels for 26%

profile of v5, /device:TPU:0, one launch (start us, length us, event | category | flops | bytes accessed | tf_op | source)
XLA Modules:
  0.0 92.7 jit_solution(6229927692357287462)
XLA Ops:
  0.7 1.1 %parameters.1.rest_0_.refs_3_.refs_12_ = f32[56,384]{1,0:T(8,128)S(1)} custom-call(f32[49,1,384]{2,1,0:T(1,128)} %bitcast.45, f32[1,384]{1,0:T(1,128)} %gain_ref.1, f32[1,384]{1,0:T(1,128)} %scale_ref.1), custom_call_target="tpu_custom_call" | custom-call | flops 550000000 | bytes 1800000 | tf_op jit(solution)/shard_map/parameters/pallas_call | solution.py:102
  3.2 2.2 %conv_norm.2 = (bf16[256,384]{1,0:T(8,128)(2,1)S(1)}, bf16[256,384]{1,0:T(8,128)(2,1)S(1)}, f32[256,128]{1,0:T(8,128)S(1)}) custom-call(s32[2]{0:T(128)S(1)} %pad_add_fusion.2.sel_ref, bf16[16,16,384]{2,1,0:T(8,128)(2,1)S(1)} %get-tuple-element.179.x_ref.refs_1_.refs_2_, f32[56,384]{1,0:T(8,128)S(1)} %parameters.1.rest_0_.refs_3_.refs_12_, ...), custom_call_target="tpu_custom_call" | custom-call | flops 2200000000 | bytes 7200000 | tf_op jit(solution)/shard_map/conv_norm/pallas_call | solution.py:145
  5.4 5.2 %pair_forward.2 = (bf16[16,16,384]{2,1,0:T(8,128)(2,1)S(1)}, bf16[16,16,384]{2,1,0:T(8,128)(2,1)S(1)}, bf16[256,384]{1,0:T(8,128)(2,1)S(1)}, f32[256,128]{1,0:T(...) custom-call(s32[5]{0:T(128)S(1)} %stack.50.refs_0_, ...), custom_call_target="tpu_custom_call" | custom-call | flops 8249999872 | bytes 27000000 | tf_op jit(solution)/shard_map/pair_forward/pallas_call | solution.py:626
  10.7 4.7 %collective-permute-start.5 = (bf16[16,16,384]{2,1,0:T(8,128)(2,1)S(1)}, bf16[16,16,384]{2,1,0:T(8,128)(2,1)S(1)}, u32[]{:S(2)}, u32[]{:S(2)}) collective-permute-start(bf16[16,16,384]{2,1,0:T(8,128)(2,1)S(1)} %get-tuple-element.105), channel_id=1, source_target_pairs={{0,2},{1,3},{4,6},{5,7},{8,10},{9,11},{12,14},{13,15},{16,18},{17,... | collective-permute-start | bytes 589832 | tf_op jit(solution)/shard_map/ppermute | solution.py:1172
  15.4 2.2 %conv_norm.3 = (bf16[256,384]{1,0:T(8,128)(2,1)S(1)}, bf16[256,384]{1,0:T(8,128)(2,1)S(1)}, f32[256,128]{1,0:T(8,128)S(1)}) custom-call(s32[2]{0:T(128)S(1)} %pad_add_fusion.1.sel_ref, bf16[16,16,384]{2,1,0:T(8,128)(2,1)S(1)} %get-tuple-element.180.x_ref.refs_1_.refs_2_, f32[56,384]{1,0:T(8,128)S(1)} %parameters.1.rest_0_.refs_3_.refs_12_, ...), custom_call_target="tpu_custom_call" | custom-call | flops 2200000000 | bytes 7200000 | tf_op jit(solution)/shard_map/conv_norm/pallas_call | solution.py:145
  17.6 5.2 %pair_forward.3 = (bf16[16,16,384]{2,1,0:T(8,128)(2,1)S(1)}, bf16[16,16,384]{2,1,0:T(8,128)(2,1)S(1)}, bf16[256,384]{1,0:T(8,128)(2,1)S(1)}, f32[256,128]{1,0:T(...) custom-call(s32[5]{0:T(128)S(1)} %stack.51.refs_0_, ...), custom_call_target="tpu_custom_call" | custom-call | flops 8249999872 | bytes 27000000 | tf_op jit(solution)/shard_map/pair_forward/pallas_call | solution.py:626
  22.8 1.3 %collective-permute-start.3 = (bf16[16,16,384]{2,1,0:T(8,128)(2,1)S(1)}, bf16[16,16,384]{2,1,0:T(8,128)(2,1)S(1)}, u32[]{:S(2)}, u32[]{:S(2)}) collective-permute-start(bf16[16,16,384]{2,1,0:T(8,128)(2,1)S(1)} %get-tuple-element.94), channel_id=1, source_target_pairs={{0,2},{1,3},{4,6},{5,7},{8,10},{9,11},{12,14},{13,15},{16,18},{17,... | collective-permute-start | bytes 589832 | tf_op jit(solution)/shard_map/ppermute | solution.py:1172
  24.1 0.7 pair_map.3
  24.9 1.3 %collective-permute-start.6 = (bf16[16,16,384]{2,1,0:T(8,128)(2,1)S(1)}, bf16[16,16,384]{2,1,0:T(8,128)(2,1)S(1)}, u32[]{:S(2)}, u32[]{:S(2)}) collective-permute-start(bf16[16,16,384]{2,1,0:T(8,128)(2,1)S(1)} %get-tuple-element.106), channel_id=1, source_target_pairs={{2,0},{3,1},{6,4},{7,5},{10,8},{11,9},{14,12},{15,13},{18,16},{19,... | collective-permute-start | bytes 589832 | tf_op jit(solution)/shard_map/ppermute | solution.py:1172
  26.2 2.5 %collective-permute-done.3.refs_1_.refs_15_ = bf16[16,16,384]{2,1,0:T(8,128)(2,1)S(1)} collective-permute-done((bf16[16,16,384]{2,1,0:T(8,128)(2,1)S(1)}, bf16[16,16,384]{2,1,0:T(8,128)(2,1)S(1)}, u32[]{:S(2)}, u32[]{:S(2)}) %collective-permute-start.3) | collective-permute-done | bytes 196640 | tf_op jit(solution)/shard_map/ppermute | solution.py:1172
  28.6 0.9 pair_map.2
  29.5 1.3 %collective-permute-start.4 = (bf16[16,16,384]{2,1,0:T(8,128)(2,1)S(1)}, bf16[16,16,384]{2,1,0:T(8,128)(2,1)S(1)}, u32[]{:S(2)}, u32[]{:S(2)}) collective-permute-start(bf16[16,16,384]{2,1,0:T(8,128)(2,1)S(1)} %get-tuple-element.95), channel_id=1, source_target_pairs={{2,0},{3,1},{6,4},{7,5},{10,8},{11,9},{14,12},{15,13},{18,16},{19,... | collective-permute-start | bytes 589832 | tf_op jit(solution)/shard_map/ppermute | solution.py:1172
  30.8 0.9 pair_grads.1
  31.7 7.4 %collective-permute-done.6.refs_1_ = bf16[16,16,384]{2,1,0:T(8,128)(2,1)S(1)} collective-permute-done((bf16[16,16,384]{2,1,0:T(8,128)(2,1)S(1)}, bf16[16,16,384]{2,1,0:T(8,128)(2,1)S(1)}, u32[]{:S(2)}, u32[]{:S(2)}) %collective-permute-start.6) | collective-permute-done | bytes 196640 | tf_op jit(solution)/shard_map/ppermute | solution.py:1172
  39.1 9.7 %pair_back.2 = (bf16[384,768]{1,0:T(8,128)(2,1)}, bf16[384,768]{1,0:T(8,128)(2,1)}, bf16[384,768]{1,0:T(8,128)(2,1)}, bf16[384,768]{1,0:T(8,128)(2,1)}, f32[64,384]{1,0:T(8,128)S(1)}, /*index=5*/f32[64,384]{1,0:T(8,128)S(1)}) custom-call(s32[5]{0:T(128)S(1)} %stack.50.refs_0_, bf16[16,16,384]{2,1,0:T(8,128)(2,1)S(1)} %collective-permute-done.6.refs_1_, ...), custom_call_target="tpu_custom_call" | custom-call | flops 9900000256 | bytes 32400000 | tf_op jit(solution)/shard_map/pair_back/pallas_call | solution.py:626
  48.8 2.9 %collective-permute-done.4.refs_1_ = bf16[16,16,384]{2,1,0:T(8,128)(2,1)S(1)} collective-permute-done((bf16[16,16,384]{2,1,0:T(8,128)(2,1)S(1)}, bf16[16,16,384]{2,1,0:T(8,128)(2,1)S(1)}, u32[]{:S(2)}, u32[]{:S(2)}) %collective-permute-start.4) | collective-permute-done | bytes 196640 | tf_op jit(solution)/shard_map/ppermute | solution.py:1172
  51.6 10.3 %pair_back.3 = (bf16[384,768]{1,0:T(8,128)(2,1)}, bf16[384,768]{1,0:T(8,128)(2,1)}, bf16[384,768]{1,0:T(8,128)(2,1)}, bf16[384,768]{1,0:T(8,128)(2,1)}, bf16[384,128]{1,0:T(8,128)(2,1)S(1)}) custom-call(s32[5]{0:T(128)S(1)} %stack.50.refs_0_, bf16[16,16,384]{2,1,0:T(8,128)(2,1)S(1)} %collective-permute-done.4.refs_1_, ...), custom_call_target="tpu_custom_call" | custom-call | flops 9900000256 | bytes 32400000 | tf_op jit(solution)/shard_map/pair_back/pallas_call | solution.py:626
  62.5 1.1 %brought.1 = bf16[384,768]{1,0:T(8,128)(2,1)S(1)} custom-call(bf16[384,768]{1,0:T(8,128)(2,1)} %get-tuple-element.153.source_ref), custom_call_target="tpu_custom_call" | custom-call | flops 1210000000 | bytes 3960000 | tf_op jit(solution)/shard_map/brought/pallas_call | solution.py:972
  63.5 0.6 collective-permute-done.7
  64.3 1.6 %collective-permute-start.8 = (bf16[4,48,896]{2,1,0:T(8,128)(2,1)S(1)}, bf16[4,48,896]{2,1,0:T(8,128)(2,1)S(1)}, u32[]{:S(2)}, u32[]{:S(2)}) collective-permute-start(bf16[4,48,896]{2,1,0:T(8,128)(2,1)S(1)} %get-tuple-element.157), channel_id=1, source_target_pairs={{0,4},{1,5},{2,6},{3,7},{4,0},{5,1},{6,2},{7,3},{8,12},{9,13},{10,... | collective-permute-start | bytes 1032200 | tf_op jit(solution)/shard_map/ppermute | solution.py:1167
  66.0 0.7 split_depths.1
  66.7 1.6 %collective-permute-start.13 = (bf16[2,48,768]{2,1,0:T(8,128)(2,1)S(1)}, bf16[2,48,768]{2,1,0:T(8,128)(2,1)S(1)}, u32[]{:S(2)}, u32[]{:S(2)}) collective-permute-start(bf16[2,48,768]{2,1,0:T(8,128)(2,1)S(1)} %get-tuple-element.165), channel_id=1, source_target_pairs={{0,8},{1,9},{2,10},{3,11},{4,12},{5,13},{6,14},{7,15},{8,0},{9,1},... | collective-permute-start | bytes 442376 | tf_op jit(solution)/shard_map/ppermute | solution.py:1167
  68.3 2.6 %collective-permute-start.14 = (bf16[2,48,768]{2,1,0:T(8,128)(2,1)S(1)}, bf16[2,48,768]{2,1,0:T(8,128)(2,1)S(1)}, u32[]{:S(2)}, u32[]{:S(2)}) collective-permute-start(bf16[2,48,768]{2,1,0:T(8,128)(2,1)S(1)} %get-tuple-element.166), channel_id=1, source_target_pairs={{0,16},{1,17},{2,18},{3,19},{4,20},{5,21},{6,22},{7,23},{8,24},{9,... | collective-permute-start | bytes 442376 | tf_op jit(solution)/shard_map/ppermute | solution.py:1167
  71.1 3.4 %collective-permute-done.8.refs_2_ = bf16[4,48,896]{2,1,0:T(8,128)(2,1)S(1)} collective-permute-done((bf16[4,48,896]{2,1,0:T(8,128)(2,1)S(1)}, bf16[4,48,896]{2,1,0:T(8,128)(2,1)S(1)}, u32[]{:S(2)}, u32[]{:S(2)}) %collective-permute-start.8) | collective-permute-done | bytes 344096 | tf_op jit(solution)/shard_map/ppermute | solution.py:1167
  74.5 0.6 to_depths.1
  75.1 2.7 %collective-permute-start.10 = (bf16[48,896]{1,0:T(8,128)(2,1)S(1)}, bf16[48,896]{1,0:T(8,128)(2,1)S(1)}, u32[]{:S(2)}, u32[]{:S(2)}) collective-permute-start(bf16[48,896]{1,0:T(8,128)(2,1)S(1)} %get-tuple-element.160), channel_id=1, source_target_pairs={{0,16},{1,17},{2,18},{3,19},{4,20},{5,21},{6,22},{7,23},{8,24},{9,... | collective-permute-start | bytes 258056 | tf_op jit(solution)/shard_map/ppermute | solution.py:1167
  77.8 1.3 %collective-permute-start.11 = (bf16[48,896]{1,0:T(8,128)(2,1)S(1)}, bf16[48,896]{1,0:T(8,128)(2,1)S(1)}, u32[]{:S(2)}, u32[]{:S(2)}) collective-permute-start(bf16[48,896]{1,0:T(8,128)(2,1)S(1)} %get-tuple-element.161), channel_id=1, source_target_pairs={{0,24},{1,25},{2,26},{3,27},{4,28},{5,29},{6,30},{7,31},{8,16},{9,... | collective-permute-start | bytes 258056 | tf_op jit(solution)/shard_map/ppermute | solution.py:1167
  79.3 6.6 %collective-permute-done.14.refs_3_ = bf16[2,48,768]{2,1,0:T(8,128)(2,1)S(1)} collective-permute-done((bf16[2,48,768]{2,1,0:T(8,128)(2,1)S(1)}, bf16[2,48,768]{2,1,0:T(8,128)(2,1)S(1)}, u32[]{:S(2)}, u32[]{:S(2)}) %collective-permute-start.14) | collective-permute-done | bytes 147488 | tf_op jit(solution)/shard_map/ppermute | solution.py:1167
  86.1 0.8 collective-permute-start.16
  86.9 3.6 %collective-permute-done.16.refs_6_ = bf16[48,768]{1,0:T(8,128)(2,1)S(1)} collective-permute-done((bf16[48,768]{1,0:T(8,128)(2,1)S(1)}, bf16[48,768]{1,0:T(8,128)(2,1)S(1)}, u32[]{:S(2)}, u32[]{:S(2)}) %collective-permute-start.16) | collective-permute-done | bytes 73760 | tf_op jit(solution)/shard_map/ppermute | solution.py:1167
  90.7 1.3 %collective-permute-done.17.refs_2_ = bf16[48,896]{1,0:T(8,128)(2,1)S(1)} collective-permute-done((bf16[48,896]{1,0:T(8,128)(2,1)S(1)}, bf16[48,896]{1,0:T(8,128)(2,1)S(1)}, u32[]{:S(2)}, u32[]{:S(2)}) %collective-permute-start.17) | collective-permute-done | bytes 86048 | tf_op jit(solution)/shard_map/ppermute | solution.py:1167
  92.0 0.8 final.1
  (38 shorter events, 3.0 us)
Async XLA Ops:
  0.6 1.6 %copy-start.3 = (bf16[1,384,768]{2,1,0:T(8,128)(2,1)S(1)}, bf16[1,384,768]{2,1,0:T(8,128)(2,1)}, u32[]{:S(2)}) copy-start(bf16[1,384,768]{2,1,0:T(8,128)(2,1)} %param.11) | copy-start | bytes 1769476
  0.6 1.7 %copy-start.4 = (bf16[1,768,384]{2,1,0:T(8,128)(2,1)S(1)}, bf16[1,768,384]{2,1,0:T(8,128)(2,1)}, u32[]{:S(2)}) copy-start(bf16[1,768,384]{2,1,0:T(8,128)(2,1)} %param.12) | copy-start | bytes 1769476
  0.7 2.4 %copy-start.1 = (bf16[4,16,16,384]{3,2,1,0:T(8,128)(2,1)S(1)}, bf16[4,16,16,384]{3,2,1,0:T(8,128)(2,1)}, u32[]{:S(2)}) copy-start(bf16[4,16,16,384]{3,2,1,0:T(8,128)(2,1)} %param.7) | copy-start | bytes 2359300
  1.7 1.3 %copy-start.2 = (bf16[4,16,16,384]{3,2,1,0:T(8,128)(2,1)S(1)}, bf16[4,16,16,384]{3,2,1,0:T(8,128)(2,1)}, u32[]{:S(2)}) copy-start(bf16[4,16,16,384]{3,2,1,0:T(8,128)(2,1)} %param.8) | copy-start | bytes 2359300
  1.8 1.5 %collective-permute-start = (f32[56,384]{1,0:T(8,128)S(1)}, f32[56,384]{1,0:T(8,128)S(1)}, u32[]{:S(2)}, u32[]{:S(2)}) collective-permute-start(f32[56,384]{1,0:T(8,128)S(1)} %parameters.1.rest_0_.refs_3_.refs_12_), channel_id=1, source_target_pairs={{0,1},{1,0},{2,3},{3,2},{4,5},{5,4},{6,7},{7,6},{8,9},{9,8},{10,11... | collective-permute-start | bytes 258056 | tf_op jit(solution)/shard_map/ppermute | solution.py:1167
  2.3 3.1 %collective-permute-start.1 = (bf16[384,768]{1,0:T(8,128)(2,1)S(1)}, bf16[384,768]{1,0:T(8,128)(2,1)}, u32[]{:S(2)}, u32[]{:S(2)}) collective-permute-start(bf16[384,768]{1,0:T(8,128)(2,1)S(1)} %bitcast.37), channel_id=1, source_target_pairs={{0,1},{1,0},{2,3},{3,2},{4,5},{5,4},{6,7},{7,6},{8,9},{9,8},{10,11... | collective-permute-start | bytes 1769480 | tf_op jit(solution)/shard_map/ppermute | solution.py:1167
  2.4 3.1 %collective-permute-start.2 = (bf16[768,384]{1,0:T(8,128)(2,1)S(1)}, bf16[768,384]{1,0:T(8,128)(2,1)}, u32[]{:S(2)}, u32[]{:S(2)}) collective-permute-start(bf16[768,384]{1,0:T(8,128)(2,1)S(1)} %bitcast.44), channel_id=1, source_target_pairs={{0,1},{1,0},{2,3},{3,2},{4,5},{5,4},{6,7},{7,6},{8,9},{9,8},{10,11... | collective-permute-start | bytes 1769480 | tf_op jit(solution)/shard_map/ppermute | solution.py:1167
  10.7 13.5 %collective-permute-start.5 = (bf16[16,16,384]{2,1,0:T(8,128)(2,1)S(1)}, bf16[16,16,384]{2,1,0:T(8,128)(2,1)S(1)}, u32[]{:S(2)}, u32[]{:S(2)}) collective-permute-start(bf16[16,16,384]{2,1,0:T(8,128)(2,1)S(1)} %get-tuple-element.105), channel_id=1, source_target_pairs={{0,2},{1,3},{4,6},{5,7},{8,10},{9,11},{12,14},{13,15},{16,18},{17,... | collective-permute-start | bytes 589832 | tf_op jit(solution)/shard_map/ppermute | solution.py:1172
  22.8 5.8 %collective-permute-start.3 = (bf16[16,16,384]{2,1,0:T(8,128)(2,1)S(1)}, bf16[16,16,384]{2,1,0:T(8,128)(2,1)S(1)}, u32[]{:S(2)}, u32[]{:S(2)}) collective-permute-start(bf16[16,16,384]{2,1,0:T(8,128)(2,1)S(1)} %get-tuple-element.94), channel_id=1, source_target_pairs={{0,2},{1,3},{4,6},{5,7},{8,10},{9,11},{12,14},{13,15},{16,18},{17,... | collective-permute-start | bytes 589832 | tf_op jit(solution)/shard_map/ppermute | solution.py:1172
  24.9 14.2 %collective-permute-start.6 = (bf16[16,16,384]{2,1,0:T(8,128)(2,1)S(1)}, bf16[16,16,384]{2,1,0:T(8,128)(2,1)S(1)}, u32[]{:S(2)}, u32[]{:S(2)}) collective-permute-start(bf16[16,16,384]{2,1,0:T(8,128)(2,1)S(1)} %get-tuple-element.106), channel_id=1, source_target_pairs={{2,0},{3,1},{6,4},{7,5},{10,8},{11,9},{14,12},{15,13},{18,16},{19,... | collective-permute-start | bytes 589832 | tf_op jit(solution)/shard_map/ppermute | solution.py:1172
  29.5 22.1 %collective-permute-start.4 = (bf16[16,16,384]{2,1,0:T(8,128)(2,1)S(1)}, bf16[16,16,384]{2,1,0:T(8,128)(2,1)S(1)}, u32[]{:S(2)}, u32[]{:S(2)}) collective-permute-start(bf16[16,16,384]{2,1,0:T(8,128)(2,1)S(1)} %get-tuple-element.95), channel_id=1, source_target_pairs={{2,0},{3,1},{6,4},{7,5},{10,8},{11,9},{14,12},{15,13},{18,16},{19,... | collective-permute-start | bytes 589832 | tf_op jit(solution)/shard_map/ppermute | solution.py:1172
  61.9 2.3 %collective-permute-start.7 = (bf16[384,768]{1,0:T(8,128)(2,1)}, bf16[384,768]{1,0:T(8,128)(2,1)S(1)}, u32[]{:S(2)}, u32[]{:S(2)}) collective-permute-start(bf16[384,768]{1,0:T(8,128)(2,1)} %get-tuple-element.154), channel_id=1, source_target_pairs={{0,1},{1,0},{2,3},{3,2},{4,5},{5,4},{6,7},{7,6},{8,9},{9,8},{10,11... | collective-permute-start | bytes 1769480 | tf_op jit(solution)/shard_map/ppermute | solution.py:1167
  62.0 4.0 %collective-permute-start.12 = (bf16[384,768]{1,0:T(8,128)(2,1)}, bf16[384,768]{1,0:T(8,128)(2,1)S(1)}, u32[]{:S(2)}, u32[]{:S(2)}) collective-permute-start(bf16[384,768]{1,0:T(8,128)(2,1)} %get-tuple-element.163), channel_id=1, source_target_pairs={{0,1},{1,0},{2,3},{3,2},{4,5},{5,4},{6,7},{7,6},{8,9},{9,8},{10,11... | collective-permute-start | bytes 1769480 | tf_op jit(solution)/shard_map/ppermute | solution.py:1167
  64.2 1.8 %copy-start = (bf16[384,768]{1,0:T(8,128)(2,1)S(1)}, bf16[384,768]{1,0:T(8,128)(2,1)}, u32[]{:S(2)}) copy-start(bf16[384,768]{1,0:T(8,128)(2,1)} %get-tuple-element.162) | copy-start | bytes 1769476
  64.3 10.2 %collective-permute-start.8 = (bf16[4,48,896]{2,1,0:T(8,128)(2,1)S(1)}, bf16[4,48,896]{2,1,0:T(8,128)(2,1)S(1)}, u32[]{:S(2)}, u32[]{:S(2)}) collective-permute-start(bf16[4,48,896]{2,1,0:T(8,128)(2,1)S(1)} %get-tuple-element.157), channel_id=1, source_target_pairs={{0,4},{1,5},{2,6},{3,7},{4,0},{5,1},{6,2},{7,3},{8,12},{9,13},{10,... | collective-permute-start | bytes 1032200 | tf_op jit(solution)/shard_map/ppermute | solution.py:1167
  66.7 12.5 %collective-permute-start.13 = (bf16[2,48,768]{2,1,0:T(8,128)(2,1)S(1)}, bf16[2,48,768]{2,1,0:T(8,128)(2,1)S(1)}, u32[]{:S(2)}, u32[]{:S(2)}) collective-permute-start(bf16[2,48,768]{2,1,0:T(8,128)(2,1)S(1)} %get-tuple-element.165), channel_id=1, source_target_pairs={{0,8},{1,9},{2,10},{3,11},{4,12},{5,13},{6,14},{7,15},{8,0},{9,1},... | collective-permute-start | bytes 442376 | tf_op jit(solution)/shard_map/ppermute | solution.py:1167
  68.3 17.7 %collective-permute-start.14 = (bf16[2,48,768]{2,1,0:T(8,128)(2,1)S(1)}, bf16[2,48,768]{2,1,0:T(8,128)(2,1)S(1)}, u32[]{:S(2)}, u32[]{:S(2)}) collective-permute-start(bf16[2,48,768]{2,1,0:T(8,128)(2,1)S(1)} %get-tuple-element.166), channel_id=1, source_target_pairs={{0,16},{1,17},{2,18},{3,19},{4,20},{5,21},{6,22},{7,23},{8,24},{9,... | collective-permute-start | bytes 442376 | tf_op jit(solution)/shard_map/ppermute | solution.py:1167
  70.9 15.1 %collective-permute-start.15 = (bf16[2,48,768]{2,1,0:T(8,128)(2,1)S(1)}, bf16[2,48,768]{2,1,0:T(8,128)(2,1)S(1)}, u32[]{:S(2)}, u32[]{:S(2)}) collective-permute-start(bf16[2,48,768]{2,1,0:T(8,128)(2,1)S(1)} %get-tuple-element.167), channel_id=1, source_target_pairs={{0,24},{1,25},{2,26},{3,27},{4,28},{5,29},{6,30},{7,31},{8,16},{9,... | collective-permute-start | bytes 442376 | tf_op jit(solution)/shard_map/ppermute | solution.py:1167
  75.1 15.4 %collective-permute-start.10 = (bf16[48,896]{1,0:T(8,128)(2,1)S(1)}, bf16[48,896]{1,0:T(8,128)(2,1)S(1)}, u32[]{:S(2)}, u32[]{:S(2)}) collective-permute-start(bf16[48,896]{1,0:T(8,128)(2,1)S(1)} %get-tuple-element.160), channel_id=1, source_target_pairs={{0,16},{1,17},{2,18},{3,19},{4,20},{5,21},{6,22},{7,23},{8,24},{9,... | collective-permute-start | bytes 258056 | tf_op jit(solution)/shard_map/ppermute | solution.py:1167
  77.8 12.8 %collective-permute-start.11 = (bf16[48,896]{1,0:T(8,128)(2,1)S(1)}, bf16[48,896]{1,0:T(8,128)(2,1)S(1)}, u32[]{:S(2)}, u32[]{:S(2)}) collective-permute-start(bf16[48,896]{1,0:T(8,128)(2,1)S(1)} %get-tuple-element.161), channel_id=1, source_target_pairs={{0,24},{1,25},{2,26},{3,27},{4,28},{5,29},{6,30},{7,31},{8,16},{9,... | collective-permute-start | bytes 258056 | tf_op jit(solution)/shard_map/ppermute | solution.py:1167
  79.1 11.4 %collective-permute-start.9 = (bf16[48,896]{1,0:T(8,128)(2,1)S(1)}, bf16[48,896]{1,0:T(8,128)(2,1)S(1)}, u32[]{:S(2)}, u32[]{:S(2)}) collective-permute-start(bf16[48,896]{1,0:T(8,128)(2,1)S(1)} %get-tuple-element.159), channel_id=1, source_target_pairs={{0,8},{1,9},{2,10},{3,11},{4,12},{5,13},{6,14},{7,15},{8,0},{9,1},... | collective-permute-start | bytes 258056 | tf_op jit(solution)/shard_map/ppermute | solution.py:1167
  86.1 4.4 %collective-permute-start.16 = (bf16[48,768]{1,0:T(8,128)(2,1)S(1)}, bf16[48,768]{1,0:T(8,128)(2,1)S(1)}, u32[]{:S(2)}, u32[]{:S(2)}) collective-permute-start(bf16[48,768]{1,0:T(8,128)(2,1)S(1)} %get-tuple-element.169), channel_id=1, source_target_pairs={{0,4},{1,5},{2,6},{3,7},{4,0},{5,1},{6,2},{7,3},{8,12},{9,13},{10,... | collective-permute-start | bytes 221192 | tf_op jit(solution)/shard_map/ppermute | solution.py:1167
  90.6 1.3 %collective-permute-start.17 = (bf16[48,896]{1,0:T(8,128)(2,1)S(1)}, bf16[48,896]{1,0:T(8,128)(2,1)S(1)}, u32[]{:S(2)}, u32[]{:S(2)}) collective-permute-start(bf16[48,896]{1,0:T(8,128)(2,1)S(1)} %get-tuple-element.171), channel_id=1, source_target_pairs={{0,1},{1,0},{2,3},{3,2},{4,5},{5,4},{6,7},{7,6},{8,9},{9,8},{10,11... | collective-permute-start | bytes 258056 | tf_op jit(solution)/shard_map/ppermute | solution.py:1167

commit v6 on v5

--- a/solution.py
+++ b/solution.py
@@ -1217,7 +1217,7 @@
 
     low = along_y(brought(grads.keep0), core0, grads.packed)
     own, *others = split_depths(levels, grads.keep1, core1, low[:1])
-    parts = [own] + [swap(v, z=flip) for v, flip in zip(others, (1, 2, 3))]
+    parts = [own] + [swap(others[flip - 1], z=flip) for flip in (2, 3, 1)]
     across, mine = join_depths(sides, parts)
     high = [mine, swap(across, y=1)]
     low = along_z(*low)

time: 94.1 us -> 92.5 us (0.983)
  transfers between devices with their start and end apart: 18 -> 18, of which waited for: 8 -> 9; matrix products, arithmetic and copies ran while one was open for 1% -> 1% of each run, Pallas kernels for 26% -> 27%
where the time goes in v6:
time: 92.5 us; the launch traced here: 91.4 us
  Pallas kernels  41.7 us (45%)
  waiting for transfers between devices  27.8 us (30%)
  starting transfers between devices  20.5 us (22%)
    pallas_call x7, Pallas kernels, named_call(): pl.pallas_call(kernel, in_specs=[pl.BlockSpec(memory_space=spaces[kind])...  32.8 us
    ppermute x14, waiting for transfers between devices, swap(): return lax.ppermute(value, ('dp', 'segment'), partners((z, y, x, c)))  15.1 us
    ppermute x4, waiting for transfers between devices, along_x(): return lax.ppermute(value, ('dp', 'segment'), pairs)  12.7 us
    ppermute x14, starting transfers between devices, swap(): return lax.ppermute(value, ('dp', 'segment'), partners((z, y, x, c)))  11.8 us
    ppermute x4, starting transfers between devices, along_x(): return lax.ppermute(value, ('dp', 'segment'), pairs)  8.62 us
    pallas_call x2, Pallas kernels, conv_norm(): pl.pallas_call(functools.partial(conv_norm_kernel, len(smalls)), in_specs...  4.37 us
    pallas_call x6, Pallas kernels, small_call(): pl.pallas_call(body, in_specs=[pl.BlockSpec(memory_space=pltpu.SMEM)] + [...  2.4 us
  transfers between devices with their start and end apart: 18, of which 9 were waited for; matrix products, arithmetic and copies ran while one was open for 1% of the time, Pallas kernels for 27%

profile of v6, /device:TPU:0, one launch (start us, length us, event | category | flops | bytes accessed | tf_op | source)
XLA Modules:
  0.0 91.4 jit_solution(9508391904251797696)
XLA Ops:
  0.7 1.1 %parameters.1.rest_0_.refs_3_.refs_12_ = f32[56,384]{1,0:T(8,128)S(1)} custom-call(f32[49,1,384]{2,1,0:T(1,128)} %bitcast.45, f32[1,384]{1,0:T(1,128)} %gain_ref.1, f32[1,384]{1,0:T(1,128)} %scale_ref.1), custom_call_target="tpu_custom_call" | custom-call | flops 550000000 | bytes 1800000 | tf_op jit(solution)/shard_map/parameters/pallas_call | solution.py:102
  3.2 2.2 %conv_norm.2 = (bf16[256,384]{1,0:T(8,128)(2,1)S(1)}, bf16[256,384]{1,0:T(8,128)(2,1)S(1)}, f32[256,128]{1,0:T(8,128)S(1)}) custom-call(s32[2]{0:T(128)S(1)} %pad_add_fusion.2.sel_ref, bf16[16,16,384]{2,1,0:T(8,128)(2,1)S(1)} %get-tuple-element.179.x_ref.refs_1_.refs_2_, f32[56,384]{1,0:T(8,128)S(1)} %parameters.1.rest_0_.refs_3_.refs_12_, ...), custom_call_target="tpu_custom_call" | custom-call | flops 2200000000 | bytes 7200000 | tf_op jit(solution)/shard_map/conv_norm/pallas_call | solution.py:145
  5.4 5.2 %pair_forward.2 = (bf16[16,16,384]{2,1,0:T(8,128)(2,1)S(1)}, bf16[16,16,384]{2,1,0:T(8,128)(2,1)S(1)}, bf16[256,384]{1,0:T(8,128)(2,1)S(1)}, f32[256,128]{1,0:T(...) custom-call(s32[5]{0:T(128)S(1)} %stack.50.refs_0_, ...), custom_call_target="tpu_custom_call" | custom-call | flops 8249999872 | bytes 27000000 | tf_op jit(solution)/shard_map/pair_forward/pallas_call | solution.py:626
  10.7 4.7 %collective-permute-start.5 = (bf16[16,16,384]{2,1,0:T(8,128)(2,1)S(1)}, bf16[16,16,384]{2,1,0:T(8,128)(2,1)S(1)}, u32[]{:S(2)}, u32[]{:S(2)}) collective-permute-start(bf16[16,16,384]{2,1,0:T(8,128)(2,1)S(1)} %get-tuple-element.105), channel_id=1, source_target_pairs={{0,2},{1,3},{4,6},{5,7},{8,10},{9,11},{12,14},{13,15},{16,18},{17,... | collective-permute-start | bytes 589832 | tf_op jit(solution)/shard_map/ppermute | solution.py:1172
  15.4 2.2 %conv_norm.3 = (bf16[256,384]{1,0:T(8,128)(2,1)S(1)}, bf16[256,384]{1,0:T(8,128)(2,1)S(1)}, f32[256,128]{1,0:T(8,128)S(1)}) custom-call(s32[2]{0:T(128)S(1)} %pad_add_fusion.1.sel_ref, bf16[16,16,384]{2,1,0:T(8,128)(2,1)S(1)} %get-tuple-element.180.x_ref.refs_1_.refs_2_, f32[56,384]{1,0:T(8,128)S(1)} %parameters.1.rest_0_.refs_3_.refs_12_, ...), custom_call_target="tpu_custom_call" | custom-call | flops 2200000000 | bytes 7200000 | tf_op jit(solution)/shard_map/conv_norm/pallas_call | solution.py:145
  17.6 5.2 %pair_forward.3 = (bf16[16,16,384]{2,1,0:T(8,128)(2,1)S(1)}, bf16[16,16,384]{2,1,0:T(8,128)(2,1)S(1)}, bf16[256,384]{1,0:T(8,128)(2,1)S(1)}, f32[256,128]{1,0:T(...) custom-call(s32[5]{0:T(128)S(1)} %stack.51.refs_0_, ...), custom_call_target="tpu_custom_call" | custom-call | flops 8249999872 | bytes 27000000 | tf_op jit(solution)/shard_map/pair_forward/pallas_call | solution.py:626
  22.8 1.3 %collective-permute-start.3 = (bf16[16,16,384]{2,1,0:T(8,128)(2,1)S(1)}, bf16[16,16,384]{2,1,0:T(8,128)(2,1)S(1)}, u32[]{:S(2)}, u32[]{:S(2)}) collective-permute-start(bf16[16,16,384]{2,1,0:T(8,128)(2,1)S(1)} %get-tuple-element.94), channel_id=1, source_target_pairs={{0,2},{1,3},{4,6},{5,7},{8,10},{9,11},{12,14},{13,15},{16,18},{17,... | collective-permute-start | bytes 589832 | tf_op jit(solution)/shard_map/ppermute | solution.py:1172
  24.1 0.7 pair_map.3
  24.9 1.3 %collective-permute-start.6 = (bf16[16,16,384]{2,1,0:T(8,128)(2,1)S(1)}, bf16[16,16,384]{2,1,0:T(8,128)(2,1)S(1)}, u32[]{:S(2)}, u32[]{:S(2)}) collective-permute-start(bf16[16,16,384]{2,1,0:T(8,128)(2,1)S(1)} %get-tuple-element.106), channel_id=1, source_target_pairs={{2,0},{3,1},{6,4},{7,5},{10,8},{11,9},{14,12},{15,13},{18,16},{19,... | collective-permute-start | bytes 589832 | tf_op jit(solution)/shard_map/ppermute | solution.py:1172
  26.2 2.5 %collective-permute-done.3.refs_1_.refs_15_ = bf16[16,16,384]{2,1,0:T(8,128)(2,1)S(1)} collective-permute-done((bf16[16,16,384]{2,1,0:T(8,128)(2,1)S(1)}, bf16[16,16,384]{2,1,0:T(8,128)(2,1)S(1)}, u32[]{:S(2)}, u32[]{:S(2)}) %collective-permute-start.3) | collective-permute-done | bytes 196640 | tf_op jit(solution)/shard_map/ppermute | solution.py:1172
  28.6 0.9 pair_map.2
  29.5 1.3 %collective-permute-start.4 = (bf16[16,16,384]{2,1,0:T(8,128)(2,1)S(1)}, bf16[16,16,384]{2,1,0:T(8,128)(2,1)S(1)}, u32[]{:S(2)}, u32[]{:S(2)}) collective-permute-start(bf16[16,16,384]{2,1,0:T(8,128)(2,1)S(1)} %get-tuple-element.95), channel_id=1, source_target_pairs={{2,0},{3,1},{6,4},{7,5},{10,8},{11,9},{14,12},{15,13},{18,16},{19,... | collective-permute-start | bytes 589832 | tf_op jit(solution)/shard_map/ppermute | solution.py:1172
  30.8 0.9 pair_grads.1
  31.7 7.4 %collective-permute-done.6.refs_1_ = bf16[16,16,384]{2,1,0:T(8,128)(2,1)S(1)} collective-permute-done((bf16[16,16,384]{2,1,0:T(8,128)(2,1)S(1)}, bf16[16,16,384]{2,1,0:T(8,128)(2,1)S(1)}, u32[]{:S(2)}, u32[]{:S(2)}) %collective-permute-start.6) | collective-permute-done | bytes 196640 | tf_op jit(solution)/shard_map/ppermute | solution.py:1172
  39.1 9.7 %pair_back.2 = (bf16[384,768]{1,0:T(8,128)(2,1)}, bf16[384,768]{1,0:T(8,128)(2,1)}, bf16[384,768]{1,0:T(8,128)(2,1)}, bf16[384,768]{1,0:T(8,128)(2,1)}, f32[64,384]{1,0:T(8,128)S(1)}, /*index=5*/f32[64,384]{1,0:T(8,128)S(1)}) custom-call(s32[5]{0:T(128)S(1)} %stack.50.refs_0_, bf16[16,16,384]{2,1,0:T(8,128)(2,1)S(1)} %collective-permute-done.6.refs_1_, ...), custom_call_target="tpu_custom_call" | custom-call | flops 9900000256 | bytes 32400000 | tf_op jit(solution)/shard_map/pair_back/pallas_call | solution.py:626
  48.8 2.9 %collective-permute-done.4.refs_1_ = bf16[16,16,384]{2,1,0:T(8,128)(2,1)S(1)} collective-permute-done((bf16[16,16,384]{2,1,0:T(8,128)(2,1)S(1)}, bf16[16,16,384]{2,1,0:T(8,128)(2,1)S(1)}, u32[]{:S(2)}, u32[]{:S(2)}) %collective-permute-start.4) | collective-permute-done | bytes 196640 | tf_op jit(solution)/shard_map/ppermute | solution.py:1172
  51.6 10.3 %pair_back.3 = (bf16[384,768]{1,0:T(8,128)(2,1)}, bf16[384,768]{1,0:T(8,128)(2,1)}, bf16[384,768]{1,0:T(8,128)(2,1)}, bf16[384,768]{1,0:T(8,128)(2,1)}, bf16[384,128]{1,0:T(8,128)(2,1)S(1)}) custom-call(s32[5]{0:T(128)S(1)} %stack.50.refs_0_, bf16[16,16,384]{2,1,0:T(8,128)(2,1)S(1)} %collective-permute-done.4.refs_1_, ...), custom_call_target="tpu_custom_call" | custom-call | flops 9900000256 | bytes 32400000 | tf_op jit(solution)/shard_map/pair_back/pallas_call | solution.py:626
  62.5 1.1 %brought.1 = bf16[384,768]{1,0:T(8,128)(2,1)S(1)} custom-call(bf16[384,768]{1,0:T(8,128)(2,1)} %get-tuple-element.153.source_ref), custom_call_target="tpu_custom_call" | custom-call | flops 1210000000 | bytes 3960000 | tf_op jit(solution)/shard_map/brought/pallas_call | solution.py:972
  63.5 0.6 collective-permute-done.7
  64.3 1.6 %collective-permute-start.8 = (bf16[4,48,896]{2,1,0:T(8,128)(2,1)S(1)}, bf16[4,48,896]{2,1,0:T(8,128)(2,1)S(1)}, u32[]{:S(2)}, u32[]{:S(2)}) collective-permute-start(bf16[4,48,896]{2,1,0:T(8,128)(2,1)S(1)} %get-tuple-element.157), channel_id=1, source_target_pairs={{0,4},{1,5},{2,6},{3,7},{4,0},{5,1},{6,2},{7,3},{8,12},{9,13},{10,... | collective-permute-start | bytes 1032200 | tf_op jit(solution)/shard_map/ppermute | solution.py:1167
  66.0 0.7 split_depths.1
  66.7 2.7 %collective-permute-start.13 = (bf16[2,48,768]{2,1,0:T(8,128)(2,1)S(1)}, bf16[2,48,768]{2,1,0:T(8,128)(2,1)S(1)}, u32[]{:S(2)}, u32[]{:S(2)}) collective-permute-start(bf16[2,48,768]{2,1,0:T(8,128)(2,1)S(1)} %get-tuple-element.165), channel_id=1, source_target_pairs={{0,16},{1,17},{2,18},{3,19},{4,20},{5,21},{6,22},{7,23},{8,24},{9,... | collective-permute-start | bytes 442376 | tf_op jit(solution)/shard_map/ppermute | solution.py:1167
  69.3 1.4 %collective-permute-start.14 = (bf16[2,48,768]{2,1,0:T(8,128)(2,1)S(1)}, bf16[2,48,768]{2,1,0:T(8,128)(2,1)S(1)}, u32[]{:S(2)}, u32[]{:S(2)}) collective-permute-start(bf16[2,48,768]{2,1,0:T(8,128)(2,1)S(1)} %get-tuple-element.166), channel_id=1, source_target_pairs={{0,24},{1,25},{2,26},{3,27},{4,28},{5,29},{6,30},{7,31},{8,16},{9,... | collective-permute-start | bytes 442376 | tf_op jit(solution)/shard_map/ppermute | solution.py:1167
  70.9 3.6 %collective-permute-done.8.refs_2_ = bf16[4,48,896]{2,1,0:T(8,128)(2,1)S(1)} collective-permute-done((bf16[4,48,896]{2,1,0:T(8,128)(2,1)S(1)}, bf16[4,48,896]{2,1,0:T(8,128)(2,1)S(1)}, u32[]{:S(2)}, u32[]{:S(2)}) %collective-permute-start.8) | collective-permute-done | bytes 344096 | tf_op jit(solution)/shard_map/ppermute | solution.py:1167
  74.5 0.6 to_depths.1
  75.1 2.7 %collective-permute-start.10 = (bf16[48,896]{1,0:T(8,128)(2,1)S(1)}, bf16[48,896]{1,0:T(8,128)(2,1)S(1)}, u32[]{:S(2)}, u32[]{:S(2)}) collective-permute-start(bf16[48,896]{1,0:T(8,128)(2,1)S(1)} %get-tuple-element.160), channel_id=1, source_target_pairs={{0,16},{1,17},{2,18},{3,19},{4,20},{5,21},{6,22},{7,23},{8,24},{9,... | collective-permute-start | bytes 258056 | tf_op jit(solution)/shard_map/ppermute | solution.py:1167
  77.8 1.3 %collective-permute-start.11 = (bf16[48,896]{1,0:T(8,128)(2,1)S(1)}, bf16[48,896]{1,0:T(8,128)(2,1)S(1)}, u32[]{:S(2)}, u32[]{:S(2)}) collective-permute-start(bf16[48,896]{1,0:T(8,128)(2,1)S(1)} %get-tuple-element.161), channel_id=1, source_target_pairs={{0,24},{1,25},{2,26},{3,27},{4,28},{5,29},{6,30},{7,31},{8,16},{9,... | collective-permute-start | bytes 258056 | tf_op jit(solution)/shard_map/ppermute | solution.py:1167
  79.1 2.6 %collective-permute-done.13.refs_2_ = bf16[2,48,768]{2,1,0:T(8,128)(2,1)S(1)} collective-permute-done((bf16[2,48,768]{2,1,0:T(8,128)(2,1)S(1)}, bf16[2,48,768]{2,1,0:T(8,128)(2,1)S(1)}, u32[]{:S(2)}, u32[]{:S(2)}) %collective-permute-start.13) | collective-permute-done | bytes 147488 | tf_op jit(solution)/shard_map/ppermute | solution.py:1167
  82.2 4.0 %collective-permute-done.16.refs_6_ = bf16[48,768]{1,0:T(8,128)(2,1)S(1)} collective-permute-done((bf16[48,768]{1,0:T(8,128)(2,1)S(1)}, bf16[48,768]{1,0:T(8,128)(2,1)S(1)}, u32[]{:S(2)}, u32[]{:S(2)}) %collective-permute-start.16) | collective-permute-done | bytes 73760 | tf_op jit(solution)/shard_map/ppermute | solution.py:1167
  86.2 3.0 %collective-permute-done.10.refs_3_ = bf16[48,896]{1,0:T(8,128)(2,1)S(1)} collective-permute-done((bf16[48,896]{1,0:T(8,128)(2,1)S(1)}, bf16[48,896]{1,0:T(8,128)(2,1)S(1)}, u32[]{:S(2)}, u32[]{:S(2)}) %collective-permute-start.10) | collective-permute-done | bytes 86048 | tf_op jit(solution)/shard_map/ppermute | solution.py:1167
  89.4 1.3 %collective-permute-done.17.refs_2_ = bf16[48,896]{1,0:T(8,128)(2,1)S(1)} collective-permute-done((bf16[48,896]{1,0:T(8,128)(2,1)S(1)}, bf16[48,896]{1,0:T(8,128)(2,1)S(1)}, u32[]{:S(2)}, u32[]{:S(2)}) %collective-permute-start.17) | collective-permute-done | bytes 86048 | tf_op jit(solution)/shard_map/ppermute | solution.py:1167
  90.7 0.8 final.1
  (38 shorter events, 3.1 us)
Async XLA Ops:
  0.6 1.6 %copy-start.3 = (bf16[1,384,768]{2,1,0:T(8,128)(2,1)S(1)}, bf16[1,384,768]{2,1,0:T(8,128)(2,1)}, u32[]{:S(2)}) copy-start(bf16[1,384,768]{2,1,0:T(8,128)(2,1)} %param.11) | copy-start | bytes 1769476
  0.6 1.7 %copy-start.4 = (bf16[1,768,384]{2,1,0:T(8,128)(2,1)S(1)}, bf16[1,768,384]{2,1,0:T(8,128)(2,1)}, u32[]{:S(2)}) copy-start(bf16[1,768,384]{2,1,0:T(8,128)(2,1)} %param.12) | copy-start | bytes 1769476
  0.7 2.4 %copy-start.1 = (bf16[4,16,16,384]{3,2,1,0:T(8,128)(2,1)S(1)}, bf16[4,16,16,384]{3,2,1,0:T(8,128)(2,1)}, u32[]{:S(2)}) copy-start(bf16[4,16,16,384]{3,2,1,0:T(8,128)(2,1)} %param.7) | copy-start | bytes 2359300
  1.7 1.3 %copy-start.2 = (bf16[4,16,16,384]{3,2,1,0:T(8,128)(2,1)S(1)}, bf16[4,16,16,384]{3,2,1,0:T(8,128)(2,1)}, u32[]{:S(2)}) copy-start(bf16[4,16,16,384]{3,2,1,0:T(8,128)(2,1)} %param.8) | copy-start | bytes 2359300
  1.8 1.5 %collective-permute-start = (f32[56,384]{1,0:T(8,128)S(1)}, f32[56,384]{1,0:T(8,128)S(1)}, u32[]{:S(2)}, u32[]{:S(2)}) collective-permute-start(f32[56,384]{1,0:T(8,128)S(1)} %parameters.1.rest_0_.refs_3_.refs_12_), channel_id=1, source_target_pairs={{0,1},{1,0},{2,3},{3,2},{4,5},{5,4},{6,7},{7,6},{8,9},{9,8},{10,11... | collective-permute-start | bytes 258056 | tf_op jit(solution)/shard_map/ppermute | solution.py:1167
  2.3 3.1 %collective-permute-start.1 = (bf16[384,768]{1,0:T(8,128)(2,1)S(1)}, bf16[384,768]{1,0:T(8,128)(2,1)}, u32[]{:S(2)}, u32[]{:S(2)}) collective-permute-start(bf16[384,768]{1,0:T(8,128)(2,1)S(1)} %bitcast.37), channel_id=1, source_target_pairs={{0,1},{1,0},{2,3},{3,2},{4,5},{5,4},{6,7},{7,6},{8,9},{9,8},{10,11... | collective-permute-start | bytes 1769480 | tf_op jit(solution)/shard_map/ppermute | solution.py:1167
  2.4 3.1 %collective-permute-start.2 = (bf16[768,384]{1,0:T(8,128)(2,1)S(1)}, bf16[768,384]{1,0:T(8,128)(2,1)}, u32[]{:S(2)}, u32[]{:S(2)}) collective-permute-start(bf16[768,384]{1,0:T(8,128)(2,1)S(1)} %bitcast.44), channel_id=1, source_target_pairs={{0,1},{1,0},{2,3},{3,2},{4,5},{5,4},{6,7},{7,6},{8,9},{9,8},{10,11... | collective-permute-start | bytes 1769480 | tf_op jit(solution)/shard_map/ppermute | solution.py:1167
  10.7 13.5 %collective-permute-start.5 = (bf16[16,16,384]{2,1,0:T(8,128)(2,1)S(1)}, bf16[16,16,384]{2,1,0:T(8,128)(2,1)S(1)}, u32[]{:S(2)}, u32[]{:S(2)}) collective-permute-start(bf16[16,16,384]{2,1,0:T(8,128)(2,1)S(1)} %get-tuple-element.105), channel_id=1, source_target_pairs={{0,2},{1,3},{4,6},{5,7},{8,10},{9,11},{12,14},{13,15},{16,18},{17,... | collective-permute-start | bytes 589832 | tf_op jit(solution)/shard_map/ppermute | solution.py:1172
  22.8 5.8 %collective-permute-start.3 = (bf16[16,16,384]{2,1,0:T(8,128)(2,1)S(1)}, bf16[16,16,384]{2,1,0:T(8,128)(2,1)S(1)}, u32[]{:S(2)}, u32[]{:S(2)}) collective-permute-start(bf16[16,16,384]{2,1,0:T(8,128)(2,1)S(1)} %get-tuple-element.94), channel_id=1, source_target_pairs={{0,2},{1,3},{4,6},{5,7},{8,10},{9,11},{12,14},{13,15},{16,18},{17,... | collective-permute-start | bytes 589832 | tf_op jit(solution)/shard_map/ppermute | solution.py:1172
  24.9 14.2 %collective-permute-start.6 = (bf16[16,16,384]{2,1,0:T(8,128)(2,1)S(1)}, bf16[16,16,384]{2,1,0:T(8,128)(2,1)S(1)}, u32[]{:S(2)}, u32[]{:S(2)}) collective-permute-start(bf16[16,16,384]{2,1,0:T(8,128)(2,1)S(1)} %get-tuple-element.106), channel_id=1, source_target_pairs={{2,0},{3,1},{6,4},{7,5},{10,8},{11,9},{14,12},{15,13},{18,16},{19,... | collective-permute-start | bytes 589832 | tf_op jit(solution)/shard_map/ppermute | solution.py:1172
  29.5 22.1 %collective-permute-start.4 = (bf16[16,16,384]{2,1,0:T(8,128)(2,1)S(1)}, bf16[16,16,384]{2,1,0:T(8,128)(2,1)S(1)}, u32[]{:S(2)}, u32[]{:S(2)}) collective-permute-start(bf16[16,16,384]{2,1,0:T(8,128)(2,1)S(1)} %get-tuple-element.95), channel_id=1, source_target_pairs={{2,0},{3,1},{6,4},{7,5},{10,8},{11,9},{14,12},{15,13},{18,16},{19,... | collective-permute-start | bytes 589832 | tf_op jit(solution)/shard_map/ppermute | solution.py:1172
  61.9 2.3 %collective-permute-start.7 = (bf16[384,768]{1,0:T(8,128)(2,1)}, bf16[384,768]{1,0:T(8,128)(2,1)S(1)}, u32[]{:S(2)}, u32[]{:S(2)}) collective-permute-start(bf16[384,768]{1,0:T(8,128)(2,1)} %get-tuple-element.154), channel_id=1, source_target_pairs={{0,1},{1,0},{2,3},{3,2},{4,5},{5,4},{6,7},{7,6},{8,9},{9,8},{10,11... | collective-permute-start | bytes 1769480 | tf_op jit(solution)/shard_map/ppermute | solution.py:1167
  62.0 4.0 %collective-permute-start.12 = (bf16[384,768]{1,0:T(8,128)(2,1)}, bf16[384,768]{1,0:T(8,128)(2,1)S(1)}, u32[]{:S(2)}, u32[]{:S(2)}) collective-permute-start(bf16[384,768]{1,0:T(8,128)(2,1)} %get-tuple-element.163), channel_id=1, source_target_pairs={{0,1},{1,0},{2,3},{3,2},{4,5},{5,4},{6,7},{7,6},{8,9},{9,8},{10,11... | collective-permute-start | bytes 1769480 | tf_op jit(solution)/shard_map/ppermute | solution.py:1167
  64.2 1.8 %copy-start = (bf16[384,768]{1,0:T(8,128)(2,1)S(1)}, bf16[384,768]{1,0:T(8,128)(2,1)}, u32[]{:S(2)}) copy-start(bf16[384,768]{1,0:T(8,128)(2,1)} %get-tuple-element.162) | copy-start | bytes 1769476
  64.3 10.2 %collective-permute-start.8 = (bf16[4,48,896]{2,1,0:T(8,128)(2,1)S(1)}, bf16[4,48,896]{2,1,0:T(8,128)(2,1)S(1)}, u32[]{:S(2)}, u32[]{:S(2)}) collective-permute-start(bf16[4,48,896]{2,1,0:T(8,128)(2,1)S(1)} %get-tuple-element.157), channel_id=1, source_target_pairs={{0,4},{1,5},{2,6},{3,7},{4,0},{5,1},{6,2},{7,3},{8,12},{9,13},{10,... | collective-permute-start | bytes 1032200 | tf_op jit(solution)/shard_map/ppermute | solution.py:1167
  66.7 15.1 %collective-permute-start.13 = (bf16[2,48,768]{2,1,0:T(8,128)(2,1)S(1)}, bf16[2,48,768]{2,1,0:T(8,128)(2,1)S(1)}, u32[]{:S(2)}, u32[]{:S(2)}) collective-permute-start(bf16[2,48,768]{2,1,0:T(8,128)(2,1)S(1)} %get-tuple-element.165), channel_id=1, source_target_pairs={{0,16},{1,17},{2,18},{3,19},{4,20},{5,21},{6,22},{7,23},{8,24},{9,... | collective-permute-start | bytes 442376 | tf_op jit(solution)/shard_map/ppermute | solution.py:1167
  69.3 12.4 %collective-permute-start.14 = (bf16[2,48,768]{2,1,0:T(8,128)(2,1)S(1)}, bf16[2,48,768]{2,1,0:T(8,128)(2,1)S(1)}, u32[]{:S(2)}, u32[]{:S(2)}) collective-permute-start(bf16[2,48,768]{2,1,0:T(8,128)(2,1)S(1)} %get-tuple-element.166), channel_id=1, source_target_pairs={{0,24},{1,25},{2,26},{3,27},{4,28},{5,29},{6,30},{7,31},{8,16},{9,... | collective-permute-start | bytes 442376 | tf_op jit(solution)/shard_map/ppermute | solution.py:1167
  70.7 11.1 %collective-permute-start.15 = (bf16[2,48,768]{2,1,0:T(8,128)(2,1)S(1)}, bf16[2,48,768]{2,1,0:T(8,128)(2,1)S(1)}, u32[]{:S(2)}, u32[]{:S(2)}) collective-permute-start(bf16[2,48,768]{2,1,0:T(8,128)(2,1)S(1)} %get-tuple-element.167), channel_id=1, source_target_pairs={{0,8},{1,9},{2,10},{3,11},{4,12},{5,13},{6,14},{7,15},{8,0},{9,1},... | collective-permute-start | bytes 442376 | tf_op jit(solution)/shard_map/ppermute | solution.py:1167
  75.1 14.1 %collective-permute-start.10 = (bf16[48,896]{1,0:T(8,128)(2,1)S(1)}, bf16[48,896]{1,0:T(8,128)(2,1)S(1)}, u32[]{:S(2)}, u32[]{:S(2)}) collective-permute-start(bf16[48,896]{1,0:T(8,128)(2,1)S(1)} %get-tuple-element.160), channel_id=1, source_target_pairs={{0,16},{1,17},{2,18},{3,19},{4,20},{5,21},{6,22},{7,23},{8,24},{9,... | collective-permute-start | bytes 258056 | tf_op jit(solution)/shard_map/ppermute | solution.py:1167
  77.8 11.5 %collective-permute-start.11 = (bf16[48,896]{1,0:T(8,128)(2,1)S(1)}, bf16[48,896]{1,0:T(8,128)(2,1)S(1)}, u32[]{:S(2)}, u32[]{:S(2)}) collective-permute-start(bf16[48,896]{1,0:T(8,128)(2,1)S(1)} %get-tuple-element.161), channel_id=1, source_target_pairs={{0,24},{1,25},{2,26},{3,27},{4,28},{5,29},{6,30},{7,31},{8,16},{9,... | collective-permute-start | bytes 258056 | tf_op jit(solution)/shard_map/ppermute | solution.py:1167
  81.7 7.5 %collective-permute-start.9 = (bf16[48,896]{1,0:T(8,128)(2,1)S(1)}, bf16[48,896]{1,0:T(8,128)(2,1)S(1)}, u32[]{:S(2)}, u32[]{:S(2)}) collective-permute-start(bf16[48,896]{1,0:T(8,128)(2,1)S(1)} %get-tuple-element.159), channel_id=1, source_target_pairs={{0,8},{1,9},{2,10},{3,11},{4,12},{5,13},{6,14},{7,15},{8,0},{9,1},... | collective-permute-start | bytes 258056 | tf_op jit(solution)/shard_map/ppermute | solution.py:1167
  81.8 4.4 %collective-permute-start.16 = (bf16[48,768]{1,0:T(8,128)(2,1)S(1)}, bf16[48,768]{1,0:T(8,128)(2,1)S(1)}, u32[]{:S(2)}, u32[]{:S(2)}) collective-permute-start(bf16[48,768]{1,0:T(8,128)(2,1)S(1)} %get-tuple-element.169), channel_id=1, source_target_pairs={{0,4},{1,5},{2,6},{3,7},{4,0},{5,1},{6,2},{7,3},{8,12},{9,13},{10,... | collective-permute-start | bytes 221192 | tf_op jit(solution)/shard_map/ppermute | solution.py:1167
  89.3 1.3 %collective-permute-start.17 = (bf16[48,896]{1,0:T(8,128)(2,1)S(1)}, bf16[48,896]{1,0:T(8,128)(2,1)S(1)}, u32[]{:S(2)}, u32[]{:S(2)}) collective-permute-start(bf16[48,896]{1,0:T(8,128)(2,1)S(1)} %get-tuple-element.171), channel_id=1, source_target_pairs={{0,1},{1,0},{2,3},{3,2},{4,5},{5,4},{6,7},{7,6},{8,9},{9,8},{10,11... | collective-permute-start | bytes 258056 | tf_op jit(solution)/shard_map/ppermute | solution.py:1167

commit v7 on v6

--- a/solution.py
+++ b/solution.py
@@ -708,10 +708,15 @@
     def body(r):
         @pl.when(r.sel[4] == 0)
         def _():
-            low, high = start_weights(r, 0, 0), start_weights(r, 1, 1)
+            low, high = start_weights(r, 0, 0), []
+
+            def low_in():
+                low[0]()
+                high.extend(start_weights(r, 1, 1))
+
             choose_small(r)
             zero_borders(r.pad)
-            mlp_body(r.normed0, *low, r.w_in.at[0], r.w_out.at[0], r.pre0, r.hid, r.acc)
+            mlp_body(r.normed0, low_in, low[1], r.w_in.at[0], r.w_out.at[0], r.pre0, r.hid, r.acc)
             residual_body(r.x, r.small.at[0], r.acc, r.branch0, r.x1)
             conv_norm_body(r.x1, r.small.at[1], r.xhat1, r.normed, r.inv1, r.pad, r.conv)
             mlp_body(r.normed, *high, r.w_in.at[1], r.w_out.at[1], r.pre1, r.hid, r.acc)
@@ -895,9 +900,14 @@
             high, waits = start_weights(r, 1, 1, True), {}
             if before is not None:
                 waits = {k: copy_old(k) for k in (2, 3)}
-            low = start_weights(r, 0, 0, True)
-            if before is not None:
-                waits.update({k: copy_old(k) for k in (0, 1)})
+            low = []
+
+            def high_out():
+                high[1]()
+                low.extend(start_weights(r, 0, 0, True))
+                if before is not None:
+                    waits.update({k: copy_old(k) for k in (0, 1)})
+
             choose_small(r)
             s0, s1 = r.small.at[0], r.small.at[1]
 
@@ -907,9 +917,9 @@
                     waits[2 * k + 1]()
                     return r.olds.at[2 * k], r.olds.at[2 * k + 1]
 
-                return both if waits else None
-
-            mlp_back_body(core, r.g, r.branch1, r.pre1, r.xhat1, r.inv1, s1, *high, r.w_in.at[1], r.w_out.at[1],
+                return both if before is not None else None
+
+            mlp_back_body(core, r.g, r.branch1, r.pre1, r.xhat1, r.inv1, s1, high[0], high_out, r.w_in.at[1], r.w_out.at[1],
                           r.grads.at[2], r.grads.at[3], r.sums8, r.gconv, *back_temps(r), before=old(1))
             copy_out(2, r.grads.at[2]).start()
             copy_out(3, r.grads.at[3]).start()

time: 92.5 us -> 92.7 us (level)
  no operation moved by 1% of the time
where the time goes in v7:
time: 92.7 us; the launch traced here: 91.6 us
  Pallas kernels  41.9 us (45%)
  waiting for transfers between devices  27.8 us (30%)
  starting transfers between devices  20.5 us (22%)
    pallas_call x7, Pallas kernels, named_call(): pl.pallas_call(kernel, in_specs=[pl.BlockSpec(memory_space=spaces[kind])...  33 us
    ppermute x14, waiting for transfers between devices, swap(): return lax.ppermute(value, ('dp', 'segment'), partners((z, y, x, c)))  15.1 us
    ppermute x4, waiting for transfers between devices, along_x(): return lax.ppermute(value, ('dp', 'segment'), pairs)  12.7 us
    ppermute x14, starting transfers between devices, swap(): return lax.ppermute(value, ('dp', 'segment'), partners((z, y, x, c)))  11.9 us
    ppermute x4, starting transfers between devices, along_x(): return lax.ppermute(value, ('dp', 'segment'), pairs)  8.62 us
    pallas_call x2, Pallas kernels, conv_norm(): pl.pallas_call(functools.partial(conv_norm_kernel, len(smalls)), in_specs...  4.37 us
    pallas_call x6, Pallas kernels, small_call(): pl.pallas_call(body, in_specs=[pl.BlockSpec(memory_space=pltpu.SMEM)] + [...  2.4 us
  transfers between devices with their start and end apart: 18, of which 9 were waited for; matrix products, arithmetic and copies ran while one was open for 1% of the time, Pallas kernels for 27%

profile of v7, /device:TPU:0, one launch (start us, length us, event | category | flops | bytes accessed | tf_op | source)
XLA Modules:
  0.0 91.6 jit_solution(9814011227865851265)
XLA Ops:
  0.7 1.1 %parameters.1.rest_0_.refs_3_.refs_12_ = f32[56,384]{1,0:T(8,128)S(1)} custom-call(f32[49,1,384]{2,1,0:T(1,128)} %bitcast.45, f32[1,384]{1,0:T(1,128)} %gain_ref.1, f32[1,384]{1,0:T(1,128)} %scale_ref.1), custom_call_target="tpu_custom_call" | custom-call | flops 550000000 | bytes 1800000 | tf_op jit(solution)/shard_map/parameters/pallas_call | solution.py:102
  3.2 2.2 %conv_norm.2 = (bf16[256,384]{1,0:T(8,128)(2,1)S(1)}, bf16[256,384]{1,0:T(8,128)(2,1)S(1)}, f32[256,128]{1,0:T(8,128)S(1)}) custom-call(s32[2]{0:T(128)S(1)} %pad_add_fusion.2.sel_ref, bf16[16,16,384]{2,1,0:T(8,128)(2,1)S(1)} %get-tuple-element.179.x_ref.refs_1_.refs_2_, f32[56,384]{1,0:T(8,128)S(1)} %parameters.1.rest_0_.refs_3_.refs_12_, ...), custom_call_target="tpu_custom_call" | custom-call | flops 2200000000 | bytes 7200000 | tf_op jit(solution)/shard_map/conv_norm/pallas_call | solution.py:145
  5.4 5.2 %pair_forward.2 = (bf16[16,16,384]{2,1,0:T(8,128)(2,1)S(1)}, bf16[16,16,384]{2,1,0:T(8,128)(2,1)S(1)}, bf16[256,384]{1,0:T(8,128)(2,1)S(1)}, f32[256,128]{1,0:T(...) custom-call(s32[5]{0:T(128)S(1)} %stack.50.refs_0_, ...), custom_call_target="tpu_custom_call" | custom-call | flops 8249999872 | bytes 27000000 | tf_op jit(solution)/shard_map/pair_forward/pallas_call | solution.py:626
  10.7 4.7 %collective-permute-start.5 = (bf16[16,16,384]{2,1,0:T(8,128)(2,1)S(1)}, bf16[16,16,384]{2,1,0:T(8,128)(2,1)S(1)}, u32[]{:S(2)}, u32[]{:S(2)}) collective-permute-start(bf16[16,16,384]{2,1,0:T(8,128)(2,1)S(1)} %get-tuple-element.105), channel_id=1, source_target_pairs={{0,2},{1,3},{4,6},{5,7},{8,10},{9,11},{12,14},{13,15},{16,18},{17,... | collective-permute-start | bytes 589832 | tf_op jit(solution)/shard_map/ppermute | solution.py:1182
  15.4 2.2 %conv_norm.3 = (bf16[256,384]{1,0:T(8,128)(2,1)S(1)}, bf16[256,384]{1,0:T(8,128)(2,1)S(1)}, f32[256,128]{1,0:T(8,128)S(1)}) custom-call(s32[2]{0:T(128)S(1)} %pad_add_fusion.1.sel_ref, bf16[16,16,384]{2,1,0:T(8,128)(2,1)S(1)} %get-tuple-element.180.x_ref.refs_1_.refs_2_, f32[56,384]{1,0:T(8,128)S(1)} %parameters.1.rest_0_.refs_3_.refs_12_, ...), custom_call_target="tpu_custom_call" | custom-call | flops 2200000000 | bytes 7200000 | tf_op jit(solution)/shard_map/conv_norm/pallas_call | solution.py:145
  17.6 5.2 %pair_forward.3 = (bf16[16,16,384]{2,1,0:T(8,128)(2,1)S(1)}, bf16[16,16,384]{2,1,0:T(8,128)(2,1)S(1)}, bf16[256,384]{1,0:T(8,128)(2,1)S(1)}, f32[256,128]{1,0:T(...) custom-call(s32[5]{0:T(128)S(1)} %stack.51.refs_0_, ...), custom_call_target="tpu_custom_call" | custom-call | flops 8249999872 | bytes 27000000 | tf_op jit(solution)/shard_map/pair_forward/pallas_call | solution.py:626
  22.8 1.3 %collective-permute-start.3 = (bf16[16,16,384]{2,1,0:T(8,128)(2,1)S(1)}, bf16[16,16,384]{2,1,0:T(8,128)(2,1)S(1)}, u32[]{:S(2)}, u32[]{:S(2)}) collective-permute-start(bf16[16,16,384]{2,1,0:T(8,128)(2,1)S(1)} %get-tuple-element.94), channel_id=1, source_target_pairs={{0,2},{1,3},{4,6},{5,7},{8,10},{9,11},{12,14},{13,15},{16,18},{17,... | collective-permute-start | bytes 589832 | tf_op jit(solution)/shard_map/ppermute | solution.py:1182
  24.2 0.7 pair_map.3
  24.9 1.3 %collective-permute-start.6 = (bf16[16,16,384]{2,1,0:T(8,128)(2,1)S(1)}, bf16[16,16,384]{2,1,0:T(8,128)(2,1)S(1)}, u32[]{:S(2)}, u32[]{:S(2)}) collective-permute-start(bf16[16,16,384]{2,1,0:T(8,128)(2,1)S(1)} %get-tuple-element.106), channel_id=1, source_target_pairs={{2,0},{3,1},{6,4},{7,5},{10,8},{11,9},{14,12},{15,13},{18,16},{19,... | collective-permute-start | bytes 589832 | tf_op jit(solution)/shard_map/ppermute | solution.py:1182
  26.2 2.5 %collective-permute-done.3.refs_1_.refs_15_ = bf16[16,16,384]{2,1,0:T(8,128)(2,1)S(1)} collective-permute-done((bf16[16,16,384]{2,1,0:T(8,128)(2,1)S(1)}, bf16[16,16,384]{2,1,0:T(8,128)(2,1)S(1)}, u32[]{:S(2)}, u32[]{:S(2)}) %collective-permute-start.3) | collective-permute-done | bytes 196640 | tf_op jit(solution)/shard_map/ppermute | solution.py:1182
  28.6 0.9 pair_map.2
  29.5 1.3 %collective-permute-start.4 = (bf16[16,16,384]{2,1,0:T(8,128)(2,1)S(1)}, bf16[16,16,384]{2,1,0:T(8,128)(2,1)S(1)}, u32[]{:S(2)}, u32[]{:S(2)}) collective-permute-start(bf16[16,16,384]{2,1,0:T(8,128)(2,1)S(1)} %get-tuple-element.95), channel_id=1, source_target_pairs={{2,0},{3,1},{6,4},{7,5},{10,8},{11,9},{14,12},{15,13},{18,16},{19,... | collective-permute-start | bytes 589832 | tf_op jit(solution)/shard_map/ppermute | solution.py:1182
  30.8 0.9 pair_grads.1
  31.7 7.4 %collective-permute-done.6.refs_1_ = bf16[16,16,384]{2,1,0:T(8,128)(2,1)S(1)} collective-permute-done((bf16[16,16,384]{2,1,0:T(8,128)(2,1)S(1)}, bf16[16,16,384]{2,1,0:T(8,128)(2,1)S(1)}, u32[]{:S(2)}, u32[]{:S(2)}) %collective-permute-start.6) | collective-permute-done | bytes 196640 | tf_op jit(solution)/shard_map/ppermute | solution.py:1182
  39.1 9.7 %pair_back.2 = (bf16[384,768]{1,0:T(8,128)(2,1)}, bf16[384,768]{1,0:T(8,128)(2,1)}, bf16[384,768]{1,0:T(8,128)(2,1)}, bf16[384,768]{1,0:T(8,128)(2,1)}, f32[64,384]{1,0:T(8,128)S(1)}, /*index=5*/f32[64,384]{1,0:T(8,128)S(1)}) custom-call(s32[5]{0:T(128)S(1)} %stack.50.refs_0_, bf16[16,16,384]{2,1,0:T(8,128)(2,1)S(1)} %collective-permute-done.6.refs_1_, ...), custom_call_target="tpu_custom_call" | custom-call | flops 9900000256 | bytes 32400000 | tf_op jit(solution)/shard_map/pair_back/pallas_call | solution.py:626
  48.8 2.9 %collective-permute-done.4.refs_1_ = bf16[16,16,384]{2,1,0:T(8,128)(2,1)S(1)} collective-permute-done((bf16[16,16,384]{2,1,0:T(8,128)(2,1)S(1)}, bf16[16,16,384]{2,1,0:T(8,128)(2,1)S(1)}, u32[]{:S(2)}, u32[]{:S(2)}) %collective-permute-start.4) | collective-permute-done | bytes 196640 | tf_op jit(solution)/shard_map/ppermute | solution.py:1182
  51.6 10.4 %pair_back.3 = (bf16[384,768]{1,0:T(8,128)(2,1)}, bf16[384,768]{1,0:T(8,128)(2,1)}, bf16[384,768]{1,0:T(8,128)(2,1)}, bf16[384,768]{1,0:T(8,128)(2,1)}, bf16[384,128]{1,0:T(8,128)(2,1)S(1)}) custom-call(s32[5]{0:T(128)S(1)} %stack.50.refs_0_, bf16[16,16,384]{2,1,0:T(8,128)(2,1)S(1)} %collective-permute-done.4.refs_1_, ...), custom_call_target="tpu_custom_call" | custom-call | flops 9900000256 | bytes 32400000 | tf_op jit(solution)/shard_map/pair_back/pallas_call | solution.py:626
  62.6 1.1 %brought.1 = bf16[384,768]{1,0:T(8,128)(2,1)S(1)} custom-call(bf16[384,768]{1,0:T(8,128)(2,1)} %get-tuple-element.153.source_ref), custom_call_target="tpu_custom_call" | custom-call | flops 1210000000 | bytes 3960000 | tf_op jit(solution)/shard_map/brought/pallas_call | solution.py:982
  63.7 0.6 collective-permute-done.7
  64.5 1.6 %collective-permute-start.8 = (bf16[4,48,896]{2,1,0:T(8,128)(2,1)S(1)}, bf16[4,48,896]{2,1,0:T(8,128)(2,1)S(1)}, u32[]{:S(2)}, u32[]{:S(2)}) collective-permute-start(bf16[4,48,896]{2,1,0:T(8,128)(2,1)S(1)} %get-tuple-element.157), channel_id=1, source_target_pairs={{0,4},{1,5},{2,6},{3,7},{4,0},{5,1},{6,2},{7,3},{8,12},{9,13},{10,... | collective-permute-start | bytes 1032200 | tf_op jit(solution)/shard_map/ppermute | solution.py:1177
  66.1 0.7 split_depths.1
  66.8 2.7 %collective-permute-start.13 = (bf16[2,48,768]{2,1,0:T(8,128)(2,1)S(1)}, bf16[2,48,768]{2,1,0:T(8,128)(2,1)S(1)}, u32[]{:S(2)}, u32[]{:S(2)}) collective-permute-start(bf16[2,48,768]{2,1,0:T(8,128)(2,1)S(1)} %get-tuple-element.165), channel_id=1, source_target_pairs={{0,16},{1,17},{2,18},{3,19},{4,20},{5,21},{6,22},{7,23},{8,24},{9,... | collective-permute-start | bytes 442376 | tf_op jit(solution)/shard_map/ppermute | solution.py:1177
  69.5 1.3 %collective-permute-start.14 = (bf16[2,48,768]{2,1,0:T(8,128)(2,1)S(1)}, bf16[2,48,768]{2,1,0:T(8,128)(2,1)S(1)}, u32[]{:S(2)}, u32[]{:S(2)}) collective-permute-start(bf16[2,48,768]{2,1,0:T(8,128)(2,1)S(1)} %get-tuple-element.166), channel_id=1, source_target_pairs={{0,24},{1,25},{2,26},{3,27},{4,28},{5,29},{6,30},{7,31},{8,16},{9,... | collective-permute-start | bytes 442376 | tf_op jit(solution)/shard_map/ppermute | solution.py:1177
  71.1 3.6 %collective-permute-done.8.refs_2_ = bf16[4,48,896]{2,1,0:T(8,128)(2,1)S(1)} collective-permute-done((bf16[4,48,896]{2,1,0:T(8,128)(2,1)S(1)}, bf16[4,48,896]{2,1,0:T(8,128)(2,1)S(1)}, u32[]{:S(2)}, u32[]{:S(2)}) %collective-permute-start.8) | collective-permute-done | bytes 344096 | tf_op jit(solution)/shard_map/ppermute | solution.py:1177
  74.6 0.6 to_depths.1
  75.3 2.7 %collective-permute-start.10 = (bf16[48,896]{1,0:T(8,128)(2,1)S(1)}, bf16[48,896]{1,0:T(8,128)(2,1)S(1)}, u32[]{:S(2)}, u32[]{:S(2)}) collective-permute-start(bf16[48,896]{1,0:T(8,128)(2,1)S(1)} %get-tuple-element.160), channel_id=1, source_target_pairs={{0,16},{1,17},{2,18},{3,19},{4,20},{5,21},{6,22},{7,23},{8,24},{9,... | collective-permute-start | bytes 258056 | tf_op jit(solution)/shard_map/ppermute | solution.py:1177
  77.9 1.3 %collective-permute-start.11 = (bf16[48,896]{1,0:T(8,128)(2,1)S(1)}, bf16[48,896]{1,0:T(8,128)(2,1)S(1)}, u32[]{:S(2)}, u32[]{:S(2)}) collective-permute-start(bf16[48,896]{1,0:T(8,128)(2,1)S(1)} %get-tuple-element.161), channel_id=1, source_target_pairs={{0,24},{1,25},{2,26},{3,27},{4,28},{5,29},{6,30},{7,31},{8,16},{9,... | collective-permute-start | bytes 258056 | tf_op jit(solution)/shard_map/ppermute | solution.py:1177
  79.3 2.6 %collective-permute-done.13.refs_2_ = bf16[2,48,768]{2,1,0:T(8,128)(2,1)S(1)} collective-permute-done((bf16[2,48,768]{2,1,0:T(8,128)(2,1)S(1)}, bf16[2,48,768]{2,1,0:T(8,128)(2,1)S(1)}, u32[]{:S(2)}, u32[]{:S(2)}) %collective-permute-start.13) | collective-permute-done | bytes 147488 | tf_op jit(solution)/shard_map/ppermute | solution.py:1177
  82.4 4.0 %collective-permute-done.16.refs_6_ = bf16[48,768]{1,0:T(8,128)(2,1)S(1)} collective-permute-done((bf16[48,768]{1,0:T(8,128)(2,1)S(1)}, bf16[48,768]{1,0:T(8,128)(2,1)S(1)}, u32[]{:S(2)}, u32[]{:S(2)}) %collective-permute-start.16) | collective-permute-done | bytes 73760 | tf_op jit(solution)/shard_map/ppermute | solution.py:1177
  86.4 3.0 %collective-permute-done.10.refs_3_ = bf16[48,896]{1,0:T(8,128)(2,1)S(1)} collective-permute-done((bf16[48,896]{1,0:T(8,128)(2,1)S(1)}, bf16[48,896]{1,0:T(8,128)(2,1)S(1)}, u32[]{:S(2)}, u32[]{:S(2)}) %collective-permute-start.10) | collective-permute-done | bytes 86048 | tf_op jit(solution)/shard_map/ppermute | solution.py:1177
  89.6 1.3 %collective-permute-done.17.refs_2_ = bf16[48,896]{1,0:T(8,128)(2,1)S(1)} collective-permute-done((bf16[48,896]{1,0:T(8,128)(2,1)S(1)}, bf16[48,896]{1,0:T(8,128)(2,1)S(1)}, u32[]{:S(2)}, u32[]{:S(2)}) %collective-permute-start.17) | collective-permute-done | bytes 86048 | tf_op jit(solution)/shard_map/ppermute | solution.py:1177
  90.8 0.8 final.1
  (38 shorter events, 3.1 us)
Async XLA Ops:
  0.6 1.6 %copy-start.3 = (bf16[1,384,768]{2,1,0:T(8,128)(2,1)S(1)}, bf16[1,384,768]{2,1,0:T(8,128)(2,1)}, u32[]{:S(2)}) copy-start(bf16[1,384,768]{2,1,0:T(8,128)(2,1)} %param.11) | copy-start | bytes 1769476
  0.6 1.7 %copy-start.4 = (bf16[1,768,384]{2,1,0:T(8,128)(2,1)S(1)}, bf16[1,768,384]{2,1,0:T(8,128)(2,1)}, u32[]{:S(2)}) copy-start(bf16[1,768,384]{2,1,0:T(8,128)(2,1)} %param.12) | copy-start | bytes 1769476
  0.7 2.4 %copy-start.1 = (bf16[4,16,16,384]{3,2,1,0:T(8,128)(2,1)S(1)}, bf16[4,16,16,384]{3,2,1,0:T(8,128)(2,1)}, u32[]{:S(2)}) copy-start(bf16[4,16,16,384]{3,2,1,0:T(8,128)(2,1)} %param.7) | copy-start | bytes 2359300
  1.7 1.3 %copy-start.2 = (bf16[4,16,16,384]{3,2,1,0:T(8,128)(2,1)S(1)}, bf16[4,16,16,384]{3,2,1,0:T(8,128)(2,1)}, u32[]{:S(2)}) copy-start(bf16[4,16,16,384]{3,2,1,0:T(8,128)(2,1)} %param.8) | copy-start | bytes 2359300
  1.8 1.5 %collective-permute-start = (f32[56,384]{1,0:T(8,128)S(1)}, f32[56,384]{1,0:T(8,128)S(1)}, u32[]{:S(2)}, u32[]{:S(2)}) collective-permute-start(f32[56,384]{1,0:T(8,128)S(1)} %parameters.1.rest_0_.refs_3_.refs_12_), channel_id=1, source_target_pairs={{0,1},{1,0},{2,3},{3,2},{4,5},{5,4},{6,7},{7,6},{8,9},{9,8},{10,11... | collective-permute-start | bytes 258056 | tf_op jit(solution)/shard_map/ppermute | solution.py:1177
  2.3 3.1 %collective-permute-start.1 = (bf16[384,768]{1,0:T(8,128)(2,1)S(1)}, bf16[384,768]{1,0:T(8,128)(2,1)}, u32[]{:S(2)}, u32[]{:S(2)}) collective-permute-start(bf16[384,768]{1,0:T(8,128)(2,1)S(1)} %bitcast.37), channel_id=1, source_target_pairs={{0,1},{1,0},{2,3},{3,2},{4,5},{5,4},{6,7},{7,6},{8,9},{9,8},{10,11... | collective-permute-start | bytes 1769480 | tf_op jit(solution)/shard_map/ppermute | solution.py:1177
  2.4 3.1 %collective-permute-start.2 = (bf16[768,384]{1,0:T(8,128)(2,1)S(1)}, bf16[768,384]{1,0:T(8,128)(2,1)}, u32[]{:S(2)}, u32[]{:S(2)}) collective-permute-start(bf16[768,384]{1,0:T(8,128)(2,1)S(1)} %bitcast.44), channel_id=1, source_target_pairs={{0,1},{1,0},{2,3},{3,2},{4,5},{5,4},{6,7},{7,6},{8,9},{9,8},{10,11... | collective-permute-start | bytes 1769480 | tf_op jit(solution)/shard_map/ppermute | solution.py:1177
  10.7 13.5 %collective-permute-start.5 = (bf16[16,16,384]{2,1,0:T(8,128)(2,1)S(1)}, bf16[16,16,384]{2,1,0:T(8,128)(2,1)S(1)}, u32[]{:S(2)}, u32[]{:S(2)}) collective-permute-start(bf16[16,16,384]{2,1,0:T(8,128)(2,1)S(1)} %get-tuple-element.105), channel_id=1, source_target_pairs={{0,2},{1,3},{4,6},{5,7},{8,10},{9,11},{12,14},{13,15},{16,18},{17,... | collective-permute-start | bytes 589832 | tf_op jit(solution)/shard_map/ppermute | solution.py:1182
  22.8 5.8 %collective-permute-start.3 = (bf16[16,16,384]{2,1,0:T(8,128)(2,1)S(1)}, bf16[16,16,384]{2,1,0:T(8,128)(2,1)S(1)}, u32[]{:S(2)}, u32[]{:S(2)}) collective-permute-start(bf16[16,16,384]{2,1,0:T(8,128)(2,1)S(1)} %get-tuple-element.94), channel_id=1, source_target_pairs={{0,2},{1,3},{4,6},{5,7},{8,10},{9,11},{12,14},{13,15},{16,18},{17,... | collective-permute-start | bytes 589832 | tf_op jit(solution)/shard_map/ppermute | solution.py:1182
  24.9 14.2 %collective-permute-start.6 = (bf16[16,16,384]{2,1,0:T(8,128)(2,1)S(1)}, bf16[16,16,384]{2,1,0:T(8,128)(2,1)S(1)}, u32[]{:S(2)}, u32[]{:S(2)}) collective-permute-start(bf16[16,16,384]{2,1,0:T(8,128)(2,1)S(1)} %get-tuple-element.106), channel_id=1, source_target_pairs={{2,0},{3,1},{6,4},{7,5},{10,8},{11,9},{14,12},{15,13},{18,16},{19,... | collective-permute-start | bytes 589832 | tf_op jit(solution)/shard_map/ppermute | solution.py:1182
  29.5 22.1 %collective-permute-start.4 = (bf16[16,16,384]{2,1,0:T(8,128)(2,1)S(1)}, bf16[16,16,384]{2,1,0:T(8,128)(2,1)S(1)}, u32[]{:S(2)}, u32[]{:S(2)}) collective-permute-start(bf16[16,16,384]{2,1,0:T(8,128)(2,1)S(1)} %get-tuple-element.95), channel_id=1, source_target_pairs={{2,0},{3,1},{6,4},{7,5},{10,8},{11,9},{14,12},{15,13},{18,16},{19,... | collective-permute-start | bytes 589832 | tf_op jit(solution)/shard_map/ppermute | solution.py:1182
  62.1 2.3 %collective-permute-start.7 = (bf16[384,768]{1,0:T(8,128)(2,1)}, bf16[384,768]{1,0:T(8,128)(2,1)S(1)}, u32[]{:S(2)}, u32[]{:S(2)}) collective-permute-start(bf16[384,768]{1,0:T(8,128)(2,1)} %get-tuple-element.154), channel_id=1, source_target_pairs={{0,1},{1,0},{2,3},{3,2},{4,5},{5,4},{6,7},{7,6},{8,9},{9,8},{10,11... | collective-permute-start | bytes 1769480 | tf_op jit(solution)/shard_map/ppermute | solution.py:1177
  62.1 4.0 %collective-permute-start.12 = (bf16[384,768]{1,0:T(8,128)(2,1)}, bf16[384,768]{1,0:T(8,128)(2,1)S(1)}, u32[]{:S(2)}, u32[]{:S(2)}) collective-permute-start(bf16[384,768]{1,0:T(8,128)(2,1)} %get-tuple-element.163), channel_id=1, source_target_pairs={{0,1},{1,0},{2,3},{3,2},{4,5},{5,4},{6,7},{7,6},{8,9},{9,8},{10,11... | collective-permute-start | bytes 1769480 | tf_op jit(solution)/shard_map/ppermute | solution.py:1177
  64.3 1.8 %copy-start = (bf16[384,768]{1,0:T(8,128)(2,1)S(1)}, bf16[384,768]{1,0:T(8,128)(2,1)}, u32[]{:S(2)}) copy-start(bf16[384,768]{1,0:T(8,128)(2,1)} %get-tuple-element.162) | copy-start | bytes 1769476
  64.5 10.2 %collective-permute-start.8 = (bf16[4,48,896]{2,1,0:T(8,128)(2,1)S(1)}, bf16[4,48,896]{2,1,0:T(8,128)(2,1)S(1)}, u32[]{:S(2)}, u32[]{:S(2)}) collective-permute-start(bf16[4,48,896]{2,1,0:T(8,128)(2,1)S(1)} %get-tuple-element.157), channel_id=1, source_target_pairs={{0,4},{1,5},{2,6},{3,7},{4,0},{5,1},{6,2},{7,3},{8,12},{9,13},{10,... | collective-permute-start | bytes 1032200 | tf_op jit(solution)/shard_map/ppermute | solution.py:1177
  66.8 15.1 %collective-permute-start.13 = (bf16[2,48,768]{2,1,0:T(8,128)(2,1)S(1)}, bf16[2,48,768]{2,1,0:T(8,128)(2,1)S(1)}, u32[]{:S(2)}, u32[]{:S(2)}) collective-permute-start(bf16[2,48,768]{2,1,0:T(8,128)(2,1)S(1)} %get-tuple-element.165), channel_id=1, source_target_pairs={{0,16},{1,17},{2,18},{3,19},{4,20},{5,21},{6,22},{7,23},{8,24},{9,... | collective-permute-start | bytes 442376 | tf_op jit(solution)/shard_map/ppermute | solution.py:1177
  69.5 12.4 %collective-permute-start.14 = (bf16[2,48,768]{2,1,0:T(8,128)(2,1)S(1)}, bf16[2,48,768]{2,1,0:T(8,128)(2,1)S(1)}, u32[]{:S(2)}, u32[]{:S(2)}) collective-permute-start(bf16[2,48,768]{2,1,0:T(8,128)(2,1)S(1)} %get-tuple-element.166), channel_id=1, source_target_pairs={{0,24},{1,25},{2,26},{3,27},{4,28},{5,29},{6,30},{7,31},{8,16},{9,... | collective-permute-start | bytes 442376 | tf_op jit(solution)/shard_map/ppermute | solution.py:1177
  70.8 11.1 %collective-permute-start.15 = (bf16[2,48,768]{2,1,0:T(8,128)(2,1)S(1)}, bf16[2,48,768]{2,1,0:T(8,128)(2,1)S(1)}, u32[]{:S(2)}, u32[]{:S(2)}) collective-permute-start(bf16[2,48,768]{2,1,0:T(8,128)(2,1)S(1)} %get-tuple-element.167), channel_id=1, source_target_pairs={{0,8},{1,9},{2,10},{3,11},{4,12},{5,13},{6,14},{7,15},{8,0},{9,1},... | collective-permute-start | bytes 442376 | tf_op jit(solution)/shard_map/ppermute | solution.py:1177
  75.3 14.1 %collective-permute-start.10 = (bf16[48,896]{1,0:T(8,128)(2,1)S(1)}, bf16[48,896]{1,0:T(8,128)(2,1)S(1)}, u32[]{:S(2)}, u32[]{:S(2)}) collective-permute-start(bf16[48,896]{1,0:T(8,128)(2,1)S(1)} %get-tuple-element.160), channel_id=1, source_target_pairs={{0,16},{1,17},{2,18},{3,19},{4,20},{5,21},{6,22},{7,23},{8,24},{9,... | collective-permute-start | bytes 258056 | tf_op jit(solution)/shard_map/ppermute | solution.py:1177
  77.9 11.5 %collective-permute-start.11 = (bf16[48,896]{1,0:T(8,128)(2,1)S(1)}, bf16[48,896]{1,0:T(8,128)(2,1)S(1)}, u32[]{:S(2)}, u32[]{:S(2)}) collective-permute-start(bf16[48,896]{1,0:T(8,128)(2,1)S(1)} %get-tuple-element.161), channel_id=1, source_target_pairs={{0,24},{1,25},{2,26},{3,27},{4,28},{5,29},{6,30},{7,31},{8,16},{9,... | collective-permute-start | bytes 258056 | tf_op jit(solution)/shard_map/ppermute | solution.py:1177
  81.9 7.5 %collective-permute-start.9 = (bf16[48,896]{1,0:T(8,128)(2,1)S(1)}, bf16[48,896]{1,0:T(8,128)(2,1)S(1)}, u32[]{:S(2)}, u32[]{:S(2)}) collective-permute-start(bf16[48,896]{1,0:T(8,128)(2,1)S(1)} %get-tuple-element.159), channel_id=1, source_target_pairs={{0,8},{1,9},{2,10},{3,11},{4,12},{5,13},{6,14},{7,15},{8,0},{9,1},... | collective-permute-start | bytes 258056 | tf_op jit(solution)/shard_map/ppermute | solution.py:1177
  82.0 4.4 %collective-permute-start.16 = (bf16[48,768]{1,0:T(8,128)(2,1)S(1)}, bf16[48,768]{1,0:T(8,128)(2,1)S(1)}, u32[]{:S(2)}, u32[]{:S(2)}) collective-permute-start(bf16[48,768]{1,0:T(8,128)(2,1)S(1)} %get-tuple-element.169), channel_id=1, source_target_pairs={{0,4},{1,5},{2,6},{3,7},{4,0},{5,1},{6,2},{7,3},{8,12},{9,13},{10,... | collective-permute-start | bytes 221192 | tf_op jit(solution)/shard_map/ppermute | solution.py:1177
  89.5 1.3 %collective-permute-start.17 = (bf16[48,896]{1,0:T(8,128)(2,1)S(1)}, bf16[48,896]{1,0:T(8,128)(2,1)S(1)}, u32[]{:S(2)}, u32[]{:S(2)}) collective-permute-start(bf16[48,896]{1,0:T(8,128)(2,1)S(1)} %get-tuple-element.171), channel_id=1, source_target_pairs={{0,1},{1,0},{2,3},{3,2},{4,5},{5,4},{6,7},{7,6},{8,9},{9,8},{10,11... | collective-permute-start | bytes 258056 | tf_op jit(solution)/shard_map/ppermute | solution.py:1177

commit v8 on v6

--- a/solution.py
+++ b/solution.py
@@ -467,7 +467,6 @@
 def conv_map_body(gconv_ref, g_ref, small_ref, out_ref, pad_ref, map_ref):
     rows, cols, channels = g_ref.shape
     tiles = channels // LANES
-    zero_borders(pad_ref)
     for c in range(tiles):
         pad_ref[c, :, 8 : cols + 8] = gconv_ref[:, c * LANES : (c + 1) * LANES].reshape(rows, cols, LANES)
 

time: 92.5 us -> 92.4 us (level)
  no operation moved by 1% of the time
where the time goes in v8:
time: 92.4 us; the launch traced here: 91.4 us
  Pallas kernels  41.7 us (45%)
  waiting for transfers between devices  27.8 us (30%)
  starting transfers between devices  20.5 us (22%)
    pallas_call x7, Pallas kernels, named_call(): pl.pallas_call(kernel, in_specs=[pl.BlockSpec(memory_space=spaces[kind])...  32.8 us
    ppermute x14, waiting for transfers between devices, swap(): return lax.ppermute(value, ('dp', 'segment'), partners((z, y, x, c)))  15.1 us
    ppermute x4, waiting for transfers between devices, along_x(): return lax.ppermute(value, ('dp', 'segment'), pairs)  12.7 us
    ppermute x14, starting transfers between devices, swap(): return lax.ppermute(value, ('dp', 'segment'), partners((z, y, x, c)))  11.9 us
    ppermute x4, starting transfers between devices, along_x(): return lax.ppermute(value, ('dp', 'segment'), pairs)  8.62 us
    pallas_call x2, Pallas kernels, conv_norm(): pl.pallas_call(functools.partial(conv_norm_kernel, len(smalls)), in_specs...  4.37 us
    pallas_call x6, Pallas kernels, small_call(): pl.pallas_call(body, in_specs=[pl.BlockSpec(memory_space=pltpu.SMEM)] + [...  2.4 us
  transfers between devices with their start and end apart: 18, of which 9 were waited for; matrix products, arithmetic and copies ran while one was open for 1% of the time, Pallas kernels for 27%

profile of v8, /device:TPU:0, one launch (start us, length us, event | category | flops | bytes accessed | tf_op | source)
XLA Modules:
  0.0 91.4 jit_solution(9688130962016296675)
XLA Ops:
  0.7 1.1 %parameters.1.rest_0_.refs_3_.refs_12_ = f32[56,384]{1,0:T(8,128)S(1)} custom-call(f32[49,1,384]{2,1,0:T(1,128)} %bitcast.45, f32[1,384]{1,0:T(1,128)} %gain_ref.1, f32[1,384]{1,0:T(1,128)} %scale_ref.1), custom_call_target="tpu_custom_call" | custom-call | flops 550000000 | bytes 1800000 | tf_op jit(solution)/shard_map/parameters/pallas_call | solution.py:102
  3.2 2.2 %conv_norm.2 = (bf16[256,384]{1,0:T(8,128)(2,1)S(1)}, bf16[256,384]{1,0:T(8,128)(2,1)S(1)}, f32[256,128]{1,0:T(8,128)S(1)}) custom-call(s32[2]{0:T(128)S(1)} %pad_add_fusion.2.sel_ref, bf16[16,16,384]{2,1,0:T(8,128)(2,1)S(1)} %get-tuple-element.179.x_ref.refs_1_.refs_2_, f32[56,384]{1,0:T(8,128)S(1)} %parameters.1.rest_0_.refs_3_.refs_12_, ...), custom_call_target="tpu_custom_call" | custom-call | flops 2200000000 | bytes 7200000 | tf_op jit(solution)/shard_map/conv_norm/pallas_call | solution.py:145
  5.4 5.2 %pair_forward.2 = (bf16[16,16,384]{2,1,0:T(8,128)(2,1)S(1)}, bf16[16,16,384]{2,1,0:T(8,128)(2,1)S(1)}, bf16[256,384]{1,0:T(8,128)(2,1)S(1)}, f32[256,128]{1,0:T(...) custom-call(s32[5]{0:T(128)S(1)} %stack.50.refs_0_, ...), custom_call_target="tpu_custom_call" | custom-call | flops 8249999872 | bytes 27000000 | tf_op jit(solution)/shard_map/pair_forward/pallas_call | solution.py:625
  10.7 4.7 %collective-permute-start.5 = (bf16[16,16,384]{2,1,0:T(8,128)(2,1)S(1)}, bf16[16,16,384]{2,1,0:T(8,128)(2,1)S(1)}, u32[]{:S(2)}, u32[]{:S(2)}) collective-permute-start(bf16[16,16,384]{2,1,0:T(8,128)(2,1)S(1)} %get-tuple-element.105), channel_id=1, source_target_pairs={{0,2},{1,3},{4,6},{5,7},{8,10},{9,11},{12,14},{13,15},{16,18},{17,... | collective-permute-start | bytes 589832 | tf_op jit(solution)/shard_map/ppermute | solution.py:1171
  15.4 2.2 %conv_norm.3 = (bf16[256,384]{1,0:T(8,128)(2,1)S(1)}, bf16[256,384]{1,0:T(8,128)(2,1)S(1)}, f32[256,128]{1,0:T(8,128)S(1)}) custom-call(s32[2]{0:T(128)S(1)} %pad_add_fusion.1.sel_ref, bf16[16,16,384]{2,1,0:T(8,128)(2,1)S(1)} %get-tuple-element.180.x_ref.refs_1_.refs_2_, f32[56,384]{1,0:T(8,128)S(1)} %parameters.1.rest_0_.refs_3_.refs_12_, ...), custom_call_target="tpu_custom_call" | custom-call | flops 2200000000 | bytes 7200000 | tf_op jit(solution)/shard_map/conv_norm/pallas_call | solution.py:145
  17.6 5.2 %pair_forward.3 = (bf16[16,16,384]{2,1,0:T(8,128)(2,1)S(1)}, bf16[16,16,384]{2,1,0:T(8,128)(2,1)S(1)}, bf16[256,384]{1,0:T(8,128)(2,1)S(1)}, f32[256,128]{1,0:T(...) custom-call(s32[5]{0:T(128)S(1)} %stack.51.refs_0_, ...), custom_call_target="tpu_custom_call" | custom-call | flops 8249999872 | bytes 27000000 | tf_op jit(solution)/shard_map/pair_forward/pallas_call | solution.py:625
  22.8 1.3 %collective-permute-start.3 = (bf16[16,16,384]{2,1,0:T(8,128)(2,1)S(1)}, bf16[16,16,384]{2,1,0:T(8,128)(2,1)S(1)}, u32[]{:S(2)}, u32[]{:S(2)}) collective-permute-start(bf16[16,16,384]{2,1,0:T(8,128)(2,1)S(1)} %get-tuple-element.94), channel_id=1, source_target_pairs={{0,2},{1,3},{4,6},{5,7},{8,10},{9,11},{12,14},{13,15},{16,18},{17,... | collective-permute-start | bytes 589832 | tf_op jit(solution)/shard_map/ppermute | solution.py:1171
  24.1 0.7 pair_map.3
  24.9 1.3 %collective-permute-start.6 = (bf16[16,16,384]{2,1,0:T(8,128)(2,1)S(1)}, bf16[16,16,384]{2,1,0:T(8,128)(2,1)S(1)}, u32[]{:S(2)}, u32[]{:S(2)}) collective-permute-start(bf16[16,16,384]{2,1,0:T(8,128)(2,1)S(1)} %get-tuple-element.106), channel_id=1, source_target_pairs={{2,0},{3,1},{6,4},{7,5},{10,8},{11,9},{14,12},{15,13},{18,16},{19,... | collective-permute-start | bytes 589832 | tf_op jit(solution)/shard_map/ppermute | solution.py:1171
  26.2 2.5 %collective-permute-done.3.refs_1_.refs_15_ = bf16[16,16,384]{2,1,0:T(8,128)(2,1)S(1)} collective-permute-done((bf16[16,16,384]{2,1,0:T(8,128)(2,1)S(1)}, bf16[16,16,384]{2,1,0:T(8,128)(2,1)S(1)}, u32[]{:S(2)}, u32[]{:S(2)}) %collective-permute-start.3) | collective-permute-done | bytes 196640 | tf_op jit(solution)/shard_map/ppermute | solution.py:1171
  28.6 0.9 pair_map.2
  29.5 1.3 %collective-permute-start.4 = (bf16[16,16,384]{2,1,0:T(8,128)(2,1)S(1)}, bf16[16,16,384]{2,1,0:T(8,128)(2,1)S(1)}, u32[]{:S(2)}, u32[]{:S(2)}) collective-permute-start(bf16[16,16,384]{2,1,0:T(8,128)(2,1)S(1)} %get-tuple-element.95), channel_id=1, source_target_pairs={{2,0},{3,1},{6,4},{7,5},{10,8},{11,9},{14,12},{15,13},{18,16},{19,... | collective-permute-start | bytes 589832 | tf_op jit(solution)/shard_map/ppermute | solution.py:1171
  30.8 0.9 pair_grads.1
  31.7 7.4 %collective-permute-done.6.refs_1_ = bf16[16,16,384]{2,1,0:T(8,128)(2,1)S(1)} collective-permute-done((bf16[16,16,384]{2,1,0:T(8,128)(2,1)S(1)}, bf16[16,16,384]{2,1,0:T(8,128)(2,1)S(1)}, u32[]{:S(2)}, u32[]{:S(2)}) %collective-permute-start.6) | collective-permute-done | bytes 196640 | tf_op jit(solution)/shard_map/ppermute | solution.py:1171
  39.1 9.7 %pair_back.2 = (bf16[384,768]{1,0:T(8,128)(2,1)}, bf16[384,768]{1,0:T(8,128)(2,1)}, bf16[384,768]{1,0:T(8,128)(2,1)}, bf16[384,768]{1,0:T(8,128)(2,1)}, f32[64,384]{1,0:T(8,128)S(1)}, /*index=5*/f32[64,384]{1,0:T(8,128)S(1)}) custom-call(s32[5]{0:T(128)S(1)} %stack.50.refs_0_, bf16[16,16,384]{2,1,0:T(8,128)(2,1)S(1)} %collective-permute-done.6.refs_1_, ...), custom_call_target="tpu_custom_call" | custom-call | flops 9900000256 | bytes 32400000 | tf_op jit(solution)/shard_map/pair_back/pallas_call | solution.py:625
  48.7 2.8 %collective-permute-done.4.refs_1_ = bf16[16,16,384]{2,1,0:T(8,128)(2,1)S(1)} collective-permute-done((bf16[16,16,384]{2,1,0:T(8,128)(2,1)S(1)}, bf16[16,16,384]{2,1,0:T(8,128)(2,1)S(1)}, u32[]{:S(2)}, u32[]{:S(2)}) %collective-permute-start.4) | collective-permute-done | bytes 196640 | tf_op jit(solution)/shard_map/ppermute | solution.py:1171
  51.6 10.3 %pair_back.3 = (bf16[384,768]{1,0:T(8,128)(2,1)}, bf16[384,768]{1,0:T(8,128)(2,1)}, bf16[384,768]{1,0:T(8,128)(2,1)}, bf16[384,768]{1,0:T(8,128)(2,1)}, bf16[384,128]{1,0:T(8,128)(2,1)S(1)}) custom-call(s32[5]{0:T(128)S(1)} %stack.50.refs_0_, bf16[16,16,384]{2,1,0:T(8,128)(2,1)S(1)} %collective-permute-done.4.refs_1_, ...), custom_call_target="tpu_custom_call" | custom-call | flops 9900000256 | bytes 32400000 | tf_op jit(solution)/shard_map/pair_back/pallas_call | solution.py:625
  62.4 1.1 %brought.1 = bf16[384,768]{1,0:T(8,128)(2,1)S(1)} custom-call(bf16[384,768]{1,0:T(8,128)(2,1)} %get-tuple-element.153.source_ref), custom_call_target="tpu_custom_call" | custom-call | flops 1210000000 | bytes 3960000 | tf_op jit(solution)/shard_map/brought/pallas_call | solution.py:971
  63.5 0.6 collective-permute-done.7
  64.3 1.6 %collective-permute-start.8 = (bf16[4,48,896]{2,1,0:T(8,128)(2,1)S(1)}, bf16[4,48,896]{2,1,0:T(8,128)(2,1)S(1)}, u32[]{:S(2)}, u32[]{:S(2)}) collective-permute-start(bf16[4,48,896]{2,1,0:T(8,128)(2,1)S(1)} %get-tuple-element.157), channel_id=1, source_target_pairs={{0,4},{1,5},{2,6},{3,7},{4,0},{5,1},{6,2},{7,3},{8,12},{9,13},{10,... | collective-permute-start | bytes 1032200 | tf_op jit(solution)/shard_map/ppermute | solution.py:1166
  65.9 0.7 split_depths.1
  66.6 2.7 %collective-permute-start.13 = (bf16[2,48,768]{2,1,0:T(8,128)(2,1)S(1)}, bf16[2,48,768]{2,1,0:T(8,128)(2,1)S(1)}, u32[]{:S(2)}, u32[]{:S(2)}) collective-permute-start(bf16[2,48,768]{2,1,0:T(8,128)(2,1)S(1)} %get-tuple-element.165), channel_id=1, source_target_pairs={{0,16},{1,17},{2,18},{3,19},{4,20},{5,21},{6,22},{7,23},{8,24},{9,... | collective-permute-start | bytes 442376 | tf_op jit(solution)/shard_map/ppermute | solution.py:1166
  69.3 1.3 %collective-permute-start.14 = (bf16[2,48,768]{2,1,0:T(8,128)(2,1)S(1)}, bf16[2,48,768]{2,1,0:T(8,128)(2,1)S(1)}, u32[]{:S(2)}, u32[]{:S(2)}) collective-permute-start(bf16[2,48,768]{2,1,0:T(8,128)(2,1)S(1)} %get-tuple-element.166), channel_id=1, source_target_pairs={{0,24},{1,25},{2,26},{3,27},{4,28},{5,29},{6,30},{7,31},{8,16},{9,... | collective-permute-start | bytes 442376 | tf_op jit(solution)/shard_map/ppermute | solution.py:1166
  70.8 3.6 %collective-permute-done.8.refs_2_ = bf16[4,48,896]{2,1,0:T(8,128)(2,1)S(1)} collective-permute-done((bf16[4,48,896]{2,1,0:T(8,128)(2,1)S(1)}, bf16[4,48,896]{2,1,0:T(8,128)(2,1)S(1)}, u32[]{:S(2)}, u32[]{:S(2)}) %collective-permute-start.8) | collective-permute-done | bytes 344096 | tf_op jit(solution)/shard_map/ppermute | solution.py:1166
  74.4 0.6 to_depths.1
  75.1 2.7 %collective-permute-start.10 = (bf16[48,896]{1,0:T(8,128)(2,1)S(1)}, bf16[48,896]{1,0:T(8,128)(2,1)S(1)}, u32[]{:S(2)}, u32[]{:S(2)}) collective-permute-start(bf16[48,896]{1,0:T(8,128)(2,1)S(1)} %get-tuple-element.160), channel_id=1, source_target_pairs={{0,16},{1,17},{2,18},{3,19},{4,20},{5,21},{6,22},{7,23},{8,24},{9,... | collective-permute-start | bytes 258056 | tf_op jit(solution)/shard_map/ppermute | solution.py:1166
  77.7 1.3 %collective-permute-start.11 = (bf16[48,896]{1,0:T(8,128)(2,1)S(1)}, bf16[48,896]{1,0:T(8,128)(2,1)S(1)}, u32[]{:S(2)}, u32[]{:S(2)}) collective-permute-start(bf16[48,896]{1,0:T(8,128)(2,1)S(1)} %get-tuple-element.161), channel_id=1, source_target_pairs={{0,24},{1,25},{2,26},{3,27},{4,28},{5,29},{6,30},{7,31},{8,16},{9,... | collective-permute-start | bytes 258056 | tf_op jit(solution)/shard_map/ppermute | solution.py:1166
  79.1 2.6 %collective-permute-done.13.refs_2_ = bf16[2,48,768]{2,1,0:T(8,128)(2,1)S(1)} collective-permute-done((bf16[2,48,768]{2,1,0:T(8,128)(2,1)S(1)}, bf16[2,48,768]{2,1,0:T(8,128)(2,1)S(1)}, u32[]{:S(2)}, u32[]{:S(2)}) %collective-permute-start.13) | collective-permute-done | bytes 147488 | tf_op jit(solution)/shard_map/ppermute | solution.py:1166
  82.2 4.0 %collective-permute-done.16.refs_6_ = bf16[48,768]{1,0:T(8,128)(2,1)S(1)} collective-permute-done((bf16[48,768]{1,0:T(8,128)(2,1)S(1)}, bf16[48,768]{1,0:T(8,128)(2,1)S(1)}, u32[]{:S(2)}, u32[]{:S(2)}) %collective-permute-start.16) | collective-permute-done | bytes 73760 | tf_op jit(solution)/shard_map/ppermute | solution.py:1166
  86.2 3.0 %collective-permute-done.10.refs_3_ = bf16[48,896]{1,0:T(8,128)(2,1)S(1)} collective-permute-done((bf16[48,896]{1,0:T(8,128)(2,1)S(1)}, bf16[48,896]{1,0:T(8,128)(2,1)S(1)}, u32[]{:S(2)}, u32[]{:S(2)}) %collective-permute-start.10) | collective-permute-done | bytes 86048 | tf_op jit(solution)/shard_map/ppermute | solution.py:1166
  89.3 1.3 %collective-permute-done.17.refs_2_ = bf16[48,896]{1,0:T(8,128)(2,1)S(1)} collective-permute-done((bf16[48,896]{1,0:T(8,128)(2,1)S(1)}, bf16[48,896]{1,0:T(8,128)(2,1)S(1)}, u32[]{:S(2)}, u32[]{:S(2)}) %collective-permute-start.17) | collective-permute-done | bytes 86048 | tf_op jit(solution)/shard_map/ppermute | solution.py:1166
  90.6 0.8 final.1
  (38 shorter events, 3.1 us)
Async XLA Ops:
  0.6 1.6 %copy-start.3 = (bf16[1,384,768]{2,1,0:T(8,128)(2,1)S(1)}, bf16[1,384,768]{2,1,0:T(8,128)(2,1)}, u32[]{:S(2)}) copy-start(bf16[1,384,768]{2,1,0:T(8,128)(2,1)} %param.11) | copy-start | bytes 1769476
  0.6 1.7 %copy-start.4 = (bf16[1,768,384]{2,1,0:T(8,128)(2,1)S(1)}, bf16[1,768,384]{2,1,0:T(8,128)(2,1)}, u32[]{:S(2)}) copy-start(bf16[1,768,384]{2,1,0:T(8,128)(2,1)} %param.12) | copy-start | bytes 1769476
  0.7 2.4 %copy-start.1 = (bf16[4,16,16,384]{3,2,1,0:T(8,128)(2,1)S(1)}, bf16[4,16,16,384]{3,2,1,0:T(8,128)(2,1)}, u32[]{:S(2)}) copy-start(bf16[4,16,16,384]{3,2,1,0:T(8,128)(2,1)} %param.7) | copy-start | bytes 2359300
  1.7 1.3 %copy-start.2 = (bf16[4,16,16,384]{3,2,1,0:T(8,128)(2,1)S(1)}, bf16[4,16,16,384]{3,2,1,0:T(8,128)(2,1)}, u32[]{:S(2)}) copy-start(bf16[4,16,16,384]{3,2,1,0:T(8,128)(2,1)} %param.8) | copy-start | bytes 2359300
  1.8 1.5 %collective-permute-start = (f32[56,384]{1,0:T(8,128)S(1)}, f32[56,384]{1,0:T(8,128)S(1)}, u32[]{:S(2)}, u32[]{:S(2)}) collective-permute-start(f32[56,384]{1,0:T(8,128)S(1)} %parameters.1.rest_0_.refs_3_.refs_12_), channel_id=1, source_target_pairs={{0,1},{1,0},{2,3},{3,2},{4,5},{5,4},{6,7},{7,6},{8,9},{9,8},{10,11... | collective-permute-start | bytes 258056 | tf_op jit(solution)/shard_map/ppermute | solution.py:1166
  2.3 3.1 %collective-permute-start.1 = (bf16[384,768]{1,0:T(8,128)(2,1)S(1)}, bf16[384,768]{1,0:T(8,128)(2,1)}, u32[]{:S(2)}, u32[]{:S(2)}) collective-permute-start(bf16[384,768]{1,0:T(8,128)(2,1)S(1)} %bitcast.37), channel_id=1, source_target_pairs={{0,1},{1,0},{2,3},{3,2},{4,5},{5,4},{6,7},{7,6},{8,9},{9,8},{10,11... | collective-permute-start | bytes 1769480 | tf_op jit(solution)/shard_map/ppermute | solution.py:1166
  2.4 3.1 %collective-permute-start.2 = (bf16[768,384]{1,0:T(8,128)(2,1)S(1)}, bf16[768,384]{1,0:T(8,128)(2,1)}, u32[]{:S(2)}, u32[]{:S(2)}) collective-permute-start(bf16[768,384]{1,0:T(8,128)(2,1)S(1)} %bitcast.44), channel_id=1, source_target_pairs={{0,1},{1,0},{2,3},{3,2},{4,5},{5,4},{6,7},{7,6},{8,9},{9,8},{10,11... | collective-permute-start | bytes 1769480 | tf_op jit(solution)/shard_map/ppermute | solution.py:1166
  10.7 13.5 %collective-permute-start.5 = (bf16[16,16,384]{2,1,0:T(8,128)(2,1)S(1)}, bf16[16,16,384]{2,1,0:T(8,128)(2,1)S(1)}, u32[]{:S(2)}, u32[]{:S(2)}) collective-permute-start(bf16[16,16,384]{2,1,0:T(8,128)(2,1)S(1)} %get-tuple-element.105), channel_id=1, source_target_pairs={{0,2},{1,3},{4,6},{5,7},{8,10},{9,11},{12,14},{13,15},{16,18},{17,... | collective-permute-start | bytes 589832 | tf_op jit(solution)/shard_map/ppermute | solution.py:1171
  22.8 5.8 %collective-permute-start.3 = (bf16[16,16,384]{2,1,0:T(8,128)(2,1)S(1)}, bf16[16,16,384]{2,1,0:T(8,128)(2,1)S(1)}, u32[]{:S(2)}, u32[]{:S(2)}) collective-permute-start(bf16[16,16,384]{2,1,0:T(8,128)(2,1)S(1)} %get-tuple-element.94), channel_id=1, source_target_pairs={{0,2},{1,3},{4,6},{5,7},{8,10},{9,11},{12,14},{13,15},{16,18},{17,... | collective-permute-start | bytes 589832 | tf_op jit(solution)/shard_map/ppermute | solution.py:1171
  24.9 14.2 %collective-permute-start.6 = (bf16[16,16,384]{2,1,0:T(8,128)(2,1)S(1)}, bf16[16,16,384]{2,1,0:T(8,128)(2,1)S(1)}, u32[]{:S(2)}, u32[]{:S(2)}) collective-permute-start(bf16[16,16,384]{2,1,0:T(8,128)(2,1)S(1)} %get-tuple-element.106), channel_id=1, source_target_pairs={{2,0},{3,1},{6,4},{7,5},{10,8},{11,9},{14,12},{15,13},{18,16},{19,... | collective-permute-start | bytes 589832 | tf_op jit(solution)/shard_map/ppermute | solution.py:1171
  29.5 22.1 %collective-permute-start.4 = (bf16[16,16,384]{2,1,0:T(8,128)(2,1)S(1)}, bf16[16,16,384]{2,1,0:T(8,128)(2,1)S(1)}, u32[]{:S(2)}, u32[]{:S(2)}) collective-permute-start(bf16[16,16,384]{2,1,0:T(8,128)(2,1)S(1)} %get-tuple-element.95), channel_id=1, source_target_pairs={{2,0},{3,1},{6,4},{7,5},{10,8},{11,9},{14,12},{15,13},{18,16},{19,... | collective-permute-start | bytes 589832 | tf_op jit(solution)/shard_map/ppermute | solution.py:1171
  61.8 2.3 %collective-permute-start.7 = (bf16[384,768]{1,0:T(8,128)(2,1)}, bf16[384,768]{1,0:T(8,128)(2,1)S(1)}, u32[]{:S(2)}, u32[]{:S(2)}) collective-permute-start(bf16[384,768]{1,0:T(8,128)(2,1)} %get-tuple-element.154), channel_id=1, source_target_pairs={{0,1},{1,0},{2,3},{3,2},{4,5},{5,4},{6,7},{7,6},{8,9},{9,8},{10,11... | collective-permute-start | bytes 1769480 | tf_op jit(solution)/shard_map/ppermute | solution.py:1166
  61.9 4.0 %collective-permute-start.12 = (bf16[384,768]{1,0:T(8,128)(2,1)}, bf16[384,768]{1,0:T(8,128)(2,1)S(1)}, u32[]{:S(2)}, u32[]{:S(2)}) collective-permute-start(bf16[384,768]{1,0:T(8,128)(2,1)} %get-tuple-element.163), channel_id=1, source_target_pairs={{0,1},{1,0},{2,3},{3,2},{4,5},{5,4},{6,7},{7,6},{8,9},{9,8},{10,11... | collective-permute-start | bytes 1769480 | tf_op jit(solution)/shard_map/ppermute | solution.py:1166
  64.1 1.8 %copy-start = (bf16[384,768]{1,0:T(8,128)(2,1)S(1)}, bf16[384,768]{1,0:T(8,128)(2,1)}, u32[]{:S(2)}) copy-start(bf16[384,768]{1,0:T(8,128)(2,1)} %get-tuple-element.162) | copy-start | bytes 1769476
  64.3 10.2 %collective-permute-start.8 = (bf16[4,48,896]{2,1,0:T(8,128)(2,1)S(1)}, bf16[4,48,896]{2,1,0:T(8,128)(2,1)S(1)}, u32[]{:S(2)}, u32[]{:S(2)}) collective-permute-start(bf16[4,48,896]{2,1,0:T(8,128)(2,1)S(1)} %get-tuple-element.157), channel_id=1, source_target_pairs={{0,4},{1,5},{2,6},{3,7},{4,0},{5,1},{6,2},{7,3},{8,12},{9,13},{10,... | collective-permute-start | bytes 1032200 | tf_op jit(solution)/shard_map/ppermute | solution.py:1166
  66.6 15.1 %collective-permute-start.13 = (bf16[2,48,768]{2,1,0:T(8,128)(2,1)S(1)}, bf16[2,48,768]{2,1,0:T(8,128)(2,1)S(1)}, u32[]{:S(2)}, u32[]{:S(2)}) collective-permute-start(bf16[2,48,768]{2,1,0:T(8,128)(2,1)S(1)} %get-tuple-element.165), channel_id=1, source_target_pairs={{0,16},{1,17},{2,18},{3,19},{4,20},{5,21},{6,22},{7,23},{8,24},{9,... | collective-permute-start | bytes 442376 | tf_op jit(solution)/shard_map/ppermute | solution.py:1166
  69.3 12.4 %collective-permute-start.14 = (bf16[2,48,768]{2,1,0:T(8,128)(2,1)S(1)}, bf16[2,48,768]{2,1,0:T(8,128)(2,1)S(1)}, u32[]{:S(2)}, u32[]{:S(2)}) collective-permute-start(bf16[2,48,768]{2,1,0:T(8,128)(2,1)S(1)} %get-tuple-element.166), channel_id=1, source_target_pairs={{0,24},{1,25},{2,26},{3,27},{4,28},{5,29},{6,30},{7,31},{8,16},{9,... | collective-permute-start | bytes 442376 | tf_op jit(solution)/shard_map/ppermute | solution.py:1166
  70.6 11.1 %collective-permute-start.15 = (bf16[2,48,768]{2,1,0:T(8,128)(2,1)S(1)}, bf16[2,48,768]{2,1,0:T(8,128)(2,1)S(1)}, u32[]{:S(2)}, u32[]{:S(2)}) collective-permute-start(bf16[2,48,768]{2,1,0:T(8,128)(2,1)S(1)} %get-tuple-element.167), channel_id=1, source_target_pairs={{0,8},{1,9},{2,10},{3,11},{4,12},{5,13},{6,14},{7,15},{8,0},{9,1},... | collective-permute-start | bytes 442376 | tf_op jit(solution)/shard_map/ppermute | solution.py:1166
  75.1 14.1 %collective-permute-start.10 = (bf16[48,896]{1,0:T(8,128)(2,1)S(1)}, bf16[48,896]{1,0:T(8,128)(2,1)S(1)}, u32[]{:S(2)}, u32[]{:S(2)}) collective-permute-start(bf16[48,896]{1,0:T(8,128)(2,1)S(1)} %get-tuple-element.160), channel_id=1, source_target_pairs={{0,16},{1,17},{2,18},{3,19},{4,20},{5,21},{6,22},{7,23},{8,24},{9,... | collective-permute-start | bytes 258056 | tf_op jit(solution)/shard_map/ppermute | solution.py:1166
  77.7 11.5 %collective-permute-start.11 = (bf16[48,896]{1,0:T(8,128)(2,1)S(1)}, bf16[48,896]{1,0:T(8,128)(2,1)S(1)}, u32[]{:S(2)}, u32[]{:S(2)}) collective-permute-start(bf16[48,896]{1,0:T(8,128)(2,1)S(1)} %get-tuple-element.161), channel_id=1, source_target_pairs={{0,24},{1,25},{2,26},{3,27},{4,28},{5,29},{6,30},{7,31},{8,16},{9,... | collective-permute-start | bytes 258056 | tf_op jit(solution)/shard_map/ppermute | solution.py:1166
  81.7 7.5 %collective-permute-start.9 = (bf16[48,896]{1,0:T(8,128)(2,1)S(1)}, bf16[48,896]{1,0:T(8,128)(2,1)S(1)}, u32[]{:S(2)}, u32[]{:S(2)}) collective-permute-start(bf16[48,896]{1,0:T(8,128)(2,1)S(1)} %get-tuple-element.159), channel_id=1, source_target_pairs={{0,8},{1,9},{2,10},{3,11},{4,12},{5,13},{6,14},{7,15},{8,0},{9,1},... | collective-permute-start | bytes 258056 | tf_op jit(solution)/shard_map/ppermute | solution.py:1166
  81.8 4.4 %collective-permute-start.16 = (bf16[48,768]{1,0:T(8,128)(2,1)S(1)}, bf16[48,768]{1,0:T(8,128)(2,1)S(1)}, u32[]{:S(2)}, u32[]{:S(2)}) collective-permute-start(bf16[48,768]{1,0:T(8,128)(2,1)S(1)} %get-tuple-element.169), channel_id=1, source_target_pairs={{0,4},{1,5},{2,6},{3,7},{4,0},{5,1},{6,2},{7,3},{8,12},{9,13},{10,... | collective-permute-start | bytes 221192 | tf_op jit(solution)/shard_map/ppermute | solution.py:1166
  89.3 1.3 %collective-permute-start.17 = (bf16[48,896]{1,0:T(8,128)(2,1)S(1)}, bf16[48,896]{1,0:T(8,128)(2,1)S(1)}, u32[]{:S(2)}, u32[]{:S(2)}) collective-permute-start(bf16[48,896]{1,0:T(8,128)(2,1)S(1)} %get-tuple-element.171), channel_id=1, source_target_pairs={{0,1},{1,0},{2,3},{3,2},{4,5},{5,4},{6,7},{7,6},{8,9},{9,8},{10,11... | collective-permute-start | bytes 258056 | tf_op jit(solution)/shard_map/ppermute | solution.py:1166
